TPU v7x, 256 devices: a whole 4x4x8 slice. The times are simulated.
256 devices in a mesh: tm: 16 (over y, x), rows: 8 (over z), sect: 2 (over core).
Axes of the slice: x: 4, y: 4, z: 8, core: 2. Of those that a mesh axis runs over, the one named last changes fastest.
Arguments:
- activations: bfloat16 [64, 64, 64, 128], P('tm', 'rows', 'sect'), as said below
- group_norm_gain: float32 [128], replicated, may hold values from 0.1 to 1.9
- group_norm_bias: float32 [128], replicated, may hold values from -3 to 3
- upstream: bfloat16 [64, 64, 64, 128], P('tm', 'rows', 'sect'), may hold values from -6 to 6
- kernel: bfloat16 [3, 3, 3, 128, 128], replicated, may hold values from -0.109375 to 0.109375
Outputs:
- input_gradient: bfloat16 [64, 64, 64, 128], P('tm', 'rows', 'sect')
- gain_grad: float32 [128], replicated
- bias_grad: float32 [128], replicated
- weight_grad: float32 [3, 3, 3, 128, 128], P(None, None, None, None, 'tm')
Inputs may be any that keep to these rules, and one draw needn't show every extreme that they name: activations vary in scale over frames, rows and channels and have channel offsets.
All inputs are finite; a program needn't handle non-finite values.
Results may differ from a plain program's by a relative error of at most 0.003.
Values may be sent and summed in bfloat16 or wider, within the bound.
No kernel may reach another device: no remote copies, remote signals or barrier semaphores. Data moves between devices by JAX's collectives and lax.ppermute only.
A program may use at most 64 MiB of HBM per device.

v0:
```python
import jax
import jax.numpy as jnp
from jax import lax
from jax.sharding import PartitionSpec as P

GROUPS = 32


def shifted(value, axis, steps):
    count = lax.axis_size(axis)
    leading, last = (max(0, -steps), min(count, count - steps))
    return lax.ppermute(value, axis, [(source, source + steps) for source in range(leading, last)])


def extended(cells, sides, width):
    for axis, dim in sides:
        count = lax.axis_size(axis)
        ends = count - 1
        head = lax.slice_in_dim(cells, 0, width, axis=dim)
        tail = lax.slice_in_dim(cells, cells.shape[dim] - width, cells.shape[dim], axis=dim)
        cells = jnp.concatenate(
            [
                lax.ppermute(tail, axis, [(i, (i + 1) % count) for i in range(ends)]),
                cells,
                lax.ppermute(head, axis, [((i + 1) % count, i) for i in range(ends)]),
            ],
            axis=dim,
        )
    return cells


def local(activations, group_norm_gain, group_norm_bias, upstream, kernel):
    frames, height, columns, channels = activations.shape
    group_size = channels // GROUPS
    total_cells = (
        frames
        * height
        * columns
        * lax.axis_size("tm")
        * lax.axis_size("rows")
        * lax.axis_size("sect")
    )
    counted = float(total_cells * group_size)
    time_first = lax.axis_index("tm") == 0
    row_first = lax.axis_index("rows") == 0
    row_last = lax.axis_index("rows") == lax.axis_size("rows") - 1
    col_first = lax.axis_index("sect") == 0
    col_last = lax.axis_index("sect") == lax.axis_size("sect") - 1
    input_tensor = activations.astype(jnp.float32)
    channel_total, channel_square = lax.psum(
        (
            jnp.sum(input_tensor, axis=(0, 1, 2)),
            jnp.sum(input_tensor * input_tensor, axis=(0, 1, 2)),
        ),
        ("tm", "rows", "sect"),
    )
    group_mean = jnp.sum(channel_total.reshape(GROUPS, group_size), axis=1) / counted
    group_square = jnp.sum(channel_square.reshape(GROUPS, group_size), axis=1) / counted
    group_rstd = lax.rsqrt(group_square - group_mean * group_mean + 1e-06)
    channel_mean = jnp.repeat(group_mean, group_size)
    channel_inverse_deviation = jnp.repeat(group_rstd, group_size)
    normalized_input = (input_tensor - channel_mean) * channel_inverse_deviation
    preactivation = normalized_input * group_norm_gain + group_norm_bias
    hidden = jax.nn.silu(preactivation).astype(jnp.bfloat16)
    earlier = shifted(hidden[frames - 2 :], "tm", 1)
    earlier = jnp.where(time_first, jnp.concatenate([hidden[:1], hidden[:1]], axis=0), earlier)
    hidden_pad = extended(jnp.concatenate([earlier, hidden], axis=0), (("rows", 1), ("sect", 2)), 1)
    hidden_pad = hidden_pad.at[:, 0].set(jnp.where(row_first, hidden_pad[:, 1], hidden_pad[:, 0]))
    hidden_pad = hidden_pad.at[:, -1].set(jnp.where(row_last, hidden_pad[:, -2], hidden_pad[:, -1]))
    hidden_pad = hidden_pad.at[:, :, 0].set(
        jnp.where(col_first, hidden_pad[:, :, 1], hidden_pad[:, :, 0])
    )
    hidden_pad = hidden_pad.at[:, :, -1].set(
        jnp.where(col_last, hidden_pad[:, :, -2], hidden_pad[:, :, -1])
    )
    later = shifted(upstream[:2], "tm", -1)
    grad_rimmed = extended(
        jnp.concatenate([upstream, later], axis=0), (("rows", 1), ("sect", 2)), 1
    )
    grad_pad = jnp.pad(grad_rimmed, ((2, 0), (1, 1), (1, 1), (0, 0)))
    flat_grad = upstream.reshape(-1, channels)
    padded_grad = jnp.zeros(((frames + 2) * (height + 2) * (columns + 2), channels), jnp.float32)
    kernel_terms = []
    for tap_time in range(3):
        for tap_row in range(3):
            grad_cat = jnp.concatenate(
                [
                    grad_pad[
                        2 - tap_time : 2 - tap_time + frames + 2,
                        2 - tap_row : 2 - tap_row + height + 2,
                        2 - tap_col : 2 - tap_col + columns + 2,
                    ].reshape(-1, channels)
                    for tap_col in range(3)
                ],
                axis=1,
            )
            kernel_cat = jnp.transpose(kernel[tap_time, tap_row], (0, 2, 1)).reshape(
                3 * channels, channels
            )
            padded_grad = padded_grad + jnp.dot(
                grad_cat, kernel_cat, preferred_element_type=jnp.float32
            )
            hidden_cat = jnp.concatenate(
                [
                    hidden_pad[
                        tap_time : tap_time + frames,
                        tap_row : tap_row + height,
                        tap_col : tap_col + columns,
                    ].reshape(-1, channels)
                    for tap_col in range(3)
                ],
                axis=1,
            )
            product = lax.dot_general(
                hidden_cat, flat_grad, (((0,), (0,)), ((), ())), preferred_element_type=jnp.float32
            )
            kernel_terms.append(product.reshape(3, channels, channels))
    kernel_local = jnp.stack(kernel_terms).reshape(3, 3, 3, channels, channels)
    padded_grad = padded_grad.reshape(frames + 2, height + 2, columns + 2, channels)
    folded = padded_grad[2:]
    folded = folded.at[0].add(jnp.where(time_first, padded_grad[0] + padded_grad[1], 0.0))
    folded = folded.at[:, 1].add(jnp.where(row_first, folded[:, 0], 0.0))
    folded = folded.at[:, -2].add(jnp.where(row_last, folded[:, -1], 0.0))[:, 1:-1]
    folded = folded.at[:, :, 1].add(jnp.where(col_first, folded[:, :, 0], 0.0))
    hidden_grad = folded.at[:, :, -2].add(jnp.where(col_last, folded[:, :, -1], 0.0))[:, :, 1:-1]
    sigmoid = jax.nn.sigmoid(preactivation)
    activation_gradient = hidden_grad * sigmoid * (1.0 + preactivation * (1.0 - sigmoid))
    bias_sum, gain_total_accum = lax.psum(
        (
            jnp.sum(activation_gradient, axis=(0, 1, 2)),
            jnp.sum(activation_gradient * normalized_input, axis=(0, 1, 2)),
        ),
        ("tm", "rows", "sect"),
    )
    leading_average = jnp.repeat(
        jnp.sum((group_norm_gain * bias_sum).reshape(GROUPS, group_size), axis=1) / counted,
        group_size,
    )
    trailing_average = jnp.repeat(
        jnp.sum((group_norm_gain * gain_total_accum).reshape(GROUPS, group_size), axis=1) / counted,
        group_size,
    )
    input_gradient = (
        channel_inverse_deviation
        * (
            activation_gradient * group_norm_gain
            - leading_average
            - normalized_input * trailing_average
        )
    ).astype(jnp.bfloat16)
    scaling = float(total_cells) ** (-0.5)
    band_sum = lax.psum(kernel_local, ("rows", "sect"))
    kernel_share = lax.psum_scatter(band_sum, "tm", scatter_dimension=4, tiled=True)
    return (input_gradient, gain_total_accum * scaling, bias_sum * scaling, kernel_share * scaling)


def solution(mesh):
    return jax.shard_map(
        local,
        mesh=mesh,
        in_specs=(P("tm", "rows", "sect", None), P(), P(), P("tm", "rows", "sect", None), P()),
        out_specs=(P("tm", "rows", "sect", None), P(), P(), P(None, None, None, None, "tm")),
        check_vma=False,
    )
```

profile of v0, /device:TPU:1, one launch (start us, length us, event | category | flops | bytes accessed | tf_op | source)
XLA Modules:
  0.0 423.8 jit_solution(16854062007852657966)
XLA Ops:
  7.2 1.0 slice.516
  8.2 1.3 collective-permute-start
  9.5 1.3 fusion.93
  10.8 3.7 collective-permute-done
  14.5 4.3 %collective-permute-start.1 = (bf16[6,1,32,128]{3,2,1,0:T(8,128)(2,1)S(1)}, bf16[6,1,32,128]{3,2,1,0:T(8,128)(2,1)S(1)}, u32[]{:S(2)}, u32[]{:S(2)}) collective-permute-start(bf16[6,1,32,128]{3,2,1,0:T(8,128)(2,1)S(1)} %get-tuple-element.189), channel_id=1, source_target_pairs={{0,2},{2,4},{4,6},{6,8},{8,10},{10,12},{12,14},{1,3},{3,5},{5,7},{... | collective-permute-start | bytes 147464 | tf_op jit(solution)/shard_map/ppermute | solution.py:23
  18.9 1.3 collective-permute-start.2
  20.5 82.9 %all-reduce.2 = (f32[32,4]{1,0:T(8,128)S(1)}, f32[32,4]{1,0:T(8,128)S(1)}) all-reduce(f32[32,4]{1,0:T(8,128)S(1)} %reshape.602, f32[32,4]{1,0:T(8,128)S(1)} %reshape.601), channel_id=1, replica_groups=mesh['tm'=16,'rows'=8,'sect'=2] {'tm','rows','sect'}, use_global_device_ids=true, to_apply=%region_4.0 | all-reduce | flops 256 | bytes 2048 | tf_op jit(solution)/shard_map/psum | solution.py:50
  103.8 1.3 collective-permute-start.3
  105.1 3.0 collective-permute-start.4
  115.4 1.9 pad_slice_fusion.1
  117.2 5.1 %pad_slice_fusion.2 = (bf16[6,10,34,128]{3,2,1,0:T(8,128)(2,1)}, bf16[6,10,34,128]{3,2,1,0:T(8,128)(2,1)}, bf16[6,10,34,128]{3,2,1,0:T(8,128)(2,1)}, bf16[6,10,3...) fusion(bf16[6,10,34,128]{3,2,1,0:T(8,128)(2,1)S(1)} %pad_maximu, ...), kind=kLoop, calls=%fused_computation.2 | loop fusion | bytes 10444800 | tf_op jit(solution)/shard_map/slice | solution.py:88
  122.3 2.1 reshape.636
  124.4 2.0 reshape.629
  129.2 1.0 reshape.637
  131.2 1.0 reshape.635
  136.1 1.0 reshape.612
  137.1 1.0 reshape.613
  138.1 1.0 reshape.615
  140.0 1.0 reshape.617
  142.0 1.0 reshape.620
  142.9 1.0 reshape.621
  145.8 1.0 reshape.625
  147.1 2.1 fusion
  160.1 1.2 fusion.91
  161.3 1.7 collective-permute-start.5
  163.0 3.2 collective-permute-done.5
  166.2 2.6 collective-permute-start.6
  168.9 1.3 collective-permute-start.7
  170.2 3.5 collective-permute-done.7
  173.8 1.3 collective-permute-start.8
  175.1 3.5 collective-permute-start.9
  180.5 1.4 fusion.95
  182.0 2.1 fusion.94
  184.1 1.8 copy.52
  185.9 1.8 copy.53
  187.7 1.8 copy.51
  191.2 1.8 copy.48
  193.1 1.8 copy.47
  194.9 1.8 copy.46
  196.7 1.8 copy.70
  201.0 1.8 copy.68
  202.9 1.8 copy.67
  204.6 1.8 copy.66
  206.5 1.8 copy.65
  226.4 2.0 copy.73
  228.5 79.8 %all-reduce.1 = (f32[128]{0:T(128)S(1)}, f32[128]{0:T(128)S(1)}) all-reduce(f32[128]{0:T(128)S(1)} %get-tuple-element.113, f32[128]{0:T(128)S(1)} %get-tuple-element.112), channel_id=1, replica_groups=mesh['tm'=16,'rows'=8,'sect'=2] {'tm','rows','sect'}, use_global_device_ids=true, to_apply=%region_10.11 | all-reduce | flops 256 | bytes 2048 | tf_op jit(solution)/shard_map/psum | solution.py:128
  310.6 104.8 %all-reduce.5.cloned.1.call-done = f32[3,3,3,128,8]{3,4,2,1,0:T(8,128)} async-done(((f32[3,3,3,128,8]{3,4,2,1,0:T(8,128)}), f32[3,3,3,128,8]{3,4,2,1,0:T(8,128)}) %all-reduce.5.cloned.1.call-update) | async-done | bytes 110608 | tf_op jit(solution)/shard_map/psum | solution.py:152
  415.4 1.5 broadcast_multiply_fusion
  (312 shorter events, 57.0 us)
Async XLA Ops:
  7.2 3.6 copy-start
  7.2 13.0 %copy-start.21 = (bf16[4,8,32,128]{3,2,1,0:T(8,128)(2,1)S(1)}, bf16[4,8,32,128]{3,2,1,0:T(8,128)(2,1)}, u32[]{:S(2)}) copy-start(bf16[4,8,32,128]{3,2,1,0:T(8,128)(2,1)} %param.23) | copy-start | bytes 786436
  7.2 302.5 %reduce-scatter.2.cloned.1.call-start = ((), (), s32[]{:S(2)}) async-start(), calls=%async_computation.1 | async-start | bytes 1880064 | tf_op jit(solution)/shard_map/reduce_scatter | solution.py:153
  8.2 6.3 %collective-permute-start = (bf16[2,8,32,128]{3,2,1,0:T(8,128)(2,1)S(1)}, bf16[2,8,32,128]{3,2,1,0:T(8,128)(2,1)S(1)}, u32[]{:S(2)}, u32[]{:S(2)}) collective-permute-start(bf16[2,8,32,128]{3,2,1,0:T(8,128)(2,1)S(1)} %slice.516), channel_id=1, source_target_pairs={{16,0},{32,16},{48,32},{64,48},{80,64},{96,80},{112,96},{128,112},... | collective-permute-start | bytes 393224 | tf_op jit(solution)/shard_map/ppermute | solution.py:12
  14.5 89.2 %collective-permute-start.1 = (bf16[6,1,32,128]{3,2,1,0:T(8,128)(2,1)S(1)}, bf16[6,1,32,128]{3,2,1,0:T(8,128)(2,1)S(1)}, u32[]{:S(2)}, u32[]{:S(2)}) collective-permute-start(bf16[6,1,32,128]{3,2,1,0:T(8,128)(2,1)S(1)} %get-tuple-element.189), channel_id=1, source_target_pairs={{0,2},{2,4},{4,6},{6,8},{8,10},{10,12},{12,14},{1,3},{3,5},{5,7},{... | collective-permute-start | bytes 147464 | tf_op jit(solution)/shard_map/ppermute | solution.py:23
  18.9 84.8 %collective-permute-start.2 = (bf16[6,1,32,128]{3,2,1,0:T(8,128)(2,1)S(1)}, bf16[6,1,32,128]{3,2,1,0:T(8,128)(2,1)S(1)}, u32[]{:S(2)}, u32[]{:S(2)}) collective-permute-start(bf16[6,1,32,128]{3,2,1,0:T(8,128)(2,1)S(1)} %get-tuple-element.190), channel_id=1, source_target_pairs={{2,0},{4,2},{6,4},{8,6},{10,8},{12,10},{14,12},{3,1},{5,3},{7,5},{... | collective-permute-start | bytes 147464 | tf_op jit(solution)/shard_map/ppermute | solution.py:25
  103.8 10.3 %collective-permute-start.3 = (bf16[6,10,1,128]{3,2,1,0:T(2,128)(2,1)S(1)}, bf16[6,10,1,128]{3,2,1,0:T(2,128)(2,1)S(1)}, u32[]{:S(2)}, u32[]{:S(2)}) collective-permute-start(bf16[6,10,1,128]{3,2,1,0:T(2,128)(2,1)S(1)} %get-tuple-element.185), channel_id=1, source_target_pairs={{0,1},{2,3},{4,5},{6,7},{8,9},{10,11},{12,13},{14,15},{16,17},{18,... | collective-permute-start | bytes 46088 | tf_op jit(solution)/shard_map/ppermute | solution.py:23
  105.1 9.0 %collective-permute-start.4 = (bf16[6,10,1,128]{3,2,1,0:T(2,128)(2,1)S(1)}, bf16[6,10,1,128]{3,2,1,0:T(2,128)(2,1)S(1)}, u32[]{:S(2)}, u32[]{:S(2)}) collective-permute-start(bf16[6,10,1,128]{3,2,1,0:T(2,128)(2,1)S(1)} %get-tuple-element.186), channel_id=1, source_target_pairs={{1,0},{3,2},{5,4},{7,6},{9,8},{11,10},{13,12},{15,14},{17,16},{19,... | collective-permute-start | bytes 46088 | tf_op jit(solution)/shard_map/ppermute | solution.py:25
  122.3 4.1 copy-start.1
  130.2 2.9 copy-start.18
  131.2 2.9 copy-start.17
  132.2 2.8 copy-start.16
  133.1 2.8 copy-start.15
  134.0 2.1 copy-start.14
  135.0 2.1 copy-start.13
  135.9 2.2 copy-start.12
  136.1 3.0 copy-start.11
  137.1 2.9 copy-start.10
  138.1 2.9 copy-start.9
  139.1 2.9 copy-start.8
  140.0 2.9 copy-start.7
  141.0 2.9 copy-start.6
  142.0 2.9 copy-start.5
  142.9 2.9 copy-start.4
  143.9 2.9 copy-start.3
  144.8 2.1 copy-start.2
  147.1 2.1 copy-start.63
  147.1 2.1 copy-start.71
  147.1 2.1 copy-start.76
  147.1 2.1 copy-start.86
  161.3 4.9 %collective-permute-start.5 = (bf16[2,8,32,128]{3,2,1,0:T(8,128)(2,1)S(1)}, bf16[2,8,32,128]{3,2,1,0:T(8,128)(2,1)S(1)}, u32[]{:S(2)}, u32[]{:S(2)}) collective-permute-start(bf16[2,8,32,128]{3,2,1,0:T(8,128)(2,1)S(1)} %slice.629), channel_id=1, source_target_pairs={{0,16},{16,32},{32,48},{48,64},{64,80},{80,96},{96,112},{112,128},... | collective-permute-start | bytes 393224 | tf_op jit(solution)/shard_map/ppermute | solution.py:12
  166.2 3.9 collective-permute-start.6
  168.9 4.8 %collective-permute-start.7 = (bf16[6,1,32,128]{3,2,1,0:T(8,128)(2,1)S(1)}, bf16[6,1,32,128]{3,2,1,0:T(8,128)(2,1)S(1)}, u32[]{:S(2)}, u32[]{:S(2)}) collective-permute-start(bf16[6,1,32,128]{3,2,1,0:T(8,128)(2,1)S(1)} %get-tuple-element.188), channel_id=1, source_target_pairs={{2,0},{4,2},{6,4},{8,6},{10,8},{12,10},{14,12},{3,1},{5,3},{7,5},{... | collective-permute-start | bytes 147464 | tf_op jit(solution)/shard_map/ppermute | solution.py:25
  173.8 4.9 %collective-permute-start.8 = (bf16[6,10,1,128]{3,2,1,0:T(2,128)(2,1)S(1)}, bf16[6,10,1,128]{3,2,1,0:T(2,128)(2,1)S(1)}, u32[]{:S(2)}, u32[]{:S(2)}) collective-permute-start(bf16[6,10,1,128]{3,2,1,0:T(2,128)(2,1)S(1)} %get-tuple-element.183), channel_id=1, source_target_pairs={{0,1},{2,3},{4,5},{6,7},{8,9},{10,11},{12,13},{14,15},{16,17},{18,... | collective-permute-start | bytes 46088 | tf_op jit(solution)/shard_map/ppermute | solution.py:23
  175.1 4.4 %collective-permute-start.9 = (bf16[6,10,1,128]{3,2,1,0:T(2,128)(2,1)S(1)}, bf16[6,10,1,128]{3,2,1,0:T(2,128)(2,1)S(1)}, u32[]{:S(2)}, u32[]{:S(2)}) collective-permute-start(bf16[6,10,1,128]{3,2,1,0:T(2,128)(2,1)S(1)} %get-tuple-element.184), channel_id=1, source_target_pairs={{1,0},{3,2},{5,4},{7,6},{9,8},{11,10},{13,12},{15,14},{17,16},{19,... | collective-permute-start | bytes 46088 | tf_op jit(solution)/shard_map/ppermute | solution.py:25
  184.1 5.4 %copy-start.31 = (bf16[4,8,32,128]{3,2,1,0:T(8,128)(2,1)S(1)}, bf16[4,8,32,128]{3,2,1,0:T(8,128)(2,1)}, u32[]{:S(2)}) copy-start(bf16[4,8,32,128]{3,2,1,0:T(8,128)(2,1)} %get-tuple-element.152) | copy-start | bytes 786436
  184.1 6.3 %copy-start.30 = (bf16[4,8,32,128]{3,2,1,0:T(8,128)(2,1)S(1)}, bf16[4,8,32,128]{3,2,1,0:T(8,128)(2,1)}, u32[]{:S(2)}) copy-start(bf16[4,8,32,128]{3,2,1,0:T(8,128)(2,1)} %get-tuple-element.153) | copy-start | bytes 786436
  189.5 9.0 %copy-start.29 = (bf16[4,8,32,128]{3,2,1,0:T(8,128)(2,1)S(1)}, bf16[4,8,32,128]{3,2,1,0:T(8,128)(2,1)}, u32[]{:S(2)}) copy-start(bf16[4,8,32,128]{3,2,1,0:T(8,128)(2,1)} %get-tuple-element.131) | copy-start | bytes 786436
  190.4 9.0 %copy-start.28 = (bf16[4,8,32,128]{3,2,1,0:T(8,128)(2,1)S(1)}, bf16[4,8,32,128]{3,2,1,0:T(8,128)(2,1)}, u32[]{:S(2)}) copy-start(bf16[4,8,32,128]{3,2,1,0:T(8,128)(2,1)} %get-tuple-element.132) | copy-start | bytes 786436
  191.2 9.0 %copy-start.27 = (bf16[4,8,32,128]{3,2,1,0:T(8,128)(2,1)S(1)}, bf16[4,8,32,128]{3,2,1,0:T(8,128)(2,1)}, u32[]{:S(2)}) copy-start(bf16[4,8,32,128]{3,2,1,0:T(8,128)(2,1)} %get-tuple-element.133) | copy-start | bytes 786436
  199.3 8.9 %copy-start.26 = (bf16[4,8,32,128]{3,2,1,0:T(8,128)(2,1)S(1)}, bf16[4,8,32,128]{3,2,1,0:T(8,128)(2,1)}, u32[]{:S(2)}) copy-start(bf16[4,8,32,128]{3,2,1,0:T(8,128)(2,1)} %get-tuple-element.138) | copy-start | bytes 786436
  200.2 8.9 %copy-start.25 = (bf16[4,8,32,128]{3,2,1,0:T(8,128)(2,1)S(1)}, bf16[4,8,32,128]{3,2,1,0:T(8,128)(2,1)}, u32[]{:S(2)}) copy-start(bf16[4,8,32,128]{3,2,1,0:T(8,128)(2,1)} %get-tuple-element.139) | copy-start | bytes 786436
  201.0 9.0 %copy-start.24 = (bf16[4,8,32,128]{3,2,1,0:T(8,128)(2,1)S(1)}, bf16[4,8,32,128]{3,2,1,0:T(8,128)(2,1)}, u32[]{:S(2)}) copy-start(bf16[4,8,32,128]{3,2,1,0:T(8,128)(2,1)} %get-tuple-element.140) | copy-start | bytes 786436
  212.6 5.2 %copy-start.49 = (bf16[1024,128]{0,1:T(8,128)(2,1)S(1)}, bf16[1024,128]{0,1:T(8,128)(2,1)}, u32[]{:S(2)}) copy-start(bf16[1024,128]{0,1:T(8,128)(2,1)} %copy.48) | copy-start | bytes 786436
  212.6 5.2 %copy-start.50 = (bf16[1024,128]{0,1:T(8,128)(2,1)S(1)}, bf16[1024,128]{0,1:T(8,128)(2,1)}, u32[]{:S(2)}) copy-start(bf16[1024,128]{0,1:T(8,128)(2,1)} %copy.47) | copy-start | bytes 786436
  213.4 4.3 %copy-start.51 = (bf16[1024,128]{0,1:T(8,128)(2,1)S(1)}, bf16[1024,128]{0,1:T(8,128)(2,1)}, u32[]{:S(2)}) copy-start(bf16[1024,128]{0,1:T(8,128)(2,1)} %copy.46) | copy-start | bytes 786436
  228.4 81.3 %copy-start.23 = (f32[4,8,32,128]{3,2,1,0:T(8,128)S(1)}, f32[4,8,32,128]{3,2,1,0:T(8,128)}, u32[]{:S(2)}) copy-start(f32[4,8,32,128]{3,2,1,0:T(8,128)} %get-tuple-element.120) | copy-start | bytes 1572868
  228.4 187.0 %all-reduce.5.cloned.1.call-start = ((), (), s32[]{:S(2)}) async-start(), calls=%async_computation.2 | async-start | bytes 221184 | tf_op jit(solution)/shard_map/psum | solution.py:152
  (53 other events, 61.0 us)
Sparse Core Ops, SparseCore 0:
  228.5 77.9 reduce-scatter.1
  309.8 105.5 all-reduce.4
where the time goes:
time: 425 us; the launch traced here: 424 us
  blocking collectives  163 us (38%)
  waiting for transfers between devices  116 us (27%)
  local copies, waits for them, and re-layouts  91 us (21%)
  starting transfers between devices  21.7 us (5%)
  between operations  15 us (4%)
  matrix products  11 us (3%)
  other arithmetic  6.26 us (1%)
    psum x1, waiting for transfers between devices, local(): band_sum = lax.psum(kernel_local, ('rows', 'sect'))  105 us
    psum x1, blocking collectives, local(): lax.psum((jnp.sum(input_tensor, axis=(0, 1, 2)), jnp.sum(input_tensor * i...  82.9 us
    psum x1, blocking collectives, local(): lax.psum((jnp.sum(activation_gradient, axis=(0, 1, 2)), jnp.sum(activatio...  79.8 us
    reshape x27, local copies, waits for them, and re-layouts, local(): hidden_cat = jnp.concatenate([hidden_pad[tap_time:tap_time + frames, tap_...  33.6 us
    reshape x27, local copies, waits for them, and re-layouts, local(): grad_cat = jnp.concatenate([grad_pad[2 - tap_time:2 - tap_time + frames +...  25.6 us
    unnamed x188, local copies, waits for them, and re-layouts  15.1 us
    ppermute x4, starting transfers between devices, extended(): lax.ppermute(tail, axis, [(i, (i + 1) % count) for i in range(ends)])  9.55 us
    ppermute x4, starting transfers between devices, extended(): lax.ppermute(head, axis, [((i + 1) % count, i) for i in range(ends)])  9.16 us
  transfers between devices with their start and end apart: 12, of which 5 were waited for; matrix products, arithmetic and copies ran while one was open for 2% of the time, Pallas kernels for 0%

commit v1 on v0

v1 whole, which is shorter than its diff:
```python
import functools

import jax
import jax.numpy as jnp
from jax import lax
from jax.experimental import pallas as pl
from jax.experimental.pallas import tpu as pltpu
from jax.sharding import PartitionSpec as P

GROUPS = 32
TAPS = 27
HALF = 14
SLOTS = HALF + 1
F32 = jnp.float32
BF16 = jnp.bfloat16
VMEM = pl.BlockSpec(memory_space=pltpu.VMEM)
SMEM = pl.BlockSpec(memory_space=pltpu.SMEM)


def call(body, outs, args, scratch=(), flops=0, smem_first=False):
    specs = [VMEM] * len(args)
    if smem_first:
        specs[0] = SMEM
    moved = sum(x.size * x.dtype.itemsize for x in list(args) + list(outs))
    return pl.pallas_call(
        body,
        out_shape=outs,
        in_specs=specs,
        out_specs=[VMEM] * len(outs),
        scratch_shapes=list(scratch),
        cost_estimate=pl.CostEstimate(flops=flops, bytes_accessed=moved, transcendentals=0),
        compiler_params=pltpu.CompilerParams(vmem_limit_bytes=48 * 1024 * 1024),
    )(*args)


def lanes_of(shape):
    return lax.broadcasted_iota(jnp.int32, shape, len(shape) - 1)


def sublanes_of(shape):
    return lax.broadcasted_iota(jnp.int32, shape, len(shape) - 2)


def group_total(v):
    lane = lanes_of(v.shape)
    v = v + jnp.where(lane % 2 == 0, pltpu.roll(v, 127, 1), pltpu.roll(v, 1, 1))
    return v + jnp.where(lane % 4 < 2, pltpu.roll(v, 126, 1), pltpu.roll(v, 2, 1))


def column_sum(v):
    part = jnp.sum(v.reshape(-1, 8, v.shape[-1]), axis=0)
    return jnp.broadcast_to(jnp.sum(part, axis=0, keepdims=True), part.shape)


def stats_kernel(x_ref, out_ref):
    x = x_ref[...].astype(F32).reshape(-1, x_ref.shape[-1])
    total = group_total(column_sum(x))
    square = group_total(column_sum(x * x))
    row = jnp.where(lanes_of(total.shape) % 4 < 2, total, square)
    out_ref[...] = jnp.broadcast_to(row[None], (out_ref.shape[0] // 8, 8, 128)).reshape(out_ref.shape)


def grad_kernel(place_ref, own_ref, side_ref, above_ref, below_ref, later_ref, kernel_ref, v_ref, dh_ref, taps_ref):
    time_first = place_ref[0] == 0
    row_first = place_ref[1] == 0
    row_last = place_ref[1] == place_ref[2] - 1
    left = place_ref[3] == 0
    column = sublanes_of((10, 32, 128))

    for a in range(3):
        for b in range(3):
            for e in range(3):
                j = (b * 3 + e) * 128
                taps_ref[a, :, j : j + 128] = kernel_ref[a, b, e]

    for f in range(6):
        if f < 4:
            mid = jnp.concatenate([own_ref[f].astype(F32), side_ref[f].astype(F32)], axis=1)
            rows = jnp.concatenate(
                [above_ref[f].astype(F32)[None], mid, below_ref[f].astype(F32)[None]], axis=0
            )
        else:
            rows = later_ref[f - 4].astype(F32)
        core = rows[:, :32]
        zero = jnp.zeros_like(core)
        ahead = pltpu.roll(rows, 47, 1)[:, :32]
        behind = pltpu.roll(rows, 1, 1)[:, :32]
        first = column == 0
        last = column == 31
        ahead = jnp.where(left, ahead + jnp.where(first, core, zero), jnp.where(last, zero, ahead))
        behind = jnp.where(left, jnp.where(first, zero, behind), behind + jnp.where(last, core, zero))
        for e, part in enumerate((ahead, core, behind)):
            for b in range(3):
                j = (b * 3 + e) * 128
                shifted = part[2 - b : 10 - b]
                if b == 0:
                    edge = shifted[0] + jnp.where(row_first, part[1], jnp.zeros_like(part[1]))
                    shifted = jnp.concatenate([edge[None], shifted[1:]], axis=0)
                if b == 2:
                    edge = shifted[7] + jnp.where(row_last, part[8], jnp.zeros_like(part[8]))
                    shifted = jnp.concatenate([shifted[:7], edge[None]], axis=0)
                v_ref[f, :, j : j + 128] = shifted.astype(BF16).reshape(256, 128)


    @pl.when(time_first)
    def _():
        both = v_ref[1].astype(F32) + v_ref[0].astype(F32)
        v_ref[6] = both.astype(BF16)
        v_ref[7] = (both + v_ref[2].astype(F32)).astype(BF16)

    @pl.when(jnp.logical_not(time_first))
    def _():
        v_ref[6] = v_ref[1]
        v_ref[7] = v_ref[2]

    dims = (((1,), (1,)), ((), ()))
    for f in range(4):
        total = None
        for a in range(3):
            source = f + 2 - a
            if f == 0 and a < 2:
                source = 7 - a
            term = lax.dot_general(v_ref[source], taps_ref[a], dims, preferred_element_type=F32)
            total = term if total is None else total + term
        dh_ref[pl.ds(f * 256, 256)] = total


def sums_to_pair(row):
    lane = lanes_of(row.shape)
    total = jnp.where(lane % 4 < 2, row, pltpu.roll(row, 2, 1))
    square = jnp.where(lane % 4 < 2, pltpu.roll(row, 126, 1), row)
    return total, square


def main_kernel(counted, place_ref, x_ref, stat_ref, gain_ref, bias_ref, dh_ref, v_ref, w_ref, da_ref, norm_ref):
    total, square = sums_to_pair(column_sum(stat_ref[...]))
    mean = total / counted
    rstd = lax.rsqrt(square / counted - mean * mean + 1e-06)
    norm_ref[0:8] = mean
    norm_ref[8:16] = rstd
    mean = mean[:1]
    rstd = rstd[:1]
    xhat = (x_ref[...].astype(F32).reshape(-1, 128) - mean) * rstd
    pre = xhat * gain_ref[...] + bias_ref[...]
    sig = 1.0 / (1.0 + jnp.exp(-pre))
    hidden = pre * sig
    da = dh_ref[...] * sig * (1.0 + pre * (1.0 - sig))
    da_ref[...] = da
    sums = jnp.where(sublanes_of((8, 128)) == 0, column_sum(da), column_sum(da * xhat))
    for half in range(2):
        w_ref[half, :, HALF] = jnp.broadcast_to(sums[None], (16, 8, 128))
    turned = hidden.T.astype(BF16)
    sect = place_ref[3]
    for a in range(3):
        if a == 2:
            product = jnp.dot(turned, v_ref[0:4].reshape(1024, 1152), preferred_element_type=F32)
        else:
            product = jnp.dot(turned[:, :256], v_ref[7 - a], preferred_element_type=F32) + jnp.dot(
                turned[:, 256:], v_ref[3 - a : 6 - a].reshape(768, 1152), preferred_element_type=F32
            )
        for j in range(9):
            tap = a * 9 + j
            block = product[:, j * 128 : (j + 1) * 128].T.reshape(16, 8, 128)
            w_ref[(tap // HALF) ^ sect, :, tap % HALF] = block
    w_ref[1 ^ sect, :, HALF - 1] = jnp.zeros((16, 8, 128), F32)


def split_sums(sums):
    row = sublanes_of(sums.shape)
    high = sums.astype(BF16).astype(F32)
    middle = (sums - high).astype(BF16).astype(F32)
    low = sums - high - middle
    return jnp.where(
        row < 2, high, jnp.where(row < 4, pltpu.roll(middle, 2, 0), pltpu.roll(low, 4, 0))
    )


def join_sums(parts):
    return parts + pltpu.roll(parts, 6, 0) + pltpu.roll(parts, 4, 0)


def pair_kernel(own_ref, other_ref, out_ref):
    rows = HALF * 8
    slot = split_sums(own_ref[0, HALF] + other_ref[0, HALF])
    for i in range(16):
        body = (own_ref[i, :HALF] + other_ref[i, :HALF]).reshape(rows, 128)
        out_ref[i] = jnp.concatenate([body, slot], axis=0).astype(BF16)


def share_kernel(in_ref, out_ref):
    rows = HALF * 8
    total = in_ref[0].astype(F32)
    for i in range(1, in_ref.shape[0]):
        total = total + in_ref[i].astype(F32)
    slot = split_sums(join_sums(total[rows:]))
    sent = jnp.concatenate([total[:rows], slot], axis=0).astype(BF16)
    for i in range(out_ref.shape[0]):
        out_ref[i] = sent


def last_sum_kernel(scaling, in_ref, half_ref, sums_ref):
    rows = HALF * 8
    total = in_ref[0].astype(F32)
    for i in range(1, in_ref.shape[0]):
        total = total + in_ref[i].astype(F32)
    half_ref[...] = total[:rows] * scaling
    sums_ref[...] = join_sums(total[rows:])


def finish_kernel(counted, scaling, x_ref, da_ref, norm_ref, sums_ref, gain_ref, out_ref, grads_ref):
    gain = gain_ref[...]
    mean = norm_ref[0:1]
    rstd = norm_ref[8:9]
    sums = sums_ref[...]
    grads_ref[...] = sums * scaling
    averages = group_total(gain * sums) / counted
    leading = averages[0:1]
    trailing = averages[1:2]
    xhat = (x_ref[...].astype(F32).reshape(-1, 128) - mean) * rstd
    grad = rstd * (da_ref[...] * gain - leading - xhat * trailing)
    out_ref[...] = grad.astype(BF16).reshape(out_ref.shape)


def shape_of(shape, dtype=F32):
    return jax.ShapeDtypeStruct(shape, dtype)


def local(activations, group_norm_gain, group_norm_bias, upstream, kernel):
    frames, height, columns, channels = activations.shape
    n_time, n_rows, n_sect = (lax.axis_size(axis) for axis in ("tm", "rows", "sect"))
    cells = frames * height * columns
    total_cells = cells * n_time * n_rows * n_sect
    counted = float(total_cells * (channels // GROUPS))
    scaling = float(total_cells) ** (-0.5)
    tm, rows, sect = (lax.axis_index(axis) for axis in ("tm", "rows", "sect"))
    place = jnp.stack([tm, rows, jnp.int32(n_rows), sect]).astype(jnp.int32)
    swap = [(0, 1), (1, 0)]

    facing = jnp.where(sect == 0, upstream[:, :, 16:], upstream[:, :, :16])
    side = lax.ppermute(facing, "sect", swap)
    (stat,) = call(stats_kernel, [shape_of((32, 128))], [activations])
    stat = lax.all_to_all(stat.reshape(32, 1, 128), ("tm", "sect"), 0, 0)
    last_row = jnp.concatenate([upstream[:, height - 1], side[:, height - 1]], axis=1)
    first_row = jnp.concatenate([upstream[:, 0], side[:, 0]], axis=1)
    above = lax.ppermute(last_row, "rows", [(i, i + 1) for i in range(n_rows - 1)])
    below = lax.ppermute(first_row, "rows", [(i + 1, i) for i in range(n_rows - 1)])
    early = jnp.concatenate(
        [above[:2, None], jnp.concatenate([upstream[:2], side[:2]], axis=2), below[:2, None]], axis=1
    )
    later = lax.ppermute(early, "tm", [(i + 1, i) for i in range(n_time - 1)])
    stat = jnp.broadcast_to(jnp.sum(stat, axis=0)[None], (n_rows, 1, 128))
    stat = lax.all_to_all(stat, "rows", 0, 0).reshape(n_rows, 128)
    spread, hidden_grad = call(
        grad_kernel,
        [shape_of((8, 256, 1152), BF16), shape_of((cells, channels))],
        [place, upstream, side, above, below, later, kernel],
        [pltpu.VMEM((3, 128, 1152), BF16)],
        flops=2 * cells * TAPS * channels * channels,
        smem_first=True,
    )
    gain = group_norm_gain.reshape(1, channels)
    bias = group_norm_bias.reshape(1, channels)
    terms, da, norm = call(
        functools.partial(main_kernel, counted),
        [shape_of((2, 16, SLOTS, 8, 128)), shape_of((cells, channels)), shape_of((16, channels))],
        [place, activations, stat, gain, bias, hidden_grad, spread],
        flops=2 * cells * TAPS * channels * channels,
        smem_first=True,
    )
    other = lax.ppermute(terms[1], "sect", swap)
    (sent,) = call(pair_kernel, [shape_of((16, SLOTS * 8, 128), BF16)], [terms[0], other])
    gathered = lax.all_to_all(sent, "tm", 0, 0)
    (sent,) = call(share_kernel, [shape_of((n_rows, SLOTS * 8, 128), BF16)], [gathered])
    gathered = lax.all_to_all(sent, "rows", 0, 0)
    half, sums = call(
        functools.partial(last_sum_kernel, scaling),
        [shape_of((HALF * 8, 128)), shape_of((8, 128))],
        [gathered],
    )
    other = lax.ppermute(half, "sect", swap)
    input_gradient, grads = call(
        functools.partial(finish_kernel, counted, scaling),
        [shape_of(activations.shape, BF16), shape_of((8, 128))],
        [activations, da, norm, sums, gain],
    )
    whole = jnp.concatenate(
        [jnp.where(sect == 0, half, other), jnp.where(sect == 0, other, half)], axis=0
    )
    weight_grad = whole[: TAPS * 8].reshape(3, 3, 3, 8, 128).transpose(0, 1, 2, 4, 3)
    return (input_gradient, grads[1], grads[0], weight_grad)


def solution(mesh):
    return jax.shard_map(
        local,
        mesh=mesh,
        in_specs=(P("tm", "rows", "sect", None), P(), P(), P("tm", "rows", "sect", None), P()),
        out_specs=(P("tm", "rows", "sect", None), P(), P(), P(None, None, None, None, "tm")),
        check_vma=False,
    )
```

time: 425 us -> 87.3 us (0.21)
  blocking collectives: 163 us -> 24.9 us
  waiting for transfers between devices: 116 us -> 15.4 us
  local copies, waits for them, and re-layouts: 91 us -> 4.08 us
  between operations: 15 us -> 0.84 us
  matrix products: 11 us -> 0 us
  Pallas kernels: 0 us -> 9.76 us
  starting transfers between devices: 21.7 us -> 31 us
  other arithmetic: 6.26 us -> 0.84 us
    psum x2 -> x0, blocking collectives: 163 us -> none  [the longest x1 82.9 us: local(): lax.psum((jnp.sum(input_tensor, axis=(0, 1, 2)), jnp.sum(input_tensor * i...]
    psum x1 -> x0, waiting for transfers between devices: 105 us -> none  [local(): band_sum = lax.psum(kernel_local, ('rows', 'sect'))]
    reshape x59 -> x0, local copies, waits for them, and re-layouts: 61.5 us -> none  [the longest x27 33.6 us: local(): hidden_cat = jnp.concatenate([hidden_pad[tap_time:tap_time + frames, tap_...]
    all_to_all x0 -> x2, blocking collectives: none -> 24.9 us  [the longest x1 13.1 us: local(): gathered = lax.all_to_all(sent, 'tm', 0, 0)]
    all_to_all x0 -> x2, starting transfers between devices: none -> 17.6 us  [the longest x1 9.52 us: local(): stat = lax.all_to_all(stat.reshape(32, 1, 128), ('tm', 'sect'), 0, 0)]
    unnamed x188 -> x10, local copies, waits for them, and re-layouts: 15.1 us -> 0.03 us
    dot_general x18 -> x0, matrix products: 11 us -> none  [the longest x9 7.67 us: local(): jnp.dot(grad_cat, kernel_cat, preferred_element_type=jnp.float32)]
    slice x14 -> x2, local copies, waits for them, and re-layouts: 12.9 us -> 2.01 us  [the longest x1 1.09 us: local(): facing = jnp.where(sect == 0, upstream[:, :, 16:], upstream[:, :, :16])]
  transfers between devices with their start and end apart: 12 -> 8, of which waited for: 5 -> 4; matrix products, arithmetic and copies ran while one was open for 2% -> 3% of each run, Pallas kernels for 0% -> 6%
where the time goes in v1:
time: 87.3 us; the launch traced here: 86.9 us
  starting transfers between devices  31 us (36%)
  blocking collectives  24.9 us (29%)
  waiting for transfers between devices  15.4 us (18%)
  Pallas kernels  9.76 us (11%)
  local copies, waits for them, and re-layouts  4.08 us (5%)
    all_to_all x1, blocking collectives, local(): gathered = lax.all_to_all(sent, 'tm', 0, 0)  13.1 us
    all_to_all x1, blocking collectives, local(): gathered = lax.all_to_all(sent, 'rows', 0, 0)  11.8 us
    pallas_call x7, Pallas kernels, call(): pl.pallas_call(body, out_shape=outs, in_specs=specs, out_specs=[VMEM] * l...  9.76 us
    all_to_all x1, starting transfers between devices, local(): stat = lax.all_to_all(stat.reshape(32, 1, 128), ('tm', 'sect'), 0, 0)  9.52 us
    all_to_all x1, starting transfers between devices, local(): stat = lax.all_to_all(stat, 'rows', 0, 0).reshape(n_rows, 128)  8.04 us
    all_to_all x1, waiting for transfers between devices, local(): stat = lax.all_to_all(stat.reshape(32, 1, 128), ('tm', 'sect'), 0, 0)  6.78 us
    ppermute x1, waiting for transfers between devices, local(): lax.ppermute(first_row, 'rows', [(i + 1, i) for i in range(n_rows - 1)])  3.7 us
    ppermute x1, starting transfers between devices, local(): other = lax.ppermute(half, 'sect', swap)  3.58 us
  transfers between devices with their start and end apart: 8, of which 4 were waited for; matrix products, arithmetic and copies ran while one was open for 3% of the time, Pallas kernels for 6%

profile of v1, /device:TPU:1, one launch (start us, length us, event | category | flops | bytes accessed | tf_op | source)
XLA Modules:
  0.0 86.9 jit_solution(2610814232368646700)
XLA Ops:
  0.6 0.0 copy-start.1
  0.6 0.0 copy-start
  0.7 0.0 copy-start.4
  0.7 1.1 %fusion = (bf16[4,8,16,128]{3,2,1,0:T(8,128)(2,1)S(1)}, bf16[4,8,16,128]{3,2,1,0:T(8,128)(2,1)S(1)}) fusion(bf16[4,8,32,128]{3,2,1,0:T(8,128)(2,1)} %own_ref.1), kind=kLoop, calls=%fused_computation.18 | loop fusion | bytes 524288 | tf_op jit(solution)/shard_map/slice | solution.py:239
  1.8 3.3 %collective-permute-start = (bf16[4,8,16,128]{3,2,0,1:T(8,128)(2,1)S(1)}, bf16[4,8,16,128]{3,2,0,1:T(8,128)(2,1)S(1)}, u32[]{:S(2)}, u32[]{:S(2)}) collective-permute-start(bf16[4,8,16,128]{3,2,0,1:T(8,128)(2,1)S(1)} %copy_select_fusion), channel_id=1, source_target_pairs={{0,1},{1,0},{2,3},{3,2},{4,5},{5,4},{6,7},{7,6},{8,9},{9,8},{10,11... | collective-permute-start | bytes 393224 | tf_op jit(solution)/shard_map/ppermute | solution.py:240
  5.1 0.9 %slice.52 = bf16[2,8,32,128]{3,2,1,0:T(8,128)(2,1)S(1)} slice(bf16[4,8,32,128]{3,2,1,0:T(8,128)(2,1)} %own_ref.1), slice={[0:2], [0:8], [0:32], [0:128]} | slice | bytes 262144 | tf_op jit(solution)/shard_map/slice | solution.py:248
  6.0 0.8 slice_bitcast_fusion.2
  6.8 0.0 collective-permute-done
  6.9 1.8 %collective-permute-start.1 = (bf16[4,48,128]{2,1,0:T(8,128)(2,1)S(1)}, bf16[4,48,128]{2,1,0:T(8,128)(2,1)S(1)}, u32[]{:S(2)}, u32[]{:S(2)}) collective-permute-start(bf16[4,48,128]{2,1,0:T(8,128)(2,1)S(1)} %pad_maximum_fusion.2), channel_id=1, source_target_pairs={{0,2},{2,4},{4,6},{6,8},{8,10},{10,12},{12,14},{1,3},{3,5},{5,7},{... | collective-permute-start | bytes 147464 | tf_op jit(solution)/shard_map/ppermute | solution.py:245
  8.7 1.3 %collective-permute-start.2 = (bf16[4,48,128]{2,1,0:T(8,128)(2,1)S(1)}, bf16[4,48,128]{2,1,0:T(8,128)(2,1)S(1)}, u32[]{:S(2)}, u32[]{:S(2)}) collective-permute-start(bf16[4,48,128]{2,1,0:T(8,128)(2,1)S(1)} %pad_maximum_fusion.3), channel_id=1, source_target_pairs={{2,0},{4,2},{6,4},{8,6},{10,8},{12,10},{14,12},{3,1},{5,3},{7,5},{... | collective-permute-start | bytes 147464 | tf_op jit(solution)/shard_map/ppermute | solution.py:246
  10.0 0.0 collective-permute-done.1.above_ref
  10.0 3.7 %collective-permute-done.2.below_ref = bf16[4,48,128]{2,1,0:T(8,128)(2,1)S(1)} collective-permute-done((bf16[4,48,128]{2,1,0:T(8,128)(2,1)S(1)}, bf16[4,48,128]{2,1,0:T(8,128)(2,1)S(1)}, u32[]{:S(2)}, u32[]{:S(2)}) %collective-permute-start.2) | collective-permute-done | bytes 49184 | tf_op jit(solution)/shard_map/ppermute | solution.py:246
  13.7 0.0 copy-start.2
  13.7 0.0 copy-start.3
  13.8 1.3 %collective-permute-start.3 = (bf16[2,10,48,128]{3,2,1,0:T(8,128)(2,1)S(1)}, bf16[2,10,48,128]{3,2,1,0:T(8,128)(2,1)S(1)}, u32[]{:S(2)}, u32[]{:S(2)}) collective-permute-start(bf16[2,10,48,128]{3,2,1,0:T(8,128)(2,1)S(1)} %pad_maximum_fusion), channel_id=1, source_target_pairs={{16,0},{32,16},{48,32},{64,48},{80,64},{96,80},{112,96},{128,112},... | collective-permute-start | bytes 737288 | tf_op jit(solution)/shard_map/ppermute | solution.py:250
  15.1 0.0 copy-done
  15.1 0.9 %shard_map.84 = f32[32,128]{1,0:T(8,128)} custom-call(bf16[4,8,32,128]{3,2,1,0:T(8,128)(2,1)S(1)} %copy-done), custom_call_target="tpu_custom_call" | custom-call | bytes 278528 | tf_op jit(solution)/shard_map/pallas_call | solution.py:25
  16.0 9.5 %all-to-all-start = ((f32[32,1,128]{2,1,0:T(1,128)}), f32[32,1,128]{2,1,0:T(1,128)S(1)}, u32[]{:S(2)}, u32[]{:S(2)}) async-start(f32[32,1,128]{2,1,0:T(1,128)} %bitcast.4), calls=%async_computation | async-start | bytes 32768 | tf_op jit(solution)/shard_map/all_to_all | solution.py:242
  25.5 0.1 pad_add_fusion.place_ref
  25.6 6.8 %all-to-all-done = f32[32,1,128]{2,1,0:T(1,128)S(1)} async-done(((f32[32,1,128]{2,1,0:T(1,128)}), f32[32,1,128]{2,1,0:T(1,128)S(1)}, u32[]{:S(2)}, u32[]{:S(2)}) %all-to-all-start) | async-done | bytes 16416 | tf_op jit(solution)/shard_map/all_to_all | solution.py:242
  32.4 0.1 reduce_sum.9
  32.4 0.6 broadcast_in_dim.12
  33.0 8.0 %all-to-all-start.1 = ((f32[8,1,128]{2,1,0:T(1,128)}), f32[8,1,128]{2,1,0:T(1,128)S(1)}, u32[]{:S(2)}, u32[]{:S(2)}) async-start(f32[8,1,128]{2,1,0:T(1,128)} %broadcast_in_dim.12), calls=%async_computation.1 | async-start | bytes 8192 | tf_op jit(solution)/shard_map/all_to_all | solution.py:252
  41.1 0.0 collective-permute-done.3.later_ref
  41.1 0.0 copy-done.1
  41.1 0.0 copy-done.4
  41.1 3.7 %shard_map.85 = (bf16[8,256,1152]{2,1,0:T(8,128)(2,1)}, f32[1024,128]{1,0:T(8,128)S(1)}) custom-call(s32[4]{0:T(128)S(1)} %pad_add_fusion.place_ref, bf16[4,8,32,128]{3,2,1,0:T(8,128)(2,1)S(1)} %copy-done.1, bf16[4,8,16,128]{3,2,1,0:T(8,128)(2,1)S(1)} %copy.21.side_ref, bf16[4,48,128]{2,1,0:T(8,128)(2,1)S(1)} %collective-permute-done.1.above_ref, ...), custom_call_target="tpu_custom_call" | custom-call | flops 905969664 | bytes 6864912 | tf_op jit(solution)/shard_map/pallas_call | solution.py:25
  44.8 2.7 %all-to-all-done.1 = f32[8,1,128]{2,1,0:T(1,128)S(1)} async-done(((f32[8,1,128]{2,1,0:T(1,128)}), f32[8,1,128]{2,1,0:T(1,128)S(1)}, u32[]{:S(2)}, u32[]{:S(2)}) %all-to-all-start.1) | async-done | bytes 4128 | tf_op jit(solution)/shard_map/all_to_all | solution.py:252
  47.5 0.0 copy-done.2
  47.5 0.0 copy-done.3
  47.5 4.0 %shard_map.86 = (f32[2,16,15,8,128]{4,3,2,1,0:T(8,128)S(1)}, f32[1024,128]{1,0:T(8,128)S(1)}, f32[16,128]{1,0:T(8,128)S(1)}) custom-call(s32[4]{0:T(128)S(1)} %pad_add_fusion.place_ref, bf16[4,8,32,128]{3,2,1,0:T(8,128)(2,1)S(1)} %copy-done, f32[8,128]{1,0:T(8,128)S(1)} %bitcast.36, f32[1,128]{1,0:T(1,128)S(1)} %bitcast.37, f32[1,128]{1,0:T(1,128)S(1)} %bitcast.39, ...), custom_call_target="tpu_custom_call" | custom-call | flops 905969664 | bytes 8008720 | tf_op jit(solution)/shard_map/pallas_call | solution.py:25
  51.5 0.1 slice_bitcast_fusion
  51.6 2.2 %collective-permute-start.4 = (f32[16,15,8,128]{3,2,1,0:T(8,128)S(1)}, f32[16,15,8,128]{3,2,1,0:T(8,128)S(1)}, u32[]{:S(2)}, u32[]{:S(2)}) collective-permute-start(f32[16,15,8,128]{3,2,1,0:T(8,128)S(1)} %get-tuple-element.22), channel_id=1, source_target_pairs={{0,1},{1,0},{2,3},{3,2},{4,5},{5,4},{6,7},{7,6},{8,9},{9,8},{10,11... | collective-permute-start | bytes 2949128 | tf_op jit(solution)/shard_map/ppermute | solution.py:270
  53.8 2.2 %collective-permute-done.4.other_ref = f32[16,15,8,128]{3,2,1,0:T(8,128)S(1)} collective-permute-done((f32[16,15,8,128]{3,2,1,0:T(8,128)S(1)}, f32[16,15,8,128]{3,2,1,0:T(8,128)S(1)}, u32[]{:S(2)}, u32[]{:S(2)}) %collective-permute-start.4) | collective-permute-done | bytes 983072 | tf_op jit(solution)/shard_map/ppermute | solution.py:270
  56.0 0.1 shard_map.87
  56.1 13.1 %all_to_all.20.in_ref = bf16[16,120,128]{2,1,0:T(8,128)(2,1)S(1)} all-to-all(bf16[16,120,128]{2,1,0:T(8,128)(2,1)S(1)} %shard_map.87), channel_id=1, replica_groups=mesh['tm'=16,'rows'=8,'sect'=2] {'tm'}, dimensions={0} | all-to-all | bytes 983040 | tf_op jit(solution)/shard_map/all_to_all | solution.py:272
  69.2 0.1 shard_map.88
  69.3 11.8 %all_to_all.21.in_ref = bf16[8,120,128]{2,1,0:T(8,128)(2,1)S(1)} all-to-all(bf16[8,120,128]{2,1,0:T(8,128)(2,1)S(1)} %shard_map.88), channel_id=1, replica_groups=mesh['tm'=16,'rows'=8,'sect'=2] {'rows'}, dimensions={0} | all-to-all | bytes 491520 | tf_op jit(solution)/shard_map/all_to_all | solution.py:274
  81.1 3.6 %collective-permute-start.5 = (f32[112,128]{1,0:T(8,128)S(1)}, f32[112,128]{1,0:T(8,128)S(1)}, u32[]{:S(2)}, u32[]{:S(2)}) collective-permute-start(f32[112,128]{1,0:T(8,128)S(1)} %get-tuple-element.21), channel_id=1, source_target_pairs={{0,1},{1,0},{2,3},{3,2},{4,5},{5,4},{6,7},{7,6},{8,9},{9,8},{10,11... | collective-permute-start | bytes 172040 | tf_op jit(solution)/shard_map/ppermute | solution.py:280
  84.7 1.0 %shard_map.90 = (bf16[4,8,32,128]{3,2,1,0:T(8,128)(2,1)}, f32[8,128]{1,0:T(8,128)S(1)}) custom-call(bf16[4,8,32,128]{3,2,1,0:T(8,128)(2,1)S(1)} %copy-done, f32[1024,128]{1,0:T(8,128)S(1)} %get-tuple-element.15.da_ref, f32[16,128]{1,0:T(8,128)S(1)} %get-tuple-element.16.norm_ref, f32[8,128]{1,0:T(8,128)S(1)} %get-tuple-element.18.sums_ref, f32[1,128]{1,0:T(1,128)S(1)} %bitcast.38), custom_call_target="tpu_custom_call" | custom-call | bytes 1065472 | tf_op jit(solution)/shard_map/pallas_call | solution.py:25
  85.7 0.5 slice_bitcast_fusion.8
  86.2 0.0 collective-permute-done.5
  86.2 0.7 pad_maximum_fusion.1
  (10 shorter events, 0.1 us)
Async XLA Ops:
  0.6 40.4 %copy-start.1 = (bf16[4,8,32,128]{3,2,1,0:T(8,128)(2,1)S(1)}, bf16[4,8,32,128]{3,2,1,0:T(8,128)(2,1)}, u32[]{:S(2)}) copy-start(bf16[4,8,32,128]{3,2,1,0:T(8,128)(2,1)} %own_ref.1) | copy-start | bytes 786436
  0.6 14.4 %copy-start = (bf16[4,8,32,128]{3,2,1,0:T(8,128)(2,1)S(1)}, bf16[4,8,32,128]{3,2,1,0:T(8,128)(2,1)}, u32[]{:S(2)}) copy-start(bf16[4,8,32,128]{3,2,1,0:T(8,128)(2,1)} %x_ref.5) | copy-start | bytes 786436
  0.7 40.4 %copy-start.4 = (bf16[3,3,3,128,128]{4,3,2,1,0:T(8,128)(2,1)S(1)}, bf16[3,3,3,128,128]{4,3,2,1,0:T(8,128)(2,1)}, u32[]{:S(2)}) copy-start(bf16[3,3,3,128,128]{4,3,2,1,0:T(8,128)(2,1)} %kernel_ref.1) | copy-start | bytes 2654212
  1.8 5.0 %collective-permute-start = (bf16[4,8,16,128]{3,2,0,1:T(8,128)(2,1)S(1)}, bf16[4,8,16,128]{3,2,0,1:T(8,128)(2,1)S(1)}, u32[]{:S(2)}, u32[]{:S(2)}) collective-permute-start(bf16[4,8,16,128]{3,2,0,1:T(8,128)(2,1)S(1)} %copy_select_fusion), channel_id=1, source_target_pairs={{0,1},{1,0},{2,3},{3,2},{4,5},{5,4},{6,7},{7,6},{8,9},{9,8},{10,11... | collective-permute-start | bytes 393224 | tf_op jit(solution)/shard_map/ppermute | solution.py:240
  6.9 3.1 %collective-permute-start.1 = (bf16[4,48,128]{2,1,0:T(8,128)(2,1)S(1)}, bf16[4,48,128]{2,1,0:T(8,128)(2,1)S(1)}, u32[]{:S(2)}, u32[]{:S(2)}) collective-permute-start(bf16[4,48,128]{2,1,0:T(8,128)(2,1)S(1)} %pad_maximum_fusion.2), channel_id=1, source_target_pairs={{0,2},{2,4},{4,6},{6,8},{8,10},{10,12},{12,14},{1,3},{3,5},{5,7},{... | collective-permute-start | bytes 147464 | tf_op jit(solution)/shard_map/ppermute | solution.py:245
  8.7 5.0 %collective-permute-start.2 = (bf16[4,48,128]{2,1,0:T(8,128)(2,1)S(1)}, bf16[4,48,128]{2,1,0:T(8,128)(2,1)S(1)}, u32[]{:S(2)}, u32[]{:S(2)}) collective-permute-start(bf16[4,48,128]{2,1,0:T(8,128)(2,1)S(1)} %pad_maximum_fusion.3), channel_id=1, source_target_pairs={{2,0},{4,2},{6,4},{8,6},{10,8},{12,10},{14,12},{3,1},{5,3},{7,5},{... | collective-permute-start | bytes 147464 | tf_op jit(solution)/shard_map/ppermute | solution.py:246
  13.7 33.8 %copy-start.2 = (f32[128]{0:T(128)S(1)}, f32[128]{0:T(128)}, u32[]{:S(2)}) copy-start(f32[128]{0:T(128)} %param.6) | copy-start | bytes 1540
  13.7 33.8 %copy-start.3 = (f32[128]{0:T(128)S(1)}, f32[128]{0:T(128)}, u32[]{:S(2)}) copy-start(f32[128]{0:T(128)} %param.7) | copy-start | bytes 1540
  13.8 27.3 %collective-permute-start.3 = (bf16[2,10,48,128]{3,2,1,0:T(8,128)(2,1)S(1)}, bf16[2,10,48,128]{3,2,1,0:T(8,128)(2,1)S(1)}, u32[]{:S(2)}, u32[]{:S(2)}) collective-permute-start(bf16[2,10,48,128]{3,2,1,0:T(8,128)(2,1)S(1)} %pad_maximum_fusion), channel_id=1, source_target_pairs={{16,0},{32,16},{48,32},{64,48},{80,64},{96,80},{112,96},{128,112},... | collective-permute-start | bytes 737288 | tf_op jit(solution)/shard_map/ppermute | solution.py:250
  16.0 16.4 %all-to-all-start = ((f32[32,1,128]{2,1,0:T(1,128)}), f32[32,1,128]{2,1,0:T(1,128)S(1)}, u32[]{:S(2)}, u32[]{:S(2)}) async-start(f32[32,1,128]{2,1,0:T(1,128)} %bitcast.4), calls=%async_computation | async-start | bytes 32768 | tf_op jit(solution)/shard_map/all_to_all | solution.py:242
  33.0 14.5 %all-to-all-start.1 = ((f32[8,1,128]{2,1,0:T(1,128)}), f32[8,1,128]{2,1,0:T(1,128)S(1)}, u32[]{:S(2)}, u32[]{:S(2)}) async-start(f32[8,1,128]{2,1,0:T(1,128)} %broadcast_in_dim.12), calls=%async_computation.1 | async-start | bytes 8192 | tf_op jit(solution)/shard_map/all_to_all | solution.py:252
  51.6 4.4 %collective-permute-start.4 = (f32[16,15,8,128]{3,2,1,0:T(8,128)S(1)}, f32[16,15,8,128]{3,2,1,0:T(8,128)S(1)}, u32[]{:S(2)}, u32[]{:S(2)}) collective-permute-start(f32[16,15,8,128]{3,2,1,0:T(8,128)S(1)} %get-tuple-element.22), channel_id=1, source_target_pairs={{0,1},{1,0},{2,3},{3,2},{4,5},{5,4},{6,7},{7,6},{8,9},{9,8},{10,11... | collective-permute-start | bytes 2949128 | tf_op jit(solution)/shard_map/ppermute | solution.py:270
  81.1 5.1 %collective-permute-start.5 = (f32[112,128]{1,0:T(8,128)S(1)}, f32[112,128]{1,0:T(8,128)S(1)}, u32[]{:S(2)}, u32[]{:S(2)}) collective-permute-start(f32[112,128]{1,0:T(8,128)S(1)} %get-tuple-element.21), channel_id=1, source_target_pairs={{0,1},{1,0},{2,3},{3,2},{4,5},{5,4},{6,7},{7,6},{8,9},{9,8},{10,11... | collective-permute-start | bytes 172040 | tf_op jit(solution)/shard_map/ppermute | solution.py:280

commit v2 on v1

--- a/solution.py
+++ b/solution.py
@@ -52,12 +52,18 @@
     return jnp.broadcast_to(jnp.sum(part, axis=0, keepdims=True), part.shape)
 
 
-def stats_kernel(x_ref, out_ref):
+def entry_kernel(place_ref, x_ref, up_ref, stat_ref, facing_ref, edge_ref, early_ref):
+    left = place_ref[3] == 0
+    up = up_ref[...]
+    facing_ref[...] = jnp.where(left, up[:, :, 16:], up[:, :, :16])
+    edge_ref[0] = up[:, 7]
+    edge_ref[1] = up[:, 0]
+    early_ref[...] = up[:2]
     x = x_ref[...].astype(F32).reshape(-1, x_ref.shape[-1])
     total = group_total(column_sum(x))
     square = group_total(column_sum(x * x))
     row = jnp.where(lanes_of(total.shape) % 4 < 2, total, square)
-    out_ref[...] = jnp.broadcast_to(row[None], (out_ref.shape[0] // 8, 8, 128)).reshape(out_ref.shape)
+    stat_ref[...] = jnp.broadcast_to(row[None], (stat_ref.shape[0] // 8, 8, 128)).reshape(stat_ref.shape)
 
 
 def grad_kernel(place_ref, own_ref, side_ref, above_ref, below_ref, later_ref, kernel_ref, v_ref, dh_ref, taps_ref):
@@ -132,37 +138,63 @@
     return total, square
 
 
-def main_kernel(counted, place_ref, x_ref, stat_ref, gain_ref, bias_ref, dh_ref, v_ref, w_ref, da_ref, norm_ref):
+def product_of(turned, v_ref, a, lo, hi):
+    if a == 2:
+        return jnp.dot(turned, v_ref[0:4, :, lo:hi].reshape(1024, hi - lo), preferred_element_type=F32)
+    first = jnp.dot(turned[:, :256], v_ref[7 - a, :, lo:hi], preferred_element_type=F32)
+    rest = v_ref[3 - a : 6 - a, :, lo:hi].reshape(768, hi - lo)
+    return first + jnp.dot(turned[:, 256:], rest, preferred_element_type=F32)
+
+
+def half_product(half, turned, v_ref, w_ref):
+    for a, lo, hi in (((0, 0, 9), (1, 0, 5)), ((1, 5, 9), (2, 0, 9)))[half]:
+        product = product_of(turned, v_ref, a, lo * 128, hi * 128)
+        for j in range(lo, hi):
+            block = product[:, (j - lo) * 128 : (j - lo + 1) * 128].T.reshape(16, 8, 128)
+            w_ref[:, (a * 9 + j) % HALF] = block
+    if half == 1:
+        w_ref[:, HALF - 1] = jnp.zeros((16, 8, 128), F32)
+
+
+def normalised(x_ref, mean, rstd, gain_ref, bias_ref):
+    xhat = (x_ref[...].astype(F32).reshape(-1, 128) - mean) * rstd
+    return xhat, xhat * gain_ref[...] + bias_ref[...]
+
+
+def away_kernel(counted, place_ref, x_ref, stat_ref, gain_ref, bias_ref, v_ref, w_ref, turned_ref, norm_ref):
     total, square = sums_to_pair(column_sum(stat_ref[...]))
     mean = total / counted
     rstd = lax.rsqrt(square / counted - mean * mean + 1e-06)
     norm_ref[0:8] = mean
     norm_ref[8:16] = rstd
-    mean = mean[:1]
-    rstd = rstd[:1]
-    xhat = (x_ref[...].astype(F32).reshape(-1, 128) - mean) * rstd
-    pre = xhat * gain_ref[...] + bias_ref[...]
+    _, pre = normalised(x_ref, mean[:1], rstd[:1], gain_ref, bias_ref)
+    turned_ref[...] = (pre * (1.0 / (1.0 + jnp.exp(-pre)))).T.astype(BF16)
+    left = place_ref[3] == 0
+
+    @pl.when(left)
+    def _():
+        half_product(1, turned_ref[...], v_ref, w_ref)
+
+    @pl.when(jnp.logical_not(left))
+    def _():
+        half_product(0, turned_ref[...], v_ref, w_ref)
+
+
+def home_kernel(place_ref, x_ref, norm_ref, gain_ref, bias_ref, dh_ref, turned_ref, v_ref, sums_ref, da_ref, w_ref):
+    xhat, pre = normalised(x_ref, norm_ref[0:1], norm_ref[8:9], gain_ref, bias_ref)
     sig = 1.0 / (1.0 + jnp.exp(-pre))
-    hidden = pre * sig
     da = dh_ref[...] * sig * (1.0 + pre * (1.0 - sig))
     da_ref[...] = da
-    sums = jnp.where(sublanes_of((8, 128)) == 0, column_sum(da), column_sum(da * xhat))
-    for half in range(2):
-        w_ref[half, :, HALF] = jnp.broadcast_to(sums[None], (16, 8, 128))
-    turned = hidden.T.astype(BF16)
-    sect = place_ref[3]
-    for a in range(3):
-        if a == 2:
-            product = jnp.dot(turned, v_ref[0:4].reshape(1024, 1152), preferred_element_type=F32)
-        else:
-            product = jnp.dot(turned[:, :256], v_ref[7 - a], preferred_element_type=F32) + jnp.dot(
-                turned[:, 256:], v_ref[3 - a : 6 - a].reshape(768, 1152), preferred_element_type=F32
-            )
-        for j in range(9):
-            tap = a * 9 + j
-            block = product[:, j * 128 : (j + 1) * 128].T.reshape(16, 8, 128)
-            w_ref[(tap // HALF) ^ sect, :, tap % HALF] = block
-    w_ref[1 ^ sect, :, HALF - 1] = jnp.zeros((16, 8, 128), F32)
+    sums_ref[...] = jnp.where(sublanes_of((8, 128)) == 0, column_sum(da), column_sum(da * xhat))
+    left = place_ref[3] == 0
+
+    @pl.when(left)
+    def _():
+        half_product(0, turned_ref[...], v_ref, w_ref)
+
+    @pl.when(jnp.logical_not(left))
+    def _():
+        half_product(1, turned_ref[...], v_ref, w_ref)
 
 
 def split_sums(sums):
@@ -179,11 +211,10 @@
     return parts + pltpu.roll(parts, 6, 0) + pltpu.roll(parts, 4, 0)
 
 
-def pair_kernel(own_ref, other_ref, out_ref):
-    rows = HALF * 8
-    slot = split_sums(own_ref[0, HALF] + other_ref[0, HALF])
+def pair_kernel(own_ref, other_ref, sums_ref, other_sums_ref, out_ref):
+    slot = split_sums(sums_ref[...] + other_sums_ref[...])
     for i in range(16):
-        body = (own_ref[i, :HALF] + other_ref[i, :HALF]).reshape(rows, 128)
+        body = (own_ref[i] + other_ref[i]).reshape(HALF * 8, 128)
         out_ref[i] = jnp.concatenate([body, slot], axis=0).astype(BF16)
 
 
@@ -192,33 +223,41 @@
     total = in_ref[0].astype(F32)
     for i in range(1, in_ref.shape[0]):
         total = total + in_ref[i].astype(F32)
-    slot = split_sums(join_sums(total[rows:]))
-    sent = jnp.concatenate([total[:rows], slot], axis=0).astype(BF16)
+    sent = jnp.concatenate([total[:rows], join_sums(total[rows:])], axis=0)
     for i in range(out_ref.shape[0]):
         out_ref[i] = sent
 
 
 def last_sum_kernel(scaling, in_ref, half_ref, sums_ref):
     rows = HALF * 8
-    total = in_ref[0].astype(F32)
+    total = in_ref[0]
     for i in range(1, in_ref.shape[0]):
-        total = total + in_ref[i].astype(F32)
+        total = total + in_ref[i]
     half_ref[...] = total[:rows] * scaling
-    sums_ref[...] = join_sums(total[rows:])
-
-
-def finish_kernel(counted, scaling, x_ref, da_ref, norm_ref, sums_ref, gain_ref, out_ref, grads_ref):
+    sums_ref[...] = total[rows:]
+
+
+def finish_kernel(counted, scaling, x_ref, da_ref, norm_ref, sums_ref, gain_ref, out_ref, gain_grad_ref, bias_grad_ref):
     gain = gain_ref[...]
     mean = norm_ref[0:1]
     rstd = norm_ref[8:9]
     sums = sums_ref[...]
-    grads_ref[...] = sums * scaling
+    bias_grad_ref[...] = sums[0:1] * scaling
+    gain_grad_ref[...] = sums[1:2] * scaling
     averages = group_total(gain * sums) / counted
     leading = averages[0:1]
     trailing = averages[1:2]
     xhat = (x_ref[...].astype(F32).reshape(-1, 128) - mean) * rstd
     grad = rstd * (da_ref[...] * gain - leading - xhat * trailing)
     out_ref[...] = grad.astype(BF16).reshape(out_ref.shape)
+
+
+def join_kernel(place_ref, half_ref, other_ref, out_ref):
+    left = place_ref[3] == 0
+    half = half_ref[...]
+    other = other_ref[...]
+    out_ref[: HALF * 8] = jnp.where(left, half, other)
+    out_ref[HALF * 8 :] = jnp.where(left, other, half)[: (TAPS - HALF) * 8]
 
 
 def shape_of(shape, dtype=F32):
@@ -236,19 +275,31 @@
     place = jnp.stack([tm, rows, jnp.int32(n_rows), sect]).astype(jnp.int32)
     swap = [(0, 1), (1, 0)]
 
-    facing = jnp.where(sect == 0, upstream[:, :, 16:], upstream[:, :, :16])
+    stat, facing, edges, first_frames = call(
+        entry_kernel,
+        [
+            shape_of((32, 128)),
+            shape_of((frames, height, 16, channels), BF16),
+            shape_of((2, frames, columns, channels), BF16),
+            shape_of((2, height, columns, channels), BF16),
+        ],
+        [place, activations, upstream],
+        smem_first=True,
+    )
     side = lax.ppermute(facing, "sect", swap)
-    (stat,) = call(stats_kernel, [shape_of((32, 128))], [activations])
-    stat = lax.all_to_all(stat.reshape(32, 1, 128), ("tm", "sect"), 0, 0)
-    last_row = jnp.concatenate([upstream[:, height - 1], side[:, height - 1]], axis=1)
-    first_row = jnp.concatenate([upstream[:, 0], side[:, 0]], axis=1)
+    last_row = jnp.concatenate([edges[0], side[:, height - 1]], axis=1)
+    first_row = jnp.concatenate([edges[1], side[:, 0]], axis=1)
+    stat, last_row, first_row = lax.optimization_barrier((stat, last_row, first_row))
     above = lax.ppermute(last_row, "rows", [(i, i + 1) for i in range(n_rows - 1)])
     below = lax.ppermute(first_row, "rows", [(i + 1, i) for i in range(n_rows - 1)])
+    stat = lax.all_to_all(stat.reshape(32, 1, 128), ("tm", "sect"), 0, 0)
+    stat = jnp.broadcast_to(jnp.sum(stat, axis=0)[None], (n_rows, 1, 128))
+    stat, above, below = lax.optimization_barrier((stat, above, below))
     early = jnp.concatenate(
-        [above[:2, None], jnp.concatenate([upstream[:2], side[:2]], axis=2), below[:2, None]], axis=1
-    )
+        [above[:2, None], jnp.concatenate([first_frames, side[:2]], axis=2), below[:2, None]], axis=1
+    )
+    stat, early = lax.optimization_barrier((stat, early))
     later = lax.ppermute(early, "tm", [(i + 1, i) for i in range(n_time - 1)])
-    stat = jnp.broadcast_to(jnp.sum(stat, axis=0)[None], (n_rows, 1, 128))
     stat = lax.all_to_all(stat, "rows", 0, 0).reshape(n_rows, 128)
     spread, hidden_grad = call(
         grad_kernel,
@@ -260,17 +311,27 @@
     )
     gain = group_norm_gain.reshape(1, channels)
     bias = group_norm_bias.reshape(1, channels)
-    terms, da, norm = call(
-        functools.partial(main_kernel, counted),
-        [shape_of((2, 16, SLOTS, 8, 128)), shape_of((cells, channels)), shape_of((16, channels))],
-        [place, activations, stat, gain, bias, hidden_grad, spread],
-        flops=2 * cells * TAPS * channels * channels,
+    away, turned, norm = call(
+        functools.partial(away_kernel, counted),
+        [shape_of((16, HALF, 8, 128)), shape_of((channels, cells), BF16), shape_of((16, channels))],
+        [place, activations, stat, gain, bias, spread],
+        flops=cells * TAPS * channels * channels,
         smem_first=True,
     )
-    other = lax.ppermute(terms[1], "sect", swap)
-    (sent,) = call(pair_kernel, [shape_of((16, SLOTS * 8, 128), BF16)], [terms[0], other])
+    arrived = lax.ppermute(away, "sect", swap)
+    sums, da, home = call(
+        home_kernel,
+        [shape_of((8, channels)), shape_of((cells, channels)), shape_of((16, HALF, 8, 128))],
+        [place, activations, norm, gain, bias, hidden_grad, turned, spread],
+        flops=cells * TAPS * channels * channels,
+        smem_first=True,
+    )
+    other_sums = lax.ppermute(sums, "sect", swap)
+    (sent,) = call(
+        pair_kernel, [shape_of((16, SLOTS * 8, 128), BF16)], [home, arrived, sums, other_sums]
+    )
     gathered = lax.all_to_all(sent, "tm", 0, 0)
-    (sent,) = call(share_kernel, [shape_of((n_rows, SLOTS * 8, 128), BF16)], [gathered])
+    (sent,) = call(share_kernel, [shape_of((n_rows, SLOTS * 8, 128))], [gathered])
     gathered = lax.all_to_all(sent, "rows", 0, 0)
     half, sums = call(
         functools.partial(last_sum_kernel, scaling),
@@ -278,16 +339,14 @@
         [gathered],
     )
     other = lax.ppermute(half, "sect", swap)
-    input_gradient, grads = call(
+    input_gradient, gain_grad, bias_grad = call(
         functools.partial(finish_kernel, counted, scaling),
-        [shape_of(activations.shape, BF16), shape_of((8, 128))],
+        [shape_of(activations.shape, BF16), shape_of((1, 128)), shape_of((1, 128))],
         [activations, da, norm, sums, gain],
     )
-    whole = jnp.concatenate(
-        [jnp.where(sect == 0, half, other), jnp.where(sect == 0, other, half)], axis=0
-    )
-    weight_grad = whole[: TAPS * 8].reshape(3, 3, 3, 8, 128).transpose(0, 1, 2, 4, 3)
-    return (input_gradient, grads[1], grads[0], weight_grad)
+    (whole,) = call(join_kernel, [shape_of((TAPS * 8, 128))], [place, half, other], smem_first=True)
+    weight_grad = whole.reshape(3, 3, 3, 8, 128).transpose(0, 1, 2, 4, 3)
+    return (input_gradient, gain_grad.reshape(128), bias_grad.reshape(128), weight_grad)
 
 
 def solution(mesh):

time: 87.3 us -> 96.7 us (1.11)
  blocking collectives: 24.9 us -> 50 us
  waiting for transfers between devices: 15.4 us -> 2.7 us
  starting transfers between devices: 31 us -> 23.6 us
  local copies, waits for them, and re-layouts: 4.08 us -> 6.98 us
  Pallas kernels: 9.76 us -> 12 us
    all_to_all x0 -> x1, blocking collectives: none -> 14.5 us  [local(): stat = lax.all_to_all(stat.reshape(32, 1, 128), ('tm', 'sect'), 0, 0)]
    all_to_all x1 -> x0, starting transfers between devices: 9.52 us -> none  [local(): stat = lax.all_to_all(stat.reshape(32, 1, 128), ('tm', 'sect'), 0, 0)]
    all_to_all x1, blocking collectives: 11.8 us -> 20.2 us  [local(): gathered = lax.all_to_all(sent, 'rows', 0, 0)]
    all_to_all x1 -> x0, waiting for transfers between devices: 6.78 us -> none  [local(): stat = lax.all_to_all(stat.reshape(32, 1, 128), ('tm', 'sect'), 0, 0)]
    unnamed x10 -> x16, local copies, waits for them, and re-layouts: 0.03 us -> 6.36 us
    ppermute x1, waiting for transfers between devices: 3.7 us -> 0.01 us  [local(): lax.ppermute(first_row, 'rows', [(i + 1, i) for i in range(n_rows - 1)])]
    all_to_all x1, blocking collectives: 13.1 us -> 15.4 us  [local(): gathered = lax.all_to_all(sent, 'tm', 0, 0)]
    pallas_call x7 -> x9, Pallas kernels: 9.76 us -> 12 us  [call(): pl.pallas_call(body, out_shape=outs, in_specs=specs, out_specs=[VMEM] * l...]
  transfers between devices with their start and end apart: 8 -> 8, of which waited for: 4 -> 3; matrix products, arithmetic and copies ran while one was open for 3% -> 0% of each run, Pallas kernels for 6% -> 8%
where the time goes in v2:
time: 96.7 us; the launch traced here: 96.2 us
  blocking collectives  50 us (52%)
  starting transfers between devices  23.6 us (24%)
  Pallas kernels  12 us (12%)
  local copies, waits for them, and re-layouts  6.98 us (7%)
  waiting for transfers between devices  2.7 us (3%)
    all_to_all x1, blocking collectives, local(): gathered = lax.all_to_all(sent, 'rows', 0, 0)  20.2 us
    all_to_all x1, blocking collectives, local(): gathered = lax.all_to_all(sent, 'tm', 0, 0)  15.4 us
    all_to_all x1, blocking collectives, local(): stat = lax.all_to_all(stat.reshape(32, 1, 128), ('tm', 'sect'), 0, 0)  14.5 us
    pallas_call x9, Pallas kernels, call(): pl.pallas_call(body, out_shape=outs, in_specs=specs, out_specs=[VMEM] * l...  12 us
    all_to_all x1, starting transfers between devices, local(): stat = lax.all_to_all(stat, 'rows', 0, 0).reshape(n_rows, 128)  10.1 us
    unnamed x16, local copies, waits for them, and re-layouts  6.36 us
    ppermute x1, starting transfers between devices, local(): other = lax.ppermute(half, 'sect', swap)  3.43 us
    ppermute x1, starting transfers between devices, local(): side = lax.ppermute(facing, 'sect', swap)  3.33 us
  transfers between devices with their start and end apart: 8, of which 3 were waited for; matrix products, arithmetic and copies ran while one was open for 0% of the time, Pallas kernels for 8%

profile of v2, /device:TPU:1, one launch (start us, length us, event | category | flops | bytes accessed | tf_op | source)
XLA Modules:
  0.0 96.2 jit_solution(7726802160416171389)
XLA Ops:
  0.6 0.0 copy-start.6
  0.6 0.0 copy-start.5
  0.7 0.1 pad_add_fusion.place_ref
  0.7 0.0 copy-start.1
  0.7 0.9 copy-done.1
  1.7 0.0 copy-start.3
  1.7 0.9 copy-done.3
  2.6 0.0 copy-start.2
  2.6 0.8 shard_map.84
  3.5 3.3 %collective-permute-start = (bf16[4,8,16,128]{3,2,0,1:T(8,128)(2,1)S(1)}, bf16[4,8,16,128]{3,2,0,1:T(8,128)(2,1)S(1)}, u32[]{:S(2)}, u32[]{:S(2)}) collective-permute-start(bf16[4,8,16,128]{3,2,0,1:T(8,128)(2,1)S(1)} %copy.12), channel_id=1, source_target_pairs={{0,1},{1,0},{2,3},{3,2},{4,5},{5,4},{6,7},{7,6},{8,9},{9,8},{10,11... | collective-permute-start | bytes 393224 | tf_op jit(solution)/shard_map/ppermute | solution.py:289
  6.8 1.0 %collective-permute-done = bf16[4,8,16,128]{3,2,0,1:T(8,128)(2,1)S(1)} collective-permute-done((bf16[4,8,16,128]{3,2,0,1:T(8,128)(2,1)S(1)}, bf16[4,8,16,128]{3,2,0,1:T(8,128)(2,1)S(1)}, u32[]{:S(2)}, u32[]{:S(2)}) %collective-permute-start) | collective-permute-done | bytes 131104 | tf_op jit(solution)/shard_map/ppermute | solution.py:289
  7.8 1.8 %collective-permute-start.1 = (bf16[4,48,128]{2,1,0:T(8,128)(2,1)S(1)}, bf16[4,48,128]{2,1,0:T(8,128)(2,1)S(1)}, u32[]{:S(2)}, u32[]{:S(2)}) collective-permute-start(bf16[4,48,128]{2,1,0:T(8,128)(2,1)S(1)} %get-tuple-element.33), channel_id=1, source_target_pairs={{0,2},{2,4},{4,6},{6,8},{8,10},{10,12},{12,14},{1,3},{3,5},{5,7},{... | collective-permute-start | bytes 147464 | tf_op jit(solution)/shard_map/ppermute | solution.py:293
  9.6 1.3 %collective-permute-start.2 = (bf16[4,48,128]{2,1,0:T(8,128)(2,1)S(1)}, bf16[4,48,128]{2,1,0:T(8,128)(2,1)S(1)}, u32[]{:S(2)}, u32[]{:S(2)}) collective-permute-start(bf16[4,48,128]{2,1,0:T(8,128)(2,1)S(1)} %get-tuple-element.34), channel_id=1, source_target_pairs={{2,0},{4,2},{6,4},{8,6},{10,8},{12,10},{14,12},{3,1},{5,3},{7,5},{... | collective-permute-start | bytes 147464 | tf_op jit(solution)/shard_map/ppermute | solution.py:294
  10.9 14.5 %all_to_all.20 = f32[32,1,128]{2,1,0:T(1,128)S(1)} all-to-all(f32[32,1,128]{2,1,0:T(1,128)S(1)} %bitcast.27), channel_id=1, replica_groups=mesh['tm'=16,'rows'=8,'sect'=2] {'tm','sect'}, dimensions={0} | all-to-all | bytes 32768 | tf_op jit(solution)/shard_map/all_to_all | solution.py:295
  25.4 0.1 reduce_sum.9
  25.4 0.0 collective-permute-done.1.above_ref
  25.4 0.0 collective-permute-done.2.below_ref
  25.5 0.6 broadcast_in_dim.12
  26.1 1.3 %collective-permute-start.3 = (bf16[2,10,48,128]{3,2,1,0:T(8,128)(2,1)S(1)}, bf16[2,10,48,128]{3,2,1,0:T(8,128)(2,1)S(1)}, u32[]{:S(2)}, u32[]{:S(2)}) collective-permute-start(bf16[2,10,48,128]{3,2,1,0:T(8,128)(2,1)S(1)} %pad_maximum_fusion), channel_id=1, source_target_pairs={{16,0},{32,16},{48,32},{64,48},{80,64},{96,80},{112,96},{128,112},... | collective-permute-start | bytes 737288 | tf_op jit(solution)/shard_map/ppermute | solution.py:302
  27.4 10.1 %all-to-all-start.1 = ((f32[8,1,128]{2,1,0:T(1,128)}), f32[8,1,128]{2,1,0:T(1,128)S(1)}, u32[]{:S(2)}, u32[]{:S(2)}) async-start(f32[8,1,128]{2,1,0:T(1,128)} %broadcast_in_dim.12), calls=%async_computation.1 | async-start | bytes 8192 | tf_op jit(solution)/shard_map/all_to_all | solution.py:303
  37.5 0.0 collective-permute-done.3.later_ref
  37.5 0.0 copy-start.4
  37.5 0.9 copy-done.4
  38.5 0.0 copy-start.7
  38.5 1.2 %copy-done.7 = bf16[3,3,3,128,128]{4,3,2,1,0:T(8,128)(2,1)S(1)} copy-done((bf16[3,3,3,128,128]{4,3,2,1,0:T(8,128)(2,1)S(1)}, bf16[3,3,3,128,128]{4,3,2,1,0:T(8,128)(2,1)}, u32[]{:S(2)}) %copy-start.7) | copy-done | bytes 884760
  39.7 3.7 %shard_map.85 = (bf16[8,256,1152]{2,1,0:T(8,128)(2,1)}, f32[1024,128]{1,0:T(8,128)S(1)}) custom-call(s32[4]{0:T(128)S(1)} %pad_add_fusion.place_ref, bf16[4,8,32,128]{3,2,1,0:T(8,128)(2,1)S(1)} %copy-done.4, bf16[4,8,16,128]{3,2,1,0:T(8,128)(2,1)S(1)} %copy.15.side_ref, bf16[4,48,128]{2,1,0:T(8,128)(2,1)S(1)} %collective-permute-done.1.above_ref, ...), custom_call_target="tpu_custom_call" | custom-call | flops 905969664 | bytes 6864912 | tf_op jit(solution)/shard_map/pallas_call | solution.py:25
  43.3 0.7 all-to-all-done.1
  44.0 0.0 copy-done.6
  44.0 0.0 copy-done.5
  44.0 0.0 copy-done.2
  44.0 0.0 copy-start
  44.0 2.3 %copy-done = bf16[8,256,1152]{2,1,0:T(8,128)(2,1)S(1)} copy-done((bf16[8,256,1152]{2,1,0:T(8,128)(2,1)S(1)}, bf16[8,256,1152]{2,1,0:T(8,128)(2,1)}, u32[]{:S(2)}) %copy-start) | copy-done | bytes 4718616
  46.3 1.7 %shard_map.86 = (f32[16,14,8,128]{3,2,1,0:T(8,128)S(1)}, bf16[128,1024]{1,0:T(8,128)(2,1)S(1)}, f32[16,128]{1,0:T(8,128)S(1)}) custom-call(s32[4]{0:T(128)S(1)} %pad_add_fusion.place_ref, bf16[4,8,32,128]{3,2,1,0:T(8,128)(2,1)S(1)} %copy-done.2, f32[8,128]{1,0:T(8,128)S(1)} %bitcast.26, f32[1,128]{1,0:T(1,128)S(1)} %bitcast.28, f32[1,128]{1,0:T(1,128)S(1)} %bitcast.31, ...), custom_call_target="tpu_custom_call" | custom-call | flops 452984832 | bytes 6173712 | tf_op jit(solution)/shard_map/pallas_call | solution.py:25
  48.1 2.1 %collective-permute-start.4 = (f32[16,14,8,128]{3,2,1,0:T(8,128)S(1)}, f32[16,14,8,128]{3,2,1,0:T(8,128)S(1)}, u32[]{:S(2)}, u32[]{:S(2)}) collective-permute-start(f32[16,14,8,128]{3,2,1,0:T(8,128)S(1)} %get-tuple-element.47), channel_id=1, source_target_pairs={{0,1},{1,0},{2,3},{3,2},{4,5},{5,4},{6,7},{7,6},{8,9},{9,8},{10,11... | collective-permute-start | bytes 2752520 | tf_op jit(solution)/shard_map/ppermute | solution.py:321
  50.1 3.4 %shard_map.87 = (f32[8,128]{1,0:T(8,128)S(1)}, f32[1024,128]{1,0:T(8,128)S(1)}, f32[16,14,8,128]{3,2,1,0:T(8,128)S(1)}) custom-call(s32[4]{0:T(128)S(1)} %pad_add_fusion.place_ref, bf16[4,8,32,128]{3,2,1,0:T(8,128)(2,1)S(1)} %copy-done.2, f32[16,128]{1,0:T(8,128)S(1)} %get-tuple-element.42.norm_ref, f32[1,128]{1,0:T(1,128)S(1)} %bitcast.29, ...), custom_call_target="tpu_custom_call" | custom-call | flops 452984832 | bytes 7222288 | tf_op jit(solution)/shard_map/pallas_call | solution.py:25
  53.5 0.2 collective-permute-start.5
  53.7 1.0 %collective-permute-done.5.other_sums_ref = f32[8,128]{1,0:T(8,128)S(1)} collective-permute-done((f32[8,128]{1,0:T(8,128)S(1)}, f32[8,128]{1,0:T(8,128)S(1)}, u32[]{:S(2)}, u32[]{:S(2)}) %collective-permute-start.5) | collective-permute-done | bytes 4128 | tf_op jit(solution)/shard_map/ppermute | solution.py:329
  54.8 0.0 collective-permute-done.4.other_ref
  54.8 0.1 shard_map.88
  54.9 15.4 %all_to_all.21.in_ref = bf16[16,120,128]{2,1,0:T(8,128)(2,1)S(1)} all-to-all(bf16[16,120,128]{2,1,0:T(8,128)(2,1)S(1)} %shard_map.88), channel_id=1, replica_groups=mesh['tm'=16,'rows'=8,'sect'=2] {'tm'}, dimensions={0} | all-to-all | bytes 983040 | tf_op jit(solution)/shard_map/all_to_all | solution.py:333
  70.3 0.1 shard_map.89
  70.3 20.2 %all_to_all.22.in_ref = f32[8,120,128]{2,1,0:T(8,128)S(1)} all-to-all(f32[8,120,128]{2,1,0:T(8,128)S(1)} %shard_map.89), channel_id=1, replica_groups=mesh['tm'=16,'rows'=8,'sect'=2] {'rows'}, dimensions={0} | all-to-all | bytes 983040 | tf_op jit(solution)/shard_map/all_to_all | solution.py:335
  90.5 3.4 %collective-permute-start.6 = (f32[112,128]{1,0:T(8,128)S(1)}, f32[112,128]{1,0:T(8,128)S(1)}, u32[]{:S(2)}, u32[]{:S(2)}) collective-permute-start(f32[112,128]{1,0:T(8,128)S(1)} %get-tuple-element.53.half_ref), channel_id=1, source_target_pairs={{0,1},{1,0},{2,3},{3,2},{4,5},{5,4},{6,7},{7,6},{8,9},{9,8},{10,11... | collective-permute-start | bytes 172040 | tf_op jit(solution)/shard_map/ppermute | solution.py:341
  94.0 1.0 %shard_map.91 = (bf16[4,8,32,128]{3,2,1,0:T(8,128)(2,1)}, f32[1,128]{1,0:T(1,128)}, f32[1,128]{1,0:T(1,128)}) custom-call(bf16[4,8,32,128]{3,2,1,0:T(8,128)(2,1)S(1)} %copy-done.2, f32[1024,128]{1,0:T(8,128)S(1)} %get-tuple-element.45.da_ref, f32[16,128]{1,0:T(8,128)S(1)} %get-tuple-element.42.norm_ref, f32[8,128]{1,0:T(8,128)S(1)} %get-tuple-element.49.sums_ref, ...), custom_call_target="tpu_custom_call" | custom-call | bytes 1062400 | tf_op jit(solution)/shard_map/pallas_call | solution.py:25
  95.0 0.0 collective-permute-done.6.other_ref
  95.0 1.2 %shard_map.92 = f32[216,128]{1,0:T(8,128)} custom-call(s32[4]{0:T(128)S(1)} %pad_add_fusion.place_ref, f32[112,128]{1,0:T(8,128)S(1)} %get-tuple-element.53.half_ref, f32[112,128]{1,0:T(8,128)S(1)} %collective-permute-done.6.other_ref), custom_call_target="tpu_custom_call" | custom-call | bytes 225296 | tf_op jit(solution)/shard_map/pallas_call | solution.py:25
  (9 shorter events, 0.1 us)
Async XLA Ops:
  0.6 43.4 %copy-start.6 = (f32[128]{0:T(128)S(1)}, f32[128]{0:T(128)}, u32[]{:S(2)}) copy-start(f32[128]{0:T(128)} %param.7) | copy-start | bytes 1540
  0.6 43.3 %copy-start.5 = (f32[128]{0:T(128)S(1)}, f32[128]{0:T(128)}, u32[]{:S(2)}) copy-start(f32[128]{0:T(128)} %param.6) | copy-start | bytes 1540
  0.7 1.0 copy-start.1
  1.7 0.9 copy-start.3
  2.6 41.4 %copy-start.2 = (bf16[4,8,32,128]{3,2,1,0:T(8,128)(2,1)S(1)}, bf16[4,8,32,128]{3,2,1,0:T(8,128)(2,1)}, u32[]{:S(2)}) copy-start(bf16[4,8,32,128]{3,2,1,0:T(8,128)(2,1)} %x_ref.7) | copy-start | bytes 786436
  3.5 4.3 %collective-permute-start = (bf16[4,8,16,128]{3,2,0,1:T(8,128)(2,1)S(1)}, bf16[4,8,16,128]{3,2,0,1:T(8,128)(2,1)S(1)}, u32[]{:S(2)}, u32[]{:S(2)}) collective-permute-start(bf16[4,8,16,128]{3,2,0,1:T(8,128)(2,1)S(1)} %copy.12), channel_id=1, source_target_pairs={{0,1},{1,0},{2,3},{3,2},{4,5},{5,4},{6,7},{7,6},{8,9},{9,8},{10,11... | collective-permute-start | bytes 393224 | tf_op jit(solution)/shard_map/ppermute | solution.py:289
  7.8 17.6 %collective-permute-start.1 = (bf16[4,48,128]{2,1,0:T(8,128)(2,1)S(1)}, bf16[4,48,128]{2,1,0:T(8,128)(2,1)S(1)}, u32[]{:S(2)}, u32[]{:S(2)}) collective-permute-start(bf16[4,48,128]{2,1,0:T(8,128)(2,1)S(1)} %get-tuple-element.33), channel_id=1, source_target_pairs={{0,2},{2,4},{4,6},{6,8},{8,10},{10,12},{12,14},{1,3},{3,5},{5,7},{... | collective-permute-start | bytes 147464 | tf_op jit(solution)/shard_map/ppermute | solution.py:293
  9.6 15.8 %collective-permute-start.2 = (bf16[4,48,128]{2,1,0:T(8,128)(2,1)S(1)}, bf16[4,48,128]{2,1,0:T(8,128)(2,1)S(1)}, u32[]{:S(2)}, u32[]{:S(2)}) collective-permute-start(bf16[4,48,128]{2,1,0:T(8,128)(2,1)S(1)} %get-tuple-element.34), channel_id=1, source_target_pairs={{2,0},{4,2},{6,4},{8,6},{10,8},{12,10},{14,12},{3,1},{5,3},{7,5},{... | collective-permute-start | bytes 147464 | tf_op jit(solution)/shard_map/ppermute | solution.py:294
  26.1 11.5 %collective-permute-start.3 = (bf16[2,10,48,128]{3,2,1,0:T(8,128)(2,1)S(1)}, bf16[2,10,48,128]{3,2,1,0:T(8,128)(2,1)S(1)}, u32[]{:S(2)}, u32[]{:S(2)}) collective-permute-start(bf16[2,10,48,128]{3,2,1,0:T(8,128)(2,1)S(1)} %pad_maximum_fusion), channel_id=1, source_target_pairs={{16,0},{32,16},{48,32},{64,48},{80,64},{96,80},{112,96},{128,112},... | collective-permute-start | bytes 737288 | tf_op jit(solution)/shard_map/ppermute | solution.py:302
  27.4 16.6 %all-to-all-start.1 = ((f32[8,1,128]{2,1,0:T(1,128)}), f32[8,1,128]{2,1,0:T(1,128)S(1)}, u32[]{:S(2)}, u32[]{:S(2)}) async-start(f32[8,1,128]{2,1,0:T(1,128)} %broadcast_in_dim.12), calls=%async_computation.1 | async-start | bytes 8192 | tf_op jit(solution)/shard_map/all_to_all | solution.py:303
  37.5 1.0 copy-start.4
  38.5 1.2 %copy-start.7 = (bf16[3,3,3,128,128]{4,3,2,1,0:T(8,128)(2,1)S(1)}, bf16[3,3,3,128,128]{4,3,2,1,0:T(8,128)(2,1)}, u32[]{:S(2)}) copy-start(bf16[3,3,3,128,128]{4,3,2,1,0:T(8,128)(2,1)} %kernel_ref.1) | copy-start | bytes 2654212
  44.0 2.3 %copy-start = (bf16[8,256,1152]{2,1,0:T(8,128)(2,1)S(1)}, bf16[8,256,1152]{2,1,0:T(8,128)(2,1)}, u32[]{:S(2)}) copy-start(bf16[8,256,1152]{2,1,0:T(8,128)(2,1)} %get-tuple-element.41.v_ref) | copy-start | bytes 14155780
  48.1 6.7 %collective-permute-start.4 = (f32[16,14,8,128]{3,2,1,0:T(8,128)S(1)}, f32[16,14,8,128]{3,2,1,0:T(8,128)S(1)}, u32[]{:S(2)}, u32[]{:S(2)}) collective-permute-start(f32[16,14,8,128]{3,2,1,0:T(8,128)S(1)} %get-tuple-element.47), channel_id=1, source_target_pairs={{0,1},{1,0},{2,3},{3,2},{4,5},{5,4},{6,7},{7,6},{8,9},{9,8},{10,11... | collective-permute-start | bytes 2752520 | tf_op jit(solution)/shard_map/ppermute | solution.py:321
  53.5 1.3 %collective-permute-start.5 = (f32[8,128]{1,0:T(8,128)S(1)}, f32[8,128]{1,0:T(8,128)S(1)}, u32[]{:S(2)}, u32[]{:S(2)}) collective-permute-start(f32[8,128]{1,0:T(8,128)S(1)} %get-tuple-element.48.sums_ref), channel_id=1, source_target_pairs={{0,1},{1,0},{2,3},{3,2},{4,5},{5,4},{6,7},{7,6},{8,9},{9,8},{10,11... | collective-permute-start | bytes 12296 | tf_op jit(solution)/shard_map/ppermute | solution.py:329
  90.5 4.5 %collective-permute-start.6 = (f32[112,128]{1,0:T(8,128)S(1)}, f32[112,128]{1,0:T(8,128)S(1)}, u32[]{:S(2)}, u32[]{:S(2)}) collective-permute-start(f32[112,128]{1,0:T(8,128)S(1)} %get-tuple-element.53.half_ref), channel_id=1, source_target_pairs={{0,1},{1,0},{2,3},{3,2},{4,5},{5,4},{6,7},{7,6},{8,9},{9,8},{10,11... | collective-permute-start | bytes 172040 | tf_op jit(solution)/shard_map/ppermute | solution.py:341

commit v3 on v2

v3 whole, which is shorter than its diff:
```python
import functools

import jax
import jax.numpy as jnp
from jax import lax
from jax.experimental import pallas as pl
from jax.experimental.pallas import tpu as pltpu
from jax.sharding import PartitionSpec as P

GROUPS = 32
TAPS = 27
HALF = 14
SLOTS = HALF + 1
F32 = jnp.float32
BF16 = jnp.bfloat16
VMEM = pl.BlockSpec(memory_space=pltpu.VMEM)
SMEM = pl.BlockSpec(memory_space=pltpu.SMEM)
ANY = pl.BlockSpec(memory_space=pl.ANY)


def call(body, outs, args, specs=None, scratch=(), flops=0):
    moved = sum(x.size * x.dtype.itemsize for x in list(args) + list(outs))
    return pl.pallas_call(
        body,
        out_shape=outs,
        in_specs=specs or [VMEM] * len(args),
        out_specs=[VMEM] * len(outs),
        scratch_shapes=list(scratch),
        cost_estimate=pl.CostEstimate(flops=flops, bytes_accessed=moved, transcendentals=0),
        compiler_params=pltpu.CompilerParams(vmem_limit_bytes=24 * 1024 * 1024),
    )(*args)


def lanes_of(shape):
    return lax.broadcasted_iota(jnp.int32, shape, len(shape) - 1)


def sublanes_of(shape):
    return lax.broadcasted_iota(jnp.int32, shape, len(shape) - 2)


def group_total(v):
    lane = lanes_of(v.shape)
    v = v + jnp.where(lane % 2 == 0, pltpu.roll(v, 127, 1), pltpu.roll(v, 1, 1))
    return v + jnp.where(lane % 4 < 2, pltpu.roll(v, 126, 1), pltpu.roll(v, 2, 1))


def column_sum(v):
    part = jnp.sum(v.reshape(-1, 8, v.shape[-1]), axis=0)
    return jnp.broadcast_to(jnp.sum(part, axis=0, keepdims=True), part.shape)


def split_row(row):
    high = row.astype(BF16).astype(F32)
    middle = (row - high).astype(BF16).astype(F32)
    low = row - high - middle
    index = sublanes_of((8, 128))
    parts = jnp.where(index == 0, high, jnp.where(index == 1, middle, low))
    return jnp.concatenate([parts, parts], axis=0).astype(BF16)


def join_row(parts):
    parts = parts.astype(F32)
    return jnp.broadcast_to(parts[0:1] + parts[1:2] + parts[2:3], (8, 128))


def entry_kernel(place_ref, x_hbm, up_hbm, x_ref, up_ref, facing_ref, stat_ref, x_sem, up_sem):
    up_copy = pltpu.make_async_copy(up_hbm, up_ref, up_sem)
    x_copy = pltpu.make_async_copy(x_hbm, x_ref, x_sem)
    x_copy.start()
    up_copy.start()
    x_copy.wait()
    x = x_ref[...].astype(F32).reshape(-1, 128)
    total = group_total(column_sum(x))
    square = group_total(column_sum(x * x))
    row = jnp.where(lanes_of(total.shape) % 4 < 2, total, square)
    stat_ref[...] = row
    facing_ref[512:] = split_row(row)
    up_copy.wait()
    left = place_ref[3] == 0
    up = up_ref[...]
    facing_ref[:512] = jnp.where(left, up[:, :, 16:], up[:, :, :16]).reshape(512, 128)


def edge_of(up_ref, side_ref, bottom):
    side = side_ref[:512].reshape(4, 8, 16, 128)
    low = jnp.concatenate([up_ref[:, 7], side[:, 7]], axis=1)
    top = jnp.concatenate([up_ref[:, 0], side[:, 0]], axis=1)
    return jnp.where(bottom, low, top).reshape(192, 128)


def first_edge_kernel(place_ref, up_ref, side_ref, stat_ref, out_ref, sum_ref):
    even = place_ref[1] % 2 == 0
    row = stat_ref[...] + join_row(side_ref[512:])
    sum_ref[...] = row
    out_ref[:192] = edge_of(up_ref, side_ref, even)
    out_ref[192:] = split_row(row)


def second_edge_kernel(place_ref, up_ref, side_ref, near_ref, stat_ref, out_ref, sum_ref):
    even = place_ref[1] % 2 == 0
    row = stat_ref[...] + join_row(near_ref[192:])
    sum_ref[...] = row
    out_ref[:192] = edge_of(up_ref, side_ref, jnp.logical_not(even))
    out_ref[192:] = split_row(row)


def beyond(place_ref, near_ref, far_ref):
    even = place_ref[1] % 2 == 0
    outside = jnp.logical_or(place_ref[1] == 0, place_ref[1] == place_ref[2] - 1)
    near = near_ref[:192].reshape(4, 48, 128)
    far = far_ref[:192].reshape(4, 48, 128)
    far = jnp.where(outside, jnp.zeros_like(far), far)
    return jnp.where(even, far, near), jnp.where(even, near, far)


def early_kernel(place_ref, up_ref, side_ref, near_ref, far_ref, stat_ref, early_ref, sent_ref):
    row = stat_ref[...] + join_row(far_ref[192:])
    sent_ref[...] = jnp.broadcast_to(row[None], (sent_ref.shape[0] // 8, 8, 128)).reshape(sent_ref.shape)
    above, below = beyond(place_ref, near_ref, far_ref)
    early_ref[:, 0] = above[:2]
    early_ref[:, 9] = below[:2]
    early_ref[:, 1:9, :32] = up_ref[:2]
    early_ref[:, 1:9, 32:] = side_ref[:256].reshape(2, 8, 16, 128)


def grad_kernel(place_ref, up_ref, side_ref, near_ref, far_ref, later_ref, kernel_hbm, v_ref, dh_ref, kernel_ref, taps_ref, sem):
    weights = pltpu.make_async_copy(kernel_hbm, kernel_ref, sem)
    weights.start()
    time_first = place_ref[0] == 0
    row_first = place_ref[1] == 0
    row_last = place_ref[1] == place_ref[2] - 1
    left = place_ref[3] == 0
    column = sublanes_of((10, 32, 128))
    first = column == 0
    last = column == 31
    above, below = beyond(place_ref, near_ref, far_ref)

    for f in range(6):
        if f < 4:
            side = side_ref[f * 128 : (f + 1) * 128].reshape(8, 16, 128)
            mid = jnp.concatenate([up_ref[f].astype(F32), side.astype(F32)], axis=1)
            rows = jnp.concatenate([above[f : f + 1].astype(F32), mid, below[f : f + 1].astype(F32)], axis=0)
        else:
            rows = later_ref[f - 4].astype(F32)
        core = rows[:, :32]
        zero = jnp.zeros_like(core)
        ahead = pltpu.roll(rows, 47, 1)[:, :32]
        behind = pltpu.roll(rows, 1, 1)[:, :32]
        ahead = jnp.where(left, ahead + jnp.where(first, core, zero), jnp.where(last, zero, ahead))
        behind = jnp.where(left, jnp.where(first, zero, behind), behind + jnp.where(last, core, zero))
        for e, part in enumerate((ahead, core, behind)):
            for b in range(3):
                j = (b * 3 + e) * 128
                shifted = part[2 - b : 10 - b]
                if b == 0:
                    edge = shifted[0] + jnp.where(row_first, part[1], jnp.zeros_like(part[1]))
                    shifted = jnp.concatenate([edge[None], shifted[1:]], axis=0)
                if b == 2:
                    edge = shifted[7] + jnp.where(row_last, part[8], jnp.zeros_like(part[8]))
                    shifted = jnp.concatenate([shifted[:7], edge[None]], axis=0)
                v_ref[f, :, j : j + 128] = shifted.astype(BF16).reshape(256, 128)

    @pl.when(time_first)
    def _():
        both = v_ref[1].astype(F32) + v_ref[0].astype(F32)
        v_ref[6] = both.astype(BF16)
        v_ref[7] = (both + v_ref[2].astype(F32)).astype(BF16)

    @pl.when(jnp.logical_not(time_first))
    def _():
        v_ref[6] = v_ref[1]
        v_ref[7] = v_ref[2]

    weights.wait()
    for a in range(3):
        for b in range(3):
            for e in range(3):
                j = (b * 3 + e) * 128
                taps_ref[a, :, j : j + 128] = kernel_ref[a, b, e]
    dims = (((1,), (1,)), ((), ()))
    for f in range(4):
        total = None
        for a in range(3):
            source = f + 2 - a
            if f == 0 and a < 2:
                source = 7 - a
            term = lax.dot_general(v_ref[source], taps_ref[a], dims, preferred_element_type=F32)
            total = term if total is None else total + term
        dh_ref[f * 256 : (f + 1) * 256] = total


def sums_to_pair(row):
    lane = lanes_of(row.shape)
    total = jnp.where(lane % 4 < 2, row, pltpu.roll(row, 2, 1))
    square = jnp.where(lane % 4 < 2, pltpu.roll(row, 126, 1), row)
    return total, square


def product_of(turned, v_ref, a, lo, hi):
    if a == 2:
        return jnp.dot(turned, v_ref[0:4, :, lo:hi].reshape(1024, hi - lo), preferred_element_type=F32)
    first = jnp.dot(turned[:, :256], v_ref[7 - a, :, lo:hi], preferred_element_type=F32)
    rest = v_ref[3 - a : 6 - a, :, lo:hi].reshape(768, hi - lo)
    return first + jnp.dot(turned[:, 256:], rest, preferred_element_type=F32)


def half_product(half, turned, v_ref, w_ref):
    for a, lo, hi in (((0, 0, 9), (1, 0, 5)), ((1, 5, 9), (2, 0, 9)))[half]:
        product = product_of(turned, v_ref, a, lo * 128, hi * 128)
        for j in range(lo, hi):
            block = product[:, (j - lo) * 128 : (j - lo + 1) * 128].T.reshape(16, 8, 128)
            w_ref[:, (a * 9 + j) % HALF] = block
    if half == 1:
        w_ref[:, HALF - 1] = jnp.zeros((16, 8, 128), F32)


def away_kernel(
    counted, place_ref, x_ref, stat_ref, gain_ref, bias_ref, dh_ref, v_ref, w_ref, turned_ref, norm_ref, da_ref, sums_ref
):
    total, square = sums_to_pair(column_sum(stat_ref[...]))
    mean = total / counted
    rstd = lax.rsqrt(square / counted - mean * mean + 1e-06)
    norm_ref[0:8] = mean
    norm_ref[8:16] = rstd
    mean, rstd = mean[:1], rstd[:1]
    gain = gain_ref[...]
    bias = bias_ref[...]
    bias_sum = jnp.zeros((8, 128), F32)
    gain_sum = jnp.zeros((8, 128), F32)
    for block in range(8):
        xhat = (x_ref[block // 2, (block % 2) * 4 : (block % 2) * 4 + 4].astype(F32).reshape(128, 128) - mean) * rstd
        pre = xhat * gain + bias
        sig = 1.0 / (1.0 + jnp.exp(-pre))
        turned_ref[:, block * 128 : (block + 1) * 128] = (pre * sig).T.astype(BF16)
        da = dh_ref[block * 128 : (block + 1) * 128] * sig * (1.0 + pre * (1.0 - sig))
        da_ref[block * 128 : (block + 1) * 128] = da
        bias_sum = bias_sum + jnp.sum(da.reshape(16, 8, 128), axis=0)
        gain_sum = gain_sum + jnp.sum((da * xhat).reshape(16, 8, 128), axis=0)
    sums_ref[...] = jnp.where(sublanes_of((8, 128)) == 0, column_sum(bias_sum), column_sum(gain_sum))
    left = place_ref[3] == 0

    @pl.when(left)
    def _():
        half_product(1, turned_ref[...], v_ref, w_ref)

    @pl.when(jnp.logical_not(left))
    def _():
        half_product(0, turned_ref[...], v_ref, w_ref)


def home_kernel(place_ref, turned_ref, v_ref, w_ref):
    left = place_ref[3] == 0

    @pl.when(left)
    def _():
        half_product(0, turned_ref[...], v_ref, w_ref)

    @pl.when(jnp.logical_not(left))
    def _():
        half_product(1, turned_ref[...], v_ref, w_ref)


def split_sums(sums):
    row = sublanes_of(sums.shape)
    high = sums.astype(BF16).astype(F32)
    middle = (sums - high).astype(BF16).astype(F32)
    low = sums - high - middle
    return jnp.where(
        row < 2, high, jnp.where(row < 4, pltpu.roll(middle, 2, 0), pltpu.roll(low, 4, 0))
    )


def join_sums(parts):
    return parts + pltpu.roll(parts, 6, 0) + pltpu.roll(parts, 4, 0)


def pair_kernel(own_ref, other_ref, sums_ref, other_sums_ref, out_ref):
    slot = split_sums(sums_ref[...] + other_sums_ref[...])
    for i in range(16):
        body = (own_ref[i] + other_ref[i]).reshape(HALF * 8, 128)
        out_ref[i] = jnp.concatenate([body, slot], axis=0).astype(BF16)


def share_kernel(in_ref, out_ref):
    rows = HALF * 8
    total = in_ref[0].astype(F32)
    for i in range(1, in_ref.shape[0]):
        total = total + in_ref[i].astype(F32)
    out_ref[:rows] = total[:rows]
    out_ref[rows:] = join_sums(total[rows:])


def finish_kernel(counted, scaling, x_ref, da_ref, norm_ref, sums_ref, gain_ref, out_ref, gain_grad_ref, bias_grad_ref):
    gain = gain_ref[...]
    mean = norm_ref[0:1]
    rstd = norm_ref[8:9]
    sums = sums_ref[HALF * 8 :]
    bias_grad_ref[...] = sums[0:1] * scaling
    gain_grad_ref[...] = sums[1:2] * scaling
    averages = group_total(gain * sums) / counted
    leading = averages[0:1]
    trailing = averages[1:2]
    xhat = (x_ref[...].astype(F32).reshape(-1, 128) - mean) * rstd
    grad = rstd * (da_ref[...] * gain - leading - xhat * trailing)
    out_ref[...] = grad.astype(BF16).reshape(out_ref.shape)


def join_kernel(scaling, place_ref, half_ref, other_ref, out_ref):
    left = place_ref[3] == 0
    half = half_ref[: HALF * 8] * scaling
    other = other_ref[: HALF * 8] * scaling
    out_ref[: HALF * 8] = jnp.where(left, half, other)
    out_ref[HALF * 8 :] = jnp.where(left, other, half)[: (TAPS - HALF) * 8]


def shape_of(shape, dtype=F32):
    return jax.ShapeDtypeStruct(shape, dtype)


def local(activations, group_norm_gain, group_norm_bias, upstream, kernel):
    frames, height, columns, channels = activations.shape
    n_time, n_rows, n_sect = (lax.axis_size(axis) for axis in ("tm", "rows", "sect"))
    cells = frames * height * columns
    total_cells = cells * n_time * n_rows * n_sect
    counted = float(total_cells * (channels // GROUPS))
    scaling = float(total_cells) ** (-0.5)
    tm, rows, sect = (lax.axis_index(axis) for axis in ("tm", "rows", "sect"))
    place = jnp.stack([tm, rows, jnp.int32(n_rows), sect]).astype(jnp.int32)
    swap = [(0, 1), (1, 0)]
    near = [(i, i ^ 1) for i in range(n_rows)]
    far = [(i, (i - 1) % n_rows if i % 2 == 0 else (i + 1) % n_rows) for i in range(n_rows)]

    x, up, facing, stat = call(
        entry_kernel,
        [
            shape_of(activations.shape, BF16),
            shape_of(upstream.shape, BF16),
            shape_of((528, channels), BF16),
            shape_of((8, channels)),
        ],
        [place, activations, upstream],
        [SMEM, ANY, ANY],
        [pltpu.SemaphoreType.DMA, pltpu.SemaphoreType.DMA],
    )
    side = lax.ppermute(facing, "sect", swap)
    message, stat = call(
        first_edge_kernel,
        [shape_of((208, channels), BF16), shape_of((8, channels))],
        [place, up, side, stat],
        [SMEM, VMEM, VMEM, VMEM],
    )
    nearer = lax.ppermute(message, "rows", near)
    message, stat = call(
        second_edge_kernel,
        [shape_of((208, channels), BF16), shape_of((8, channels))],
        [place, up, side, nearer, stat],
        [SMEM, VMEM, VMEM, VMEM, VMEM],
    )
    farther = lax.ppermute(message, "rows", far)
    pairs = [(0, 3), (1, 6), (2, 5), (4, 7)]
    groups = [[t * n_rows + r for t in range(n_time) for r in pair] for pair in pairs]
    early, stat = call(
        early_kernel,
        [shape_of((2, 10, 48, channels), BF16), shape_of((len(groups[0]), channels))],
        [place, up, side, nearer, farther, stat],
        [SMEM, VMEM, VMEM, VMEM, VMEM, VMEM],
    )
    later = lax.ppermute(early, "tm", [(i + 1, i) for i in range(n_time - 1)])
    stat = lax.all_to_all(stat[:, None], ("tm", "rows"), 0, 0, axis_index_groups=groups).reshape(-1, channels)
    spread, hidden_grad = call(
        grad_kernel,
        [shape_of((8, 256, 1152), BF16), shape_of((cells, channels))],
        [place, up, side, nearer, farther, later, kernel],
        [SMEM, VMEM, VMEM, VMEM, VMEM, VMEM, ANY],
        [pltpu.VMEM((3, 3, 3, 128, 128), BF16), pltpu.VMEM((3, 128, 1152), BF16), pltpu.SemaphoreType.DMA],
        flops=2 * cells * TAPS * channels * channels,
    )
    gain = group_norm_gain.reshape(1, channels)
    bias = group_norm_bias.reshape(1, channels)
    away, turned, norm, da, sums = call(
        functools.partial(away_kernel, counted),
        [
            shape_of((16, HALF, 8, 128)),
            shape_of((channels, cells), BF16),
            shape_of((16, channels)),
            shape_of((cells, channels)),
            shape_of((8, channels)),
        ],
        [place, x, stat, gain, bias, hidden_grad, spread],
        [SMEM] + [VMEM] * 6,
        flops=cells * TAPS * channels * channels,
    )
    arrived = lax.ppermute(away, "sect", swap)
    other_sums = lax.ppermute(sums, "sect", swap)
    (home,) = call(
        home_kernel,
        [shape_of((16, HALF, 8, 128))],
        [place, turned, spread],
        [SMEM, VMEM, VMEM],
        flops=cells * TAPS * channels * channels,
    )
    (sent,) = call(
        pair_kernel, [shape_of((16, SLOTS * 8, 128), BF16)], [home, arrived, sums, other_sums]
    )
    gathered = lax.all_to_all(sent, "tm", 0, 0)
    (half,) = call(share_kernel, [shape_of((SLOTS * 8, 128))], [gathered])
    for bits in (1, 2, 7):
        half = half + lax.ppermute(half, "rows", [(i, i ^ bits) for i in range(n_rows)])
    other = lax.ppermute(half, "sect", swap)
    input_gradient, gain_grad, bias_grad = call(
        functools.partial(finish_kernel, counted, scaling),
        [shape_of(activations.shape, BF16), shape_of((1, 128)), shape_of((1, 128))],
        [x, da, norm, half, gain],
    )
    (whole,) = call(
        functools.partial(join_kernel, scaling),
        [shape_of((TAPS * 8, 128))],
        [place, half, other],
        [SMEM, VMEM, VMEM],
    )
    weight_grad = whole.reshape(3, 3, 3, 8, 128).transpose(0, 1, 2, 4, 3)
    return (input_gradient, gain_grad.reshape(128), bias_grad.reshape(128), weight_grad)


def solution(mesh):
    return jax.shard_map(
        local,
        mesh=mesh,
        in_specs=(P("tm", "rows", "sect", None), P(), P(), P("tm", "rows", "sect", None), P()),
        out_specs=(P("tm", "rows", "sect", None), P(), P(), P(None, None, None, None, "tm")),
        check_vma=False,
    )
```

time: 96.7 us -> 84 us (0.87)
  blocking collectives: 50 us -> 13.8 us
  starting transfers between devices: 23.6 us -> 35.7 us
  waiting for transfers between devices: 2.7 us -> 13.4 us
    all_to_all x2 -> x0, blocking collectives: 34.6 us -> none  [the longest x1 20.2 us: local(): gathered = lax.all_to_all(sent, 'rows', 0, 0)]
    ppermute x2 -> x5, waiting for transfers between devices: 0.01 us -> 9.79 us  [the longest x3 5.3 us: local(): lax.ppermute(half, 'rows', [(i, i ^ bits) for i in range(n_rows)])]
    ppermute x2 -> x5, starting transfers between devices: 3.1 us -> 12.5 us  [the longest x3 8.49 us: local(): lax.ppermute(half, 'rows', [(i, i ^ bits) for i in range(n_rows)])]
    ppermute x1, starting transfers between devices: 2.07 us -> 4.17 us  [local(): arrived = lax.ppermute(away, 'sect', swap)]
    all_to_all x1, blocking collectives: 15.4 us -> 13.8 us  [local(): gathered = lax.all_to_all(sent, 'tm', 0, 0)]
    ppermute x1, starting transfers between devices: 3.43 us -> 5.03 us  [local(): other = lax.ppermute(half, 'sect', swap)]
    all_to_all x1, waiting for transfers between devices: 0.67 us -> 1.89 us  [local(): lax.all_to_all(stat[:, None], ('tm', 'rows'), 0, 0, axis_index_groups=gro...]
    unnamed x16, local copies, waits for them, and re-layouts: 6.36 us -> 7.55 us
  transfers between devices with their start and end apart: 8 -> 11, of which waited for: 3 -> 8; matrix products, arithmetic and copies ran while one was open for 0% -> 0% of each run, Pallas kernels for 8% -> 7%
where the time goes in v3:
time: 84 us; the launch traced here: 83.6 us
  starting transfers between devices  35.7 us (43%)
  blocking collectives  13.8 us (16%)
  waiting for transfers between devices  13.4 us (16%)
  Pallas kernels  12.3 us (15%)
  local copies, waits for them, and re-layouts  7.55 us (9%)
    all_to_all x1, blocking collectives, local(): gathered = lax.all_to_all(sent, 'tm', 0, 0)  13.8 us
    pallas_call x11, Pallas kernels, call(): pl.pallas_call(body, out_shape=outs, in_specs=specs or [VMEM] * len(args)...  12.3 us
    all_to_all x1, starting transfers between devices, local(): lax.all_to_all(stat[:, None], ('tm', 'rows'), 0, 0, axis_index_groups=gro...  9.29 us
    ppermute x3, starting transfers between devices, local(): lax.ppermute(half, 'rows', [(i, i ^ bits) for i in range(n_rows)])  8.49 us
    unnamed x16, local copies, waits for them, and re-layouts  7.55 us
    ppermute x3, waiting for transfers between devices, local(): lax.ppermute(half, 'rows', [(i, i ^ bits) for i in range(n_rows)])  5.3 us
    ppermute x1, starting transfers between devices, local(): other = lax.ppermute(half, 'sect', swap)  5.03 us
    ppermute x1, starting transfers between devices, local(): arrived = lax.ppermute(away, 'sect', swap)  4.17 us
  transfers between devices with their start and end apart: 11, of which 8 were waited for; matrix products, arithmetic and copies ran while one was open for 0% of the time, Pallas kernels for 7%

profile of v3, /device:TPU:1, one launch (start us, length us, event | category | flops | bytes accessed | tf_op | source)
XLA Modules:
  0.0 83.6 jit_solution(15448519270911386628)
XLA Ops:
  0.6 0.0 copy-start.6
  0.6 0.0 copy-start.5
  0.7 0.1 pad_add_fusion.place_ref
  0.7 0.0 copy-start.3
  0.7 0.9 %copy-done.3 = bf16[4,8,32,128]{3,2,1,0:T(8,128)(2,1)S(1)} copy-done((bf16[4,8,32,128]{3,2,1,0:T(8,128)(2,1)S(1)}, bf16[4,8,32,128]{3,2,1,0:T(8,128)(2,1)}, u32[]{:S(2)}) %copy-start.3) | copy-done | bytes 262168
  1.7 0.9 %copy-done.4 = bf16[4,8,32,128]{3,2,1,0:T(8,128)(2,1)S(1)} copy-done((bf16[4,8,32,128]{3,2,1,0:T(8,128)(2,1)S(1)}, bf16[4,8,32,128]{3,2,1,0:T(8,128)(2,1)}, u32[]{:S(2)}) %copy-start.4) | copy-done | bytes 262168
  2.6 0.9 %shard_map.84 = (bf16[4,8,32,128]{3,2,1,0:T(8,128)(2,1)S(1)}, bf16[4,8,32,128]{3,2,1,0:T(8,128)(2,1)S(1)}, bf16[528,128]{1,0:T(8,128)(2,1)S(1)}, f32[8,128]{1,0:T(8,128)S(1)}) custom-call(s32[4]{0:T(128)S(1)} %pad_add_fusion.place_ref, bf16[4,8,32,128]{3,2,1,0:T(8,128)(2,1)S(1)} %copy-done.3, bf16[4,8,32,128]{3,2,1,0:T(8,128)(2,1)S(1)} %copy-done.4), custom_call_target="tpu_custom_call" | custom-call | bytes 1187856 | tf_op jit(solution)/shard_map/pallas_call | solution.py:23
  3.6 3.3 %collective-permute-start = (bf16[528,128]{1,0:T(8,128)(2,1)S(1)}, bf16[528,128]{1,0:T(8,128)(2,1)S(1)}, u32[]{:S(2)}, u32[]{:S(2)}) collective-permute-start(bf16[528,128]{1,0:T(8,128)(2,1)S(1)} %get-tuple-element.26), channel_id=1, source_target_pairs={{0,1},{1,0},{2,3},{3,2},{4,5},{5,4},{6,7},{7,6},{8,9},{9,8},{10,11... | collective-permute-start | bytes 405512 | tf_op jit(solution)/shard_map/ppermute | solution.py:346
  6.9 1.0 %collective-permute-done.side_ref = bf16[528,128]{1,0:T(8,128)(2,1)S(1)} collective-permute-done((bf16[528,128]{1,0:T(8,128)(2,1)S(1)}, bf16[528,128]{1,0:T(8,128)(2,1)S(1)}, u32[]{:S(2)}, u32[]{:S(2)}) %collective-permute-start) | collective-permute-done | bytes 135200 | tf_op jit(solution)/shard_map/ppermute | solution.py:346
  7.9 0.6 shard_map.85
  8.5 0.1 collective-permute-start.1
  8.6 3.0 %collective-permute-done.1.near_ref = bf16[208,128]{1,0:T(8,128)(2,1)S(1)} collective-permute-done((bf16[208,128]{1,0:T(8,128)(2,1)S(1)}, bf16[208,128]{1,0:T(8,128)(2,1)S(1)}, u32[]{:S(2)}, u32[]{:S(2)}) %collective-permute-start.1) | collective-permute-done | bytes 53280 | tf_op jit(solution)/shard_map/ppermute | solution.py:353
  11.5 0.6 shard_map.86
  12.1 3.9 %collective-permute-start.2 = (bf16[208,128]{1,0:T(8,128)(2,1)S(1)}, bf16[208,128]{1,0:T(8,128)(2,1)S(1)}, u32[]{:S(2)}, u32[]{:S(2)}) collective-permute-start(bf16[208,128]{1,0:T(8,128)(2,1)S(1)} %get-tuple-element.30), channel_id=1, source_target_pairs={{0,14},{2,4},{4,2},{6,8},{8,6},{10,12},{12,10},{14,0},{1,15},{3,5}... | collective-permute-start | bytes 159752 | tf_op jit(solution)/shard_map/ppermute | solution.py:360
  16.0 1.5 %collective-permute-done.2.far_ref = bf16[208,128]{1,0:T(8,128)(2,1)S(1)} collective-permute-done((bf16[208,128]{1,0:T(8,128)(2,1)S(1)}, bf16[208,128]{1,0:T(8,128)(2,1)S(1)}, u32[]{:S(2)}, u32[]{:S(2)}) %collective-permute-start.2) | collective-permute-done | bytes 53280 | tf_op jit(solution)/shard_map/ppermute | solution.py:360
  17.5 1.2 %shard_map.87 = (bf16[2,10,48,128]{3,2,1,0:T(8,128)(2,1)S(1)}, f32[32,128]{1,0:T(8,128)}) custom-call(s32[4]{0:T(128)S(1)} %pad_add_fusion.place_ref, bf16[4,8,32,128]{3,2,1,0:T(8,128)(2,1)S(1)} %get-tuple-element.25.up_ref, bf16[528,128]{1,0:T(8,128)(2,1)S(1)} %collective-permute-done.side_ref, bf16[208,128]{1,0:T(8,128)(2,1)S(1)} %collective-permute-done.1.near_ref, ...), custom_call_target="tpu_custom_call" | custom-call | bytes 770064 | tf_op jit(solution)/shard_map/pallas_call | solution.py:23
  18.7 1.3 %collective-permute-start.3 = (bf16[2,10,48,128]{3,2,1,0:T(8,128)(2,1)S(1)}, bf16[2,10,48,128]{3,2,1,0:T(8,128)(2,1)S(1)}, u32[]{:S(2)}, u32[]{:S(2)}) collective-permute-start(bf16[2,10,48,128]{3,2,1,0:T(8,128)(2,1)S(1)} %get-tuple-element.33), channel_id=1, source_target_pairs={{16,0},{32,16},{48,32},{64,48},{80,64},{96,80},{112,96},{128,112},... | collective-permute-start | bytes 737288 | tf_op jit(solution)/shard_map/ppermute | solution.py:369
  20.0 9.3 %all-to-all-start = ((f32[32,1,128]{2,1,0:T(1,128)}), f32[32,1,128]{2,1,0:T(1,128)S(1)}, u32[]{:S(2)}, u32[]{:S(2)}) async-start(f32[32,1,128]{2,1,0:T(1,128)} %bitcast.4), calls=%async_computation | async-start | bytes 32768 | tf_op jit(solution)/shard_map/all_to_all | solution.py:370
  29.3 0.0 collective-permute-done.3.later_ref
  29.3 0.0 copy-start.7
  29.3 1.2 %copy-done.7 = bf16[3,3,3,128,128]{4,3,2,1,0:T(8,128)(2,1)S(1)} copy-done((bf16[3,3,3,128,128]{4,3,2,1,0:T(8,128)(2,1)S(1)}, bf16[3,3,3,128,128]{4,3,2,1,0:T(8,128)(2,1)}, u32[]{:S(2)}) %copy-start.7) | copy-done | bytes 884760
  30.5 3.6 %shard_map.88 = (bf16[8,256,1152]{2,1,0:T(8,128)(2,1)S(1)}, f32[1024,128]{1,0:T(8,128)S(1)}) custom-call(s32[4]{0:T(128)S(1)} %pad_add_fusion.place_ref, bf16[4,8,32,128]{3,2,1,0:T(8,128)(2,1)S(1)} %get-tuple-element.25.up_ref, bf16[528,128]{1,0:T(8,128)(2,1)S(1)} %collective-permute-done.side_ref, bf16[208,128]{1,0:T(8,128)(2,1)S(1)} %collective-permute-done.1.near_ref, ...), custom_call_target="tpu_custom_call" | custom-call | flops 905969664 | bytes 6877200 | tf_op jit(solution)/shard_map/pallas_call | solution.py:23
  34.1 0.0 copy-start
  34.1 2.1 %copy-done = bf16[8,256,1152]{2,1,0:T(8,128)(2,1)} copy-done((bf16[8,256,1152]{2,1,0:T(8,128)(2,1)}, bf16[8,256,1152]{2,1,0:T(8,128)(2,1)S(1)}, u32[]{:S(2)}) %copy-start) | copy-done | bytes 4718616
  36.2 1.9 %all-to-all-done = f32[32,1,128]{2,1,0:T(1,128)S(1)} async-done(((f32[32,1,128]{2,1,0:T(1,128)}), f32[32,1,128]{2,1,0:T(1,128)S(1)}, u32[]{:S(2)}, u32[]{:S(2)}) %all-to-all-start) | async-done | bytes 16416 | tf_op jit(solution)/shard_map/all_to_all | solution.py:370
  38.1 0.0 copy-done.6
  38.1 0.0 copy-done.5
  38.1 2.3 %copy-done.1 = bf16[8,256,1152]{2,1,0:T(8,128)(2,1)S(1)} copy-done((bf16[8,256,1152]{2,1,0:T(8,128)(2,1)S(1)}, bf16[8,256,1152]{2,1,0:T(8,128)(2,1)}, u32[]{:S(2)}) %copy-start.1) | copy-done | bytes 4718616
  40.5 1.8 %shard_map.89 = (f32[16,14,8,128]{3,2,1,0:T(8,128)S(1)}, bf16[128,1024]{1,0:T(8,128)(2,1)S(1)}, f32[16,128]{1,0:T(8,128)S(1)}, f32[1024,128]{1,0:T(8,128)S(1)}, f32[8,128]{1,0:T(8,128)S(1)}) custom-call(s32[4]{0:T(128)S(1)} %pad_add_fusion.place_ref, bf16[4,8,32,128]{3,2,1,0:T(8,128)(2,1)S(1)} %get-tuple-element.24.x_ref, f32[32,128]{1,0:T(8,128)S(1)} %bitcast.14, ...), custom_call_target="tpu_custom_call" | custom-call | flops 452984832 | bytes 7238672 | tf_op jit(solution)/shard_map/pallas_call | solution.py:23
  42.3 4.2 %collective-permute-start.4 = (f32[16,14,8,128]{3,2,1,0:T(8,128)S(1)}, f32[16,14,8,128]{3,2,1,0:T(8,128)S(1)}, u32[]{:S(2)}, u32[]{:S(2)}) collective-permute-start(f32[16,14,8,128]{3,2,1,0:T(8,128)S(1)} %get-tuple-element.39), channel_id=1, source_target_pairs={{0,1},{1,0},{2,3},{3,2},{4,5},{5,4},{6,7},{7,6},{8,9},{9,8},{10,11... | collective-permute-start | bytes 2752520 | tf_op jit(solution)/shard_map/ppermute | solution.py:394
  46.5 0.1 collective-permute-start.5
  46.6 0.0 copy-done.2
  46.6 1.3 %shard_map.90.own_ref = f32[16,14,8,128]{3,2,1,0:T(8,128)S(1)} custom-call(s32[4]{0:T(128)S(1)} %pad_add_fusion.place_ref, bf16[128,1024]{1,0:T(8,128)(2,1)S(1)} %get-tuple-element.38.turned_ref, bf16[8,256,1152]{2,1,0:T(8,128)(2,1)S(1)} %copy-done.2), custom_call_target="tpu_custom_call" | custom-call | flops 452984832 | bytes 5898256 | tf_op jit(solution)/shard_map/pallas_call | solution.py:23
  47.9 0.7 collective-permute-done.5.other_sums_ref
  48.6 0.0 collective-permute-done.4.other_ref
  48.6 0.1 shard_map.91
  48.7 13.8 %all_to_all.10.in_ref = bf16[16,120,128]{2,1,0:T(8,128)(2,1)S(1)} all-to-all(bf16[16,120,128]{2,1,0:T(8,128)(2,1)S(1)} %shard_map.91), channel_id=1, replica_groups=mesh['tm'=16,'rows'=8,'sect'=2] {'tm'}, dimensions={0} | all-to-all | bytes 983040 | tf_op jit(solution)/shard_map/all_to_all | solution.py:406
  62.5 0.1 shard_map.92
  62.5 2.3 %collective-permute-start.6 = (f32[120,128]{1,0:T(8,128)S(1)}, f32[120,128]{1,0:T(8,128)S(1)}, u32[]{:S(2)}, u32[]{:S(2)}) collective-permute-start(f32[120,128]{1,0:T(8,128)S(1)} %shard_map.92), channel_id=1, source_target_pairs={{0,2},{2,0},{4,6},{6,4},{8,10},{10,8},{12,14},{14,12},{1,3},{3,1},... | collective-permute-start | bytes 184328 | tf_op jit(solution)/shard_map/ppermute | solution.py:409
  64.9 1.6 %collective-permute-done.6 = f32[120,128]{1,0:T(8,128)S(1)} collective-permute-done((f32[120,128]{1,0:T(8,128)S(1)}, f32[120,128]{1,0:T(8,128)S(1)}, u32[]{:S(2)}, u32[]{:S(2)}) %collective-permute-start.6) | collective-permute-done | bytes 61472 | tf_op jit(solution)/shard_map/ppermute | solution.py:409
  66.5 2.0 %collective-permute-start.7 = (f32[120,128]{1,0:T(8,128)S(1)}, f32[120,128]{1,0:T(8,128)S(1)}, u32[]{:S(2)}, u32[]{:S(2)}) collective-permute-start(f32[120,128]{1,0:T(8,128)S(1)} %add.9), channel_id=1, source_target_pairs={{0,4},{2,6},{4,0},{6,2},{8,12},{10,14},{12,8},{14,10},{1,5},{3,7},... | collective-permute-start | bytes 184328 | tf_op jit(solution)/shard_map/ppermute | solution.py:409
  68.5 2.1 %collective-permute-done.7 = f32[120,128]{1,0:T(8,128)S(1)} collective-permute-done((f32[120,128]{1,0:T(8,128)S(1)}, f32[120,128]{1,0:T(8,128)S(1)}, u32[]{:S(2)}, u32[]{:S(2)}) %collective-permute-start.7) | collective-permute-done | bytes 61472 | tf_op jit(solution)/shard_map/ppermute | solution.py:409
  70.6 4.2 %collective-permute-start.8 = (f32[120,128]{1,0:T(8,128)S(1)}, f32[120,128]{1,0:T(8,128)S(1)}, u32[]{:S(2)}, u32[]{:S(2)}) collective-permute-start(f32[120,128]{1,0:T(8,128)S(1)} %add.10), channel_id=1, source_target_pairs={{0,14},{2,12},{4,10},{6,8},{8,6},{10,4},{12,2},{14,0},{1,15},{3,13... | collective-permute-start | bytes 184328 | tf_op jit(solution)/shard_map/ppermute | solution.py:409
  74.8 1.6 %collective-permute-done.8 = f32[120,128]{1,0:T(8,128)S(1)} collective-permute-done((f32[120,128]{1,0:T(8,128)S(1)}, f32[120,128]{1,0:T(8,128)S(1)}, u32[]{:S(2)}, u32[]{:S(2)}) %collective-permute-start.8) | collective-permute-done | bytes 61472 | tf_op jit(solution)/shard_map/ppermute | solution.py:409
  76.4 5.0 %collective-permute-start.9 = (f32[120,128]{1,0:T(8,128)S(1)}, f32[120,128]{1,0:T(8,128)S(1)}, u32[]{:S(2)}, u32[]{:S(2)}) collective-permute-start(f32[120,128]{1,0:T(8,128)S(1)} %add.11.sums_ref.half_ref), channel_id=1, source_target_pairs={{0,1},{1,0},{2,3},{3,2},{4,5},{5,4},{6,7},{7,6},{8,9},{9,8},{10,11... | collective-permute-start | bytes 184328 | tf_op jit(solution)/shard_map/ppermute | solution.py:410
  81.4 1.0 %shard_map.93 = (bf16[4,8,32,128]{3,2,1,0:T(8,128)(2,1)}, f32[1,128]{1,0:T(1,128)}, f32[1,128]{1,0:T(1,128)}) custom-call(bf16[4,8,32,128]{3,2,1,0:T(8,128)(2,1)S(1)} %get-tuple-element.24.x_ref, f32[1024,128]{1,0:T(8,128)S(1)} %get-tuple-element.36.da_ref, f32[16,128]{1,0:T(8,128)S(1)} %get-tuple-element.37.norm_ref, f32[120,128]{1,0:T(8,128)S(1)} %add.11.sums_ref.half_ref, ...), custom_call_target="tpu_custom_call" | custom-call | bytes 1119744 | tf_op jit(solution)/shard_map/pallas_call | solution.py:23
  82.4 0.0 collective-permute-done.9.other_ref
  82.4 1.2 %shard_map.94 = f32[216,128]{1,0:T(8,128)} custom-call(s32[4]{0:T(128)S(1)} %pad_add_fusion.place_ref, f32[120,128]{1,0:T(8,128)S(1)} %add.11.sums_ref.half_ref, f32[120,128]{1,0:T(8,128)S(1)} %collective-permute-done.9.other_ref), custom_call_target="tpu_custom_call" | custom-call | bytes 233488 | tf_op jit(solution)/shard_map/pallas_call | solution.py:23
  (6 shorter events, 0.0 us)
Async XLA Ops:
  0.6 37.5 %copy-start.6 = (f32[128]{0:T(128)S(1)}, f32[128]{0:T(128)}, u32[]{:S(2)}) copy-start(f32[128]{0:T(128)} %param.7) | copy-start | bytes 1540
  0.6 37.5 %copy-start.5 = (f32[128]{0:T(128)S(1)}, f32[128]{0:T(128)}, u32[]{:S(2)}) copy-start(f32[128]{0:T(128)} %param.6) | copy-start | bytes 1540
  0.7 1.0 %copy-start.3 = (bf16[4,8,32,128]{3,2,1,0:T(8,128)(2,1)S(1)}, bf16[4,8,32,128]{3,2,1,0:T(8,128)(2,1)}, u32[]{:S(2)}) copy-start(bf16[4,8,32,128]{3,2,1,0:T(8,128)(2,1)} %x_hbm.1) | copy-start | bytes 786436
  1.7 0.9 %copy-start.4 = (bf16[4,8,32,128]{3,2,1,0:T(8,128)(2,1)S(1)}, bf16[4,8,32,128]{3,2,1,0:T(8,128)(2,1)}, u32[]{:S(2)}) copy-start(bf16[4,8,32,128]{3,2,1,0:T(8,128)(2,1)} %up_hbm.1) | copy-start | bytes 786436
  3.6 4.3 %collective-permute-start = (bf16[528,128]{1,0:T(8,128)(2,1)S(1)}, bf16[528,128]{1,0:T(8,128)(2,1)S(1)}, u32[]{:S(2)}, u32[]{:S(2)}) collective-permute-start(bf16[528,128]{1,0:T(8,128)(2,1)S(1)} %get-tuple-element.26), channel_id=1, source_target_pairs={{0,1},{1,0},{2,3},{3,2},{4,5},{5,4},{6,7},{7,6},{8,9},{9,8},{10,11... | collective-permute-start | bytes 405512 | tf_op jit(solution)/shard_map/ppermute | solution.py:346
  8.5 3.1 %collective-permute-start.1 = (bf16[208,128]{1,0:T(8,128)(2,1)S(1)}, bf16[208,128]{1,0:T(8,128)(2,1)S(1)}, u32[]{:S(2)}, u32[]{:S(2)}) collective-permute-start(bf16[208,128]{1,0:T(8,128)(2,1)S(1)} %get-tuple-element.28), channel_id=1, source_target_pairs={{0,2},{2,0},{4,6},{6,4},{8,10},{10,8},{12,14},{14,12},{1,3},{3,1},... | collective-permute-start | bytes 159752 | tf_op jit(solution)/shard_map/ppermute | solution.py:353
  12.1 5.5 %collective-permute-start.2 = (bf16[208,128]{1,0:T(8,128)(2,1)S(1)}, bf16[208,128]{1,0:T(8,128)(2,1)S(1)}, u32[]{:S(2)}, u32[]{:S(2)}) collective-permute-start(bf16[208,128]{1,0:T(8,128)(2,1)S(1)} %get-tuple-element.30), channel_id=1, source_target_pairs={{0,14},{2,4},{4,2},{6,8},{8,6},{10,12},{12,10},{14,0},{1,15},{3,5}... | collective-permute-start | bytes 159752 | tf_op jit(solution)/shard_map/ppermute | solution.py:360
  18.7 10.6 %collective-permute-start.3 = (bf16[2,10,48,128]{3,2,1,0:T(8,128)(2,1)S(1)}, bf16[2,10,48,128]{3,2,1,0:T(8,128)(2,1)S(1)}, u32[]{:S(2)}, u32[]{:S(2)}) collective-permute-start(bf16[2,10,48,128]{3,2,1,0:T(8,128)(2,1)S(1)} %get-tuple-element.33), channel_id=1, source_target_pairs={{16,0},{32,16},{48,32},{64,48},{80,64},{96,80},{112,96},{128,112},... | collective-permute-start | bytes 737288 | tf_op jit(solution)/shard_map/ppermute | solution.py:369
  20.0 18.1 %all-to-all-start = ((f32[32,1,128]{2,1,0:T(1,128)}), f32[32,1,128]{2,1,0:T(1,128)S(1)}, u32[]{:S(2)}, u32[]{:S(2)}) async-start(f32[32,1,128]{2,1,0:T(1,128)} %bitcast.4), calls=%async_computation | async-start | bytes 32768 | tf_op jit(solution)/shard_map/all_to_all | solution.py:370
  29.3 1.2 %copy-start.7 = (bf16[3,3,3,128,128]{4,3,2,1,0:T(8,128)(2,1)S(1)}, bf16[3,3,3,128,128]{4,3,2,1,0:T(8,128)(2,1)}, u32[]{:S(2)}) copy-start(bf16[3,3,3,128,128]{4,3,2,1,0:T(8,128)(2,1)} %kernel_hbm.1) | copy-start | bytes 2654212
  34.1 2.1 %copy-start = (bf16[8,256,1152]{2,1,0:T(8,128)(2,1)}, bf16[8,256,1152]{2,1,0:T(8,128)(2,1)S(1)}, u32[]{:S(2)}) copy-start(bf16[8,256,1152]{2,1,0:T(8,128)(2,1)S(1)} %get-tuple-element.35.v_ref) | copy-start | bytes 14155780
  38.1 2.3 %copy-start.1 = (bf16[8,256,1152]{2,1,0:T(8,128)(2,1)S(1)}, bf16[8,256,1152]{2,1,0:T(8,128)(2,1)}, u32[]{:S(2)}) copy-start(bf16[8,256,1152]{2,1,0:T(8,128)(2,1)} %copy-done) | copy-start | bytes 14155780
  40.5 6.1 %copy-start.2 = (bf16[8,256,1152]{2,1,0:T(8,128)(2,1)S(1)}, bf16[8,256,1152]{2,1,0:T(8,128)(2,1)}, u32[]{:S(2)}) copy-start(bf16[8,256,1152]{2,1,0:T(8,128)(2,1)} %copy-done) | copy-start | bytes 14155780
  42.3 6.3 %collective-permute-start.4 = (f32[16,14,8,128]{3,2,1,0:T(8,128)S(1)}, f32[16,14,8,128]{3,2,1,0:T(8,128)S(1)}, u32[]{:S(2)}, u32[]{:S(2)}) collective-permute-start(f32[16,14,8,128]{3,2,1,0:T(8,128)S(1)} %get-tuple-element.39), channel_id=1, source_target_pairs={{0,1},{1,0},{2,3},{3,2},{4,5},{5,4},{6,7},{7,6},{8,9},{9,8},{10,11... | collective-permute-start | bytes 2752520 | tf_op jit(solution)/shard_map/ppermute | solution.py:394
  46.5 2.1 %collective-permute-start.5 = (f32[8,128]{1,0:T(8,128)S(1)}, f32[8,128]{1,0:T(8,128)S(1)}, u32[]{:S(2)}, u32[]{:S(2)}) collective-permute-start(f32[8,128]{1,0:T(8,128)S(1)} %get-tuple-element.40.sums_ref), channel_id=1, source_target_pairs={{0,1},{1,0},{2,3},{3,2},{4,5},{5,4},{6,7},{7,6},{8,9},{9,8},{10,11... | collective-permute-start | bytes 12296 | tf_op jit(solution)/shard_map/ppermute | solution.py:395
  62.5 4.0 %collective-permute-start.6 = (f32[120,128]{1,0:T(8,128)S(1)}, f32[120,128]{1,0:T(8,128)S(1)}, u32[]{:S(2)}, u32[]{:S(2)}) collective-permute-start(f32[120,128]{1,0:T(8,128)S(1)} %shard_map.92), channel_id=1, source_target_pairs={{0,2},{2,0},{4,6},{6,4},{8,10},{10,8},{12,14},{14,12},{1,3},{3,1},... | collective-permute-start | bytes 184328 | tf_op jit(solution)/shard_map/ppermute | solution.py:409
  66.5 4.1 %collective-permute-start.7 = (f32[120,128]{1,0:T(8,128)S(1)}, f32[120,128]{1,0:T(8,128)S(1)}, u32[]{:S(2)}, u32[]{:S(2)}) collective-permute-start(f32[120,128]{1,0:T(8,128)S(1)} %add.9), channel_id=1, source_target_pairs={{0,4},{2,6},{4,0},{6,2},{8,12},{10,14},{12,8},{14,10},{1,5},{3,7},... | collective-permute-start | bytes 184328 | tf_op jit(solution)/shard_map/ppermute | solution.py:409
  70.6 5.8 %collective-permute-start.8 = (f32[120,128]{1,0:T(8,128)S(1)}, f32[120,128]{1,0:T(8,128)S(1)}, u32[]{:S(2)}, u32[]{:S(2)}) collective-permute-start(f32[120,128]{1,0:T(8,128)S(1)} %add.10), channel_id=1, source_target_pairs={{0,14},{2,12},{4,10},{6,8},{8,6},{10,4},{12,2},{14,0},{1,15},{3,13... | collective-permute-start | bytes 184328 | tf_op jit(solution)/shard_map/ppermute | solution.py:409
  76.4 6.0 %collective-permute-start.9 = (f32[120,128]{1,0:T(8,128)S(1)}, f32[120,128]{1,0:T(8,128)S(1)}, u32[]{:S(2)}, u32[]{:S(2)}) collective-permute-start(f32[120,128]{1,0:T(8,128)S(1)} %add.11.sums_ref.half_ref), channel_id=1, source_target_pairs={{0,1},{1,0},{2,3},{3,2},{4,5},{5,4},{6,7},{7,6},{8,9},{9,8},{10,11... | collective-permute-start | bytes 184328 | tf_op jit(solution)/shard_map/ppermute | solution.py:410

commit v4 on v3

--- a/solution.py
+++ b/solution.py
@@ -1,4 +1,5 @@
 import functools
+import math
 
 import jax
 import jax.numpy as jnp
@@ -15,17 +16,22 @@
 BF16 = jnp.bfloat16
 VMEM = pl.BlockSpec(memory_space=pltpu.VMEM)
 SMEM = pl.BlockSpec(memory_space=pltpu.SMEM)
-ANY = pl.BlockSpec(memory_space=pl.ANY)
-
-
-def call(body, outs, args, specs=None, scratch=(), flops=0):
-    moved = sum(x.size * x.dtype.itemsize for x in list(args) + list(outs))
+HBM = pl.BlockSpec(memory_space=pltpu.HBM)
+
+
+def held(x, space):
+    return pltpu.with_memory_space_constraint(x, space)
+
+
+def call(body, outs, args, specs=None, scratch=(), flops=0, aliases=None):
+    moved = sum(math.prod(x.shape) * jnp.dtype(x.dtype).itemsize for x in list(args) + list(outs))
     return pl.pallas_call(
         body,
         out_shape=outs,
         in_specs=specs or [VMEM] * len(args),
         out_specs=[VMEM] * len(outs),
         scratch_shapes=list(scratch),
+        input_output_aliases=aliases or {},
         cost_estimate=pl.CostEstimate(flops=flops, bytes_accessed=moved, transcendentals=0),
         compiler_params=pltpu.CompilerParams(vmem_limit_bytes=24 * 1024 * 1024),
     )(*args)
@@ -124,70 +130,104 @@
     early_ref[:, 1:9, 32:] = side_ref[:256].reshape(2, 8, 16, 128)
 
 
-def grad_kernel(place_ref, up_ref, side_ref, near_ref, far_ref, later_ref, kernel_hbm, v_ref, dh_ref, kernel_ref, taps_ref, sem):
+def column_taps(place_ref, rows):
+    left = place_ref[3] == 0
+    core = rows[:, :32]
+    column = sublanes_of(core.shape)
+    first = column == 0
+    last = column == 31
+    zero = jnp.zeros_like(core)
+    ahead = pltpu.roll(rows, 47, 1)[:, :32]
+    behind = pltpu.roll(rows, 1, 1)[:, :32]
+    ahead = jnp.where(left, ahead + jnp.where(first, core, zero), jnp.where(last, zero, ahead))
+    behind = jnp.where(left, jnp.where(first, zero, behind), behind + jnp.where(last, core, zero))
+    return ahead, core, behind
+
+
+def put(v_ref, f, r, b, e, rows):
+    j = (b * 3 + e) * 128
+    count = rows.shape[0]
+    v_ref[f, r * 32 : (r + count) * 32, j : j + 128] = rows.astype(BF16).reshape(count * 32, 128)
+
+
+def times_taps(lhs, taps_ref, a):
+    return lax.dot_general(lhs, taps_ref[a], (((1,), (1,)), ((), ())), preferred_element_type=F32)
+
+
+def own_kernel(place_ref, up_ref, side_ref, kernel_hbm, v_ref, dh_ref, taps_ref, kernel_ref, sem):
     weights = pltpu.make_async_copy(kernel_hbm, kernel_ref, sem)
     weights.start()
-    time_first = place_ref[0] == 0
     row_first = place_ref[1] == 0
     row_last = place_ref[1] == place_ref[2] - 1
-    left = place_ref[3] == 0
-    column = sublanes_of((10, 32, 128))
-    first = column == 0
-    last = column == 31
-    above, below = beyond(place_ref, near_ref, far_ref)
-
-    for f in range(6):
-        if f < 4:
-            side = side_ref[f * 128 : (f + 1) * 128].reshape(8, 16, 128)
-            mid = jnp.concatenate([up_ref[f].astype(F32), side.astype(F32)], axis=1)
-            rows = jnp.concatenate([above[f : f + 1].astype(F32), mid, below[f : f + 1].astype(F32)], axis=0)
-        else:
-            rows = later_ref[f - 4].astype(F32)
-        core = rows[:, :32]
-        zero = jnp.zeros_like(core)
-        ahead = pltpu.roll(rows, 47, 1)[:, :32]
-        behind = pltpu.roll(rows, 1, 1)[:, :32]
-        ahead = jnp.where(left, ahead + jnp.where(first, core, zero), jnp.where(last, zero, ahead))
-        behind = jnp.where(left, jnp.where(first, zero, behind), behind + jnp.where(last, core, zero))
-        for e, part in enumerate((ahead, core, behind)):
-            for b in range(3):
-                j = (b * 3 + e) * 128
-                shifted = part[2 - b : 10 - b]
-                if b == 0:
-                    edge = shifted[0] + jnp.where(row_first, part[1], jnp.zeros_like(part[1]))
-                    shifted = jnp.concatenate([edge[None], shifted[1:]], axis=0)
-                if b == 2:
-                    edge = shifted[7] + jnp.where(row_last, part[8], jnp.zeros_like(part[8]))
-                    shifted = jnp.concatenate([shifted[:7], edge[None]], axis=0)
-                v_ref[f, :, j : j + 128] = shifted.astype(BF16).reshape(256, 128)
-
-    @pl.when(time_first)
-    def _():
-        both = v_ref[1].astype(F32) + v_ref[0].astype(F32)
-        v_ref[6] = both.astype(BF16)
-        v_ref[7] = (both + v_ref[2].astype(F32)).astype(BF16)
-
-    @pl.when(jnp.logical_not(time_first))
-    def _():
-        v_ref[6] = v_ref[1]
-        v_ref[7] = v_ref[2]
-
+    for f in range(4):
+        side = side_ref[f * 128 : (f + 1) * 128].reshape(8, 16, 128)
+        rows = jnp.concatenate([up_ref[f].astype(F32), side.astype(F32)], axis=1)
+        for e, part in enumerate(column_taps(place_ref, rows)):
+            zero = jnp.zeros_like(part[0])
+            top = part[1] + jnp.where(row_first, part[0], zero)
+            low = part[6] + jnp.where(row_last, part[7], zero)
+            put(v_ref, f, 0, 0, e, top[None])
+            put(v_ref, f, 1, 0, e, part[2:8])
+            put(v_ref, f, 0, 1, e, part)
+            put(v_ref, f, 1, 2, e, part[0:6])
+            put(v_ref, f, 7, 2, e, low[None])
     weights.wait()
     for a in range(3):
         for b in range(3):
             for e in range(3):
                 j = (b * 3 + e) * 128
                 taps_ref[a, :, j : j + 128] = kernel_ref[a, b, e]
-    dims = (((1,), (1,)), ((), ()))
     for f in range(4):
         total = None
         for a in range(3):
-            source = f + 2 - a
-            if f == 0 and a < 2:
-                source = 7 - a
-            term = lax.dot_general(v_ref[source], taps_ref[a], dims, preferred_element_type=F32)
-            total = term if total is None else total + term
-        dh_ref[f * 256 : (f + 1) * 256] = total
+            if f + 2 - a < 4:
+                term = times_taps(v_ref[f + 2 - a, 32:224], taps_ref, a)
+                total = term if total is None else total + term
+        dh_ref[f * 256 + 32 : f * 256 + 224] = total
+
+
+def grad_kernel(place_ref, up_ref, side_ref, near_ref, far_ref, later_ref, taps_ref, part_ref, own_ref, v_ref, dh_ref):
+    time_first = place_ref[0] == 0
+    above, below = beyond(place_ref, near_ref, far_ref)
+    row_first = place_ref[1] == 0
+    row_last = place_ref[1] == place_ref[2] - 1
+    outer = jnp.concatenate([above, below], axis=0).astype(F32)
+    for e, part in enumerate(column_taps(place_ref, outer)):
+        for f in range(4):
+            put(v_ref, f, 0, 2, e, part[f : f + 1])
+            put(v_ref, f, 7, 0, e, part[f + 4 : f + 5])
+    for f in range(2):
+        for e, part in enumerate(column_taps(place_ref, later_ref[f].astype(F32))):
+            zero = jnp.zeros_like(part[0])
+            top = part[2] + jnp.where(row_first, part[1], zero)
+            low = part[7] + jnp.where(row_last, part[8], zero)
+            put(v_ref, f + 4, 0, 0, e, top[None])
+            put(v_ref, f + 4, 1, 0, e, part[3:10])
+            put(v_ref, f + 4, 0, 1, e, part[1:9])
+            put(v_ref, f + 4, 0, 2, e, part[0:7])
+            put(v_ref, f + 4, 7, 2, e, low[None])
+
+    def edges(lo, hi):
+        return jnp.concatenate([v_ref[lo:hi, 0:32], v_ref[lo:hi, 224:256]], axis=1).reshape((hi - lo) * 64, 1152)
+
+    outer = times_taps(edges(0, 4), taps_ref, 2)
+    one = times_taps(edges(1, 4), taps_ref, 1)
+    two = times_taps(edges(2, 4), taps_ref, 0)
+    outer = outer + jnp.concatenate([one, jnp.zeros((64, 128), F32)], axis=0)
+    outer = outer + jnp.concatenate([two, jnp.zeros((128, 128), F32)], axis=0)
+    for f in range(4):
+        dh_ref[f * 256 : f * 256 + 32] = outer[f * 64 : f * 64 + 32]
+        dh_ref[f * 256 + 32 : f * 256 + 224] = part_ref[f * 256 + 32 : f * 256 + 224]
+        dh_ref[f * 256 + 224 : f * 256 + 256] = outer[f * 64 + 32 : f * 64 + 64]
+    dh_ref[768:1024] += times_taps(v_ref[4], taps_ref, 1)
+    dh_ref[512:1024] += times_taps(v_ref[4:6].reshape(512, 1152), taps_ref, 0)
+
+    @pl.when(time_first)
+    def _():
+        both = v_ref[1].astype(F32) + v_ref[0].astype(F32)
+        v_ref[6] = both.astype(BF16)
+        v_ref[7] = (both + v_ref[2].astype(F32)).astype(BF16)
+        dh_ref[0:256] += times_taps(v_ref[0], taps_ref, 1) + times_taps(v_ref[6], taps_ref, 0)
 
 
 def sums_to_pair(row):
@@ -197,17 +237,18 @@
     return total, square
 
 
-def product_of(turned, v_ref, a, lo, hi):
+def product_of(place_ref, turned, v_ref, a, lo, hi):
     if a == 2:
         return jnp.dot(turned, v_ref[0:4, :, lo:hi].reshape(1024, hi - lo), preferred_element_type=F32)
-    first = jnp.dot(turned[:, :256], v_ref[7 - a, :, lo:hi], preferred_element_type=F32)
+    source = jnp.where(place_ref[0] == 0, 7 - a, 2 - a)
+    first = jnp.dot(turned[:, :256], v_ref[source, :, lo:hi], preferred_element_type=F32)
     rest = v_ref[3 - a : 6 - a, :, lo:hi].reshape(768, hi - lo)
     return first + jnp.dot(turned[:, 256:], rest, preferred_element_type=F32)
 
 
-def half_product(half, turned, v_ref, w_ref):
+def half_product(place_ref, half, turned, v_ref, w_ref):
     for a, lo, hi in (((0, 0, 9), (1, 0, 5)), ((1, 5, 9), (2, 0, 9)))[half]:
-        product = product_of(turned, v_ref, a, lo * 128, hi * 128)
+        product = product_of(place_ref, turned, v_ref, a, lo * 128, hi * 128)
         for j in range(lo, hi):
             block = product[:, (j - lo) * 128 : (j - lo + 1) * 128].T.reshape(16, 8, 128)
             w_ref[:, (a * 9 + j) % HALF] = block
@@ -242,11 +283,11 @@
 
     @pl.when(left)
     def _():
-        half_product(1, turned_ref[...], v_ref, w_ref)
+        half_product(place_ref, 1, turned_ref[...], v_ref, w_ref)
 
     @pl.when(jnp.logical_not(left))
     def _():
-        half_product(0, turned_ref[...], v_ref, w_ref)
+        half_product(place_ref, 0, turned_ref[...], v_ref, w_ref)
 
 
 def home_kernel(place_ref, turned_ref, v_ref, w_ref):
@@ -254,11 +295,11 @@
 
     @pl.when(left)
     def _():
-        half_product(0, turned_ref[...], v_ref, w_ref)
+        half_product(place_ref, 0, turned_ref[...], v_ref, w_ref)
 
     @pl.when(jnp.logical_not(left))
     def _():
-        half_product(1, turned_ref[...], v_ref, w_ref)
+        half_product(place_ref, 1, turned_ref[...], v_ref, w_ref)
 
 
 def split_sums(sums):
@@ -339,8 +380,8 @@
             shape_of((528, channels), BF16),
             shape_of((8, channels)),
         ],
-        [place, activations, upstream],
-        [SMEM, ANY, ANY],
+        [place, held(activations, pltpu.HBM), held(upstream, pltpu.HBM)],
+        [SMEM, HBM, HBM],
         [pltpu.SemaphoreType.DMA, pltpu.SemaphoreType.DMA],
     )
     side = lax.ppermute(facing, "sect", swap)
@@ -351,6 +392,19 @@
         [SMEM, VMEM, VMEM, VMEM],
     )
     nearer = lax.ppermute(message, "rows", near)
+    spread, inner, taps = call(
+        own_kernel,
+        [
+            pltpu.VMEM((8, 256, 1152), BF16),
+            shape_of((cells, channels)),
+            shape_of((3, channels, 9 * channels), BF16),
+        ],
+        [place, up, side, held(kernel, pltpu.HBM)],
+        [SMEM, VMEM, VMEM, HBM],
+        [pltpu.VMEM((3, 3, 3, 128, 128), BF16), pltpu.SemaphoreType.DMA],
+        flops=cells * TAPS * channels * channels,
+    )
+    nearer, inner = lax.optimization_barrier((nearer, inner))
     message, stat = call(
         second_edge_kernel,
         [shape_of((208, channels), BF16), shape_of((8, channels))],
@@ -368,13 +422,14 @@
     )
     later = lax.ppermute(early, "tm", [(i + 1, i) for i in range(n_time - 1)])
     stat = lax.all_to_all(stat[:, None], ("tm", "rows"), 0, 0, axis_index_groups=groups).reshape(-1, channels)
+    stat, later = lax.optimization_barrier((stat, later))
     spread, hidden_grad = call(
         grad_kernel,
-        [shape_of((8, 256, 1152), BF16), shape_of((cells, channels))],
-        [place, up, side, nearer, farther, later, kernel],
-        [SMEM, VMEM, VMEM, VMEM, VMEM, VMEM, ANY],
-        [pltpu.VMEM((3, 3, 3, 128, 128), BF16), pltpu.VMEM((3, 128, 1152), BF16), pltpu.SemaphoreType.DMA],
-        flops=2 * cells * TAPS * channels * channels,
+        [pltpu.VMEM((8, 256, 1152), BF16), shape_of((cells, channels))],
+        [place, up, side, nearer, farther, later, taps, inner, held(spread, pltpu.VMEM)],
+        [SMEM] + [VMEM] * 8,
+        flops=cells * TAPS * channels * channels,
+        aliases={8: 0},
     )
     gain = group_norm_gain.reshape(1, channels)
     bias = group_norm_bias.reshape(1, channels)
@@ -387,7 +442,7 @@
             shape_of((cells, channels)),
             shape_of((8, channels)),
         ],
-        [place, x, stat, gain, bias, hidden_grad, spread],
+        [place, x, stat, gain, bias, hidden_grad, held(spread, pltpu.VMEM)],
         [SMEM] + [VMEM] * 6,
         flops=cells * TAPS * channels * channels,
     )
@@ -396,7 +451,7 @@
     (home,) = call(
         home_kernel,
         [shape_of((16, HALF, 8, 128))],
-        [place, turned, spread],
+        [place, turned, held(spread, pltpu.VMEM)],
         [SMEM, VMEM, VMEM],
         flops=cells * TAPS * channels * channels,
     )

time: 84 us -> 81.4 us (0.969); the launches traced: 83.6 us -> 80.1 us
  blocking collectives: 13.8 us -> 31.1 us
  starting transfers between devices: 35.7 us -> 22.9 us
  local copies, waits for them, and re-layouts: 7.55 us -> 0.01 us
  waiting for transfers between devices: 13.4 us -> 11.1 us
  Pallas kernels: 12.3 us -> 14.1 us
    all_to_all x0 -> x1, blocking collectives: none -> 18 us  [local(): lax.all_to_all(stat[:, None], ('tm', 'rows'), 0, 0, axis_index_groups=gro...]
    all_to_all x1 -> x0, starting transfers between devices: 9.29 us -> none  [local(): lax.all_to_all(stat[:, None], ('tm', 'rows'), 0, 0, axis_index_groups=gro...]
    unnamed x16 -> x4, local copies, waits for them, and re-layouts: 7.55 us -> 0.01 us
    ppermute x3, starting transfers between devices: 8.49 us -> 5.26 us  [local(): lax.ppermute(half, 'rows', [(i, i ^ bits) for i in range(n_rows)])]
    ppermute x1, waiting for transfers between devices: 2.97 us -> 0.01 us  [local(): nearer = lax.ppermute(message, 'rows', near)]
    ppermute x3, waiting for transfers between devices: 5.3 us -> 7.85 us  [local(): lax.ppermute(half, 'rows', [(i, i ^ bits) for i in range(n_rows)])]
    all_to_all x1 -> x0, waiting for transfers between devices: 1.89 us -> none  [local(): lax.all_to_all(stat[:, None], ('tm', 'rows'), 0, 0, axis_index_groups=gro...]
    pallas_call x11 -> x12, Pallas kernels: 12.3 us -> 14.1 us  [call(): pl.pallas_call(body, out_shape=outs, in_specs=specs or [VMEM] * len(args)...]
  transfers between devices with their start and end apart: 11 -> 10, of which waited for: 8 -> 6; matrix products, arithmetic and copies ran while one was open for 0% -> 0% of each run, Pallas kernels for 7% -> 7%
where the time goes in v4:
time: 81.4 us; the launch traced here: 80.1 us
  blocking collectives  31.1 us (38%)
  starting transfers between devices  22.9 us (28%)
  Pallas kernels  14.1 us (17%)
  waiting for transfers between devices  11.1 us (14%)
    all_to_all x1, blocking collectives, local(): lax.all_to_all(stat[:, None], ('tm', 'rows'), 0, 0, axis_index_groups=gro...  18 us
    pallas_call x12, Pallas kernels, call(): pl.pallas_call(body, out_shape=outs, in_specs=specs or [VMEM] * len(args)...  14.1 us
    all_to_all x1, blocking collectives, local(): gathered = lax.all_to_all(sent, 'tm', 0, 0)  13.2 us
    ppermute x3, waiting for transfers between devices, local(): lax.ppermute(half, 'rows', [(i, i ^ bits) for i in range(n_rows)])  7.85 us
    ppermute x3, starting transfers between devices, local(): lax.ppermute(half, 'rows', [(i, i ^ bits) for i in range(n_rows)])  5.26 us
    ppermute x1, starting transfers between devices, local(): other = lax.ppermute(half, 'sect', swap)  4.75 us
    ppermute x1, starting transfers between devices, local(): farther = lax.ppermute(message, 'rows', far)  4.64 us
    ppermute x1, starting transfers between devices, local(): arrived = lax.ppermute(away, 'sect', swap)  3.41 us
  transfers between devices with their start and end apart: 10, of which 6 were waited for; matrix products, arithmetic and copies ran while one was open for 0% of the time, Pallas kernels for 7%

profile of v4, /device:TPU:1, one launch (start us, length us, event | category | flops | bytes accessed | tf_op | source)
XLA Modules:
  0.0 80.1 jit_solution(6118285553367131772)
XLA Ops:
  0.6 0.1 pad_add_fusion.place_ref
  0.7 1.8 %shard_map.84 = (bf16[4,8,32,128]{3,2,1,0:T(8,128)(2,1)S(1)}, bf16[4,8,32,128]{3,2,1,0:T(8,128)(2,1)S(1)}, bf16[528,128]{1,0:T(8,128)(2,1)S(1)}, f32[8,128]{1,0:T(8,128)S(1)}) custom-call(s32[4]{0:T(128)S(1)} %pad_add_fusion.place_ref, bf16[4,8,32,128]{3,2,1,0:T(8,128)(2,1)} %x_hbm.1, bf16[4,8,32,128]{3,2,1,0:T(8,128)(2,1)} %up_hbm.1), custom_call_target="tpu_custom_call" | custom-call | bytes 1187856 | tf_op jit(solution)/shard_map/pallas_call | solution.py:28
  2.6 3.3 %collective-permute-start = (bf16[528,128]{1,0:T(8,128)(2,1)S(1)}, bf16[528,128]{1,0:T(8,128)(2,1)S(1)}, u32[]{:S(2)}, u32[]{:S(2)}) collective-permute-start(bf16[528,128]{1,0:T(8,128)(2,1)S(1)} %get-tuple-element.33), channel_id=1, source_target_pairs={{0,1},{1,0},{2,3},{3,2},{4,5},{5,4},{6,7},{7,6},{8,9},{9,8},{10,11... | collective-permute-start | bytes 405512 | tf_op jit(solution)/shard_map/ppermute | solution.py:387
  5.9 1.0 %collective-permute-done.side_ref = bf16[528,128]{1,0:T(8,128)(2,1)S(1)} collective-permute-done((bf16[528,128]{1,0:T(8,128)(2,1)S(1)}, bf16[528,128]{1,0:T(8,128)(2,1)S(1)}, u32[]{:S(2)}, u32[]{:S(2)}) %collective-permute-start) | collective-permute-done | bytes 135200 | tf_op jit(solution)/shard_map/ppermute | solution.py:387
  6.9 0.6 shard_map.85
  7.4 0.0 copy-start
  7.5 0.0 copy-start.1
  7.5 0.1 collective-permute-start.1
  7.6 3.0 %shard_map.86 = (bf16[8,256,1152]{2,1,0:T(8,128)(2,1)S(1)}, f32[1024,128]{1,0:T(8,128)S(1)}, bf16[3,128,1152]{2,1,0:T(8,128)(2,1)S(1)}) custom-call(s32[4]{0:T(128)S(1)} %pad_add_fusion.place_ref, bf16[4,8,32,128]{3,2,1,0:T(8,128)(2,1)S(1)} %get-tuple-element.32.up_ref, bf16[528,128]{1,0:T(8,128)(2,1)S(1)} %collective-permute-done.side_ref, ...), custom_call_target="tpu_custom_call" | custom-call | flops 452984832 | bytes 7409680 | tf_op jit(solution)/shard_map/pallas_call | solution.py:28
  10.6 0.0 collective-permute-done.1.near_ref
  10.6 0.6 shard_map.87
  11.1 4.6 %collective-permute-start.2 = (bf16[208,128]{1,0:T(8,128)(2,1)S(1)}, bf16[208,128]{1,0:T(8,128)(2,1)S(1)}, u32[]{:S(2)}, u32[]{:S(2)}) collective-permute-start(bf16[208,128]{1,0:T(8,128)(2,1)S(1)} %get-tuple-element.39), channel_id=1, source_target_pairs={{0,14},{2,4},{4,2},{6,8},{8,6},{10,12},{12,10},{14,0},{1,15},{3,5}... | collective-permute-start | bytes 159752 | tf_op jit(solution)/shard_map/ppermute | solution.py:414
  15.8 1.5 %collective-permute-done.2.far_ref = bf16[208,128]{1,0:T(8,128)(2,1)S(1)} collective-permute-done((bf16[208,128]{1,0:T(8,128)(2,1)S(1)}, bf16[208,128]{1,0:T(8,128)(2,1)S(1)}, u32[]{:S(2)}, u32[]{:S(2)}) %collective-permute-start.2) | collective-permute-done | bytes 53280 | tf_op jit(solution)/shard_map/ppermute | solution.py:414
  17.3 0.6 shard_map.88
  17.9 1.3 %collective-permute-start.3 = (bf16[2,10,48,128]{3,2,1,0:T(8,128)(2,1)S(1)}, bf16[2,10,48,128]{3,2,1,0:T(8,128)(2,1)S(1)}, u32[]{:S(2)}, u32[]{:S(2)}) collective-permute-start(bf16[2,10,48,128]{3,2,1,0:T(8,128)(2,1)S(1)} %get-tuple-element.42), channel_id=1, source_target_pairs={{16,0},{32,16},{48,32},{64,48},{80,64},{96,80},{112,96},{128,112},... | collective-permute-start | bytes 737288 | tf_op jit(solution)/shard_map/ppermute | solution.py:423
  19.2 18.0 %all_to_all.10 = f32[32,1,128]{2,1,0:T(1,128)S(1)} all-to-all(f32[32,1,128]{2,1,0:T(1,128)S(1)} %bitcast.15), channel_id=1, replica_groups={{0,6,16,22,32,38,48,54,64,70,80,86,96,102,112,118,128,134,144,150,160,1..., dimensions={0} | all-to-all | bytes 32768 | tf_op jit(solution)/shard_map/all_to_all | solution.py:424
  37.1 0.0 collective-permute-done.3.later_ref
  37.1 2.0 %shard_map.89 = (bf16[8,256,1152]{2,1,0:T(8,128)(2,1)S(1)}, f32[1024,128]{1,0:T(8,128)S(1)}) custom-call(s32[4]{0:T(128)S(1)} %pad_add_fusion.place_ref, bf16[4,8,32,128]{3,2,1,0:T(8,128)(2,1)S(1)} %get-tuple-element.32.up_ref, bf16[528,128]{1,0:T(8,128)(2,1)S(1)} %collective-permute-done.side_ref, ...), custom_call_target="tpu_custom_call", output_to_operand_aliasing={{0}: (8, {})} | custom-call | flops 452984832 | bytes 12120080 | tf_op jit(solution)/shard_map/pallas_call | solution.py:28
  39.2 0.0 copy-done
  39.2 0.0 copy-done.1
  39.2 1.9 %shard_map.90 = (f32[16,14,8,128]{3,2,1,0:T(8,128)S(1)}, bf16[128,1024]{1,0:T(8,128)(2,1)S(1)}, f32[16,128]{1,0:T(8,128)S(1)}, f32[1024,128]{1,0:T(8,128)S(1)}, f32[8,128]{1,0:T(8,128)S(1)}) custom-call(s32[4]{0:T(128)S(1)} %pad_add_fusion.place_ref, bf16[4,8,32,128]{3,2,1,0:T(8,128)(2,1)S(1)} %get-tuple-element.31.x_ref, f32[32,128]{1,0:T(8,128)S(1)} %bitcast.14, ...), custom_call_target="tpu_custom_call" | custom-call | flops 452984832 | bytes 7238672 | tf_op jit(solution)/shard_map/pallas_call | solution.py:28
  41.1 3.4 %collective-permute-start.4 = (f32[16,14,8,128]{3,2,1,0:T(8,128)S(1)}, f32[16,14,8,128]{3,2,1,0:T(8,128)S(1)}, u32[]{:S(2)}, u32[]{:S(2)}) collective-permute-start(f32[16,14,8,128]{3,2,1,0:T(8,128)S(1)} %get-tuple-element.53), channel_id=1, source_target_pairs={{0,1},{1,0},{2,3},{3,2},{4,5},{5,4},{6,7},{7,6},{8,9},{9,8},{10,11... | collective-permute-start | bytes 2752520 | tf_op jit(solution)/shard_map/ppermute | solution.py:449
  44.5 0.1 collective-permute-start.5
  44.6 1.3 %shard_map.91.own_ref = f32[16,14,8,128]{3,2,1,0:T(8,128)S(1)} custom-call(s32[4]{0:T(128)S(1)} %pad_add_fusion.place_ref, bf16[128,1024]{1,0:T(8,128)(2,1)S(1)} %get-tuple-element.52.turned_ref, bf16[8,256,1152]{2,1,0:T(8,128)(2,1)S(1)} %get-tuple-element.49.v_ref), custom_call_target="tpu_custom_call" | custom-call | flops 452984832 | bytes 5898256 | tf_op jit(solution)/shard_map/pallas_call | solution.py:28
  45.9 0.7 collective-permute-done.5.other_sums_ref
  46.6 0.0 collective-permute-done.4.other_ref
  46.6 0.2 shard_map.92
  46.8 13.2 %all_to_all.11.in_ref = bf16[16,120,128]{2,1,0:T(8,128)(2,1)S(1)} all-to-all(bf16[16,120,128]{2,1,0:T(8,128)(2,1)S(1)} %shard_map.92), channel_id=1, replica_groups=mesh['tm'=16,'rows'=8,'sect'=2] {'tm'}, dimensions={0} | all-to-all | bytes 983040 | tf_op jit(solution)/shard_map/all_to_all | solution.py:461
  59.9 0.1 shard_map.93
  60.0 3.1 %collective-permute-start.6 = (f32[120,128]{1,0:T(8,128)S(1)}, f32[120,128]{1,0:T(8,128)S(1)}, u32[]{:S(2)}, u32[]{:S(2)}) collective-permute-start(f32[120,128]{1,0:T(8,128)S(1)} %shard_map.93), channel_id=1, source_target_pairs={{0,2},{2,0},{4,6},{6,4},{8,10},{10,8},{12,14},{14,12},{1,3},{3,1},... | collective-permute-start | bytes 184328 | tf_op jit(solution)/shard_map/ppermute | solution.py:464
  63.1 1.6 %collective-permute-done.6 = f32[120,128]{1,0:T(8,128)S(1)} collective-permute-done((f32[120,128]{1,0:T(8,128)S(1)}, f32[120,128]{1,0:T(8,128)S(1)}, u32[]{:S(2)}, u32[]{:S(2)}) %collective-permute-start.6) | collective-permute-done | bytes 61472 | tf_op jit(solution)/shard_map/ppermute | solution.py:464
  64.7 2.0 %collective-permute-start.7 = (f32[120,128]{1,0:T(8,128)S(1)}, f32[120,128]{1,0:T(8,128)S(1)}, u32[]{:S(2)}, u32[]{:S(2)}) collective-permute-start(f32[120,128]{1,0:T(8,128)S(1)} %add.9), channel_id=1, source_target_pairs={{0,4},{2,6},{4,0},{6,2},{8,12},{10,14},{12,8},{14,10},{1,5},{3,7},... | collective-permute-start | bytes 184328 | tf_op jit(solution)/shard_map/ppermute | solution.py:464
  66.6 2.1 %collective-permute-done.7 = f32[120,128]{1,0:T(8,128)S(1)} collective-permute-done((f32[120,128]{1,0:T(8,128)S(1)}, f32[120,128]{1,0:T(8,128)S(1)}, u32[]{:S(2)}, u32[]{:S(2)}) %collective-permute-start.7) | collective-permute-done | bytes 61472 | tf_op jit(solution)/shard_map/ppermute | solution.py:464
  68.8 0.2 collective-permute-start.8
  69.0 4.1 %collective-permute-done.8 = f32[120,128]{1,0:T(8,128)S(1)} collective-permute-done((f32[120,128]{1,0:T(8,128)S(1)}, f32[120,128]{1,0:T(8,128)S(1)}, u32[]{:S(2)}, u32[]{:S(2)}) %collective-permute-start.8) | collective-permute-done | bytes 61472 | tf_op jit(solution)/shard_map/ppermute | solution.py:464
  73.1 4.8 %collective-permute-start.9 = (f32[120,128]{1,0:T(8,128)S(1)}, f32[120,128]{1,0:T(8,128)S(1)}, u32[]{:S(2)}, u32[]{:S(2)}) collective-permute-start(f32[120,128]{1,0:T(8,128)S(1)} %add.11.sums_ref.half_ref), channel_id=1, source_target_pairs={{0,1},{1,0},{2,3},{3,2},{4,5},{5,4},{6,7},{7,6},{8,9},{9,8},{10,11... | collective-permute-start | bytes 184328 | tf_op jit(solution)/shard_map/ppermute | solution.py:465
  77.9 1.0 %shard_map.94 = (bf16[4,8,32,128]{3,2,1,0:T(8,128)(2,1)}, f32[1,128]{1,0:T(1,128)}, f32[1,128]{1,0:T(1,128)}) custom-call(bf16[4,8,32,128]{3,2,1,0:T(8,128)(2,1)S(1)} %get-tuple-element.31.x_ref, f32[1024,128]{1,0:T(8,128)S(1)} %get-tuple-element.50.da_ref, f32[16,128]{1,0:T(8,128)S(1)} %get-tuple-element.51.norm_ref, f32[120,128]{1,0:T(8,128)S(1)} %add.11.sums_ref.half_ref, ...), custom_call_target="tpu_custom_call" | custom-call | bytes 1119744 | tf_op jit(solution)/shard_map/pallas_call | solution.py:28
  78.9 0.0 collective-permute-done.9.other_ref
  78.9 1.2 %shard_map.95 = f32[216,128]{1,0:T(8,128)} custom-call(s32[4]{0:T(128)S(1)} %pad_add_fusion.place_ref, f32[120,128]{1,0:T(8,128)S(1)} %add.11.sums_ref.half_ref, f32[120,128]{1,0:T(8,128)S(1)} %collective-permute-done.9.other_ref), custom_call_target="tpu_custom_call" | custom-call | bytes 233488 | tf_op jit(solution)/shard_map/pallas_call | solution.py:28
  (3 shorter events, 0.0 us)
Async XLA Ops:
  2.6 4.3 %collective-permute-start = (bf16[528,128]{1,0:T(8,128)(2,1)S(1)}, bf16[528,128]{1,0:T(8,128)(2,1)S(1)}, u32[]{:S(2)}, u32[]{:S(2)}) collective-permute-start(bf16[528,128]{1,0:T(8,128)(2,1)S(1)} %get-tuple-element.33), channel_id=1, source_target_pairs={{0,1},{1,0},{2,3},{3,2},{4,5},{5,4},{6,7},{7,6},{8,9},{9,8},{10,11... | collective-permute-start | bytes 405512 | tf_op jit(solution)/shard_map/ppermute | solution.py:387
  7.4 31.8 %copy-start = (f32[128]{0:T(128)S(1)}, f32[128]{0:T(128)}, u32[]{:S(2)}) copy-start(f32[128]{0:T(128)} %param.6) | copy-start | bytes 1540
  7.5 31.7 %copy-start.1 = (f32[128]{0:T(128)S(1)}, f32[128]{0:T(128)}, u32[]{:S(2)}) copy-start(f32[128]{0:T(128)} %param.7) | copy-start | bytes 1540
  7.5 3.1 %collective-permute-start.1 = (bf16[208,128]{1,0:T(8,128)(2,1)S(1)}, bf16[208,128]{1,0:T(8,128)(2,1)S(1)}, u32[]{:S(2)}, u32[]{:S(2)}) collective-permute-start(bf16[208,128]{1,0:T(8,128)(2,1)S(1)} %get-tuple-element.35), channel_id=1, source_target_pairs={{0,2},{2,0},{4,6},{6,4},{8,10},{10,8},{12,14},{14,12},{1,3},{3,1},... | collective-permute-start | bytes 159752 | tf_op jit(solution)/shard_map/ppermute | solution.py:394
  11.1 6.2 %collective-permute-start.2 = (bf16[208,128]{1,0:T(8,128)(2,1)S(1)}, bf16[208,128]{1,0:T(8,128)(2,1)S(1)}, u32[]{:S(2)}, u32[]{:S(2)}) collective-permute-start(bf16[208,128]{1,0:T(8,128)(2,1)S(1)} %get-tuple-element.39), channel_id=1, source_target_pairs={{0,14},{2,4},{4,2},{6,8},{8,6},{10,12},{12,10},{14,0},{1,15},{3,5}... | collective-permute-start | bytes 159752 | tf_op jit(solution)/shard_map/ppermute | solution.py:414
  17.9 19.3 %collective-permute-start.3 = (bf16[2,10,48,128]{3,2,1,0:T(8,128)(2,1)S(1)}, bf16[2,10,48,128]{3,2,1,0:T(8,128)(2,1)S(1)}, u32[]{:S(2)}, u32[]{:S(2)}) collective-permute-start(bf16[2,10,48,128]{3,2,1,0:T(8,128)(2,1)S(1)} %get-tuple-element.42), channel_id=1, source_target_pairs={{16,0},{32,16},{48,32},{64,48},{80,64},{96,80},{112,96},{128,112},... | collective-permute-start | bytes 737288 | tf_op jit(solution)/shard_map/ppermute | solution.py:423
  41.1 5.5 %collective-permute-start.4 = (f32[16,14,8,128]{3,2,1,0:T(8,128)S(1)}, f32[16,14,8,128]{3,2,1,0:T(8,128)S(1)}, u32[]{:S(2)}, u32[]{:S(2)}) collective-permute-start(f32[16,14,8,128]{3,2,1,0:T(8,128)S(1)} %get-tuple-element.53), channel_id=1, source_target_pairs={{0,1},{1,0},{2,3},{3,2},{4,5},{5,4},{6,7},{7,6},{8,9},{9,8},{10,11... | collective-permute-start | bytes 2752520 | tf_op jit(solution)/shard_map/ppermute | solution.py:449
  44.5 2.1 %collective-permute-start.5 = (f32[8,128]{1,0:T(8,128)S(1)}, f32[8,128]{1,0:T(8,128)S(1)}, u32[]{:S(2)}, u32[]{:S(2)}) collective-permute-start(f32[8,128]{1,0:T(8,128)S(1)} %get-tuple-element.54.sums_ref), channel_id=1, source_target_pairs={{0,1},{1,0},{2,3},{3,2},{4,5},{5,4},{6,7},{7,6},{8,9},{9,8},{10,11... | collective-permute-start | bytes 12296 | tf_op jit(solution)/shard_map/ppermute | solution.py:450
  60.0 4.7 %collective-permute-start.6 = (f32[120,128]{1,0:T(8,128)S(1)}, f32[120,128]{1,0:T(8,128)S(1)}, u32[]{:S(2)}, u32[]{:S(2)}) collective-permute-start(f32[120,128]{1,0:T(8,128)S(1)} %shard_map.93), channel_id=1, source_target_pairs={{0,2},{2,0},{4,6},{6,4},{8,10},{10,8},{12,14},{14,12},{1,3},{3,1},... | collective-permute-start | bytes 184328 | tf_op jit(solution)/shard_map/ppermute | solution.py:464
  64.7 4.1 %collective-permute-start.7 = (f32[120,128]{1,0:T(8,128)S(1)}, f32[120,128]{1,0:T(8,128)S(1)}, u32[]{:S(2)}, u32[]{:S(2)}) collective-permute-start(f32[120,128]{1,0:T(8,128)S(1)} %add.9), channel_id=1, source_target_pairs={{0,4},{2,6},{4,0},{6,2},{8,12},{10,14},{12,8},{14,10},{1,5},{3,7},... | collective-permute-start | bytes 184328 | tf_op jit(solution)/shard_map/ppermute | solution.py:464
  68.8 4.4 %collective-permute-start.8 = (f32[120,128]{1,0:T(8,128)S(1)}, f32[120,128]{1,0:T(8,128)S(1)}, u32[]{:S(2)}, u32[]{:S(2)}) collective-permute-start(f32[120,128]{1,0:T(8,128)S(1)} %add.10), channel_id=1, source_target_pairs={{0,14},{2,12},{4,10},{6,8},{8,6},{10,4},{12,2},{14,0},{1,15},{3,13... | collective-permute-start | bytes 184328 | tf_op jit(solution)/shard_map/ppermute | solution.py:464
  73.1 5.8 %collective-permute-start.9 = (f32[120,128]{1,0:T(8,128)S(1)}, f32[120,128]{1,0:T(8,128)S(1)}, u32[]{:S(2)}, u32[]{:S(2)}) collective-permute-start(f32[120,128]{1,0:T(8,128)S(1)} %add.11.sums_ref.half_ref), channel_id=1, source_target_pairs={{0,1},{1,0},{2,3},{3,2},{4,5},{5,4},{6,7},{7,6},{8,9},{9,8},{10,11... | collective-permute-start | bytes 184328 | tf_op jit(solution)/shard_map/ppermute | solution.py:465

commit v5 on v4

--- a/solution.py
+++ b/solution.py
@@ -15,7 +15,6 @@
 F32 = jnp.float32
 BF16 = jnp.bfloat16
 VMEM = pl.BlockSpec(memory_space=pltpu.VMEM)
-SMEM = pl.BlockSpec(memory_space=pltpu.SMEM)
 HBM = pl.BlockSpec(memory_space=pltpu.HBM)
 
 
@@ -70,7 +69,7 @@
     return jnp.broadcast_to(parts[0:1] + parts[1:2] + parts[2:3], (8, 128))
 
 
-def entry_kernel(place_ref, x_hbm, up_hbm, x_ref, up_ref, facing_ref, stat_ref, x_sem, up_sem):
+def entry_kernel(x_hbm, up_hbm, x_ref, up_ref, facing_ref, stat_ref, x_sem, up_sem):
     up_copy = pltpu.make_async_copy(up_hbm, up_ref, up_sem)
     x_copy = pltpu.make_async_copy(x_hbm, x_ref, x_sem)
     x_copy.start()
@@ -83,7 +82,7 @@
     stat_ref[...] = row
     facing_ref[512:] = split_row(row)
     up_copy.wait()
-    left = place_ref[3] == 0
+    left = lax.axis_index("sect") == 0
     up = up_ref[...]
     facing_ref[:512] = jnp.where(left, up[:, :, 16:], up[:, :, :16]).reshape(512, 128)
 
@@ -95,43 +94,43 @@
     return jnp.where(bottom, low, top).reshape(192, 128)
 
 
-def first_edge_kernel(place_ref, up_ref, side_ref, stat_ref, out_ref, sum_ref):
-    even = place_ref[1] % 2 == 0
+def first_edge_kernel(up_ref, side_ref, stat_ref, out_ref, sum_ref):
+    even = lax.axis_index("rows") % 2 == 0
     row = stat_ref[...] + join_row(side_ref[512:])
     sum_ref[...] = row
     out_ref[:192] = edge_of(up_ref, side_ref, even)
     out_ref[192:] = split_row(row)
 
 
-def second_edge_kernel(place_ref, up_ref, side_ref, near_ref, stat_ref, out_ref, sum_ref):
-    even = place_ref[1] % 2 == 0
+def second_edge_kernel(up_ref, side_ref, near_ref, stat_ref, out_ref, sum_ref):
+    even = lax.axis_index("rows") % 2 == 0
     row = stat_ref[...] + join_row(near_ref[192:])
     sum_ref[...] = row
     out_ref[:192] = edge_of(up_ref, side_ref, jnp.logical_not(even))
     out_ref[192:] = split_row(row)
 
 
-def beyond(place_ref, near_ref, far_ref):
-    even = place_ref[1] % 2 == 0
-    outside = jnp.logical_or(place_ref[1] == 0, place_ref[1] == place_ref[2] - 1)
+def beyond(near_ref, far_ref):
+    even = lax.axis_index("rows") % 2 == 0
+    outside = jnp.logical_or(lax.axis_index("rows") == 0, lax.axis_index("rows") == lax.axis_size("rows") - 1)
     near = near_ref[:192].reshape(4, 48, 128)
     far = far_ref[:192].reshape(4, 48, 128)
     far = jnp.where(outside, jnp.zeros_like(far), far)
     return jnp.where(even, far, near), jnp.where(even, near, far)
 
 
-def early_kernel(place_ref, up_ref, side_ref, near_ref, far_ref, stat_ref, early_ref, sent_ref):
+def early_kernel(up_ref, side_ref, near_ref, far_ref, stat_ref, early_ref, sent_ref):
     row = stat_ref[...] + join_row(far_ref[192:])
     sent_ref[...] = jnp.broadcast_to(row[None], (sent_ref.shape[0] // 8, 8, 128)).reshape(sent_ref.shape)
-    above, below = beyond(place_ref, near_ref, far_ref)
+    above, below = beyond(near_ref, far_ref)
     early_ref[:, 0] = above[:2]
     early_ref[:, 9] = below[:2]
     early_ref[:, 1:9, :32] = up_ref[:2]
     early_ref[:, 1:9, 32:] = side_ref[:256].reshape(2, 8, 16, 128)
 
 
-def column_taps(place_ref, rows):
-    left = place_ref[3] == 0
+def column_taps(rows):
+    left = lax.axis_index("sect") == 0
     core = rows[:, :32]
     column = sublanes_of(core.shape)
     first = column == 0
@@ -154,15 +153,15 @@
     return lax.dot_general(lhs, taps_ref[a], (((1,), (1,)), ((), ())), preferred_element_type=F32)
 
 
-def own_kernel(place_ref, up_ref, side_ref, kernel_hbm, v_ref, dh_ref, taps_ref, kernel_ref, sem):
+def own_kernel(up_ref, side_ref, kernel_hbm, v_ref, dh_ref, taps_ref, kernel_ref, sem):
     weights = pltpu.make_async_copy(kernel_hbm, kernel_ref, sem)
     weights.start()
-    row_first = place_ref[1] == 0
-    row_last = place_ref[1] == place_ref[2] - 1
+    row_first = lax.axis_index("rows") == 0
+    row_last = lax.axis_index("rows") == lax.axis_size("rows") - 1
     for f in range(4):
         side = side_ref[f * 128 : (f + 1) * 128].reshape(8, 16, 128)
         rows = jnp.concatenate([up_ref[f].astype(F32), side.astype(F32)], axis=1)
-        for e, part in enumerate(column_taps(place_ref, rows)):
+        for e, part in enumerate(column_taps(rows)):
             zero = jnp.zeros_like(part[0])
             top = part[1] + jnp.where(row_first, part[0], zero)
             low = part[6] + jnp.where(row_last, part[7], zero)
@@ -186,18 +185,17 @@
         dh_ref[f * 256 + 32 : f * 256 + 224] = total
 
 
-def grad_kernel(place_ref, up_ref, side_ref, near_ref, far_ref, later_ref, taps_ref, part_ref, own_ref, v_ref, dh_ref):
-    time_first = place_ref[0] == 0
-    above, below = beyond(place_ref, near_ref, far_ref)
-    row_first = place_ref[1] == 0
-    row_last = place_ref[1] == place_ref[2] - 1
+def spread_kernel(near_ref, far_ref, later_ref, own_ref, v_ref):
+    above, below = beyond(near_ref, far_ref)
+    row_first = lax.axis_index("rows") == 0
+    row_last = lax.axis_index("rows") == lax.axis_size("rows") - 1
     outer = jnp.concatenate([above, below], axis=0).astype(F32)
-    for e, part in enumerate(column_taps(place_ref, outer)):
+    for e, part in enumerate(column_taps(outer)):
         for f in range(4):
             put(v_ref, f, 0, 2, e, part[f : f + 1])
             put(v_ref, f, 7, 0, e, part[f + 4 : f + 5])
     for f in range(2):
-        for e, part in enumerate(column_taps(place_ref, later_ref[f].astype(F32))):
+        for e, part in enumerate(column_taps(later_ref[f].astype(F32))):
             zero = jnp.zeros_like(part[0])
             top = part[2] + jnp.where(row_first, part[1], zero)
             low = part[7] + jnp.where(row_last, part[8], zero)
@@ -207,6 +205,14 @@
             put(v_ref, f + 4, 0, 2, e, part[0:7])
             put(v_ref, f + 4, 7, 2, e, low[None])
 
+    @pl.when(lax.axis_index("tm") == 0)
+    def _():
+        both = v_ref[1].astype(F32) + v_ref[0].astype(F32)
+        v_ref[6] = both.astype(BF16)
+        v_ref[7] = (both + v_ref[2].astype(F32)).astype(BF16)
+
+
+def grad_kernel(x_ref, norm_ref, gain_ref, bias_ref, taps_ref, part_ref, v_ref, da_ref, sums_ref, dh_ref):
     def edges(lo, hi):
         return jnp.concatenate([v_ref[lo:hi, 0:32], v_ref[lo:hi, 224:256]], axis=1).reshape((hi - lo) * 64, 1152)
 
@@ -222,12 +228,20 @@
     dh_ref[768:1024] += times_taps(v_ref[4], taps_ref, 1)
     dh_ref[512:1024] += times_taps(v_ref[4:6].reshape(512, 1152), taps_ref, 0)
 
-    @pl.when(time_first)
+    @pl.when(lax.axis_index("tm") == 0)
     def _():
-        both = v_ref[1].astype(F32) + v_ref[0].astype(F32)
-        v_ref[6] = both.astype(BF16)
-        v_ref[7] = (both + v_ref[2].astype(F32)).astype(BF16)
         dh_ref[0:256] += times_taps(v_ref[0], taps_ref, 1) + times_taps(v_ref[6], taps_ref, 0)
+
+    bias_sum = jnp.zeros((8, 128), F32)
+    gain_sum = jnp.zeros((8, 128), F32)
+    for block in range(8):
+        xhat, pre = block_of(x_ref, norm_ref, gain_ref, bias_ref, block)
+        sig = 1.0 / (1.0 + jnp.exp(-pre))
+        da = dh_ref[block * 128 : (block + 1) * 128] * sig * (1.0 + pre * (1.0 - sig))
+        da_ref[block * 128 : (block + 1) * 128] = da
+        bias_sum = bias_sum + jnp.sum(da.reshape(16, 8, 128), axis=0)
+        gain_sum = gain_sum + jnp.sum((da * xhat).reshape(16, 8, 128), axis=0)
+    sums_ref[...] = jnp.where(sublanes_of((8, 128)) == 0, column_sum(bias_sum), column_sum(gain_sum))
 
 
 def sums_to_pair(row):
@@ -237,18 +251,18 @@
     return total, square
 
 
-def product_of(place_ref, turned, v_ref, a, lo, hi):
+def product_of(turned, v_ref, a, lo, hi):
     if a == 2:
         return jnp.dot(turned, v_ref[0:4, :, lo:hi].reshape(1024, hi - lo), preferred_element_type=F32)
-    source = jnp.where(place_ref[0] == 0, 7 - a, 2 - a)
+    source = jnp.where(lax.axis_index("tm") == 0, 7 - a, 2 - a)
     first = jnp.dot(turned[:, :256], v_ref[source, :, lo:hi], preferred_element_type=F32)
     rest = v_ref[3 - a : 6 - a, :, lo:hi].reshape(768, hi - lo)
     return first + jnp.dot(turned[:, 256:], rest, preferred_element_type=F32)
 
 
-def half_product(place_ref, half, turned, v_ref, w_ref):
+def half_product(half, turned, v_ref, w_ref):
     for a, lo, hi in (((0, 0, 9), (1, 0, 5)), ((1, 5, 9), (2, 0, 9)))[half]:
-        product = product_of(place_ref, turned, v_ref, a, lo * 128, hi * 128)
+        product = product_of(turned, v_ref, a, lo * 128, hi * 128)
         for j in range(lo, hi):
             block = product[:, (j - lo) * 128 : (j - lo + 1) * 128].T.reshape(16, 8, 128)
             w_ref[:, (a * 9 + j) % HALF] = block
@@ -256,50 +270,43 @@
         w_ref[:, HALF - 1] = jnp.zeros((16, 8, 128), F32)
 
 
-def away_kernel(
-    counted, place_ref, x_ref, stat_ref, gain_ref, bias_ref, dh_ref, v_ref, w_ref, turned_ref, norm_ref, da_ref, sums_ref
-):
+def block_of(x_ref, norm_ref, gain_ref, bias_ref, block):
+    half = (block % 2) * 4
+    x = x_ref[block // 2, half : half + 4].astype(F32).reshape(128, 128)
+    xhat = (x - norm_ref[0:1]) * norm_ref[8:9]
+    return xhat, xhat * gain_ref[...] + bias_ref[...]
+
+
+def away_kernel(counted, x_ref, stat_ref, gain_ref, bias_ref, v_ref, w_ref, turned_ref, norm_ref):
     total, square = sums_to_pair(column_sum(stat_ref[...]))
     mean = total / counted
-    rstd = lax.rsqrt(square / counted - mean * mean + 1e-06)
     norm_ref[0:8] = mean
-    norm_ref[8:16] = rstd
-    mean, rstd = mean[:1], rstd[:1]
-    gain = gain_ref[...]
-    bias = bias_ref[...]
-    bias_sum = jnp.zeros((8, 128), F32)
-    gain_sum = jnp.zeros((8, 128), F32)
+    norm_ref[8:16] = lax.rsqrt(square / counted - mean * mean + 1e-06)
     for block in range(8):
-        xhat = (x_ref[block // 2, (block % 2) * 4 : (block % 2) * 4 + 4].astype(F32).reshape(128, 128) - mean) * rstd
-        pre = xhat * gain + bias
-        sig = 1.0 / (1.0 + jnp.exp(-pre))
-        turned_ref[:, block * 128 : (block + 1) * 128] = (pre * sig).T.astype(BF16)
-        da = dh_ref[block * 128 : (block + 1) * 128] * sig * (1.0 + pre * (1.0 - sig))
-        da_ref[block * 128 : (block + 1) * 128] = da
-        bias_sum = bias_sum + jnp.sum(da.reshape(16, 8, 128), axis=0)
-        gain_sum = gain_sum + jnp.sum((da * xhat).reshape(16, 8, 128), axis=0)
-    sums_ref[...] = jnp.where(sublanes_of((8, 128)) == 0, column_sum(bias_sum), column_sum(gain_sum))
-    left = place_ref[3] == 0
+        _, pre = block_of(x_ref, norm_ref, gain_ref, bias_ref, block)
+        hidden = pre * (1.0 / (1.0 + jnp.exp(-pre)))
+        turned_ref[:, block * 128 : (block + 1) * 128] = hidden.T.astype(BF16)
+    left = lax.axis_index("sect") == 0
 
     @pl.when(left)
     def _():
-        half_product(place_ref, 1, turned_ref[...], v_ref, w_ref)
+        half_product(1, turned_ref[...], v_ref, w_ref)
 
     @pl.when(jnp.logical_not(left))
     def _():
-        half_product(place_ref, 0, turned_ref[...], v_ref, w_ref)
-
-
-def home_kernel(place_ref, turned_ref, v_ref, w_ref):
-    left = place_ref[3] == 0
+        half_product(0, turned_ref[...], v_ref, w_ref)
+
+
+def home_kernel(turned_ref, v_ref, w_ref):
+    left = lax.axis_index("sect") == 0
 
     @pl.when(left)
     def _():
-        half_product(place_ref, 0, turned_ref[...], v_ref, w_ref)
+        half_product(0, turned_ref[...], v_ref, w_ref)
 
     @pl.when(jnp.logical_not(left))
     def _():
-        half_product(place_ref, 1, turned_ref[...], v_ref, w_ref)
+        half_product(1, turned_ref[...], v_ref, w_ref)
 
 
 def split_sums(sums):
@@ -323,20 +330,46 @@
         out_ref[i] = jnp.concatenate([body, slot], axis=0).astype(BF16)
 
 
+def power_for(values):
+    most = jnp.max(jnp.max(jnp.abs(values), axis=0, keepdims=True), axis=1, keepdims=True)
+    bits = jnp.log(jnp.maximum(most, 1e-30)) * 1.4426950408889634
+    return jnp.clip(jnp.floor(14.0 - bits), -100.0, 100.0)
+
+
 def share_kernel(in_ref, out_ref):
     rows = HALF * 8
     total = in_ref[0].astype(F32)
     for i in range(1, in_ref.shape[0]):
         total = total + in_ref[i].astype(F32)
-    out_ref[:rows] = total[:rows]
-    out_ref[rows:] = join_sums(total[rows:])
+    body = total[:rows]
+    sums = join_sums(total[rows:])
+    index = sublanes_of(sums.shape)
+    sums = jnp.where(index < 2, sums, jnp.zeros_like(sums))
+    power = power_for(body)
+    power_of_sums = power_for(sums)
+    slot = split_sums(sums * jnp.exp2(power_of_sums))
+    slot = jnp.where(index == 6, power, jnp.where(index == 7, power_of_sums, slot))
+    out_ref[:rows] = body * jnp.exp2(power)
+    out_ref[rows:] = slot
+
+
+def last_sum_kernel(scaling, in_ref, half_ref, sums_ref):
+    rows = HALF * 8
+    total = jnp.zeros((rows, 128), F32)
+    sums = jnp.zeros((8, 128), F32)
+    for i in range(in_ref.shape[0]):
+        slot = in_ref[i, rows:]
+        total = total + in_ref[i, :rows] * jnp.exp2(-slot[6:7])
+        sums = sums + join_sums(slot) * jnp.exp2(-slot[7:8])
+    half_ref[...] = total * scaling
+    sums_ref[...] = sums
 
 
 def finish_kernel(counted, scaling, x_ref, da_ref, norm_ref, sums_ref, gain_ref, out_ref, gain_grad_ref, bias_grad_ref):
     gain = gain_ref[...]
     mean = norm_ref[0:1]
     rstd = norm_ref[8:9]
-    sums = sums_ref[HALF * 8 :]
+    sums = sums_ref[...]
     bias_grad_ref[...] = sums[0:1] * scaling
     gain_grad_ref[...] = sums[1:2] * scaling
     averages = group_total(gain * sums) / counted
@@ -347,10 +380,10 @@
     out_ref[...] = grad.astype(BF16).reshape(out_ref.shape)
 
 
-def join_kernel(scaling, place_ref, half_ref, other_ref, out_ref):
-    left = place_ref[3] == 0
-    half = half_ref[: HALF * 8] * scaling
-    other = other_ref[: HALF * 8] * scaling
+def join_kernel(half_ref, other_ref, out_ref):
+    left = lax.axis_index("sect") == 0
+    half = half_ref[...]
+    other = other_ref[...]
     out_ref[: HALF * 8] = jnp.where(left, half, other)
     out_ref[HALF * 8 :] = jnp.where(left, other, half)[: (TAPS - HALF) * 8]
 
@@ -366,8 +399,6 @@
     total_cells = cells * n_time * n_rows * n_sect
     counted = float(total_cells * (channels // GROUPS))
     scaling = float(total_cells) ** (-0.5)
-    tm, rows, sect = (lax.axis_index(axis) for axis in ("tm", "rows", "sect"))
-    place = jnp.stack([tm, rows, jnp.int32(n_rows), sect]).astype(jnp.int32)
     swap = [(0, 1), (1, 0)]
     near = [(i, i ^ 1) for i in range(n_rows)]
     far = [(i, (i - 1) % n_rows if i % 2 == 0 else (i + 1) % n_rows) for i in range(n_rows)]
@@ -380,16 +411,16 @@
             shape_of((528, channels), BF16),
             shape_of((8, channels)),
         ],
-        [place, held(activations, pltpu.HBM), held(upstream, pltpu.HBM)],
-        [SMEM, HBM, HBM],
+        [held(activations, pltpu.HBM), held(upstream, pltpu.HBM)],
+        [HBM, HBM],
         [pltpu.SemaphoreType.DMA, pltpu.SemaphoreType.DMA],
     )
     side = lax.ppermute(facing, "sect", swap)
     message, stat = call(
         first_edge_kernel,
         [shape_of((208, channels), BF16), shape_of((8, channels))],
-        [place, up, side, stat],
-        [SMEM, VMEM, VMEM, VMEM],
+        [up, side, stat],
+        [VMEM, VMEM, VMEM],
     )
     nearer = lax.ppermute(message, "rows", near)
     spread, inner, taps = call(
@@ -399,8 +430,8 @@
             shape_of((cells, channels)),
             shape_of((3, channels, 9 * channels), BF16),
         ],
-        [place, up, side, held(kernel, pltpu.HBM)],
-        [SMEM, VMEM, VMEM, HBM],
+        [up, side, held(kernel, pltpu.HBM)],
+        [VMEM, VMEM, HBM],
         [pltpu.VMEM((3, 3, 3, 128, 128), BF16), pltpu.SemaphoreType.DMA],
         flops=cells * TAPS * channels * channels,
     )
@@ -408,8 +439,8 @@
     message, stat = call(
         second_edge_kernel,
         [shape_of((208, channels), BF16), shape_of((8, channels))],
-        [place, up, side, nearer, stat],
-        [SMEM, VMEM, VMEM, VMEM, VMEM],
+        [up, side, nearer, stat],
+        [VMEM, VMEM, VMEM, VMEM],
     )
     farther = lax.ppermute(message, "rows", far)
     pairs = [(0, 3), (1, 6), (2, 5), (4, 7)]
@@ -417,63 +448,60 @@
     early, stat = call(
         early_kernel,
         [shape_of((2, 10, 48, channels), BF16), shape_of((len(groups[0]), channels))],
-        [place, up, side, nearer, farther, stat],
-        [SMEM, VMEM, VMEM, VMEM, VMEM, VMEM],
+        [up, side, nearer, farther, stat],
+        [VMEM, VMEM, VMEM, VMEM, VMEM],
     )
     later = lax.ppermute(early, "tm", [(i + 1, i) for i in range(n_time - 1)])
     stat = lax.all_to_all(stat[:, None], ("tm", "rows"), 0, 0, axis_index_groups=groups).reshape(-1, channels)
     stat, later = lax.optimization_barrier((stat, later))
-    spread, hidden_grad = call(
-        grad_kernel,
-        [pltpu.VMEM((8, 256, 1152), BF16), shape_of((cells, channels))],
-        [place, up, side, nearer, farther, later, taps, inner, held(spread, pltpu.VMEM)],
-        [SMEM] + [VMEM] * 8,
-        flops=cells * TAPS * channels * channels,
-        aliases={8: 0},
+    (spread,) = call(
+        spread_kernel,
+        [pltpu.VMEM((8, 256, 1152), BF16)],
+        [nearer, farther, later, held(spread, pltpu.VMEM)],
+        aliases={3: 0},
     )
     gain = group_norm_gain.reshape(1, channels)
     bias = group_norm_bias.reshape(1, channels)
-    away, turned, norm, da, sums = call(
+    away, turned, norm = call(
         functools.partial(away_kernel, counted),
-        [
-            shape_of((16, HALF, 8, 128)),
-            shape_of((channels, cells), BF16),
-            shape_of((16, channels)),
-            shape_of((cells, channels)),
-            shape_of((8, channels)),
-        ],
-        [place, x, stat, gain, bias, hidden_grad, held(spread, pltpu.VMEM)],
-        [SMEM] + [VMEM] * 6,
+        [shape_of((16, HALF, 8, 128)), shape_of((channels, cells), BF16), shape_of((16, channels))],
+        [x, stat, gain, bias, held(spread, pltpu.VMEM)],
         flops=cells * TAPS * channels * channels,
     )
     arrived = lax.ppermute(away, "sect", swap)
+    da, sums = call(
+        grad_kernel,
+        [shape_of((cells, channels)), shape_of((8, channels))],
+        [x, norm, gain, bias, taps, inner, held(spread, pltpu.VMEM)],
+        scratch=[pltpu.VMEM((cells, channels), F32)],
+        flops=cells * TAPS * channels * channels,
+    )
     other_sums = lax.ppermute(sums, "sect", swap)
     (home,) = call(
         home_kernel,
         [shape_of((16, HALF, 8, 128))],
-        [place, turned, held(spread, pltpu.VMEM)],
-        [SMEM, VMEM, VMEM],
+        [turned, held(spread, pltpu.VMEM)],
         flops=cells * TAPS * channels * channels,
     )
     (sent,) = call(
         pair_kernel, [shape_of((16, SLOTS * 8, 128), BF16)], [home, arrived, sums, other_sums]
     )
     gathered = lax.all_to_all(sent, "tm", 0, 0)
-    (half,) = call(share_kernel, [shape_of((SLOTS * 8, 128))], [gathered])
-    for bits in (1, 2, 7):
-        half = half + lax.ppermute(half, "rows", [(i, i ^ bits) for i in range(n_rows)])
+    (share,) = call(share_kernel, [shape_of((SLOTS * 8, 128))], [gathered])
+    share = jnp.broadcast_to(share.astype(jnp.float16)[None], (n_rows, SLOTS * 8, 128))
+    shares = lax.all_to_all(share, "rows", 0, 0).astype(F32)
+    half, sums = call(
+        functools.partial(last_sum_kernel, scaling),
+        [shape_of((HALF * 8, 128)), shape_of((8, 128))],
+        [shares],
+    )
     other = lax.ppermute(half, "sect", swap)
     input_gradient, gain_grad, bias_grad = call(
         functools.partial(finish_kernel, counted, scaling),
         [shape_of(activations.shape, BF16), shape_of((1, 128)), shape_of((1, 128))],
-        [x, da, norm, half, gain],
-    )
-    (whole,) = call(
-        functools.partial(join_kernel, scaling),
-        [shape_of((TAPS * 8, 128))],
-        [place, half, other],
-        [SMEM, VMEM, VMEM],
-    )
+        [x, da, norm, sums, gain],
+    )
+    (whole,) = call(join_kernel, [shape_of((TAPS * 8, 128))], [half, other])
     weight_grad = whole.reshape(3, 3, 3, 8, 128).transpose(0, 1, 2, 4, 3)
     return (input_gradient, gain_grad.reshape(128), bias_grad.reshape(128), weight_grad)
 

time: 81.4 us -> 77 us (0.946); the launches traced: 80.1 us -> 76.7 us
  blocking collectives: 31.1 us -> 46.2 us
  waiting for transfers between devices: 11.1 us -> 3.42 us
  starting transfers between devices: 22.9 us -> 16 us
  Pallas kernels: 14.1 us -> 10.2 us
    all_to_all x0 -> x1, blocking collectives: none -> 14.8 us  [local(): shares = lax.all_to_all(share, 'rows', 0, 0).astype(F32)]
    ppermute x3 -> x0, waiting for transfers between devices: 7.85 us -> none  [local(): lax.ppermute(half, 'rows', [(i, i ^ bits) for i in range(n_rows)])]
    ppermute x3 -> x0, starting transfers between devices: 5.26 us -> none  [local(): lax.ppermute(half, 'rows', [(i, i ^ bits) for i in range(n_rows)])]
    pallas_call x12 -> x14, Pallas kernels: 14.1 us -> 10.2 us  [call(): pl.pallas_call(body, out_shape=outs, in_specs=specs or [VMEM] * len(args)...]
    ppermute x1, starting transfers between devices: 4.75 us -> 3.05 us  [local(): other = lax.ppermute(half, 'sect', swap)]
  transfers between devices with their start and end apart: 10 -> 7, of which waited for: 6 -> 4; matrix products, arithmetic and copies ran while one was open for 0% -> 0% of each run, Pallas kernels for 7% -> 8%
where the time goes in v5:
time: 77 us; the launch traced here: 76.7 us
  blocking collectives  46.2 us (60%)
  starting transfers between devices  16 us (21%)
  Pallas kernels  10.2 us (13%)
  waiting for transfers between devices  3.42 us (4%)
    all_to_all x1, blocking collectives, local(): lax.all_to_all(stat[:, None], ('tm', 'rows'), 0, 0, axis_index_groups=gro...  18 us
    all_to_all x1, blocking collectives, local(): shares = lax.all_to_all(share, 'rows', 0, 0).astype(F32)  14.8 us
    all_to_all x1, blocking collectives, local(): gathered = lax.all_to_all(sent, 'tm', 0, 0)  13.4 us
    pallas_call x14, Pallas kernels, call(): pl.pallas_call(body, out_shape=outs, in_specs=specs or [VMEM] * len(args)...  10.2 us
    ppermute x1, starting transfers between devices, local(): farther = lax.ppermute(message, 'rows', far)  4.16 us
    ppermute x1, starting transfers between devices, local(): arrived = lax.ppermute(away, 'sect', swap)  3.93 us
    ppermute x1, starting transfers between devices, local(): side = lax.ppermute(facing, 'sect', swap)  3.33 us
    ppermute x1, starting transfers between devices, local(): other = lax.ppermute(half, 'sect', swap)  3.05 us
  transfers between devices with their start and end apart: 7, of which 4 were waited for; matrix products, arithmetic and copies ran while one was open for 0% of the time, Pallas kernels for 8%

profile of v5, /device:TPU:1, one launch (start us, length us, event | category | flops | bytes accessed | tf_op | source)
XLA Modules:
  0.0 76.7 jit_solution(15300947487790503004)
XLA Ops:
  0.6 1.3 %shard_map.84 = (bf16[4,8,32,128]{3,2,1,0:T(8,128)(2,1)S(1)}, bf16[4,8,32,128]{3,2,1,0:T(8,128)(2,1)S(1)}, bf16[528,128]{1,0:T(8,128)(2,1)S(1)}, f32[8,128]{1,0:T(8,128)S(1)}) custom-call(bf16[4,8,32,128]{3,2,1,0:T(8,128)(2,1)} %x_hbm.1, bf16[4,8,32,128]{3,2,1,0:T(8,128)(2,1)} %up_hbm.1), custom_call_target="tpu_custom_call" | custom-call | bytes 1187840 | tf_op jit(solution)/shard_map/pallas_call | solution.py:27
  1.9 3.3 %collective-permute-start = (bf16[528,128]{1,0:T(8,128)(2,1)S(1)}, bf16[528,128]{1,0:T(8,128)(2,1)S(1)}, u32[]{:S(2)}, u32[]{:S(2)}) collective-permute-start(bf16[528,128]{1,0:T(8,128)(2,1)S(1)} %get-tuple-element.33), channel_id=1, source_target_pairs={{0,1},{1,0},{2,3},{3,2},{4,5},{5,4},{6,7},{7,6},{8,9},{9,8},{10,11... | collective-permute-start | bytes 405512 | tf_op jit(solution)/shard_map/ppermute | solution.py:418
  5.3 1.0 %collective-permute-done.side_ref = bf16[528,128]{1,0:T(8,128)(2,1)S(1)} collective-permute-done((bf16[528,128]{1,0:T(8,128)(2,1)S(1)}, bf16[528,128]{1,0:T(8,128)(2,1)S(1)}, u32[]{:S(2)}, u32[]{:S(2)}) %collective-permute-start) | collective-permute-done | bytes 135200 | tf_op jit(solution)/shard_map/ppermute | solution.py:418
  6.3 0.1 collective-permute-start.1
  6.4 2.5 %shard_map.86 = (bf16[8,256,1152]{2,1,0:T(8,128)(2,1)S(1)}, f32[1024,128]{1,0:T(8,128)S(1)}, bf16[3,128,1152]{2,1,0:T(8,128)(2,1)S(1)}) custom-call(bf16[4,8,32,128]{3,2,1,0:T(8,128)(2,1)S(1)} %get-tuple-element.32.up_ref, bf16[528,128]{1,0:T(8,128)(2,1)S(1)} %collective-permute-done.side_ref, bf16[3,3,3,128,128]{4,3,2,1,0:T(8,128)(2,1)} %kernel_hbm.1), custom_call_target="tpu_custom_call" | custom-call | flops 452984832 | bytes 7409664 | tf_op jit(solution)/shard_map/pallas_call | solution.py:27
  8.9 0.5 collective-permute-done.1.near_ref
  9.4 4.2 %collective-permute-start.2 = (bf16[208,128]{1,0:T(8,128)(2,1)S(1)}, bf16[208,128]{1,0:T(8,128)(2,1)S(1)}, u32[]{:S(2)}, u32[]{:S(2)}) collective-permute-start(bf16[208,128]{1,0:T(8,128)(2,1)S(1)} %get-tuple-element.39), channel_id=1, source_target_pairs={{0,14},{2,4},{4,2},{6,8},{8,6},{10,12},{12,10},{14,0},{1,15},{3,5}... | collective-permute-start | bytes 159752 | tf_op jit(solution)/shard_map/ppermute | solution.py:445
  13.6 1.5 %collective-permute-done.2.far_ref = bf16[208,128]{1,0:T(8,128)(2,1)S(1)} collective-permute-done((bf16[208,128]{1,0:T(8,128)(2,1)S(1)}, bf16[208,128]{1,0:T(8,128)(2,1)S(1)}, u32[]{:S(2)}, u32[]{:S(2)}) %collective-permute-start.2) | collective-permute-done | bytes 53280 | tf_op jit(solution)/shard_map/ppermute | solution.py:445
  15.1 1.3 %collective-permute-start.3 = (bf16[2,10,48,128]{3,2,1,0:T(8,128)(2,1)S(1)}, bf16[2,10,48,128]{3,2,1,0:T(8,128)(2,1)S(1)}, u32[]{:S(2)}, u32[]{:S(2)}) collective-permute-start(bf16[2,10,48,128]{3,2,1,0:T(8,128)(2,1)S(1)} %get-tuple-element.42), channel_id=1, source_target_pairs={{16,0},{32,16},{48,32},{64,48},{80,64},{96,80},{112,96},{128,112},... | collective-permute-start | bytes 737288 | tf_op jit(solution)/shard_map/ppermute | solution.py:454
  16.4 18.0 %all_to_all.15 = f32[32,1,128]{2,1,0:T(1,128)S(1)} all-to-all(f32[32,1,128]{2,1,0:T(1,128)S(1)} %bitcast.12), channel_id=1, replica_groups={{0,6,16,22,32,38,48,54,64,70,80,86,96,102,112,118,128,134,144,150,160,1..., dimensions={0} | all-to-all | bytes 32768 | tf_op jit(solution)/shard_map/all_to_all | solution.py:455
  34.4 0.0 collective-permute-done.3.later_ref
  34.4 0.0 copy-start
  34.4 0.0 copy-start.1
  34.4 0.5 shard_map.89.v_ref
  34.9 0.1 copy-done
  35.0 0.0 copy-done.1
  35.1 1.2 %shard_map.90 = (f32[16,14,8,128]{3,2,1,0:T(8,128)S(1)}, bf16[128,1024]{1,0:T(8,128)(2,1)S(1)}, f32[16,128]{1,0:T(8,128)S(1)}) custom-call(bf16[4,8,32,128]{3,2,1,0:T(8,128)(2,1)S(1)} %get-tuple-element.31.x_ref, f32[32,128]{1,0:T(8,128)S(1)} %bitcast.11, f32[1,128]{1,0:T(1,128)S(1)} %bitcast.13, f32[1,128]{1,0:T(1,128)S(1)} %bitcast.16, ...), custom_call_target="tpu_custom_call" | custom-call | flops 452984832 | bytes 6185984 | tf_op jit(solution)/shard_map/pallas_call | solution.py:27
  36.2 3.9 %collective-permute-start.4 = (f32[16,14,8,128]{3,2,1,0:T(8,128)S(1)}, f32[16,14,8,128]{3,2,1,0:T(8,128)S(1)}, u32[]{:S(2)}, u32[]{:S(2)}) collective-permute-start(f32[16,14,8,128]{3,2,1,0:T(8,128)S(1)} %get-tuple-element.51), channel_id=1, source_target_pairs={{0,1},{1,0},{2,3},{3,2},{4,5},{5,4},{6,7},{7,6},{8,9},{9,8},{10,11... | collective-permute-start | bytes 2752520 | tf_op jit(solution)/shard_map/ppermute | solution.py:471
  40.2 1.8 %shard_map.91 = (f32[1024,128]{1,0:T(8,128)S(1)}, f32[8,128]{1,0:T(8,128)S(1)}) custom-call(bf16[4,8,32,128]{3,2,1,0:T(8,128)(2,1)S(1)} %get-tuple-element.31.x_ref, f32[16,128]{1,0:T(8,128)S(1)} %get-tuple-element.46.norm_ref, f32[1,128]{1,0:T(1,128)S(1)} %bitcast.14, f32[1,128]{1,0:T(1,128)S(1)} %bitcast.17, ...), custom_call_target="tpu_custom_call" | custom-call | flops 452984832 | bytes 6927360 | tf_op jit(solution)/shard_map/pallas_call | solution.py:27
  42.0 0.1 collective-permute-start.5
  42.1 0.7 shard_map.92.own_ref
  42.8 0.4 collective-permute-done.5.other_sums_ref
  43.2 0.0 collective-permute-done.4.other_ref
  43.2 0.2 shard_map.93
  43.4 13.4 %all_to_all.16.in_ref = bf16[16,120,128]{2,1,0:T(8,128)(2,1)S(1)} all-to-all(bf16[16,120,128]{2,1,0:T(8,128)(2,1)S(1)} %shard_map.93), channel_id=1, replica_groups=mesh['tm'=16,'rows'=8,'sect'=2] {'tm'}, dimensions={0} | all-to-all | bytes 983040 | tf_op jit(solution)/shard_map/all_to_all | solution.py:489
  56.8 0.2 shard_map.94
  57.1 14.8 %all_to_all.17 = f16[8,120,128]{2,1,0:T(8,128)(2,1)S(1)} all-to-all(f16[8,120,128]{2,1,0:T(8,128)(2,1)S(1)} %broadcast_in_dim.10), channel_id=1, replica_groups=mesh['tm'=16,'rows'=8,'sect'=2] {'rows'}, dimensions={0} | all-to-all | bytes 491520 | tf_op jit(solution)/shard_map/all_to_all | solution.py:492
  72.0 3.0 %collective-permute-start.6 = (f32[112,128]{1,0:T(8,128)S(1)}, f32[112,128]{1,0:T(8,128)S(1)}, u32[]{:S(2)}, u32[]{:S(2)}) collective-permute-start(f32[112,128]{1,0:T(8,128)S(1)} %get-tuple-element.57.half_ref), channel_id=1, source_target_pairs={{0,1},{1,0},{2,3},{3,2},{4,5},{5,4},{6,7},{7,6},{8,9},{9,8},{10,11... | collective-permute-start | bytes 172040 | tf_op jit(solution)/shard_map/ppermute | solution.py:498
  75.0 1.0 %shard_map.96 = (bf16[4,8,32,128]{3,2,1,0:T(8,128)(2,1)}, f32[1,128]{1,0:T(1,128)}, f32[1,128]{1,0:T(1,128)}) custom-call(bf16[4,8,32,128]{3,2,1,0:T(8,128)(2,1)S(1)} %get-tuple-element.31.x_ref, f32[1024,128]{1,0:T(8,128)S(1)} %get-tuple-element.49.da_ref, f32[16,128]{1,0:T(8,128)S(1)} %get-tuple-element.46.norm_ref, ...), custom_call_target="tpu_custom_call" | custom-call | bytes 1062400 | tf_op jit(solution)/shard_map/pallas_call | solution.py:27
  76.0 0.0 collective-permute-done.6.other_ref
  76.0 0.7 shard_map.97
  (7 shorter events, 0.2 us)
Async XLA Ops:
  1.9 4.3 %collective-permute-start = (bf16[528,128]{1,0:T(8,128)(2,1)S(1)}, bf16[528,128]{1,0:T(8,128)(2,1)S(1)}, u32[]{:S(2)}, u32[]{:S(2)}) collective-permute-start(bf16[528,128]{1,0:T(8,128)(2,1)S(1)} %get-tuple-element.33), channel_id=1, source_target_pairs={{0,1},{1,0},{2,3},{3,2},{4,5},{5,4},{6,7},{7,6},{8,9},{9,8},{10,11... | collective-permute-start | bytes 405512 | tf_op jit(solution)/shard_map/ppermute | solution.py:418
  6.3 3.1 %collective-permute-start.1 = (bf16[208,128]{1,0:T(8,128)(2,1)S(1)}, bf16[208,128]{1,0:T(8,128)(2,1)S(1)}, u32[]{:S(2)}, u32[]{:S(2)}) collective-permute-start(bf16[208,128]{1,0:T(8,128)(2,1)S(1)} %get-tuple-element.35), channel_id=1, source_target_pairs={{0,2},{2,0},{4,6},{6,4},{8,10},{10,8},{12,14},{14,12},{1,3},{3,1},... | collective-permute-start | bytes 159752 | tf_op jit(solution)/shard_map/ppermute | solution.py:425
  9.4 5.7 %collective-permute-start.2 = (bf16[208,128]{1,0:T(8,128)(2,1)S(1)}, bf16[208,128]{1,0:T(8,128)(2,1)S(1)}, u32[]{:S(2)}, u32[]{:S(2)}) collective-permute-start(bf16[208,128]{1,0:T(8,128)(2,1)S(1)} %get-tuple-element.39), channel_id=1, source_target_pairs={{0,14},{2,4},{4,2},{6,8},{8,6},{10,12},{12,10},{14,0},{1,15},{3,5}... | collective-permute-start | bytes 159752 | tf_op jit(solution)/shard_map/ppermute | solution.py:445
  15.1 19.3 %collective-permute-start.3 = (bf16[2,10,48,128]{3,2,1,0:T(8,128)(2,1)S(1)}, bf16[2,10,48,128]{3,2,1,0:T(8,128)(2,1)S(1)}, u32[]{:S(2)}, u32[]{:S(2)}) collective-permute-start(bf16[2,10,48,128]{3,2,1,0:T(8,128)(2,1)S(1)} %get-tuple-element.42), channel_id=1, source_target_pairs={{16,0},{32,16},{48,32},{64,48},{80,64},{96,80},{112,96},{128,112},... | collective-permute-start | bytes 737288 | tf_op jit(solution)/shard_map/ppermute | solution.py:454
  34.4 0.7 copy-start
  34.4 0.7 copy-start.1
  36.2 7.0 %collective-permute-start.4 = (f32[16,14,8,128]{3,2,1,0:T(8,128)S(1)}, f32[16,14,8,128]{3,2,1,0:T(8,128)S(1)}, u32[]{:S(2)}, u32[]{:S(2)}) collective-permute-start(f32[16,14,8,128]{3,2,1,0:T(8,128)S(1)} %get-tuple-element.51), channel_id=1, source_target_pairs={{0,1},{1,0},{2,3},{3,2},{4,5},{5,4},{6,7},{7,6},{8,9},{9,8},{10,11... | collective-permute-start | bytes 2752520 | tf_op jit(solution)/shard_map/ppermute | solution.py:471
  42.0 1.3 %collective-permute-start.5 = (f32[8,128]{1,0:T(8,128)S(1)}, f32[8,128]{1,0:T(8,128)S(1)}, u32[]{:S(2)}, u32[]{:S(2)}) collective-permute-start(f32[8,128]{1,0:T(8,128)S(1)} %get-tuple-element.52.sums_ref), channel_id=1, source_target_pairs={{0,1},{1,0},{2,3},{3,2},{4,5},{5,4},{6,7},{7,6},{8,9},{9,8},{10,11... | collective-permute-start | bytes 12296 | tf_op jit(solution)/shard_map/ppermute | solution.py:479
  72.0 4.1 %collective-permute-start.6 = (f32[112,128]{1,0:T(8,128)S(1)}, f32[112,128]{1,0:T(8,128)S(1)}, u32[]{:S(2)}, u32[]{:S(2)}) collective-permute-start(f32[112,128]{1,0:T(8,128)S(1)} %get-tuple-element.57.half_ref), channel_id=1, source_target_pairs={{0,1},{1,0},{2,3},{3,2},{4,5},{5,4},{6,7},{7,6},{8,9},{9,8},{10,11... | collective-permute-start | bytes 172040 | tf_op jit(solution)/shard_map/ppermute | solution.py:498

commit v6 on v5

--- a/solution.py
+++ b/solution.py
@@ -22,13 +22,13 @@
     return pltpu.with_memory_space_constraint(x, space)
 
 
-def call(body, outs, args, specs=None, scratch=(), flops=0, aliases=None):
+def call(body, outs, args, specs=None, scratch=(), flops=0, aliases=None, out_specs=None):
     moved = sum(math.prod(x.shape) * jnp.dtype(x.dtype).itemsize for x in list(args) + list(outs))
     return pl.pallas_call(
         body,
         out_shape=outs,
         in_specs=specs or [VMEM] * len(args),
-        out_specs=[VMEM] * len(outs),
+        out_specs=out_specs or [VMEM] * len(outs),
         scratch_shapes=list(scratch),
         input_output_aliases=aliases or {},
         cost_estimate=pl.CostEstimate(flops=flops, bytes_accessed=moved, transcendentals=0),
@@ -69,37 +69,37 @@
     return jnp.broadcast_to(parts[0:1] + parts[1:2] + parts[2:3], (8, 128))
 
 
-def entry_kernel(x_hbm, up_hbm, x_ref, up_ref, facing_ref, stat_ref, x_sem, up_sem):
-    up_copy = pltpu.make_async_copy(up_hbm, up_ref, up_sem)
-    x_copy = pltpu.make_async_copy(x_hbm, x_ref, x_sem)
-    x_copy.start()
-    up_copy.start()
-    x_copy.wait()
+def entry_kernel(up_hbm, x_hbm, gain_hbm, bias_hbm, up_ref, x_ref, gain_ref, bias_ref, facing_ref, sems):
+    pairs = ((up_hbm, up_ref), (x_hbm, x_ref), (gain_hbm, gain_ref), (bias_hbm, bias_ref))
+    copies = [pltpu.make_async_copy(source, target, sems.at[i]) for i, (source, target) in enumerate(pairs)]
+    for copy in copies:
+        copy.start()
+    copies[0].wait()
+    left = lax.axis_index("sect") == 0
+    up = up_ref[...]
+    facing_ref[...] = jnp.where(left, up[:, :, 16:], up[:, :, :16]).reshape(512, 128)
+    for copy in copies[1:]:
+        copy.wait()
+
+
+def stats_kernel(x_ref, stat_ref):
     x = x_ref[...].astype(F32).reshape(-1, 128)
     total = group_total(column_sum(x))
     square = group_total(column_sum(x * x))
-    row = jnp.where(lanes_of(total.shape) % 4 < 2, total, square)
-    stat_ref[...] = row
-    facing_ref[512:] = split_row(row)
-    up_copy.wait()
-    left = lax.axis_index("sect") == 0
-    up = up_ref[...]
-    facing_ref[:512] = jnp.where(left, up[:, :, 16:], up[:, :, :16]).reshape(512, 128)
+    stat_ref[...] = jnp.where(lanes_of(total.shape) % 4 < 2, total, square)
 
 
 def edge_of(up_ref, side_ref, bottom):
-    side = side_ref[:512].reshape(4, 8, 16, 128)
+    side = side_ref[...].reshape(4, 8, 16, 128)
     low = jnp.concatenate([up_ref[:, 7], side[:, 7]], axis=1)
     top = jnp.concatenate([up_ref[:, 0], side[:, 0]], axis=1)
     return jnp.where(bottom, low, top).reshape(192, 128)
 
 
-def first_edge_kernel(up_ref, side_ref, stat_ref, out_ref, sum_ref):
+def first_edge_kernel(up_ref, side_ref, stat_ref, out_ref):
     even = lax.axis_index("rows") % 2 == 0
-    row = stat_ref[...] + join_row(side_ref[512:])
-    sum_ref[...] = row
     out_ref[:192] = edge_of(up_ref, side_ref, even)
-    out_ref[192:] = split_row(row)
+    out_ref[192:] = split_row(stat_ref[...])
 
 
 def second_edge_kernel(up_ref, side_ref, near_ref, stat_ref, out_ref, sum_ref):
@@ -365,19 +365,25 @@
     sums_ref[...] = sums
 
 
-def finish_kernel(counted, scaling, x_ref, da_ref, norm_ref, sums_ref, gain_ref, out_ref, gain_grad_ref, bias_grad_ref):
+def finish_kernel(counted, scaling, x_ref, da_ref, norm_ref, sums_ref, gain_ref, out_hbm, gain_grad_ref, bias_grad_ref, out_ref, sems):
     gain = gain_ref[...]
-    mean = norm_ref[0:1]
-    rstd = norm_ref[8:9]
     sums = sums_ref[...]
     bias_grad_ref[...] = sums[0:1] * scaling
     gain_grad_ref[...] = sums[1:2] * scaling
     averages = group_total(gain * sums) / counted
+    mean = norm_ref[0:1]
+    rstd = norm_ref[8:9]
     leading = averages[0:1]
     trailing = averages[1:2]
-    xhat = (x_ref[...].astype(F32).reshape(-1, 128) - mean) * rstd
-    grad = rstd * (da_ref[...] * gain - leading - xhat * trailing)
-    out_ref[...] = grad.astype(BF16).reshape(out_ref.shape)
+    copies = []
+    for f in range(4):
+        xhat = (x_ref[f].astype(F32).reshape(256, 128) - mean) * rstd
+        grad = rstd * (da_ref[f * 256 : (f + 1) * 256] * gain - leading - xhat * trailing)
+        out_ref[f] = grad.astype(BF16).reshape(8, 32, 128)
+        copies.append(pltpu.make_async_copy(out_ref.at[f], out_hbm.at[f], sems.at[f]))
+        copies[-1].start()
+    for copy in copies:
+        copy.wait()
 
 
 def join_kernel(half_ref, other_ref, out_ref):
@@ -403,25 +409,27 @@
     near = [(i, i ^ 1) for i in range(n_rows)]
     far = [(i, (i - 1) % n_rows if i % 2 == 0 else (i + 1) % n_rows) for i in range(n_rows)]
 
-    x, up, facing, stat = call(
+    up, x, gain, bias, facing = call(
         entry_kernel,
         [
+            shape_of(upstream.shape, BF16),
             shape_of(activations.shape, BF16),
-            shape_of(upstream.shape, BF16),
-            shape_of((528, channels), BF16),
-            shape_of((8, channels)),
+            shape_of((1, channels)),
+            shape_of((1, channels)),
+            shape_of((512, channels), BF16),
         ],
-        [held(activations, pltpu.HBM), held(upstream, pltpu.HBM)],
-        [HBM, HBM],
-        [pltpu.SemaphoreType.DMA, pltpu.SemaphoreType.DMA],
+        [
+            held(upstream, pltpu.HBM),
+            held(activations, pltpu.HBM),
+            held(group_norm_gain.reshape(1, channels), pltpu.HBM),
+            held(group_norm_bias.reshape(1, channels), pltpu.HBM),
+        ],
+        [HBM] * 4,
+        [pltpu.SemaphoreType.DMA((4,))],
     )
     side = lax.ppermute(facing, "sect", swap)
-    message, stat = call(
-        first_edge_kernel,
-        [shape_of((208, channels), BF16), shape_of((8, channels))],
-        [up, side, stat],
-        [VMEM, VMEM, VMEM],
-    )
+    (stat,) = call(stats_kernel, [shape_of((8, channels))], [x])
+    (message,) = call(first_edge_kernel, [shape_of((208, channels), BF16)], [up, side, stat])
     nearer = lax.ppermute(message, "rows", near)
     spread, inner, taps = call(
         own_kernel,
@@ -444,7 +452,10 @@
     )
     farther = lax.ppermute(message, "rows", far)
     pairs = [(0, 3), (1, 6), (2, 5), (4, 7)]
-    groups = [[t * n_rows + r for t in range(n_time) for r in pair] for pair in pairs]
+    groups = [
+        [(t * n_rows + r) * n_sect + c for t in range(n_time) for r in pair for c in range(n_sect)]
+        for pair in pairs
+    ]
     early, stat = call(
         early_kernel,
         [shape_of((2, 10, 48, channels), BF16), shape_of((len(groups[0]), channels))],
@@ -452,7 +463,7 @@
         [VMEM, VMEM, VMEM, VMEM, VMEM],
     )
     later = lax.ppermute(early, "tm", [(i + 1, i) for i in range(n_time - 1)])
-    stat = lax.all_to_all(stat[:, None], ("tm", "rows"), 0, 0, axis_index_groups=groups).reshape(-1, channels)
+    stat = lax.all_to_all(stat[:, None], ("tm", "rows", "sect"), 0, 0, axis_index_groups=groups).reshape(-1, channels)
     stat, later = lax.optimization_barrier((stat, later))
     (spread,) = call(
         spread_kernel,
@@ -460,8 +471,6 @@
         [nearer, farther, later, held(spread, pltpu.VMEM)],
         aliases={3: 0},
     )
-    gain = group_norm_gain.reshape(1, channels)
-    bias = group_norm_bias.reshape(1, channels)
     away, turned, norm = call(
         functools.partial(away_kernel, counted),
         [shape_of((16, HALF, 8, 128)), shape_of((channels, cells), BF16), shape_of((16, channels))],
@@ -500,6 +509,8 @@
         functools.partial(finish_kernel, counted, scaling),
         [shape_of(activations.shape, BF16), shape_of((1, 128)), shape_of((1, 128))],
         [x, da, norm, sums, gain],
+        scratch=[pltpu.VMEM(activations.shape, BF16), pltpu.SemaphoreType.DMA((4,))],
+        out_specs=[HBM, VMEM, VMEM],
     )
     (whole,) = call(join_kernel, [shape_of((TAPS * 8, 128))], [half, other])
     weight_grad = whole.reshape(3, 3, 3, 8, 128).transpose(0, 1, 2, 4, 3)

time: 77 us -> 77.5 us (level)
  blocking collectives: 46.2 us -> 49.8 us
  starting transfers between devices: 16 us -> 12.8 us
    all_to_all x1, blocking collectives: 18 us -> 21.6 us  [local(): lax.all_to_all(stat[:, None], ('tm', 'rows', 'sect'), 0, 0, axis_index_gr...]
    ppermute x1, starting transfers between devices: 3.93 us -> 0.76 us  [local(): arrived = lax.ppermute(away, 'sect', swap)]
    pallas_call x14 -> x15, Pallas kernels: 10.2 us -> 10.6 us  [call(): pl.pallas_call(body, out_shape=outs, in_specs=specs or [VMEM] * len(args)...]
  transfers between devices with their start and end apart: 7 -> 7, of which waited for: 4 -> 4; matrix products, arithmetic and copies ran while one was open for 0% -> 0% of each run, Pallas kernels for 8% -> 9%
where the time goes in v6:
time: 77.5 us; the launch traced here: 77.2 us
  blocking collectives  49.8 us (64%)
  starting transfers between devices  12.8 us (17%)
  Pallas kernels  10.6 us (14%)
  waiting for transfers between devices  3.13 us (4%)
    all_to_all x1, blocking collectives, local(): lax.all_to_all(stat[:, None], ('tm', 'rows', 'sect'), 0, 0, axis_index_gr...  21.6 us
    all_to_all x1, blocking collectives, local(): shares = lax.all_to_all(share, 'rows', 0, 0).astype(F32)  14.8 us
    all_to_all x1, blocking collectives, local(): gathered = lax.all_to_all(sent, 'tm', 0, 0)  13.5 us
    pallas_call x15, Pallas kernels, call(): pl.pallas_call(body, out_shape=outs, in_specs=specs or [VMEM] * len(args)...  10.6 us
    ppermute x1, starting transfers between devices, local(): farther = lax.ppermute(message, 'rows', far)  4.16 us
    ppermute x1, starting transfers between devices, local(): side = lax.ppermute(facing, 'sect', swap)  3.33 us
    ppermute x1, starting transfers between devices, local(): other = lax.ppermute(half, 'sect', swap)  3.04 us
  transfers between devices with their start and end apart: 7, of which 4 were waited for; matrix products, arithmetic and copies ran while one was open for 0% of the time, Pallas kernels for 9%

profile of v6, /device:TPU:1, one launch (start us, length us, event | category | flops | bytes accessed | tf_op | source)
XLA Modules:
  0.0 77.2 jit_solution(18008988693302068620)
XLA Ops:
  0.6 1.1 %shard_map.84 = (bf16[4,8,32,128]{3,2,1,0:T(8,128)(2,1)S(1)}, bf16[4,8,32,128]{3,2,1,0:T(8,128)(2,1)S(1)}, f32[1,128]{1,0:T(1,128)S(1)}, f32[1,128]{1,0:T(1,128)S(1)}, bf16[512,128]{1,0:T(8,128)(2,1)S(1)}) custom-call(bf16[4,8,32,128]{3,2,1,0:T(8,128)(2,1)} %up_hbm.1, bf16[4,8,32,128]{3,2,1,0:T(8,128)(2,1)} %x_hbm.1, f32[1,128]{1,0:T(1,128)} %bitcast.14, ...), custom_call_target="tpu_custom_call" | custom-call | bytes 1181696 | tf_op jit(solution)/shard_map/pallas_call | solution.py:27
  1.7 3.3 %collective-permute-start = (bf16[512,128]{1,0:T(8,128)(2,1)S(1)}, bf16[512,128]{1,0:T(8,128)(2,1)S(1)}, u32[]{:S(2)}, u32[]{:S(2)}) collective-permute-start(bf16[512,128]{1,0:T(8,128)(2,1)S(1)} %get-tuple-element.32), channel_id=1, source_target_pairs={{0,1},{1,0},{2,3},{3,2},{4,5},{5,4},{6,7},{7,6},{8,9},{9,8},{10,11... | collective-permute-start | bytes 393224 | tf_op jit(solution)/shard_map/ppermute | solution.py:430
  5.0 0.3 shard_map.85.stat_ref
  5.3 0.7 collective-permute-done.side_ref
  6.0 0.1 collective-permute-start.1
  6.1 2.5 %shard_map.87 = (bf16[8,256,1152]{2,1,0:T(8,128)(2,1)S(1)}, f32[1024,128]{1,0:T(8,128)S(1)}, bf16[3,128,1152]{2,1,0:T(8,128)(2,1)S(1)}) custom-call(bf16[4,8,32,128]{3,2,1,0:T(8,128)(2,1)S(1)} %get-tuple-element.31.up_ref, bf16[512,128]{1,0:T(8,128)(2,1)S(1)} %collective-permute-done.side_ref, bf16[3,3,3,128,128]{4,3,2,1,0:T(8,128)(2,1)} %kernel_hbm.1), custom_call_target="tpu_custom_call" | custom-call | flops 452984832 | bytes 7405568 | tf_op jit(solution)/shard_map/pallas_call | solution.py:27
  8.6 0.5 collective-permute-done.1.near_ref
  9.1 4.2 %collective-permute-start.2 = (bf16[208,128]{1,0:T(8,128)(2,1)S(1)}, bf16[208,128]{1,0:T(8,128)(2,1)S(1)}, u32[]{:S(2)}, u32[]{:S(2)}) collective-permute-start(bf16[208,128]{1,0:T(8,128)(2,1)S(1)} %get-tuple-element.35), channel_id=1, source_target_pairs={{0,14},{2,4},{4,2},{6,8},{8,6},{10,12},{12,10},{14,0},{1,15},{3,5}... | collective-permute-start | bytes 159752 | tf_op jit(solution)/shard_map/ppermute | solution.py:453
  13.3 1.5 %collective-permute-done.2.far_ref = bf16[208,128]{1,0:T(8,128)(2,1)S(1)} collective-permute-done((bf16[208,128]{1,0:T(8,128)(2,1)S(1)}, bf16[208,128]{1,0:T(8,128)(2,1)S(1)}, u32[]{:S(2)}, u32[]{:S(2)}) %collective-permute-start.2) | collective-permute-done | bytes 53280 | tf_op jit(solution)/shard_map/ppermute | solution.py:453
  14.9 1.3 %collective-permute-start.3 = (bf16[2,10,48,128]{3,2,1,0:T(8,128)(2,1)S(1)}, bf16[2,10,48,128]{3,2,1,0:T(8,128)(2,1)S(1)}, u32[]{:S(2)}, u32[]{:S(2)}) collective-permute-start(bf16[2,10,48,128]{3,2,1,0:T(8,128)(2,1)S(1)} %get-tuple-element.38), channel_id=1, source_target_pairs={{16,0},{32,16},{48,32},{64,48},{80,64},{96,80},{112,96},{128,112},... | collective-permute-start | bytes 737288 | tf_op jit(solution)/shard_map/ppermute | solution.py:465
  16.2 21.6 %all_to_all.15 = f32[64,1,128]{2,1,0:T(1,128)S(1)} all-to-all(f32[64,1,128]{2,1,0:T(1,128)S(1)} %bitcast.12), channel_id=1, replica_groups={{0,1,6,7,16,17,22,23,32,33,38,39,48,49,54,55,64,65,70,71,80,81,86,87,96..., dimensions={0} | all-to-all | bytes 65536 | tf_op jit(solution)/shard_map/all_to_all | solution.py:466
  37.8 0.0 collective-permute-done.3.later_ref
  37.8 0.5 shard_map.90.v_ref
  38.3 1.2 %shard_map.91 = (f32[16,14,8,128]{3,2,1,0:T(8,128)S(1)}, bf16[128,1024]{1,0:T(8,128)(2,1)S(1)}, f32[16,128]{1,0:T(8,128)S(1)}) custom-call(bf16[4,8,32,128]{3,2,1,0:T(8,128)(2,1)S(1)} %get-tuple-element.30.x_ref, f32[64,128]{1,0:T(8,128)S(1)} %bitcast.11, f32[1,128]{1,0:T(1,128)S(1)} %get-tuple-element.40.gain_ref, f32[1,128]{1,0:T(1,128)S(1)} %get-tuple-element.41.bias_ref, ...), custom_call_target="tpu_custom_call" | custom-call | flops 452984832 | bytes 6202368 | tf_op jit(solution)/shard_map/pallas_call | solution.py:27
  39.5 0.8 collective-permute-start.4
  40.2 1.8 %shard_map.92 = (f32[1024,128]{1,0:T(8,128)S(1)}, f32[8,128]{1,0:T(8,128)S(1)}) custom-call(bf16[4,8,32,128]{3,2,1,0:T(8,128)(2,1)S(1)} %get-tuple-element.30.x_ref, f32[16,128]{1,0:T(8,128)S(1)} %get-tuple-element.44.norm_ref, f32[1,128]{1,0:T(1,128)S(1)} %get-tuple-element.40.gain_ref, f32[1,128]{1,0:T(1,128)S(1)} %get-tuple-element.41.bias_ref, ...), custom_call_target="tpu_custom_call" | custom-call | flops 452984832 | bytes 6927360 | tf_op jit(solution)/shard_map/pallas_call | solution.py:27
  42.0 0.1 collective-permute-start.5
  42.1 0.7 shard_map.93.own_ref
  42.9 0.4 collective-permute-done.5.other_sums_ref
  43.3 0.0 collective-permute-done.4.other_ref
  43.3 0.2 shard_map.94
  43.5 13.5 %all_to_all.16.in_ref = bf16[16,120,128]{2,1,0:T(8,128)(2,1)S(1)} all-to-all(bf16[16,120,128]{2,1,0:T(8,128)(2,1)S(1)} %shard_map.94), channel_id=1, replica_groups=mesh['tm'=16,'rows'=8,'sect'=2] {'tm'}, dimensions={0} | all-to-all | bytes 983040 | tf_op jit(solution)/shard_map/all_to_all | solution.py:498
  56.9 0.2 shard_map.95
  57.2 14.8 %all_to_all.17 = f16[8,120,128]{2,1,0:T(8,128)(2,1)S(1)} all-to-all(f16[8,120,128]{2,1,0:T(8,128)(2,1)S(1)} %broadcast_in_dim.10), channel_id=1, replica_groups=mesh['tm'=16,'rows'=8,'sect'=2] {'rows'}, dimensions={0} | all-to-all | bytes 491520 | tf_op jit(solution)/shard_map/all_to_all | solution.py:501
  72.1 3.0 %collective-permute-start.6 = (f32[112,128]{1,0:T(8,128)S(1)}, f32[112,128]{1,0:T(8,128)S(1)}, u32[]{:S(2)}, u32[]{:S(2)}) collective-permute-start(f32[112,128]{1,0:T(8,128)S(1)} %get-tuple-element.55.half_ref), channel_id=1, source_target_pairs={{0,1},{1,0},{2,3},{3,2},{4,5},{5,4},{6,7},{7,6},{8,9},{9,8},{10,11... | collective-permute-start | bytes 172040 | tf_op jit(solution)/shard_map/ppermute | solution.py:507
  75.1 1.4 %shard_map.97 = (bf16[4,8,32,128]{3,2,1,0:T(8,128)(2,1)}, f32[1,128]{1,0:T(1,128)}, f32[1,128]{1,0:T(1,128)}) custom-call(bf16[4,8,32,128]{3,2,1,0:T(8,128)(2,1)S(1)} %get-tuple-element.30.x_ref, f32[1024,128]{1,0:T(8,128)S(1)} %get-tuple-element.47.da_ref, f32[16,128]{1,0:T(8,128)S(1)} %get-tuple-element.44.norm_ref, ...), custom_call_target="tpu_custom_call" | custom-call | bytes 1062400 | tf_op jit(solution)/shard_map/pallas_call | solution.py:27
  76.5 0.0 collective-permute-done.6.other_ref
  76.5 0.7 shard_map.98
  (7 shorter events, 0.2 us)
Async XLA Ops:
  1.7 4.3 %collective-permute-start = (bf16[512,128]{1,0:T(8,128)(2,1)S(1)}, bf16[512,128]{1,0:T(8,128)(2,1)S(1)}, u32[]{:S(2)}, u32[]{:S(2)}) collective-permute-start(bf16[512,128]{1,0:T(8,128)(2,1)S(1)} %get-tuple-element.32), channel_id=1, source_target_pairs={{0,1},{1,0},{2,3},{3,2},{4,5},{5,4},{6,7},{7,6},{8,9},{9,8},{10,11... | collective-permute-start | bytes 393224 | tf_op jit(solution)/shard_map/ppermute | solution.py:430
  6.0 3.1 %collective-permute-start.1 = (bf16[208,128]{1,0:T(8,128)(2,1)S(1)}, bf16[208,128]{1,0:T(8,128)(2,1)S(1)}, u32[]{:S(2)}, u32[]{:S(2)}) collective-permute-start(bf16[208,128]{1,0:T(8,128)(2,1)S(1)} %shard_map.86), channel_id=1, source_target_pairs={{0,2},{2,0},{4,6},{6,4},{8,10},{10,8},{12,14},{14,12},{1,3},{3,1},... | collective-permute-start | bytes 159752 | tf_op jit(solution)/shard_map/ppermute | solution.py:433
  9.1 5.7 %collective-permute-start.2 = (bf16[208,128]{1,0:T(8,128)(2,1)S(1)}, bf16[208,128]{1,0:T(8,128)(2,1)S(1)}, u32[]{:S(2)}, u32[]{:S(2)}) collective-permute-start(bf16[208,128]{1,0:T(8,128)(2,1)S(1)} %get-tuple-element.35), channel_id=1, source_target_pairs={{0,14},{2,4},{4,2},{6,8},{8,6},{10,12},{12,10},{14,0},{1,15},{3,5}... | collective-permute-start | bytes 159752 | tf_op jit(solution)/shard_map/ppermute | solution.py:453
  14.9 22.9 %collective-permute-start.3 = (bf16[2,10,48,128]{3,2,1,0:T(8,128)(2,1)S(1)}, bf16[2,10,48,128]{3,2,1,0:T(8,128)(2,1)S(1)}, u32[]{:S(2)}, u32[]{:S(2)}) collective-permute-start(bf16[2,10,48,128]{3,2,1,0:T(8,128)(2,1)S(1)} %get-tuple-element.38), channel_id=1, source_target_pairs={{16,0},{32,16},{48,32},{64,48},{80,64},{96,80},{112,96},{128,112},... | collective-permute-start | bytes 737288 | tf_op jit(solution)/shard_map/ppermute | solution.py:465
  39.5 3.8 %collective-permute-start.4 = (f32[16,14,8,128]{3,2,1,0:T(8,128)S(1)}, f32[16,14,8,128]{3,2,1,0:T(8,128)S(1)}, u32[]{:S(2)}, u32[]{:S(2)}) collective-permute-start(f32[16,14,8,128]{3,2,1,0:T(8,128)S(1)} %get-tuple-element.49), channel_id=1, source_target_pairs={{0,1},{1,0},{2,3},{3,2},{4,5},{5,4},{6,7},{7,6},{8,9},{9,8},{10,11... | collective-permute-start | bytes 2752520 | tf_op jit(solution)/shard_map/ppermute | solution.py:480
  42.0 1.3 %collective-permute-start.5 = (f32[8,128]{1,0:T(8,128)S(1)}, f32[8,128]{1,0:T(8,128)S(1)}, u32[]{:S(2)}, u32[]{:S(2)}) collective-permute-start(f32[8,128]{1,0:T(8,128)S(1)} %get-tuple-element.50.sums_ref), channel_id=1, source_target_pairs={{0,1},{1,0},{2,3},{3,2},{4,5},{5,4},{6,7},{7,6},{8,9},{9,8},{10,11... | collective-permute-start | bytes 12296 | tf_op jit(solution)/shard_map/ppermute | solution.py:488
  72.1 4.5 %collective-permute-start.6 = (f32[112,128]{1,0:T(8,128)S(1)}, f32[112,128]{1,0:T(8,128)S(1)}, u32[]{:S(2)}, u32[]{:S(2)}) collective-permute-start(f32[112,128]{1,0:T(8,128)S(1)} %get-tuple-element.55.half_ref), channel_id=1, source_target_pairs={{0,1},{1,0},{2,3},{3,2},{4,5},{5,4},{6,7},{7,6},{8,9},{9,8},{10,11... | collective-permute-start | bytes 172040 | tf_op jit(solution)/shard_map/ppermute | solution.py:507

commit v7 on v5

--- a/solution.py
+++ b/solution.py
@@ -69,22 +69,23 @@
     return jnp.broadcast_to(parts[0:1] + parts[1:2] + parts[2:3], (8, 128))
 
 
-def entry_kernel(x_hbm, up_hbm, x_ref, up_ref, facing_ref, stat_ref, x_sem, up_sem):
-    up_copy = pltpu.make_async_copy(up_hbm, up_ref, up_sem)
-    x_copy = pltpu.make_async_copy(x_hbm, x_ref, x_sem)
-    x_copy.start()
-    up_copy.start()
-    x_copy.wait()
+def entry_kernel(up_hbm, x_hbm, gain_hbm, bias_hbm, up_ref, x_ref, gain_ref, bias_ref, facing_ref, stat_ref, sems):
+    pairs = ((up_hbm, up_ref), (x_hbm, x_ref), (gain_hbm, gain_ref), (bias_hbm, bias_ref))
+    copies = [pltpu.make_async_copy(source, target, sems.at[i]) for i, (source, target) in enumerate(pairs)]
+    for copy in copies:
+        copy.start()
+    copies[0].wait()
+    left = lax.axis_index("sect") == 0
+    up = up_ref[...]
+    facing_ref[:512] = jnp.where(left, up[:, :, 16:], up[:, :, :16]).reshape(512, 128)
+    for copy in copies[1:]:
+        copy.wait()
     x = x_ref[...].astype(F32).reshape(-1, 128)
     total = group_total(column_sum(x))
     square = group_total(column_sum(x * x))
     row = jnp.where(lanes_of(total.shape) % 4 < 2, total, square)
     stat_ref[...] = row
     facing_ref[512:] = split_row(row)
-    up_copy.wait()
-    left = lax.axis_index("sect") == 0
-    up = up_ref[...]
-    facing_ref[:512] = jnp.where(left, up[:, :, 16:], up[:, :, :16]).reshape(512, 128)
 
 
 def edge_of(up_ref, side_ref, bottom):
@@ -94,20 +95,13 @@
     return jnp.where(bottom, low, top).reshape(192, 128)
 
 
-def first_edge_kernel(up_ref, side_ref, stat_ref, out_ref, sum_ref):
+def edge_kernel(up_ref, side_ref, stat_ref, near_ref, far_ref, sum_ref):
     even = lax.axis_index("rows") % 2 == 0
     row = stat_ref[...] + join_row(side_ref[512:])
     sum_ref[...] = row
-    out_ref[:192] = edge_of(up_ref, side_ref, even)
-    out_ref[192:] = split_row(row)
-
-
-def second_edge_kernel(up_ref, side_ref, near_ref, stat_ref, out_ref, sum_ref):
-    even = lax.axis_index("rows") % 2 == 0
-    row = stat_ref[...] + join_row(near_ref[192:])
-    sum_ref[...] = row
-    out_ref[:192] = edge_of(up_ref, side_ref, jnp.logical_not(even))
-    out_ref[192:] = split_row(row)
+    near_ref[:192] = edge_of(up_ref, side_ref, even)
+    near_ref[192:] = split_row(row)
+    far_ref[...] = edge_of(up_ref, side_ref, jnp.logical_not(even))
 
 
 def beyond(near_ref, far_ref):
@@ -120,7 +114,7 @@
 
 
 def early_kernel(up_ref, side_ref, near_ref, far_ref, stat_ref, early_ref, sent_ref):
-    row = stat_ref[...] + join_row(far_ref[192:])
+    row = stat_ref[...] + join_row(near_ref[192:])
     sent_ref[...] = jnp.broadcast_to(row[None], (sent_ref.shape[0] // 8, 8, 128)).reshape(sent_ref.shape)
     above, below = beyond(near_ref, far_ref)
     early_ref[:, 0] = above[:2]
@@ -403,26 +397,33 @@
     near = [(i, i ^ 1) for i in range(n_rows)]
     far = [(i, (i - 1) % n_rows if i % 2 == 0 else (i + 1) % n_rows) for i in range(n_rows)]
 
-    x, up, facing, stat = call(
+    up, x, gain, bias, facing, stat = call(
         entry_kernel,
         [
+            shape_of(upstream.shape, BF16),
             shape_of(activations.shape, BF16),
-            shape_of(upstream.shape, BF16),
+            shape_of((1, channels)),
+            shape_of((1, channels)),
             shape_of((528, channels), BF16),
             shape_of((8, channels)),
         ],
-        [held(activations, pltpu.HBM), held(upstream, pltpu.HBM)],
-        [HBM, HBM],
-        [pltpu.SemaphoreType.DMA, pltpu.SemaphoreType.DMA],
+        [
+            held(upstream, pltpu.HBM),
+            held(activations, pltpu.HBM),
+            held(group_norm_gain.reshape(1, channels), pltpu.HBM),
+            held(group_norm_bias.reshape(1, channels), pltpu.HBM),
+        ],
+        [HBM] * 4,
+        [pltpu.SemaphoreType.DMA((4,))],
     )
     side = lax.ppermute(facing, "sect", swap)
-    message, stat = call(
-        first_edge_kernel,
-        [shape_of((208, channels), BF16), shape_of((8, channels))],
+    nearer, farther, stat = call(
+        edge_kernel,
+        [shape_of((208, channels), BF16), shape_of((192, channels), BF16), shape_of((8, channels))],
         [up, side, stat],
-        [VMEM, VMEM, VMEM],
-    )
-    nearer = lax.ppermute(message, "rows", near)
+    )
+    nearer = lax.ppermute(nearer, "rows", near)
+    farther = lax.ppermute(farther, "rows", far)
     spread, inner, taps = call(
         own_kernel,
         [
@@ -436,15 +437,7 @@
         flops=cells * TAPS * channels * channels,
     )
     nearer, inner = lax.optimization_barrier((nearer, inner))
-    message, stat = call(
-        second_edge_kernel,
-        [shape_of((208, channels), BF16), shape_of((8, channels))],
-        [up, side, nearer, stat],
-        [VMEM, VMEM, VMEM, VMEM],
-    )
-    farther = lax.ppermute(message, "rows", far)
-    pairs = [(0, 3), (1, 6), (2, 5), (4, 7)]
-    groups = [[t * n_rows + r for t in range(n_time) for r in pair] for pair in pairs]
+    groups = [[t * n_rows + r for t in range(n_time) for r in range(p, n_rows, 2)] for p in range(2)]
     early, stat = call(
         early_kernel,
         [shape_of((2, 10, 48, channels), BF16), shape_of((len(groups[0]), channels))],
@@ -460,8 +453,6 @@
         [nearer, farther, later, held(spread, pltpu.VMEM)],
         aliases={3: 0},
     )
-    gain = group_norm_gain.reshape(1, channels)
-    bias = group_norm_bias.reshape(1, channels)
     away, turned, norm = call(
         functools.partial(away_kernel, counted),
         [shape_of((16, HALF, 8, 128)), shape_of((channels, cells), BF16), shape_of((16, channels))],

time: 77 us -> 75.9 us (0.986)
  waiting for transfers between devices: 3.42 us -> 1.41 us
  blocking collectives: 46.2 us -> 47.5 us
    all_to_all x1, blocking collectives: 18 us -> 21.9 us  [local(): lax.all_to_all(stat[:, None], ('tm', 'rows'), 0, 0, axis_index_groups=gro...]
    all_to_all x1, blocking collectives: 14.8 us -> 12.1 us  [local(): shares = lax.all_to_all(share, 'rows', 0, 0).astype(F32)]
    ppermute x2, waiting for transfers between devices: 2.01 us -> 0.01 us  [the longest x1 0.01 us: local(): farther = lax.ppermute(farther, 'rows', far)]
    pallas_call x14 -> x13, Pallas kernels: 10.2 us -> 10.2 us  [call(): pl.pallas_call(body, out_shape=outs, in_specs=specs or [VMEM] * len(args)...]
  transfers between devices with their start and end apart: 7 -> 7, of which waited for: 4 -> 2; matrix products, arithmetic and copies ran while one was open for 0% -> 0% of each run, Pallas kernels for 8% -> 8%
where the time goes in v7:
time: 75.9 us; the launch traced here: 75.6 us
  blocking collectives  47.5 us (63%)
  starting transfers between devices  15.7 us (21%)
  Pallas kernels  10.2 us (13%)
  waiting for transfers between devices  1.41 us (2%)
    all_to_all x1, blocking collectives, local(): lax.all_to_all(stat[:, None], ('tm', 'rows'), 0, 0, axis_index_groups=gro...  21.9 us
    all_to_all x1, blocking collectives, local(): gathered = lax.all_to_all(sent, 'tm', 0, 0)  13.5 us
    all_to_all x1, blocking collectives, local(): shares = lax.all_to_all(share, 'rows', 0, 0).astype(F32)  12.1 us
    pallas_call x13, Pallas kernels, call(): pl.pallas_call(body, out_shape=outs, in_specs=specs or [VMEM] * len(args)...  10.2 us
    ppermute x1, starting transfers between devices, local(): farther = lax.ppermute(farther, 'rows', far)  4.55 us
    ppermute x1, starting transfers between devices, local(): arrived = lax.ppermute(away, 'sect', swap)  3.5 us
    ppermute x1, starting transfers between devices, local(): side = lax.ppermute(facing, 'sect', swap)  3.33 us
    ppermute x1, starting transfers between devices, local(): other = lax.ppermute(half, 'sect', swap)  2.83 us
  transfers between devices with their start and end apart: 7, of which 2 were waited for; matrix products, arithmetic and copies ran while one was open for 0% of the time, Pallas kernels for 8%

profile of v7, /device:TPU:1, one launch (start us, length us, event | category | flops | bytes accessed | tf_op | source)
XLA Modules:
  0.0 75.6 jit_solution(13942338393645384333)
XLA Ops:
  0.6 1.4 %shard_map.84 = (bf16[4,8,32,128]{3,2,1,0:T(8,128)(2,1)S(1)}, bf16[4,8,32,128]{3,2,1,0:T(8,128)(2,1)S(1)}, f32[1,128]{1,0:T(1,128)S(1)}, f32[1,128]{1,0:T(1,128)...) custom-call(bf16[4,8,32,128]{3,2,1,0:T(8,128)(2,1)} %up_hbm.1, bf16[4,8,32,128]{3,2,1,0:T(8,128)(2,1)} %x_hbm.1, ...), custom_call_target="tpu_custom_call" | custom-call | bytes 1189888 | tf_op jit(solution)/shard_map/pallas_call | solution.py:27
  2.0 3.3 %collective-permute-start = (bf16[528,128]{1,0:T(8,128)(2,1)S(1)}, bf16[528,128]{1,0:T(8,128)(2,1)S(1)}, u32[]{:S(2)}, u32[]{:S(2)}) collective-permute-start(bf16[528,128]{1,0:T(8,128)(2,1)S(1)} %get-tuple-element.34), channel_id=1, source_target_pairs={{0,1},{1,0},{2,3},{3,2},{4,5},{5,4},{6,7},{7,6},{8,9},{9,8},{10,11... | collective-permute-start | bytes 405512 | tf_op jit(solution)/shard_map/ppermute | solution.py:419
  5.3 1.0 %collective-permute-done.side_ref = bf16[528,128]{1,0:T(8,128)(2,1)S(1)} collective-permute-done((bf16[528,128]{1,0:T(8,128)(2,1)S(1)}, bf16[528,128]{1,0:T(8,128)(2,1)S(1)}, u32[]{:S(2)}, u32[]{:S(2)}) %collective-permute-start) | collective-permute-done | bytes 135200 | tf_op jit(solution)/shard_map/ppermute | solution.py:419
  6.4 0.1 collective-permute-start.1
  6.5 4.6 %collective-permute-start.2 = (bf16[192,128]{1,0:T(8,128)(2,1)S(1)}, bf16[192,128]{1,0:T(8,128)(2,1)S(1)}, u32[]{:S(2)}, u32[]{:S(2)}) collective-permute-start(bf16[192,128]{1,0:T(8,128)(2,1)S(1)} %get-tuple-element.39), channel_id=1, source_target_pairs={{0,14},{2,4},{4,2},{6,8},{8,6},{10,12},{12,10},{14,0},{1,15},{3,5}... | collective-permute-start | bytes 147464 | tf_op jit(solution)/shard_map/ppermute | solution.py:426
  11.0 2.5 %shard_map.86 = (bf16[8,256,1152]{2,1,0:T(8,128)(2,1)S(1)}, f32[1024,128]{1,0:T(8,128)S(1)}, bf16[3,128,1152]{2,1,0:T(8,128)(2,1)S(1)}) custom-call(bf16[4,8,32,128]{3,2,1,0:T(8,128)(2,1)S(1)} %get-tuple-element.33.up_ref, bf16[528,128]{1,0:T(8,128)(2,1)S(1)} %collective-permute-done.side_ref, bf16[3,3,3,128,128]{4,3,2,1,0:T(8,128)(2,1)} %kernel_hbm.1), custom_call_target="tpu_custom_call" | custom-call | flops 452984832 | bytes 7409664 | tf_op jit(solution)/shard_map/pallas_call | solution.py:27
  13.5 0.0 collective-permute-done.1.near_ref
  13.5 0.0 collective-permute-done.2.far_ref
  13.5 1.3 %collective-permute-start.3 = (bf16[2,10,48,128]{3,2,1,0:T(8,128)(2,1)S(1)}, bf16[2,10,48,128]{3,2,1,0:T(8,128)(2,1)S(1)}, u32[]{:S(2)}, u32[]{:S(2)}) collective-permute-start(bf16[2,10,48,128]{3,2,1,0:T(8,128)(2,1)S(1)} %get-tuple-element.42), channel_id=1, source_target_pairs={{16,0},{32,16},{48,32},{64,48},{80,64},{96,80},{112,96},{128,112},... | collective-permute-start | bytes 737288 | tf_op jit(solution)/shard_map/ppermute | solution.py:447
  14.8 21.9 %all_to_all.15 = f32[64,1,128]{2,1,0:T(1,128)S(1)} all-to-all(f32[64,1,128]{2,1,0:T(1,128)S(1)} %bitcast.12), channel_id=1, replica_groups={{0,4,8,12,16,20,24,28,32,36,40,44,48,52,56,60,64,68,72,76,80,84,88,92,9..., dimensions={0} | all-to-all | bytes 65536 | tf_op jit(solution)/shard_map/all_to_all | solution.py:448
  36.7 0.0 collective-permute-done.3.later_ref
  36.7 0.5 shard_map.88.v_ref
  37.3 1.2 %shard_map.89 = (f32[16,14,8,128]{3,2,1,0:T(8,128)S(1)}, bf16[128,1024]{1,0:T(8,128)(2,1)S(1)}, f32[16,128]{1,0:T(8,128)S(1)}) custom-call(bf16[4,8,32,128]{3,2,1,0:T(8,128)(2,1)S(1)} %get-tuple-element.32.x_ref, f32[64,128]{1,0:T(8,128)S(1)} %bitcast.11, f32[1,128]{1,0:T(1,128)S(1)} %get-tuple-element.44.gain_ref, f32[1,128]{1,0:T(1,128)S(1)} %get-tuple-element.45.bias_ref, ...), custom_call_target="tpu_custom_call" | custom-call | flops 452984832 | bytes 6202368 | tf_op jit(solution)/shard_map/pallas_call | solution.py:27
  38.5 3.5 %collective-permute-start.4 = (f32[16,14,8,128]{3,2,1,0:T(8,128)S(1)}, f32[16,14,8,128]{3,2,1,0:T(8,128)S(1)}, u32[]{:S(2)}, u32[]{:S(2)}) collective-permute-start(f32[16,14,8,128]{3,2,1,0:T(8,128)S(1)} %get-tuple-element.53), channel_id=1, source_target_pairs={{0,1},{1,0},{2,3},{3,2},{4,5},{5,4},{6,7},{7,6},{8,9},{9,8},{10,11... | collective-permute-start | bytes 2752520 | tf_op jit(solution)/shard_map/ppermute | solution.py:462
  41.9 1.8 %shard_map.90 = (f32[1024,128]{1,0:T(8,128)S(1)}, f32[8,128]{1,0:T(8,128)S(1)}) custom-call(bf16[4,8,32,128]{3,2,1,0:T(8,128)(2,1)S(1)} %get-tuple-element.32.x_ref, f32[16,128]{1,0:T(8,128)S(1)} %get-tuple-element.48.norm_ref, f32[1,128]{1,0:T(1,128)S(1)} %get-tuple-element.44.gain_ref, f32[1,128]{1,0:T(1,128)S(1)} %get-tuple-element.45.bias_ref, ...), custom_call_target="tpu_custom_call" | custom-call | flops 452984832 | bytes 6927360 | tf_op jit(solution)/shard_map/pallas_call | solution.py:27
  43.8 0.1 collective-permute-start.5
  43.9 0.7 shard_map.91.own_ref
  44.6 0.4 collective-permute-done.5.other_sums_ref
  45.0 0.0 collective-permute-done.4.other_ref
  45.0 0.2 shard_map.92
  45.2 13.5 %all_to_all.16.in_ref = bf16[16,120,128]{2,1,0:T(8,128)(2,1)S(1)} all-to-all(bf16[16,120,128]{2,1,0:T(8,128)(2,1)S(1)} %shard_map.92), channel_id=1, replica_groups=mesh['tm'=16,'rows'=8,'sect'=2] {'tm'}, dimensions={0} | all-to-all | bytes 983040 | tf_op jit(solution)/shard_map/all_to_all | solution.py:480
  58.6 0.2 shard_map.93
  58.9 12.1 %all_to_all.17 = f16[8,120,128]{2,1,0:T(8,128)(2,1)S(1)} all-to-all(f16[8,120,128]{2,1,0:T(8,128)(2,1)S(1)} %broadcast_in_dim.10), channel_id=1, replica_groups=mesh['tm'=16,'rows'=8,'sect'=2] {'rows'}, dimensions={0} | all-to-all | bytes 491520 | tf_op jit(solution)/shard_map/all_to_all | solution.py:483
  71.1 2.8 %collective-permute-start.6 = (f32[112,128]{1,0:T(8,128)S(1)}, f32[112,128]{1,0:T(8,128)S(1)}, u32[]{:S(2)}, u32[]{:S(2)}) collective-permute-start(f32[112,128]{1,0:T(8,128)S(1)} %get-tuple-element.59.half_ref), channel_id=1, source_target_pairs={{0,1},{1,0},{2,3},{3,2},{4,5},{5,4},{6,7},{7,6},{8,9},{9,8},{10,11... | collective-permute-start | bytes 172040 | tf_op jit(solution)/shard_map/ppermute | solution.py:489
  73.9 1.0 %shard_map.95 = (bf16[4,8,32,128]{3,2,1,0:T(8,128)(2,1)}, f32[1,128]{1,0:T(1,128)}, f32[1,128]{1,0:T(1,128)}) custom-call(bf16[4,8,32,128]{3,2,1,0:T(8,128)(2,1)S(1)} %get-tuple-element.32.x_ref, f32[1024,128]{1,0:T(8,128)S(1)} %get-tuple-element.51.da_ref, f32[16,128]{1,0:T(8,128)S(1)} %get-tuple-element.48.norm_ref, ...), custom_call_target="tpu_custom_call" | custom-call | bytes 1062400 | tf_op jit(solution)/shard_map/pallas_call | solution.py:27
  74.9 0.0 collective-permute-done.6.other_ref
  74.9 0.7 shard_map.96
  (6 shorter events, 0.2 us)
Async XLA Ops:
  2.0 4.3 %collective-permute-start = (bf16[528,128]{1,0:T(8,128)(2,1)S(1)}, bf16[528,128]{1,0:T(8,128)(2,1)S(1)}, u32[]{:S(2)}, u32[]{:S(2)}) collective-permute-start(bf16[528,128]{1,0:T(8,128)(2,1)S(1)} %get-tuple-element.34), channel_id=1, source_target_pairs={{0,1},{1,0},{2,3},{3,2},{4,5},{5,4},{6,7},{7,6},{8,9},{9,8},{10,11... | collective-permute-start | bytes 405512 | tf_op jit(solution)/shard_map/ppermute | solution.py:419
  6.4 7.1 %collective-permute-start.1 = (bf16[208,128]{1,0:T(8,128)(2,1)S(1)}, bf16[208,128]{1,0:T(8,128)(2,1)S(1)}, u32[]{:S(2)}, u32[]{:S(2)}) collective-permute-start(bf16[208,128]{1,0:T(8,128)(2,1)S(1)} %get-tuple-element.36), channel_id=1, source_target_pairs={{0,2},{2,0},{4,6},{6,4},{8,10},{10,8},{12,14},{14,12},{1,3},{3,1},... | collective-permute-start | bytes 159752 | tf_op jit(solution)/shard_map/ppermute | solution.py:425
  6.5 7.0 %collective-permute-start.2 = (bf16[192,128]{1,0:T(8,128)(2,1)S(1)}, bf16[192,128]{1,0:T(8,128)(2,1)S(1)}, u32[]{:S(2)}, u32[]{:S(2)}) collective-permute-start(bf16[192,128]{1,0:T(8,128)(2,1)S(1)} %get-tuple-element.39), channel_id=1, source_target_pairs={{0,14},{2,4},{4,2},{6,8},{8,6},{10,12},{12,10},{14,0},{1,15},{3,5}... | collective-permute-start | bytes 147464 | tf_op jit(solution)/shard_map/ppermute | solution.py:426
  13.5 23.2 %collective-permute-start.3 = (bf16[2,10,48,128]{3,2,1,0:T(8,128)(2,1)S(1)}, bf16[2,10,48,128]{3,2,1,0:T(8,128)(2,1)S(1)}, u32[]{:S(2)}, u32[]{:S(2)}) collective-permute-start(bf16[2,10,48,128]{3,2,1,0:T(8,128)(2,1)S(1)} %get-tuple-element.42), channel_id=1, source_target_pairs={{16,0},{32,16},{48,32},{64,48},{80,64},{96,80},{112,96},{128,112},... | collective-permute-start | bytes 737288 | tf_op jit(solution)/shard_map/ppermute | solution.py:447
  38.5 6.6 %collective-permute-start.4 = (f32[16,14,8,128]{3,2,1,0:T(8,128)S(1)}, f32[16,14,8,128]{3,2,1,0:T(8,128)S(1)}, u32[]{:S(2)}, u32[]{:S(2)}) collective-permute-start(f32[16,14,8,128]{3,2,1,0:T(8,128)S(1)} %get-tuple-element.53), channel_id=1, source_target_pairs={{0,1},{1,0},{2,3},{3,2},{4,5},{5,4},{6,7},{7,6},{8,9},{9,8},{10,11... | collective-permute-start | bytes 2752520 | tf_op jit(solution)/shard_map/ppermute | solution.py:462
  43.8 1.3 %collective-permute-start.5 = (f32[8,128]{1,0:T(8,128)S(1)}, f32[8,128]{1,0:T(8,128)S(1)}, u32[]{:S(2)}, u32[]{:S(2)}) collective-permute-start(f32[8,128]{1,0:T(8,128)S(1)} %get-tuple-element.54.sums_ref), channel_id=1, source_target_pairs={{0,1},{1,0},{2,3},{3,2},{4,5},{5,4},{6,7},{7,6},{8,9},{9,8},{10,11... | collective-permute-start | bytes 12296 | tf_op jit(solution)/shard_map/ppermute | solution.py:470
  71.1 3.8 %collective-permute-start.6 = (f32[112,128]{1,0:T(8,128)S(1)}, f32[112,128]{1,0:T(8,128)S(1)}, u32[]{:S(2)}, u32[]{:S(2)}) collective-permute-start(f32[112,128]{1,0:T(8,128)S(1)} %get-tuple-element.59.half_ref), channel_id=1, source_target_pairs={{0,1},{1,0},{2,3},{3,2},{4,5},{5,4},{6,7},{7,6},{8,9},{9,8},{10,11... | collective-permute-start | bytes 172040 | tf_op jit(solution)/shard_map/ppermute | solution.py:489

commit v8 on v7

--- a/solution.py
+++ b/solution.py
@@ -76,8 +76,8 @@
         copy.start()
     copies[0].wait()
     left = lax.axis_index("sect") == 0
-    up = up_ref[...]
-    facing_ref[:512] = jnp.where(left, up[:, :, 16:], up[:, :, :16]).reshape(512, 128)
+    facing = jnp.where(left, up_ref[:, :, 16:].astype(F32)[:, :, 15], up_ref[:, :, :16].astype(F32)[:, :, 0])
+    facing_ref[:32] = facing.reshape(32, 128).astype(BF16)
     for copy in copies[1:]:
         copy.wait()
     x = x_ref[...].astype(F32).reshape(-1, 128)
@@ -85,55 +85,67 @@
     square = group_total(column_sum(x * x))
     row = jnp.where(lanes_of(total.shape) % 4 < 2, total, square)
     stat_ref[...] = row
-    facing_ref[512:] = split_row(row)
-
-
-def edge_of(up_ref, side_ref, bottom):
-    side = side_ref[:512].reshape(4, 8, 16, 128)
-    low = jnp.concatenate([up_ref[:, 7], side[:, 7]], axis=1)
-    top = jnp.concatenate([up_ref[:, 0], side[:, 0]], axis=1)
-    return jnp.where(bottom, low, top).reshape(192, 128)
+    facing_ref[32:] = split_row(row)
+
+
+def columns_of(side_ref):
+    return side_ref[:32].astype(F32).reshape(4, 8, 128)
+
+
+def edge_of(up_ref, side_ref, bottom, row):
+    columns = columns_of(side_ref)
+    parts = split_row(row)[:8].astype(F32)[:4]
+    tail = [jnp.where(bottom, columns[:, 7], columns[:, 0]), parts, jnp.zeros((8, 128), F32)]
+    main = jnp.where(bottom, up_ref[:, 7], up_ref[:, 0]).reshape(128, 128)
+    return main, jnp.concatenate(tail, axis=0).astype(BF16)
 
 
 def edge_kernel(up_ref, side_ref, stat_ref, near_ref, far_ref, sum_ref):
     even = lax.axis_index("rows") % 2 == 0
-    row = stat_ref[...] + join_row(side_ref[512:])
+    row = stat_ref[...] + join_row(side_ref[32:])
     sum_ref[...] = row
-    near_ref[:192] = edge_of(up_ref, side_ref, even)
-    near_ref[192:] = split_row(row)
-    far_ref[...] = edge_of(up_ref, side_ref, jnp.logical_not(even))
+    near_ref[:128], near_ref[128:] = edge_of(up_ref, side_ref, even, row)
+    far_ref[:128], far_ref[128:] = edge_of(up_ref, side_ref, jnp.logical_not(even), row)
 
 
 def beyond(near_ref, far_ref):
     even = lax.axis_index("rows") % 2 == 0
     outside = jnp.logical_or(lax.axis_index("rows") == 0, lax.axis_index("rows") == lax.axis_size("rows") - 1)
-    near = near_ref[:192].reshape(4, 48, 128)
-    far = far_ref[:192].reshape(4, 48, 128)
+    near = near_ref[:128].reshape(4, 32, 128)
+    far = far_ref[:128].reshape(4, 32, 128)
     far = jnp.where(outside, jnp.zeros_like(far), far)
-    return jnp.where(even, far, near), jnp.where(even, near, far)
+    near_column = near_ref[128:].astype(F32)[:4]
+    far_column = far_ref[128:].astype(F32)[:4]
+    far_column = jnp.where(outside, jnp.zeros_like(far_column), far_column)
+    above = jnp.where(even, far, near), jnp.where(even, far_column, near_column)
+    below = jnp.where(even, near, far), jnp.where(even, near_column, far_column)
+    return above, below
 
 
 def early_kernel(up_ref, side_ref, near_ref, far_ref, stat_ref, early_ref, sent_ref):
-    row = stat_ref[...] + join_row(near_ref[192:])
+    row = stat_ref[...] + join_row(near_ref[128:].astype(F32)[4:8])
     sent_ref[...] = jnp.broadcast_to(row[None], (sent_ref.shape[0] // 8, 8, 128)).reshape(sent_ref.shape)
-    above, below = beyond(near_ref, far_ref)
-    early_ref[:, 0] = above[:2]
-    early_ref[:, 9] = below[:2]
-    early_ref[:, 1:9, :32] = up_ref[:2]
-    early_ref[:, 1:9, 32:] = side_ref[:256].reshape(2, 8, 16, 128)
-
-
-def column_taps(rows):
+    (above, above_column), (below, below_column) = beyond(near_ref, far_ref)
+    columns = columns_of(side_ref)
+    for f in range(2):
+        early_ref[f * 320 : f * 320 + 32] = above[f]
+        early_ref[f * 320 + 32 : f * 320 + 288] = up_ref[f].reshape(256, 128)
+        early_ref[f * 320 + 288 : f * 320 + 320] = below[f]
+        column = [above_column[f : f + 1], columns[f], below_column[f : f + 1], jnp.zeros((6, 128), F32)]
+        early_ref[640 + f * 16 : 656 + f * 16] = jnp.concatenate(column, axis=0).astype(BF16)
+
+
+def column_taps(core, beside):
     left = lax.axis_index("sect") == 0
-    core = rows[:, :32]
-    column = sublanes_of(core.shape)
-    first = column == 0
-    last = column == 31
+    index = sublanes_of(core.shape)
+    first = index == 0
+    last = index == 31
     zero = jnp.zeros_like(core)
-    ahead = pltpu.roll(rows, 47, 1)[:, :32]
-    behind = pltpu.roll(rows, 1, 1)[:, :32]
-    ahead = jnp.where(left, ahead + jnp.where(first, core, zero), jnp.where(last, zero, ahead))
-    behind = jnp.where(left, jnp.where(first, zero, behind), behind + jnp.where(last, core, zero))
+    beside = jnp.broadcast_to(beside[:, None, :], core.shape)
+    ahead = jnp.where(last, jnp.where(left, beside, zero), pltpu.roll(core, 31, 1))
+    behind = jnp.where(first, jnp.where(left, zero, beside), pltpu.roll(core, 1, 1))
+    ahead = ahead + jnp.where(first, jnp.where(left, core, zero), zero)
+    behind = behind + jnp.where(last, jnp.where(left, zero, core), zero)
     return ahead, core, behind
 
 
@@ -152,10 +164,9 @@
     weights.start()
     row_first = lax.axis_index("rows") == 0
     row_last = lax.axis_index("rows") == lax.axis_size("rows") - 1
+    columns = columns_of(side_ref)
     for f in range(4):
-        side = side_ref[f * 128 : (f + 1) * 128].reshape(8, 16, 128)
-        rows = jnp.concatenate([up_ref[f].astype(F32), side.astype(F32)], axis=1)
-        for e, part in enumerate(column_taps(rows)):
+        for e, part in enumerate(column_taps(up_ref[f].astype(F32), columns[f])):
             zero = jnp.zeros_like(part[0])
             top = part[1] + jnp.where(row_first, part[0], zero)
             low = part[6] + jnp.where(row_last, part[7], zero)
@@ -180,16 +191,19 @@
 
 
 def spread_kernel(near_ref, far_ref, later_ref, own_ref, v_ref):
-    above, below = beyond(near_ref, far_ref)
+    (above, above_column), (below, below_column) = beyond(near_ref, far_ref)
     row_first = lax.axis_index("rows") == 0
     row_last = lax.axis_index("rows") == lax.axis_size("rows") - 1
     outer = jnp.concatenate([above, below], axis=0).astype(F32)
-    for e, part in enumerate(column_taps(outer)):
+    outer_column = jnp.concatenate([above_column, below_column], axis=0)
+    for e, part in enumerate(column_taps(outer, outer_column)):
         for f in range(4):
             put(v_ref, f, 0, 2, e, part[f : f + 1])
             put(v_ref, f, 7, 0, e, part[f + 4 : f + 5])
     for f in range(2):
-        for e, part in enumerate(column_taps(later_ref[f].astype(F32))):
+        later = later_ref[f * 320 : f * 320 + 320].astype(F32).reshape(10, 32, 128)
+        column = later_ref[640 + f * 16 : 656 + f * 16].astype(F32)[:10]
+        for e, part in enumerate(column_taps(later, column)):
             zero = jnp.zeros_like(part[0])
             top = part[2] + jnp.where(row_first, part[1], zero)
             low = part[7] + jnp.where(row_last, part[8], zero)
@@ -404,7 +418,7 @@
             shape_of(activations.shape, BF16),
             shape_of((1, channels)),
             shape_of((1, channels)),
-            shape_of((528, channels), BF16),
+            shape_of((48, channels), BF16),
             shape_of((8, channels)),
         ],
         [
@@ -419,7 +433,7 @@
     side = lax.ppermute(facing, "sect", swap)
     nearer, farther, stat = call(
         edge_kernel,
-        [shape_of((208, channels), BF16), shape_of((192, channels), BF16), shape_of((8, channels))],
+        [shape_of((144, channels), BF16), shape_of((144, channels), BF16), shape_of((8, channels))],
         [up, side, stat],
     )
     nearer = lax.ppermute(nearer, "rows", near)
@@ -440,7 +454,7 @@
     groups = [[t * n_rows + r for t in range(n_time) for r in range(p, n_rows, 2)] for p in range(2)]
     early, stat = call(
         early_kernel,
-        [shape_of((2, 10, 48, channels), BF16), shape_of((len(groups[0]), channels))],
+        [shape_of((672, channels), BF16), shape_of((len(groups[0]), channels))],
         [up, side, nearer, farther, stat],
         [VMEM, VMEM, VMEM, VMEM, VMEM],
     )

time: 75.9 us -> 75.6 us (level)
  no operation moved by 1% of the time
where the time goes in v8:
time: 75.6 us; the launch traced here: 75.3 us
  blocking collectives  47.3 us (63%)
  starting transfers between devices  15.7 us (21%)
  Pallas kernels  10.2 us (13%)
  waiting for transfers between devices  1.25 us (2%)
    all_to_all x1, blocking collectives, local(): lax.all_to_all(stat[:, None], ('tm', 'rows'), 0, 0, axis_index_groups=gro...  21.7 us
    all_to_all x1, blocking collectives, local(): gathered = lax.all_to_all(sent, 'tm', 0, 0)  13.5 us
    all_to_all x1, blocking collectives, local(): shares = lax.all_to_all(share, 'rows', 0, 0).astype(F32)  12.1 us
    pallas_call x13, Pallas kernels, call(): pl.pallas_call(body, out_shape=outs, in_specs=specs or [VMEM] * len(args)...  10.2 us
    ppermute x1, starting transfers between devices, local(): farther = lax.ppermute(farther, 'rows', far)  4.55 us
    ppermute x1, starting transfers between devices, local(): arrived = lax.ppermute(away, 'sect', swap)  3.48 us
    ppermute x1, starting transfers between devices, local(): side = lax.ppermute(facing, 'sect', swap)  3.33 us
    ppermute x1, starting transfers between devices, local(): other = lax.ppermute(half, 'sect', swap)  2.83 us
  transfers between devices with their start and end apart: 7, of which 2 were waited for; matrix products, arithmetic and copies ran while one was open for 0% of the time, Pallas kernels for 8%

profile of v8, /device:TPU:1, one launch (start us, length us, event | category | flops | bytes accessed | tf_op | source)
XLA Modules:
  0.0 75.3 jit_solution(9273822270782037136)
XLA Ops:
  0.6 1.4 %shard_map.84 = (bf16[4,8,32,128]{3,2,1,0:T(8,128)(2,1)S(1)}, bf16[4,8,32,128]{3,2,1,0:T(8,128)(2,1)S(1)}, f32[1,128]{1,0:T(1,128)S(1)}, f32[1,128]{1,0:T(1,128)...) custom-call(bf16[4,8,32,128]{3,2,1,0:T(8,128)(2,1)} %up_hbm.1, bf16[4,8,32,128]{3,2,1,0:T(8,128)(2,1)} %x_hbm.1, ...), custom_call_target="tpu_custom_call" | custom-call | bytes 1067008 | tf_op jit(solution)/shard_map/pallas_call | solution.py:27
  2.0 3.3 %collective-permute-start = (bf16[48,128]{1,0:T(8,128)(2,1)S(1)}, bf16[48,128]{1,0:T(8,128)(2,1)S(1)}, u32[]{:S(2)}, u32[]{:S(2)}) collective-permute-start(bf16[48,128]{1,0:T(8,128)(2,1)S(1)} %get-tuple-element.34), channel_id=1, source_target_pairs={{0,1},{1,0},{2,3},{3,2},{4,5},{5,4},{6,7},{7,6},{8,9},{9,8},{10,11... | collective-permute-start | bytes 36872 | tf_op jit(solution)/shard_map/ppermute | solution.py:433
  5.3 0.8 %collective-permute-done.side_ref = bf16[48,128]{1,0:T(8,128)(2,1)S(1)} collective-permute-done((bf16[48,128]{1,0:T(8,128)(2,1)S(1)}, bf16[48,128]{1,0:T(8,128)(2,1)S(1)}, u32[]{:S(2)}, u32[]{:S(2)}) %collective-permute-start) | collective-permute-done | bytes 12320 | tf_op jit(solution)/shard_map/ppermute | solution.py:433
  6.2 0.1 collective-permute-start.1
  6.3 4.6 %collective-permute-start.2 = (bf16[144,128]{1,0:T(8,128)(2,1)S(1)}, bf16[144,128]{1,0:T(8,128)(2,1)S(1)}, u32[]{:S(2)}, u32[]{:S(2)}) collective-permute-start(bf16[144,128]{1,0:T(8,128)(2,1)S(1)} %get-tuple-element.39), channel_id=1, source_target_pairs={{0,14},{2,4},{4,2},{6,8},{8,6},{10,12},{12,10},{14,0},{1,15},{3,5}... | collective-permute-start | bytes 110600 | tf_op jit(solution)/shard_map/ppermute | solution.py:440
  10.9 2.5 %shard_map.86 = (bf16[8,256,1152]{2,1,0:T(8,128)(2,1)S(1)}, f32[1024,128]{1,0:T(8,128)S(1)}, bf16[3,128,1152]{2,1,0:T(8,128)(2,1)S(1)}) custom-call(bf16[4,8,32,128]{3,2,1,0:T(8,128)(2,1)S(1)} %get-tuple-element.33.up_ref, bf16[48,128]{1,0:T(8,128)(2,1)S(1)} %collective-permute-done.side_ref, bf16[3,3,3,128,128]{4,3,2,1,0:T(8,128)(2,1)} %kernel_hbm.1), custom_call_target="tpu_custom_call" | custom-call | flops 452984832 | bytes 7286784 | tf_op jit(solution)/shard_map/pallas_call | solution.py:27
  13.3 0.0 collective-permute-done.1.near_ref
  13.3 0.0 collective-permute-done.2.far_ref
  13.4 1.3 %collective-permute-start.3 = (bf16[672,128]{1,0:T(8,128)(2,1)S(1)}, bf16[672,128]{1,0:T(8,128)(2,1)S(1)}, u32[]{:S(2)}, u32[]{:S(2)}) collective-permute-start(bf16[672,128]{1,0:T(8,128)(2,1)S(1)} %get-tuple-element.42), channel_id=1, source_target_pairs={{16,0},{32,16},{48,32},{64,48},{80,64},{96,80},{112,96},{128,112},... | collective-permute-start | bytes 516104 | tf_op jit(solution)/shard_map/ppermute | solution.py:461
  14.7 21.7 %all_to_all.15 = f32[64,1,128]{2,1,0:T(1,128)S(1)} all-to-all(f32[64,1,128]{2,1,0:T(1,128)S(1)} %bitcast.12), channel_id=1, replica_groups={{0,4,8,12,16,20,24,28,32,36,40,44,48,52,56,60,64,68,72,76,80,84,88,92,9..., dimensions={0} | all-to-all | bytes 65536 | tf_op jit(solution)/shard_map/all_to_all | solution.py:462
  36.4 0.0 collective-permute-done.3.later_ref
  36.4 0.5 shard_map.88.v_ref
  37.0 1.2 %shard_map.89 = (f32[16,14,8,128]{3,2,1,0:T(8,128)S(1)}, bf16[128,1024]{1,0:T(8,128)(2,1)S(1)}, f32[16,128]{1,0:T(8,128)S(1)}) custom-call(bf16[4,8,32,128]{3,2,1,0:T(8,128)(2,1)S(1)} %get-tuple-element.32.x_ref, f32[64,128]{1,0:T(8,128)S(1)} %bitcast.11, f32[1,128]{1,0:T(1,128)S(1)} %get-tuple-element.44.gain_ref, f32[1,128]{1,0:T(1,128)S(1)} %get-tuple-element.45.bias_ref, ...), custom_call_target="tpu_custom_call" | custom-call | flops 452984832 | bytes 6202368 | tf_op jit(solution)/shard_map/pallas_call | solution.py:27
  38.2 3.5 %collective-permute-start.4 = (f32[16,14,8,128]{3,2,1,0:T(8,128)S(1)}, f32[16,14,8,128]{3,2,1,0:T(8,128)S(1)}, u32[]{:S(2)}, u32[]{:S(2)}) collective-permute-start(f32[16,14,8,128]{3,2,1,0:T(8,128)S(1)} %get-tuple-element.53), channel_id=1, source_target_pairs={{0,1},{1,0},{2,3},{3,2},{4,5},{5,4},{6,7},{7,6},{8,9},{9,8},{10,11... | collective-permute-start | bytes 2752520 | tf_op jit(solution)/shard_map/ppermute | solution.py:476
  41.6 1.8 %shard_map.90 = (f32[1024,128]{1,0:T(8,128)S(1)}, f32[8,128]{1,0:T(8,128)S(1)}) custom-call(bf16[4,8,32,128]{3,2,1,0:T(8,128)(2,1)S(1)} %get-tuple-element.32.x_ref, f32[16,128]{1,0:T(8,128)S(1)} %get-tuple-element.48.norm_ref, f32[1,128]{1,0:T(1,128)S(1)} %get-tuple-element.44.gain_ref, f32[1,128]{1,0:T(1,128)S(1)} %get-tuple-element.45.bias_ref, ...), custom_call_target="tpu_custom_call" | custom-call | flops 452984832 | bytes 6927360 | tf_op jit(solution)/shard_map/pallas_call | solution.py:27
  43.4 0.1 collective-permute-start.5
  43.5 0.7 shard_map.91.own_ref
  44.3 0.4 collective-permute-done.5.other_sums_ref
  44.7 0.0 collective-permute-done.4.other_ref
  44.7 0.2 shard_map.92
  44.9 13.5 %all_to_all.16.in_ref = bf16[16,120,128]{2,1,0:T(8,128)(2,1)S(1)} all-to-all(bf16[16,120,128]{2,1,0:T(8,128)(2,1)S(1)} %shard_map.92), channel_id=1, replica_groups=mesh['tm'=16,'rows'=8,'sect'=2] {'tm'}, dimensions={0} | all-to-all | bytes 983040 | tf_op jit(solution)/shard_map/all_to_all | solution.py:494
  58.3 0.2 shard_map.93
  58.6 12.1 %all_to_all.17 = f16[8,120,128]{2,1,0:T(8,128)(2,1)S(1)} all-to-all(f16[8,120,128]{2,1,0:T(8,128)(2,1)S(1)} %broadcast_in_dim.10), channel_id=1, replica_groups=mesh['tm'=16,'rows'=8,'sect'=2] {'rows'}, dimensions={0} | all-to-all | bytes 491520 | tf_op jit(solution)/shard_map/all_to_all | solution.py:497
  70.8 2.8 %collective-permute-start.6 = (f32[112,128]{1,0:T(8,128)S(1)}, f32[112,128]{1,0:T(8,128)S(1)}, u32[]{:S(2)}, u32[]{:S(2)}) collective-permute-start(f32[112,128]{1,0:T(8,128)S(1)} %get-tuple-element.59.half_ref), channel_id=1, source_target_pairs={{0,1},{1,0},{2,3},{3,2},{4,5},{5,4},{6,7},{7,6},{8,9},{9,8},{10,11... | collective-permute-start | bytes 172040 | tf_op jit(solution)/shard_map/ppermute | solution.py:503
  73.6 1.0 %shard_map.95 = (bf16[4,8,32,128]{3,2,1,0:T(8,128)(2,1)}, f32[1,128]{1,0:T(1,128)}, f32[1,128]{1,0:T(1,128)}) custom-call(bf16[4,8,32,128]{3,2,1,0:T(8,128)(2,1)S(1)} %get-tuple-element.32.x_ref, f32[1024,128]{1,0:T(8,128)S(1)} %get-tuple-element.51.da_ref, f32[16,128]{1,0:T(8,128)S(1)} %get-tuple-element.48.norm_ref, ...), custom_call_target="tpu_custom_call" | custom-call | bytes 1062400 | tf_op jit(solution)/shard_map/pallas_call | solution.py:27
  74.6 0.0 collective-permute-done.6.other_ref
  74.6 0.7 shard_map.96
  (6 shorter events, 0.2 us)
Async XLA Ops:
  2.0 4.2 %collective-permute-start = (bf16[48,128]{1,0:T(8,128)(2,1)S(1)}, bf16[48,128]{1,0:T(8,128)(2,1)S(1)}, u32[]{:S(2)}, u32[]{:S(2)}) collective-permute-start(bf16[48,128]{1,0:T(8,128)(2,1)S(1)} %get-tuple-element.34), channel_id=1, source_target_pairs={{0,1},{1,0},{2,3},{3,2},{4,5},{5,4},{6,7},{7,6},{8,9},{9,8},{10,11... | collective-permute-start | bytes 36872 | tf_op jit(solution)/shard_map/ppermute | solution.py:433
  6.2 7.1 %collective-permute-start.1 = (bf16[144,128]{1,0:T(8,128)(2,1)S(1)}, bf16[144,128]{1,0:T(8,128)(2,1)S(1)}, u32[]{:S(2)}, u32[]{:S(2)}) collective-permute-start(bf16[144,128]{1,0:T(8,128)(2,1)S(1)} %get-tuple-element.36), channel_id=1, source_target_pairs={{0,2},{2,0},{4,6},{6,4},{8,10},{10,8},{12,14},{14,12},{1,3},{3,1},... | collective-permute-start | bytes 110600 | tf_op jit(solution)/shard_map/ppermute | solution.py:439
  6.3 7.0 %collective-permute-start.2 = (bf16[144,128]{1,0:T(8,128)(2,1)S(1)}, bf16[144,128]{1,0:T(8,128)(2,1)S(1)}, u32[]{:S(2)}, u32[]{:S(2)}) collective-permute-start(bf16[144,128]{1,0:T(8,128)(2,1)S(1)} %get-tuple-element.39), channel_id=1, source_target_pairs={{0,14},{2,4},{4,2},{6,8},{8,6},{10,12},{12,10},{14,0},{1,15},{3,5}... | collective-permute-start | bytes 110600 | tf_op jit(solution)/shard_map/ppermute | solution.py:440
  13.4 23.0 %collective-permute-start.3 = (bf16[672,128]{1,0:T(8,128)(2,1)S(1)}, bf16[672,128]{1,0:T(8,128)(2,1)S(1)}, u32[]{:S(2)}, u32[]{:S(2)}) collective-permute-start(bf16[672,128]{1,0:T(8,128)(2,1)S(1)} %get-tuple-element.42), channel_id=1, source_target_pairs={{16,0},{32,16},{48,32},{64,48},{80,64},{96,80},{112,96},{128,112},... | collective-permute-start | bytes 516104 | tf_op jit(solution)/shard_map/ppermute | solution.py:461
  38.2 6.5 %collective-permute-start.4 = (f32[16,14,8,128]{3,2,1,0:T(8,128)S(1)}, f32[16,14,8,128]{3,2,1,0:T(8,128)S(1)}, u32[]{:S(2)}, u32[]{:S(2)}) collective-permute-start(f32[16,14,8,128]{3,2,1,0:T(8,128)S(1)} %get-tuple-element.53), channel_id=1, source_target_pairs={{0,1},{1,0},{2,3},{3,2},{4,5},{5,4},{6,7},{7,6},{8,9},{9,8},{10,11... | collective-permute-start | bytes 2752520 | tf_op jit(solution)/shard_map/ppermute | solution.py:476
  43.4 1.3 %collective-permute-start.5 = (f32[8,128]{1,0:T(8,128)S(1)}, f32[8,128]{1,0:T(8,128)S(1)}, u32[]{:S(2)}, u32[]{:S(2)}) collective-permute-start(f32[8,128]{1,0:T(8,128)S(1)} %get-tuple-element.54.sums_ref), channel_id=1, source_target_pairs={{0,1},{1,0},{2,3},{3,2},{4,5},{5,4},{6,7},{7,6},{8,9},{9,8},{10,11... | collective-permute-start | bytes 12296 | tf_op jit(solution)/shard_map/ppermute | solution.py:484
  70.8 3.8 %collective-permute-start.6 = (f32[112,128]{1,0:T(8,128)S(1)}, f32[112,128]{1,0:T(8,128)S(1)}, u32[]{:S(2)}, u32[]{:S(2)}) collective-permute-start(f32[112,128]{1,0:T(8,128)S(1)} %get-tuple-element.59.half_ref), channel_id=1, source_target_pairs={{0,1},{1,0},{2,3},{3,2},{4,5},{5,4},{6,7},{7,6},{8,9},{9,8},{10,11... | collective-permute-start | bytes 172040 | tf_op jit(solution)/shard_map/ppermute | solution.py:503

commit v9 on v8

--- a/solution.py
+++ b/solution.py
@@ -451,7 +451,7 @@
         flops=cells * TAPS * channels * channels,
     )
     nearer, inner = lax.optimization_barrier((nearer, inner))
-    groups = [[t * n_rows + r for t in range(n_time) for r in range(p, n_rows, 2)] for p in range(2)]
+    groups = [[t * n_rows + r for t in range(n_time) for r in chosen] for chosen in ((1, 2, 4, 7), (0, 3, 5, 6))]
     early, stat = call(
         early_kernel,
         [shape_of((672, channels), BF16), shape_of((len(groups[0]), channels))],

time: 75.6 us -> 74.4 us (0.984)
  blocking collectives: 47.3 us -> 46.4 us
    all_to_all x1, blocking collectives: 21.7 us -> 19.6 us  [local(): lax.all_to_all(stat[:, None], ('tm', 'rows'), 0, 0, axis_index_groups=gro...]
    all_to_all x1, blocking collectives: 12.1 us -> 13.4 us  [local(): shares = lax.all_to_all(share, 'rows', 0, 0).astype(F32)]
where the time goes in v9:
time: 74.4 us; the launch traced here: 74.2 us
  blocking collectives  46.4 us (62%)
  starting transfers between devices  15.5 us (21%)
  Pallas kernels  10.2 us (14%)
  waiting for transfers between devices  1.25 us (2%)
  between operations  0.75 us (1%)
    all_to_all x1, blocking collectives, local(): lax.all_to_all(stat[:, None], ('tm', 'rows'), 0, 0, axis_index_groups=gro...  19.6 us
    all_to_all x1, blocking collectives, local(): gathered = lax.all_to_all(sent, 'tm', 0, 0)  13.5 us
    all_to_all x1, blocking collectives, local(): shares = lax.all_to_all(share, 'rows', 0, 0).astype(F32)  13.4 us
    pallas_call x13, Pallas kernels, call(): pl.pallas_call(body, out_shape=outs, in_specs=specs or [VMEM] * len(args)...  10.2 us
    ppermute x1, starting transfers between devices, local(): farther = lax.ppermute(farther, 'rows', far)  4.55 us
    ppermute x1, starting transfers between devices, local(): side = lax.ppermute(facing, 'sect', swap)  3.33 us
    ppermute x1, starting transfers between devices, local(): other = lax.ppermute(half, 'sect', swap)  3.05 us
    ppermute x1, starting transfers between devices, local(): arrived = lax.ppermute(away, 'sect', swap)  3.04 us
  transfers between devices with their start and end apart: 7, of which 2 were waited for; matrix products, arithmetic and copies ran while one was open for 0% of the time, Pallas kernels for 8%

profile of v9, /device:TPU:1, one launch (start us, length us, event | category | flops | bytes accessed | tf_op | source)
XLA Modules:
  0.0 74.2 jit_solution(14072089498163931716)
XLA Ops:
  0.6 1.4 %shard_map.84 = (bf16[4,8,32,128]{3,2,1,0:T(8,128)(2,1)S(1)}, bf16[4,8,32,128]{3,2,1,0:T(8,128)(2,1)S(1)}, f32[1,128]{1,0:T(1,128)S(1)}, f32[1,128]{1,0:T(1,128)...) custom-call(bf16[4,8,32,128]{3,2,1,0:T(8,128)(2,1)} %up_hbm.1, bf16[4,8,32,128]{3,2,1,0:T(8,128)(2,1)} %x_hbm.1, ...), custom_call_target="tpu_custom_call" | custom-call | bytes 1067008 | tf_op jit(solution)/shard_map/pallas_call | solution.py:27
  2.0 3.3 %collective-permute-start = (bf16[48,128]{1,0:T(8,128)(2,1)S(1)}, bf16[48,128]{1,0:T(8,128)(2,1)S(1)}, u32[]{:S(2)}, u32[]{:S(2)}) collective-permute-start(bf16[48,128]{1,0:T(8,128)(2,1)S(1)} %get-tuple-element.34), channel_id=1, source_target_pairs={{0,1},{1,0},{2,3},{3,2},{4,5},{5,4},{6,7},{7,6},{8,9},{9,8},{10,11... | collective-permute-start | bytes 36872 | tf_op jit(solution)/shard_map/ppermute | solution.py:433
  5.3 0.8 %collective-permute-done.side_ref = bf16[48,128]{1,0:T(8,128)(2,1)S(1)} collective-permute-done((bf16[48,128]{1,0:T(8,128)(2,1)S(1)}, bf16[48,128]{1,0:T(8,128)(2,1)S(1)}, u32[]{:S(2)}, u32[]{:S(2)}) %collective-permute-start) | collective-permute-done | bytes 12320 | tf_op jit(solution)/shard_map/ppermute | solution.py:433
  6.2 0.1 collective-permute-start.1
  6.3 4.6 %collective-permute-start.2 = (bf16[144,128]{1,0:T(8,128)(2,1)S(1)}, bf16[144,128]{1,0:T(8,128)(2,1)S(1)}, u32[]{:S(2)}, u32[]{:S(2)}) collective-permute-start(bf16[144,128]{1,0:T(8,128)(2,1)S(1)} %get-tuple-element.39), channel_id=1, source_target_pairs={{0,14},{2,4},{4,2},{6,8},{8,6},{10,12},{12,10},{14,0},{1,15},{3,5}... | collective-permute-start | bytes 110600 | tf_op jit(solution)/shard_map/ppermute | solution.py:440
  10.9 2.5 %shard_map.86 = (bf16[8,256,1152]{2,1,0:T(8,128)(2,1)S(1)}, f32[1024,128]{1,0:T(8,128)S(1)}, bf16[3,128,1152]{2,1,0:T(8,128)(2,1)S(1)}) custom-call(bf16[4,8,32,128]{3,2,1,0:T(8,128)(2,1)S(1)} %get-tuple-element.33.up_ref, bf16[48,128]{1,0:T(8,128)(2,1)S(1)} %collective-permute-done.side_ref, bf16[3,3,3,128,128]{4,3,2,1,0:T(8,128)(2,1)} %kernel_hbm.1), custom_call_target="tpu_custom_call" | custom-call | flops 452984832 | bytes 7286784 | tf_op jit(solution)/shard_map/pallas_call | solution.py:27
  13.3 0.0 collective-permute-done.1.near_ref
  13.3 0.0 collective-permute-done.2.far_ref
  13.4 1.3 %collective-permute-start.3 = (bf16[672,128]{1,0:T(8,128)(2,1)S(1)}, bf16[672,128]{1,0:T(8,128)(2,1)S(1)}, u32[]{:S(2)}, u32[]{:S(2)}) collective-permute-start(bf16[672,128]{1,0:T(8,128)(2,1)S(1)} %get-tuple-element.42), channel_id=1, source_target_pairs={{16,0},{32,16},{48,32},{64,48},{80,64},{96,80},{112,96},{128,112},... | collective-permute-start | bytes 516104 | tf_op jit(solution)/shard_map/ppermute | solution.py:461
  14.7 19.6 %all_to_all.15 = f32[64,1,128]{2,1,0:T(1,128)S(1)} all-to-all(f32[64,1,128]{2,1,0:T(1,128)S(1)} %bitcast.12), channel_id=1, replica_groups={{2,4,8,14,18,20,24,30,34,36,40,46,50,52,56,62,66,68,72,78,82,84,88,94,9..., dimensions={0} | all-to-all | bytes 65536 | tf_op jit(solution)/shard_map/all_to_all | solution.py:462
  34.3 0.0 collective-permute-done.3.later_ref
  34.3 0.5 shard_map.88.v_ref
  34.8 1.2 %shard_map.89 = (f32[16,14,8,128]{3,2,1,0:T(8,128)S(1)}, bf16[128,1024]{1,0:T(8,128)(2,1)S(1)}, f32[16,128]{1,0:T(8,128)S(1)}) custom-call(bf16[4,8,32,128]{3,2,1,0:T(8,128)(2,1)S(1)} %get-tuple-element.32.x_ref, f32[64,128]{1,0:T(8,128)S(1)} %bitcast.11, f32[1,128]{1,0:T(1,128)S(1)} %get-tuple-element.44.gain_ref, f32[1,128]{1,0:T(1,128)S(1)} %get-tuple-element.45.bias_ref, ...), custom_call_target="tpu_custom_call" | custom-call | flops 452984832 | bytes 6202368 | tf_op jit(solution)/shard_map/pallas_call | solution.py:27
  36.0 3.0 %collective-permute-start.4 = (f32[16,14,8,128]{3,2,1,0:T(8,128)S(1)}, f32[16,14,8,128]{3,2,1,0:T(8,128)S(1)}, u32[]{:S(2)}, u32[]{:S(2)}) collective-permute-start(f32[16,14,8,128]{3,2,1,0:T(8,128)S(1)} %get-tuple-element.53), channel_id=1, source_target_pairs={{0,1},{1,0},{2,3},{3,2},{4,5},{5,4},{6,7},{7,6},{8,9},{9,8},{10,11... | collective-permute-start | bytes 2752520 | tf_op jit(solution)/shard_map/ppermute | solution.py:476
  39.1 1.8 %shard_map.90 = (f32[1024,128]{1,0:T(8,128)S(1)}, f32[8,128]{1,0:T(8,128)S(1)}) custom-call(bf16[4,8,32,128]{3,2,1,0:T(8,128)(2,1)S(1)} %get-tuple-element.32.x_ref, f32[16,128]{1,0:T(8,128)S(1)} %get-tuple-element.48.norm_ref, f32[1,128]{1,0:T(1,128)S(1)} %get-tuple-element.44.gain_ref, f32[1,128]{1,0:T(1,128)S(1)} %get-tuple-element.45.bias_ref, ...), custom_call_target="tpu_custom_call" | custom-call | flops 452984832 | bytes 6927360 | tf_op jit(solution)/shard_map/pallas_call | solution.py:27
  40.9 0.1 collective-permute-start.5
  41.0 0.7 %shard_map.91.own_ref = f32[16,14,8,128]{3,2,1,0:T(8,128)S(1)} custom-call(bf16[128,1024]{1,0:T(8,128)(2,1)S(1)} %get-tuple-element.52.turned_ref, bf16[8,256,1152]{2,1,0:T(8,128)(2,1)S(1)} %shard_map.88.v_ref), custom_call_target="tpu_custom_call" | custom-call | flops 452984832 | bytes 5898240 | tf_op jit(solution)/shard_map/pallas_call | solution.py:27
  41.7 0.4 collective-permute-done.5.other_sums_ref
  42.1 0.0 collective-permute-done.4.other_ref
  42.1 0.2 shard_map.92
  42.3 13.5 %all_to_all.16.in_ref = bf16[16,120,128]{2,1,0:T(8,128)(2,1)S(1)} all-to-all(bf16[16,120,128]{2,1,0:T(8,128)(2,1)S(1)} %shard_map.92), channel_id=1, replica_groups=mesh['tm'=16,'rows'=8,'sect'=2] {'tm'}, dimensions={0} | all-to-all | bytes 983040 | tf_op jit(solution)/shard_map/all_to_all | solution.py:494
  55.8 0.2 shard_map.93
  56.0 13.4 %all_to_all.17 = f16[8,120,128]{2,1,0:T(8,128)(2,1)S(1)} all-to-all(f16[8,120,128]{2,1,0:T(8,128)(2,1)S(1)} %broadcast_in_dim.10), channel_id=1, replica_groups=mesh['tm'=16,'rows'=8,'sect'=2] {'rows'}, dimensions={0} | all-to-all | bytes 491520 | tf_op jit(solution)/shard_map/all_to_all | solution.py:497
  69.5 3.0 %collective-permute-start.6 = (f32[112,128]{1,0:T(8,128)S(1)}, f32[112,128]{1,0:T(8,128)S(1)}, u32[]{:S(2)}, u32[]{:S(2)}) collective-permute-start(f32[112,128]{1,0:T(8,128)S(1)} %get-tuple-element.59.half_ref), channel_id=1, source_target_pairs={{0,1},{1,0},{2,3},{3,2},{4,5},{5,4},{6,7},{7,6},{8,9},{9,8},{10,11... | collective-permute-start | bytes 172040 | tf_op jit(solution)/shard_map/ppermute | solution.py:503
  72.5 1.0 %shard_map.95 = (bf16[4,8,32,128]{3,2,1,0:T(8,128)(2,1)}, f32[1,128]{1,0:T(1,128)}, f32[1,128]{1,0:T(1,128)}) custom-call(bf16[4,8,32,128]{3,2,1,0:T(8,128)(2,1)S(1)} %get-tuple-element.32.x_ref, f32[1024,128]{1,0:T(8,128)S(1)} %get-tuple-element.51.da_ref, f32[16,128]{1,0:T(8,128)S(1)} %get-tuple-element.48.norm_ref, ...), custom_call_target="tpu_custom_call" | custom-call | bytes 1062400 | tf_op jit(solution)/shard_map/pallas_call | solution.py:27
  73.5 0.0 collective-permute-done.6.other_ref
  73.5 0.7 shard_map.96
  (6 shorter events, 0.2 us)
Async XLA Ops:
  2.0 4.2 %collective-permute-start = (bf16[48,128]{1,0:T(8,128)(2,1)S(1)}, bf16[48,128]{1,0:T(8,128)(2,1)S(1)}, u32[]{:S(2)}, u32[]{:S(2)}) collective-permute-start(bf16[48,128]{1,0:T(8,128)(2,1)S(1)} %get-tuple-element.34), channel_id=1, source_target_pairs={{0,1},{1,0},{2,3},{3,2},{4,5},{5,4},{6,7},{7,6},{8,9},{9,8},{10,11... | collective-permute-start | bytes 36872 | tf_op jit(solution)/shard_map/ppermute | solution.py:433
  6.2 7.1 %collective-permute-start.1 = (bf16[144,128]{1,0:T(8,128)(2,1)S(1)}, bf16[144,128]{1,0:T(8,128)(2,1)S(1)}, u32[]{:S(2)}, u32[]{:S(2)}) collective-permute-start(bf16[144,128]{1,0:T(8,128)(2,1)S(1)} %get-tuple-element.36), channel_id=1, source_target_pairs={{0,2},{2,0},{4,6},{6,4},{8,10},{10,8},{12,14},{14,12},{1,3},{3,1},... | collective-permute-start | bytes 110600 | tf_op jit(solution)/shard_map/ppermute | solution.py:439
  6.3 7.0 %collective-permute-start.2 = (bf16[144,128]{1,0:T(8,128)(2,1)S(1)}, bf16[144,128]{1,0:T(8,128)(2,1)S(1)}, u32[]{:S(2)}, u32[]{:S(2)}) collective-permute-start(bf16[144,128]{1,0:T(8,128)(2,1)S(1)} %get-tuple-element.39), channel_id=1, source_target_pairs={{0,14},{2,4},{4,2},{6,8},{8,6},{10,12},{12,10},{14,0},{1,15},{3,5}... | collective-permute-start | bytes 110600 | tf_op jit(solution)/shard_map/ppermute | solution.py:440
  13.4 20.9 %collective-permute-start.3 = (bf16[672,128]{1,0:T(8,128)(2,1)S(1)}, bf16[672,128]{1,0:T(8,128)(2,1)S(1)}, u32[]{:S(2)}, u32[]{:S(2)}) collective-permute-start(bf16[672,128]{1,0:T(8,128)(2,1)S(1)} %get-tuple-element.42), channel_id=1, source_target_pairs={{16,0},{32,16},{48,32},{64,48},{80,64},{96,80},{112,96},{128,112},... | collective-permute-start | bytes 516104 | tf_op jit(solution)/shard_map/ppermute | solution.py:461
  36.0 6.1 %collective-permute-start.4 = (f32[16,14,8,128]{3,2,1,0:T(8,128)S(1)}, f32[16,14,8,128]{3,2,1,0:T(8,128)S(1)}, u32[]{:S(2)}, u32[]{:S(2)}) collective-permute-start(f32[16,14,8,128]{3,2,1,0:T(8,128)S(1)} %get-tuple-element.53), channel_id=1, source_target_pairs={{0,1},{1,0},{2,3},{3,2},{4,5},{5,4},{6,7},{7,6},{8,9},{9,8},{10,11... | collective-permute-start | bytes 2752520 | tf_op jit(solution)/shard_map/ppermute | solution.py:476
  40.9 1.3 %collective-permute-start.5 = (f32[8,128]{1,0:T(8,128)S(1)}, f32[8,128]{1,0:T(8,128)S(1)}, u32[]{:S(2)}, u32[]{:S(2)}) collective-permute-start(f32[8,128]{1,0:T(8,128)S(1)} %get-tuple-element.54.sums_ref), channel_id=1, source_target_pairs={{0,1},{1,0},{2,3},{3,2},{4,5},{5,4},{6,7},{7,6},{8,9},{9,8},{10,11... | collective-permute-start | bytes 12296 | tf_op jit(solution)/shard_map/ppermute | solution.py:484
  69.5 4.1 %collective-permute-start.6 = (f32[112,128]{1,0:T(8,128)S(1)}, f32[112,128]{1,0:T(8,128)S(1)}, u32[]{:S(2)}, u32[]{:S(2)}) collective-permute-start(f32[112,128]{1,0:T(8,128)S(1)} %get-tuple-element.59.half_ref), channel_id=1, source_target_pairs={{0,1},{1,0},{2,3},{3,2},{4,5},{5,4},{6,7},{7,6},{8,9},{9,8},{10,11... | collective-permute-start | bytes 172040 | tf_op jit(solution)/shard_map/ppermute | solution.py:503

commit v10 on v9

--- a/solution.py
+++ b/solution.py
@@ -69,8 +69,10 @@
     return jnp.broadcast_to(parts[0:1] + parts[1:2] + parts[2:3], (8, 128))
 
 
-def entry_kernel(up_hbm, x_hbm, gain_hbm, bias_hbm, up_ref, x_ref, gain_ref, bias_ref, facing_ref, stat_ref, sems):
-    pairs = ((up_hbm, up_ref), (x_hbm, x_ref), (gain_hbm, gain_ref), (bias_hbm, bias_ref))
+def entry_kernel(
+    up_hbm, x_hbm, gain_hbm, bias_hbm, kernel_hbm, up_ref, x_ref, gain_ref, bias_ref, kernel_ref, facing_ref, stat_ref, sems
+):
+    pairs = ((up_hbm, up_ref), (x_hbm, x_ref), (gain_hbm, gain_ref), (bias_hbm, bias_ref), (kernel_hbm, kernel_ref))
     copies = [pltpu.make_async_copy(source, target, sems.at[i]) for i, (source, target) in enumerate(pairs)]
     for copy in copies:
         copy.start()
@@ -78,14 +80,15 @@
     left = lax.axis_index("sect") == 0
     facing = jnp.where(left, up_ref[:, :, 16:].astype(F32)[:, :, 15], up_ref[:, :, :16].astype(F32)[:, :, 0])
     facing_ref[:32] = facing.reshape(32, 128).astype(BF16)
-    for copy in copies[1:]:
-        copy.wait()
+    copies[1].wait()
     x = x_ref[...].astype(F32).reshape(-1, 128)
     total = group_total(column_sum(x))
     square = group_total(column_sum(x * x))
     row = jnp.where(lanes_of(total.shape) % 4 < 2, total, square)
     stat_ref[...] = row
     facing_ref[32:] = split_row(row)
+    for copy in copies[2:]:
+        copy.wait()
 
 
 def columns_of(side_ref):
@@ -159,28 +162,33 @@
     return lax.dot_general(lhs, taps_ref[a], (((1,), (1,)), ((), ())), preferred_element_type=F32)
 
 
-def own_kernel(up_ref, side_ref, kernel_hbm, v_ref, dh_ref, taps_ref, kernel_ref, sem):
-    weights = pltpu.make_async_copy(kernel_hbm, kernel_ref, sem)
-    weights.start()
-    row_first = lax.axis_index("rows") == 0
-    row_last = lax.axis_index("rows") == lax.axis_size("rows") - 1
-    columns = columns_of(side_ref)
-    for f in range(4):
-        for e, part in enumerate(column_taps(up_ref[f].astype(F32), columns[f])):
-            zero = jnp.zeros_like(part[0])
-            top = part[1] + jnp.where(row_first, part[0], zero)
-            low = part[6] + jnp.where(row_last, part[7], zero)
-            put(v_ref, f, 0, 0, e, top[None])
-            put(v_ref, f, 1, 0, e, part[2:8])
-            put(v_ref, f, 0, 1, e, part)
-            put(v_ref, f, 1, 2, e, part[0:6])
-            put(v_ref, f, 7, 2, e, low[None])
-    weights.wait()
+def put_own(v_ref, f, e, part):
+    zero = jnp.zeros_like(part[0])
+    top = part[1] + jnp.where(lax.axis_index("rows") == 0, part[0], zero)
+    low = part[6] + jnp.where(lax.axis_index("rows") == lax.axis_size("rows") - 1, part[7], zero)
+    put(v_ref, f, 0, 0, e, top[None])
+    put(v_ref, f, 1, 0, e, part[2:8])
+    put(v_ref, f, 0, 1, e, part)
+    put(v_ref, f, 1, 2, e, part[0:6])
+    put(v_ref, f, 7, 2, e, low[None])
+
+
+def taps_kernel(up_ref, kernel_ref, v_ref, taps_ref):
     for a in range(3):
         for b in range(3):
             for e in range(3):
                 j = (b * 3 + e) * 128
                 taps_ref[a, :, j : j + 128] = kernel_ref[a, b, e]
+    for f in range(4):
+        put_own(v_ref, f, 1, up_ref[f].astype(F32))
+
+
+def own_kernel(up_ref, side_ref, taps_ref, begun_ref, v_ref, dh_ref):
+    columns = columns_of(side_ref)
+    for f in range(4):
+        ahead, _, behind = column_taps(up_ref[f].astype(F32), columns[f])
+        put_own(v_ref, f, 0, ahead)
+        put_own(v_ref, f, 2, behind)
     for f in range(4):
         total = None
         for a in range(3):
@@ -411,13 +419,14 @@
     near = [(i, i ^ 1) for i in range(n_rows)]
     far = [(i, (i - 1) % n_rows if i % 2 == 0 else (i + 1) % n_rows) for i in range(n_rows)]
 
-    up, x, gain, bias, facing, stat = call(
+    up, x, gain, bias, weights, facing, stat = call(
         entry_kernel,
         [
             shape_of(upstream.shape, BF16),
             shape_of(activations.shape, BF16),
             shape_of((1, channels)),
             shape_of((1, channels)),
+            shape_of(kernel.shape, BF16),
             shape_of((48, channels), BF16),
             shape_of((8, channels)),
         ],
@@ -426,11 +435,18 @@
             held(activations, pltpu.HBM),
             held(group_norm_gain.reshape(1, channels), pltpu.HBM),
             held(group_norm_bias.reshape(1, channels), pltpu.HBM),
+            held(kernel, pltpu.HBM),
         ],
-        [HBM] * 4,
-        [pltpu.SemaphoreType.DMA((4,))],
+        [HBM] * 5,
+        [pltpu.SemaphoreType.DMA((5,))],
     )
     side = lax.ppermute(facing, "sect", swap)
+    spread, taps = call(
+        taps_kernel,
+        [pltpu.VMEM((8, 256, 1152), BF16), shape_of((3, channels, 9 * channels), BF16)],
+        [up, weights],
+    )
+    side, taps = lax.optimization_barrier((side, taps))
     nearer, farther, stat = call(
         edge_kernel,
         [shape_of((144, channels), BF16), shape_of((144, channels), BF16), shape_of((8, channels))],
@@ -438,17 +454,12 @@
     )
     nearer = lax.ppermute(nearer, "rows", near)
     farther = lax.ppermute(farther, "rows", far)
-    spread, inner, taps = call(
+    spread, inner = call(
         own_kernel,
-        [
-            pltpu.VMEM((8, 256, 1152), BF16),
-            shape_of((cells, channels)),
-            shape_of((3, channels, 9 * channels), BF16),
-        ],
-        [up, side, held(kernel, pltpu.HBM)],
-        [VMEM, VMEM, HBM],
-        [pltpu.VMEM((3, 3, 3, 128, 128), BF16), pltpu.SemaphoreType.DMA],
+        [pltpu.VMEM((8, 256, 1152), BF16), shape_of((cells, channels))],
+        [up, side, taps, held(spread, pltpu.VMEM)],
         flops=cells * TAPS * channels * channels,
+        aliases={3: 0},
     )
     nearer, inner = lax.optimization_barrier((nearer, inner))
     groups = [[t * n_rows + r for t in range(n_time) for r in chosen] for chosen in ((1, 2, 4, 7), (0, 3, 5, 6))]

time: 74.4 us -> 74.5 us (level)
  blocking collectives: 46.4 us -> 47.5 us
  Pallas kernels: 10.2 us -> 9.3 us
    all_to_all x1, blocking collectives: 19.6 us -> 20.6 us  [local(): lax.all_to_all(stat[:, None], ('tm', 'rows'), 0, 0, axis_index_groups=gro...]
    pallas_call x13 -> x14, Pallas kernels: 10.2 us -> 9.3 us  [call(): pl.pallas_call(body, out_shape=outs, in_specs=specs or [VMEM] * len(args)...]
  transfers between devices with their start and end apart: 7 -> 7, of which waited for: 2 -> 2; matrix products, arithmetic and copies ran while one was open for 0% -> 0% of each run, Pallas kernels for 8% -> 7%
where the time goes in v10:
time: 74.5 us; the launch traced here: 74.2 us
  blocking collectives  47.5 us (64%)
  starting transfers between devices  15.6 us (21%)
  Pallas kernels  9.3 us (12%)
  waiting for transfers between devices  1.04 us (1%)
    all_to_all x1, blocking collectives, local(): lax.all_to_all(stat[:, None], ('tm', 'rows'), 0, 0, axis_index_groups=gro...  20.6 us
    all_to_all x1, blocking collectives, local(): gathered = lax.all_to_all(sent, 'tm', 0, 0)  13.5 us
    all_to_all x1, blocking collectives, local(): shares = lax.all_to_all(share, 'rows', 0, 0).astype(F32)  13.4 us
    pallas_call x14, Pallas kernels, call(): pl.pallas_call(body, out_shape=outs, in_specs=specs or [VMEM] * len(args)...  9.3 us
    ppermute x1, starting transfers between devices, local(): farther = lax.ppermute(farther, 'rows', far)  4.55 us
    ppermute x1, starting transfers between devices, local(): side = lax.ppermute(facing, 'sect', swap)  3.33 us
    ppermute x1, starting transfers between devices, local(): arrived = lax.ppermute(away, 'sect', swap)  3.18 us
    ppermute x1, starting transfers between devices, local(): other = lax.ppermute(half, 'sect', swap)  3.04 us
  transfers between devices with their start and end apart: 7, of which 2 were waited for; matrix products, arithmetic and copies ran while one was open for 0% of the time, Pallas kernels for 7%

profile of v10, /device:TPU:1, one launch (start us, length us, event | category | flops | bytes accessed | tf_op | source)
XLA Modules:
  0.0 74.2 jit_solution(11909672239518984542)
XLA Ops:
  0.6 1.4 %shard_map.84 = (bf16[4,8,32,128]{3,2,1,0:T(8,128)(2,1)S(1)}, bf16[4,8,32,128]{3,2,1,0:T(8,128)(2,1)S(1)}, f32[1,128]{1,0:T(1,128)S(1)}, f32[1,128]{1,0:T(1,128)...) custom-call(bf16[4,8,32,128]{3,2,1,0:T(8,128)(2,1)} %up_hbm.1, ...), custom_call_target="tpu_custom_call" | custom-call | bytes 2836480 | tf_op jit(solution)/shard_map/pallas_call | solution.py:27
  2.0 3.3 %collective-permute-start = (bf16[48,128]{1,0:T(8,128)(2,1)S(1)}, bf16[48,128]{1,0:T(8,128)(2,1)S(1)}, u32[]{:S(2)}, u32[]{:S(2)}) collective-permute-start(bf16[48,128]{1,0:T(8,128)(2,1)S(1)} %get-tuple-element.38), channel_id=1, source_target_pairs={{0,1},{1,0},{2,3},{3,2},{4,5},{5,4},{6,7},{7,6},{8,9},{9,8},{10,11... | collective-permute-start | bytes 36872 | tf_op jit(solution)/shard_map/ppermute | solution.py:443
  5.4 0.2 shard_map.85
  5.6 0.6 collective-permute-done.side_ref
  6.2 0.1 collective-permute-start.1
  6.3 4.6 %collective-permute-start.2 = (bf16[144,128]{1,0:T(8,128)(2,1)S(1)}, bf16[144,128]{1,0:T(8,128)(2,1)S(1)}, u32[]{:S(2)}, u32[]{:S(2)}) collective-permute-start(bf16[144,128]{1,0:T(8,128)(2,1)S(1)} %get-tuple-element.48), channel_id=1, source_target_pairs={{0,14},{2,4},{4,2},{6,8},{8,6},{10,12},{12,10},{14,0},{1,15},{3,5}... | collective-permute-start | bytes 110600 | tf_op jit(solution)/shard_map/ppermute | solution.py:456
  10.9 1.3 %shard_map.87 = (bf16[8,256,1152]{2,1,0:T(8,128)(2,1)S(1)}, f32[1024,128]{1,0:T(8,128)S(1)}) custom-call(bf16[4,8,32,128]{3,2,1,0:T(8,128)(2,1)S(1)} %get-tuple-element.37.up_ref, bf16[48,128]{1,0:T(8,128)(2,1)S(1)} %collective-permute-done.side_ref, bf16[3,128,1152]{2,1,0:T(8,128)(2,1)S(1)} %get-tuple-element.44.taps_ref, ...), custom_call_target="tpu_custom_call", output_to_operand_aliasing={{0}: (3, {})} | custom-call | flops 452984832 | bytes 11120640 | tf_op jit(solution)/shard_map/pallas_call | solution.py:27
  12.2 0.0 collective-permute-done.1.near_ref
  12.2 0.0 collective-permute-done.2.far_ref
  12.3 1.3 %collective-permute-start.3 = (bf16[672,128]{1,0:T(8,128)(2,1)S(1)}, bf16[672,128]{1,0:T(8,128)(2,1)S(1)}, u32[]{:S(2)}, u32[]{:S(2)}) collective-permute-start(bf16[672,128]{1,0:T(8,128)(2,1)S(1)} %get-tuple-element.51), channel_id=1, source_target_pairs={{16,0},{32,16},{48,32},{64,48},{80,64},{96,80},{112,96},{128,112},... | collective-permute-start | bytes 516104 | tf_op jit(solution)/shard_map/ppermute | solution.py:472
  13.6 20.6 %all_to_all.15 = f32[64,1,128]{2,1,0:T(1,128)S(1)} all-to-all(f32[64,1,128]{2,1,0:T(1,128)S(1)} %bitcast.12), channel_id=1, replica_groups={{2,4,8,14,18,20,24,30,34,36,40,46,50,52,56,62,66,68,72,78,82,84,88,94,9..., dimensions={0} | all-to-all | bytes 65536 | tf_op jit(solution)/shard_map/all_to_all | solution.py:473
  34.2 0.0 collective-permute-done.3.later_ref
  34.2 0.5 shard_map.89.v_ref
  34.7 1.2 %shard_map.90 = (f32[16,14,8,128]{3,2,1,0:T(8,128)S(1)}, bf16[128,1024]{1,0:T(8,128)(2,1)S(1)}, f32[16,128]{1,0:T(8,128)S(1)}) custom-call(bf16[4,8,32,128]{3,2,1,0:T(8,128)(2,1)S(1)} %get-tuple-element.36.x_ref, f32[64,128]{1,0:T(8,128)S(1)} %bitcast.11, f32[1,128]{1,0:T(1,128)S(1)} %get-tuple-element.53.gain_ref, f32[1,128]{1,0:T(1,128)S(1)} %get-tuple-element.54.bias_ref, ...), custom_call_target="tpu_custom_call" | custom-call | flops 452984832 | bytes 6202368 | tf_op jit(solution)/shard_map/pallas_call | solution.py:27
  35.9 3.2 %collective-permute-start.4 = (f32[16,14,8,128]{3,2,1,0:T(8,128)S(1)}, f32[16,14,8,128]{3,2,1,0:T(8,128)S(1)}, u32[]{:S(2)}, u32[]{:S(2)}) collective-permute-start(f32[16,14,8,128]{3,2,1,0:T(8,128)S(1)} %get-tuple-element.61), channel_id=1, source_target_pairs={{0,1},{1,0},{2,3},{3,2},{4,5},{5,4},{6,7},{7,6},{8,9},{9,8},{10,11... | collective-permute-start | bytes 2752520 | tf_op jit(solution)/shard_map/ppermute | solution.py:487
  39.1 1.8 %shard_map.91 = (f32[1024,128]{1,0:T(8,128)S(1)}, f32[8,128]{1,0:T(8,128)S(1)}) custom-call(bf16[4,8,32,128]{3,2,1,0:T(8,128)(2,1)S(1)} %get-tuple-element.36.x_ref, f32[16,128]{1,0:T(8,128)S(1)} %get-tuple-element.57.norm_ref, f32[1,128]{1,0:T(1,128)S(1)} %get-tuple-element.53.gain_ref, f32[1,128]{1,0:T(1,128)S(1)} %get-tuple-element.54.bias_ref, ...), custom_call_target="tpu_custom_call" | custom-call | flops 452984832 | bytes 6927360 | tf_op jit(solution)/shard_map/pallas_call | solution.py:27
  40.9 0.1 collective-permute-start.5
  41.0 0.7 %shard_map.92.own_ref = f32[16,14,8,128]{3,2,1,0:T(8,128)S(1)} custom-call(bf16[128,1024]{1,0:T(8,128)(2,1)S(1)} %get-tuple-element.60.turned_ref, bf16[8,256,1152]{2,1,0:T(8,128)(2,1)S(1)} %shard_map.89.v_ref), custom_call_target="tpu_custom_call" | custom-call | flops 452984832 | bytes 5898240 | tf_op jit(solution)/shard_map/pallas_call | solution.py:27
  41.8 0.4 collective-permute-done.5.other_sums_ref
  42.2 0.0 collective-permute-done.4.other_ref
  42.2 0.2 shard_map.93
  42.3 13.5 %all_to_all.16.in_ref = bf16[16,120,128]{2,1,0:T(8,128)(2,1)S(1)} all-to-all(bf16[16,120,128]{2,1,0:T(8,128)(2,1)S(1)} %shard_map.93), channel_id=1, replica_groups=mesh['tm'=16,'rows'=8,'sect'=2] {'tm'}, dimensions={0} | all-to-all | bytes 983040 | tf_op jit(solution)/shard_map/all_to_all | solution.py:505
  55.8 0.2 shard_map.94
  56.0 13.4 %all_to_all.17 = f16[8,120,128]{2,1,0:T(8,128)(2,1)S(1)} all-to-all(f16[8,120,128]{2,1,0:T(8,128)(2,1)S(1)} %broadcast_in_dim.10), channel_id=1, replica_groups=mesh['tm'=16,'rows'=8,'sect'=2] {'rows'}, dimensions={0} | all-to-all | bytes 491520 | tf_op jit(solution)/shard_map/all_to_all | solution.py:508
  69.5 3.0 %collective-permute-start.6 = (f32[112,128]{1,0:T(8,128)S(1)}, f32[112,128]{1,0:T(8,128)S(1)}, u32[]{:S(2)}, u32[]{:S(2)}) collective-permute-start(f32[112,128]{1,0:T(8,128)S(1)} %get-tuple-element.67.half_ref), channel_id=1, source_target_pairs={{0,1},{1,0},{2,3},{3,2},{4,5},{5,4},{6,7},{7,6},{8,9},{9,8},{10,11... | collective-permute-start | bytes 172040 | tf_op jit(solution)/shard_map/ppermute | solution.py:514
  72.6 1.0 %shard_map.96 = (bf16[4,8,32,128]{3,2,1,0:T(8,128)(2,1)}, f32[1,128]{1,0:T(1,128)}, f32[1,128]{1,0:T(1,128)}) custom-call(bf16[4,8,32,128]{3,2,1,0:T(8,128)(2,1)S(1)} %get-tuple-element.36.x_ref, f32[1024,128]{1,0:T(8,128)S(1)} %get-tuple-element.59.da_ref, f32[16,128]{1,0:T(8,128)S(1)} %get-tuple-element.57.norm_ref, ...), custom_call_target="tpu_custom_call" | custom-call | bytes 1062400 | tf_op jit(solution)/shard_map/pallas_call | solution.py:27
  73.6 0.0 collective-permute-done.6.other_ref
  73.6 0.7 shard_map.97
  (6 shorter events, 0.2 us)
Async XLA Ops:
  2.0 4.2 %collective-permute-start = (bf16[48,128]{1,0:T(8,128)(2,1)S(1)}, bf16[48,128]{1,0:T(8,128)(2,1)S(1)}, u32[]{:S(2)}, u32[]{:S(2)}) collective-permute-start(bf16[48,128]{1,0:T(8,128)(2,1)S(1)} %get-tuple-element.38), channel_id=1, source_target_pairs={{0,1},{1,0},{2,3},{3,2},{4,5},{5,4},{6,7},{7,6},{8,9},{9,8},{10,11... | collective-permute-start | bytes 36872 | tf_op jit(solution)/shard_map/ppermute | solution.py:443
  6.2 6.0 %collective-permute-start.1 = (bf16[144,128]{1,0:T(8,128)(2,1)S(1)}, bf16[144,128]{1,0:T(8,128)(2,1)S(1)}, u32[]{:S(2)}, u32[]{:S(2)}) collective-permute-start(bf16[144,128]{1,0:T(8,128)(2,1)S(1)} %get-tuple-element.43), channel_id=1, source_target_pairs={{0,2},{2,0},{4,6},{6,4},{8,10},{10,8},{12,14},{14,12},{1,3},{3,1},... | collective-permute-start | bytes 110600 | tf_op jit(solution)/shard_map/ppermute | solution.py:455
  6.3 5.9 %collective-permute-start.2 = (bf16[144,128]{1,0:T(8,128)(2,1)S(1)}, bf16[144,128]{1,0:T(8,128)(2,1)S(1)}, u32[]{:S(2)}, u32[]{:S(2)}) collective-permute-start(bf16[144,128]{1,0:T(8,128)(2,1)S(1)} %get-tuple-element.48), channel_id=1, source_target_pairs={{0,14},{2,4},{4,2},{6,8},{8,6},{10,12},{12,10},{14,0},{1,15},{3,5}... | collective-permute-start | bytes 110600 | tf_op jit(solution)/shard_map/ppermute | solution.py:456
  12.3 21.9 %collective-permute-start.3 = (bf16[672,128]{1,0:T(8,128)(2,1)S(1)}, bf16[672,128]{1,0:T(8,128)(2,1)S(1)}, u32[]{:S(2)}, u32[]{:S(2)}) collective-permute-start(bf16[672,128]{1,0:T(8,128)(2,1)S(1)} %get-tuple-element.51), channel_id=1, source_target_pairs={{16,0},{32,16},{48,32},{64,48},{80,64},{96,80},{112,96},{128,112},... | collective-permute-start | bytes 516104 | tf_op jit(solution)/shard_map/ppermute | solution.py:472
  35.9 6.2 %collective-permute-start.4 = (f32[16,14,8,128]{3,2,1,0:T(8,128)S(1)}, f32[16,14,8,128]{3,2,1,0:T(8,128)S(1)}, u32[]{:S(2)}, u32[]{:S(2)}) collective-permute-start(f32[16,14,8,128]{3,2,1,0:T(8,128)S(1)} %get-tuple-element.61), channel_id=1, source_target_pairs={{0,1},{1,0},{2,3},{3,2},{4,5},{5,4},{6,7},{7,6},{8,9},{9,8},{10,11... | collective-permute-start | bytes 2752520 | tf_op jit(solution)/shard_map/ppermute | solution.py:487
  40.9 1.3 %collective-permute-start.5 = (f32[8,128]{1,0:T(8,128)S(1)}, f32[8,128]{1,0:T(8,128)S(1)}, u32[]{:S(2)}, u32[]{:S(2)}) collective-permute-start(f32[8,128]{1,0:T(8,128)S(1)} %get-tuple-element.62.sums_ref), channel_id=1, source_target_pairs={{0,1},{1,0},{2,3},{3,2},{4,5},{5,4},{6,7},{7,6},{8,9},{9,8},{10,11... | collective-permute-start | bytes 12296 | tf_op jit(solution)/shard_map/ppermute | solution.py:495
  69.5 4.1 %collective-permute-start.6 = (f32[112,128]{1,0:T(8,128)S(1)}, f32[112,128]{1,0:T(8,128)S(1)}, u32[]{:S(2)}, u32[]{:S(2)}) collective-permute-start(f32[112,128]{1,0:T(8,128)S(1)} %get-tuple-element.67.half_ref), channel_id=1, source_target_pairs={{0,1},{1,0},{2,3},{3,2},{4,5},{5,4},{6,7},{7,6},{8,9},{9,8},{10,11... | collective-permute-start | bytes 172040 | tf_op jit(solution)/shard_map/ppermute | solution.py:514

commit v11 on v10

--- a/solution.py
+++ b/solution.py
@@ -197,8 +197,19 @@
                 total = term if total is None else total + term
         dh_ref[f * 256 + 32 : f * 256 + 224] = total
 
-
-def spread_kernel(near_ref, far_ref, later_ref, own_ref, v_ref):
+    @pl.when(lax.axis_index("tm") == 0)
+    def _():
+        fold_first(v_ref, 32, 224)
+        dh_ref[32:224] += times_taps(v_ref[0, 32:224], taps_ref, 1) + times_taps(v_ref[6, 32:224], taps_ref, 0)
+
+
+def fold_first(v_ref, lo, hi):
+    both = v_ref[1, lo:hi].astype(F32) + v_ref[0, lo:hi].astype(F32)
+    v_ref[6, lo:hi] = both.astype(BF16)
+    v_ref[7, lo:hi] = (both + v_ref[2, lo:hi].astype(F32)).astype(BF16)
+
+
+def spread_edges(near_ref, far_ref, later_ref, v_ref):
     (above, above_column), (below, below_column) = beyond(near_ref, far_ref)
     row_first = lax.axis_index("rows") == 0
     row_last = lax.axis_index("rows") == lax.axis_size("rows") - 1
@@ -223,9 +234,8 @@
 
     @pl.when(lax.axis_index("tm") == 0)
     def _():
-        both = v_ref[1].astype(F32) + v_ref[0].astype(F32)
-        v_ref[6] = both.astype(BF16)
-        v_ref[7] = (both + v_ref[2].astype(F32)).astype(BF16)
+        fold_first(v_ref, 0, 32)
+        fold_first(v_ref, 224, 256)
 
 
 def grad_kernel(x_ref, norm_ref, gain_ref, bias_ref, taps_ref, part_ref, v_ref, da_ref, sums_ref, dh_ref):
@@ -246,7 +256,9 @@
 
     @pl.when(lax.axis_index("tm") == 0)
     def _():
-        dh_ref[0:256] += times_taps(v_ref[0], taps_ref, 1) + times_taps(v_ref[6], taps_ref, 0)
+        more = times_taps(edges(0, 1), taps_ref, 1) + times_taps(edges(6, 7), taps_ref, 0)
+        dh_ref[0:32] += more[:32]
+        dh_ref[224:256] += more[32:]
 
     bias_sum = jnp.zeros((8, 128), F32)
     gain_sum = jnp.zeros((8, 128), F32)
@@ -293,7 +305,10 @@
     return xhat, xhat * gain_ref[...] + bias_ref[...]
 
 
-def away_kernel(counted, x_ref, stat_ref, gain_ref, bias_ref, v_ref, w_ref, turned_ref, norm_ref):
+def away_kernel(
+    counted, near_ref, far_ref, later_ref, x_ref, stat_ref, gain_ref, bias_ref, begun_ref, w_ref, turned_ref, norm_ref, v_ref
+):
+    spread_edges(near_ref, far_ref, later_ref, v_ref)
     total, square = sums_to_pair(column_sum(stat_ref[...]))
     mean = total / counted
     norm_ref[0:8] = mean
@@ -472,17 +487,17 @@
     later = lax.ppermute(early, "tm", [(i + 1, i) for i in range(n_time - 1)])
     stat = lax.all_to_all(stat[:, None], ("tm", "rows"), 0, 0, axis_index_groups=groups).reshape(-1, channels)
     stat, later = lax.optimization_barrier((stat, later))
-    (spread,) = call(
-        spread_kernel,
-        [pltpu.VMEM((8, 256, 1152), BF16)],
-        [nearer, farther, later, held(spread, pltpu.VMEM)],
-        aliases={3: 0},
-    )
-    away, turned, norm = call(
+    away, turned, norm, spread = call(
         functools.partial(away_kernel, counted),
-        [shape_of((16, HALF, 8, 128)), shape_of((channels, cells), BF16), shape_of((16, channels))],
-        [x, stat, gain, bias, held(spread, pltpu.VMEM)],
+        [
+            shape_of((16, HALF, 8, 128)),
+            shape_of((channels, cells), BF16),
+            shape_of((16, channels)),
+            pltpu.VMEM((8, 256, 1152), BF16),
+        ],
+        [nearer, farther, later, x, stat, gain, bias, held(spread, pltpu.VMEM)],
         flops=cells * TAPS * channels * channels,
+        aliases={7: 3},
     )
     arrived = lax.ppermute(away, "sect", swap)
     da, sums = call(

time: 74.5 us -> 73.8 us (level)
  blocking collectives: 47.5 us -> 46.3 us
    pallas_call x14 -> x13, Pallas kernels: 9.3 us -> 9.37 us  [call(): pl.pallas_call(body, out_shape=outs, in_specs=specs or [VMEM] * len(args)...]
where the time goes in v11:
time: 73.8 us; the launch traced here: 73.6 us
  blocking collectives  46.3 us (63%)
  starting transfers between devices  16.1 us (22%)
  Pallas kernels  9.37 us (13%)
  waiting for transfers between devices  1.02 us (1%)
  between operations  0.74 us (1%)
    all_to_all x1, blocking collectives, local(): lax.all_to_all(stat[:, None], ('tm', 'rows'), 0, 0, axis_index_groups=gro...  20.2 us
    all_to_all x1, blocking collectives, local(): gathered = lax.all_to_all(sent, 'tm', 0, 0)  13.2 us
    all_to_all x1, blocking collectives, local(): shares = lax.all_to_all(share, 'rows', 0, 0).astype(F32)  12.8 us
    pallas_call x13, Pallas kernels, call(): pl.pallas_call(body, out_shape=outs, in_specs=specs or [VMEM] * len(args)...  9.37 us
    ppermute x1, starting transfers between devices, local(): farther = lax.ppermute(farther, 'rows', far)  4.55 us
    ppermute x1, starting transfers between devices, local(): other = lax.ppermute(half, 'sect', swap)  3.6 us
    ppermute x1, starting transfers between devices, local(): side = lax.ppermute(facing, 'sect', swap)  3.33 us
    ppermute x1, starting transfers between devices, local(): arrived = lax.ppermute(away, 'sect', swap)  3.16 us
  transfers between devices with their start and end apart: 7, of which 2 were waited for; matrix products, arithmetic and copies ran while one was open for 0% of the time, Pallas kernels for 7%

profile of v11, /device:TPU:1, one launch (start us, length us, event | category | flops | bytes accessed | tf_op | source)
XLA Modules:
  0.0 73.6 jit_solution(15614743708701664429)
XLA Ops:
  0.6 1.4 %shard_map.84 = (bf16[4,8,32,128]{3,2,1,0:T(8,128)(2,1)S(1)}, bf16[4,8,32,128]{3,2,1,0:T(8,128)(2,1)S(1)}, f32[1,128]{1,0:T(1,128)S(1)}, f32[1,128]{1,0:T(1,128)...) custom-call(bf16[4,8,32,128]{3,2,1,0:T(8,128)(2,1)} %up_hbm.1, ...), custom_call_target="tpu_custom_call" | custom-call | bytes 2836480 | tf_op jit(solution)/shard_map/pallas_call | solution.py:27
  2.0 3.3 %collective-permute-start = (bf16[48,128]{1,0:T(8,128)(2,1)S(1)}, bf16[48,128]{1,0:T(8,128)(2,1)S(1)}, u32[]{:S(2)}, u32[]{:S(2)}) collective-permute-start(bf16[48,128]{1,0:T(8,128)(2,1)S(1)} %get-tuple-element.39), channel_id=1, source_target_pairs={{0,1},{1,0},{2,3},{3,2},{4,5},{5,4},{6,7},{7,6},{8,9},{9,8},{10,11... | collective-permute-start | bytes 36872 | tf_op jit(solution)/shard_map/ppermute | solution.py:458
  5.4 0.2 shard_map.85
  5.6 0.6 collective-permute-done.side_ref
  6.2 0.1 collective-permute-start.1
  6.3 4.6 %collective-permute-start.2 = (bf16[144,128]{1,0:T(8,128)(2,1)S(1)}, bf16[144,128]{1,0:T(8,128)(2,1)S(1)}, u32[]{:S(2)}, u32[]{:S(2)}) collective-permute-start(bf16[144,128]{1,0:T(8,128)(2,1)S(1)} %get-tuple-element.49), channel_id=1, source_target_pairs={{0,14},{2,4},{4,2},{6,8},{8,6},{10,12},{12,10},{14,0},{1,15},{3,5}... | collective-permute-start | bytes 110600 | tf_op jit(solution)/shard_map/ppermute | solution.py:471
  10.9 1.7 %shard_map.87 = (bf16[8,256,1152]{2,1,0:T(8,128)(2,1)S(1)}, f32[1024,128]{1,0:T(8,128)S(1)}) custom-call(bf16[4,8,32,128]{3,2,1,0:T(8,128)(2,1)S(1)} %get-tuple-element.38.up_ref, bf16[48,128]{1,0:T(8,128)(2,1)S(1)} %collective-permute-done.side_ref, bf16[3,128,1152]{2,1,0:T(8,128)(2,1)S(1)} %get-tuple-element.45.taps_ref, ...), custom_call_target="tpu_custom_call", output_to_operand_aliasing={{0}: (3, {})} | custom-call | flops 452984832 | bytes 11120640 | tf_op jit(solution)/shard_map/pallas_call | solution.py:27
  12.6 0.0 collective-permute-done.1.near_ref
  12.6 0.0 collective-permute-done.2.far_ref
  12.7 1.3 %collective-permute-start.3 = (bf16[672,128]{1,0:T(8,128)(2,1)S(1)}, bf16[672,128]{1,0:T(8,128)(2,1)S(1)}, u32[]{:S(2)}, u32[]{:S(2)}) collective-permute-start(bf16[672,128]{1,0:T(8,128)(2,1)S(1)} %get-tuple-element.52), channel_id=1, source_target_pairs={{16,0},{32,16},{48,32},{64,48},{80,64},{96,80},{112,96},{128,112},... | collective-permute-start | bytes 516104 | tf_op jit(solution)/shard_map/ppermute | solution.py:487
  14.0 20.2 %all_to_all.15 = f32[64,1,128]{2,1,0:T(1,128)S(1)} all-to-all(f32[64,1,128]{2,1,0:T(1,128)S(1)} %bitcast.12), channel_id=1, replica_groups={{2,4,8,14,18,20,24,30,34,36,40,46,50,52,56,62,66,68,72,78,82,84,88,94,9..., dimensions={0} | all-to-all | bytes 65536 | tf_op jit(solution)/shard_map/all_to_all | solution.py:488
  34.2 0.0 collective-permute-done.3.later_ref
  34.2 1.5 %shard_map.89 = (f32[16,14,8,128]{3,2,1,0:T(8,128)S(1)}, bf16[128,1024]{1,0:T(8,128)(2,1)S(1)}, f32[16,128]{1,0:T(8,128)S(1)}, bf16[8,256,1152]{2,1,0:T(8,128)(2,1)S(1)}) custom-call(bf16[144,128]{1,0:T(8,128)(2,1)S(1)} %collective-permute-done.1.near_ref, bf16[144,128]{1,0:T(8,128)(2,1)S(1)} %collective-permute-done.2.far_ref, ...), custom_call_target="tpu_custom_call", output_to_operand_aliasing={{3}: (7, {})} | custom-call | flops 452984832 | bytes 11166720 | tf_op jit(solution)/shard_map/pallas_call | solution.py:27
  35.7 3.2 %collective-permute-start.4 = (f32[16,14,8,128]{3,2,1,0:T(8,128)S(1)}, f32[16,14,8,128]{3,2,1,0:T(8,128)S(1)}, u32[]{:S(2)}, u32[]{:S(2)}) collective-permute-start(f32[16,14,8,128]{3,2,1,0:T(8,128)S(1)} %get-tuple-element.63), channel_id=1, source_target_pairs={{0,1},{1,0},{2,3},{3,2},{4,5},{5,4},{6,7},{7,6},{8,9},{9,8},{10,11... | collective-permute-start | bytes 2752520 | tf_op jit(solution)/shard_map/ppermute | solution.py:502
  38.9 1.7 %shard_map.90 = (f32[1024,128]{1,0:T(8,128)S(1)}, f32[8,128]{1,0:T(8,128)S(1)}) custom-call(bf16[4,8,32,128]{3,2,1,0:T(8,128)(2,1)S(1)} %get-tuple-element.37.x_ref, f32[16,128]{1,0:T(8,128)S(1)} %get-tuple-element.58.norm_ref, f32[1,128]{1,0:T(1,128)S(1)} %get-tuple-element.55.gain_ref, f32[1,128]{1,0:T(1,128)S(1)} %get-tuple-element.56.bias_ref, ...), custom_call_target="tpu_custom_call" | custom-call | flops 452984832 | bytes 6927360 | tf_op jit(solution)/shard_map/pallas_call | solution.py:27
  40.6 0.1 collective-permute-start.5
  40.7 0.7 shard_map.91.own_ref
  41.4 0.4 collective-permute-done.5.other_sums_ref
  41.8 0.0 collective-permute-done.4.other_ref
  41.8 0.2 shard_map.92
  42.0 13.2 %all_to_all.16.in_ref = bf16[16,120,128]{2,1,0:T(8,128)(2,1)S(1)} all-to-all(bf16[16,120,128]{2,1,0:T(8,128)(2,1)S(1)} %shard_map.92), channel_id=1, replica_groups=mesh['tm'=16,'rows'=8,'sect'=2] {'tm'}, dimensions={0} | all-to-all | bytes 983040 | tf_op jit(solution)/shard_map/all_to_all | solution.py:520
  55.2 0.2 shard_map.93
  55.4 12.8 %all_to_all.17 = f16[8,120,128]{2,1,0:T(8,128)(2,1)S(1)} all-to-all(f16[8,120,128]{2,1,0:T(8,128)(2,1)S(1)} %broadcast_in_dim.10), channel_id=1, replica_groups=mesh['tm'=16,'rows'=8,'sect'=2] {'rows'}, dimensions={0} | all-to-all | bytes 491520 | tf_op jit(solution)/shard_map/all_to_all | solution.py:523
  68.3 3.6 %collective-permute-start.6 = (f32[112,128]{1,0:T(8,128)S(1)}, f32[112,128]{1,0:T(8,128)S(1)}, u32[]{:S(2)}, u32[]{:S(2)}) collective-permute-start(f32[112,128]{1,0:T(8,128)S(1)} %get-tuple-element.69.half_ref), channel_id=1, source_target_pairs={{0,1},{1,0},{2,3},{3,2},{4,5},{5,4},{6,7},{7,6},{8,9},{9,8},{10,11... | collective-permute-start | bytes 172040 | tf_op jit(solution)/shard_map/ppermute | solution.py:529
  71.9 1.0 %shard_map.95 = (bf16[4,8,32,128]{3,2,1,0:T(8,128)(2,1)}, f32[1,128]{1,0:T(1,128)}, f32[1,128]{1,0:T(1,128)}) custom-call(bf16[4,8,32,128]{3,2,1,0:T(8,128)(2,1)S(1)} %get-tuple-element.37.x_ref, f32[1024,128]{1,0:T(8,128)S(1)} %get-tuple-element.61.da_ref, f32[16,128]{1,0:T(8,128)S(1)} %get-tuple-element.58.norm_ref, ...), custom_call_target="tpu_custom_call" | custom-call | bytes 1062400 | tf_op jit(solution)/shard_map/pallas_call | solution.py:27
  73.0 0.0 collective-permute-done.6.other_ref
  73.0 0.7 shard_map.96
  (6 shorter events, 0.2 us)
Async XLA Ops:
  2.0 4.2 %collective-permute-start = (bf16[48,128]{1,0:T(8,128)(2,1)S(1)}, bf16[48,128]{1,0:T(8,128)(2,1)S(1)}, u32[]{:S(2)}, u32[]{:S(2)}) collective-permute-start(bf16[48,128]{1,0:T(8,128)(2,1)S(1)} %get-tuple-element.39), channel_id=1, source_target_pairs={{0,1},{1,0},{2,3},{3,2},{4,5},{5,4},{6,7},{7,6},{8,9},{9,8},{10,11... | collective-permute-start | bytes 36872 | tf_op jit(solution)/shard_map/ppermute | solution.py:458
  6.2 6.4 %collective-permute-start.1 = (bf16[144,128]{1,0:T(8,128)(2,1)S(1)}, bf16[144,128]{1,0:T(8,128)(2,1)S(1)}, u32[]{:S(2)}, u32[]{:S(2)}) collective-permute-start(bf16[144,128]{1,0:T(8,128)(2,1)S(1)} %get-tuple-element.44), channel_id=1, source_target_pairs={{0,2},{2,0},{4,6},{6,4},{8,10},{10,8},{12,14},{14,12},{1,3},{3,1},... | collective-permute-start | bytes 110600 | tf_op jit(solution)/shard_map/ppermute | solution.py:470
  6.3 6.3 %collective-permute-start.2 = (bf16[144,128]{1,0:T(8,128)(2,1)S(1)}, bf16[144,128]{1,0:T(8,128)(2,1)S(1)}, u32[]{:S(2)}, u32[]{:S(2)}) collective-permute-start(bf16[144,128]{1,0:T(8,128)(2,1)S(1)} %get-tuple-element.49), channel_id=1, source_target_pairs={{0,14},{2,4},{4,2},{6,8},{8,6},{10,12},{12,10},{14,0},{1,15},{3,5}... | collective-permute-start | bytes 110600 | tf_op jit(solution)/shard_map/ppermute | solution.py:471
  12.7 21.5 %collective-permute-start.3 = (bf16[672,128]{1,0:T(8,128)(2,1)S(1)}, bf16[672,128]{1,0:T(8,128)(2,1)S(1)}, u32[]{:S(2)}, u32[]{:S(2)}) collective-permute-start(bf16[672,128]{1,0:T(8,128)(2,1)S(1)} %get-tuple-element.52), channel_id=1, source_target_pairs={{16,0},{32,16},{48,32},{64,48},{80,64},{96,80},{112,96},{128,112},... | collective-permute-start | bytes 516104 | tf_op jit(solution)/shard_map/ppermute | solution.py:487
  35.7 6.1 %collective-permute-start.4 = (f32[16,14,8,128]{3,2,1,0:T(8,128)S(1)}, f32[16,14,8,128]{3,2,1,0:T(8,128)S(1)}, u32[]{:S(2)}, u32[]{:S(2)}) collective-permute-start(f32[16,14,8,128]{3,2,1,0:T(8,128)S(1)} %get-tuple-element.63), channel_id=1, source_target_pairs={{0,1},{1,0},{2,3},{3,2},{4,5},{5,4},{6,7},{7,6},{8,9},{9,8},{10,11... | collective-permute-start | bytes 2752520 | tf_op jit(solution)/shard_map/ppermute | solution.py:502
  40.6 1.3 %collective-permute-start.5 = (f32[8,128]{1,0:T(8,128)S(1)}, f32[8,128]{1,0:T(8,128)S(1)}, u32[]{:S(2)}, u32[]{:S(2)}) collective-permute-start(f32[8,128]{1,0:T(8,128)S(1)} %get-tuple-element.64.sums_ref), channel_id=1, source_target_pairs={{0,1},{1,0},{2,3},{3,2},{4,5},{5,4},{6,7},{7,6},{8,9},{9,8},{10,11... | collective-permute-start | bytes 12296 | tf_op jit(solution)/shard_map/ppermute | solution.py:510
  68.3 4.6 %collective-permute-start.6 = (f32[112,128]{1,0:T(8,128)S(1)}, f32[112,128]{1,0:T(8,128)S(1)}, u32[]{:S(2)}, u32[]{:S(2)}) collective-permute-start(f32[112,128]{1,0:T(8,128)S(1)} %get-tuple-element.69.half_ref), channel_id=1, source_target_pairs={{0,1},{1,0},{2,3},{3,2},{4,5},{5,4},{6,7},{7,6},{8,9},{9,8},{10,11... | collective-permute-start | bytes 172040 | tf_op jit(solution)/shard_map/ppermute | solution.py:529

commit v12 on v11

--- a/solution.py
+++ b/solution.py
@@ -34,6 +34,21 @@
         cost_estimate=pl.CostEstimate(flops=flops, bytes_accessed=moved, transcendentals=0),
         compiler_params=pltpu.CompilerParams(vmem_limit_bytes=24 * 1024 * 1024),
     )(*args)
+
+
+class Frames:
+    def __init__(self, refs):
+        self.refs = refs
+
+    def __getitem__(self, index):
+        index = index if isinstance(index, tuple) else (index,)
+        rest = index[1:] or (slice(None),)
+        if isinstance(index[0], slice):
+            return jnp.stack([ref[rest] for ref in self.refs[index[0]]])
+        return self.refs[index[0]][rest]
+
+    def __setitem__(self, index, value):
+        self.refs[index[0]][index[1:]] = value
 
 
 def lanes_of(shape):
@@ -125,7 +140,9 @@
     return above, below
 
 
-def early_kernel(up_ref, side_ref, near_ref, far_ref, stat_ref, early_ref, sent_ref):
+def early_kernel(up_ref, side_ref, near_ref, far_ref, stat_ref, early_ref, sent_ref, near_kept_ref, far_kept_ref):
+    near_kept_ref[...] = near_ref[...]
+    far_kept_ref[...] = far_ref[...]
     row = stat_ref[...] + join_row(near_ref[128:].astype(F32)[4:8])
     sent_ref[...] = jnp.broadcast_to(row[None], (sent_ref.shape[0] // 8, 8, 128)).reshape(sent_ref.shape)
     (above, above_column), (below, below_column) = beyond(near_ref, far_ref)
@@ -173,7 +190,8 @@
     put(v_ref, f, 7, 2, e, low[None])
 
 
-def taps_kernel(up_ref, kernel_ref, v_ref, taps_ref):
+def taps_kernel(up_ref, kernel_ref, taps_ref, *v_refs):
+    v_ref = Frames(v_refs)
     for a in range(3):
         for b in range(3):
             for e in range(3):
@@ -183,7 +201,9 @@
         put_own(v_ref, f, 1, up_ref[f].astype(F32))
 
 
-def own_kernel(up_ref, side_ref, taps_ref, begun_ref, v_ref, dh_ref):
+def own_kernel(up_ref, side_ref, taps_ref, *refs):
+    dh_ref = refs[8]
+    v_ref = Frames(refs[4:8])
     columns = columns_of(side_ref)
     for f in range(4):
         ahead, _, behind = column_taps(up_ref[f].astype(F32), columns[f])
@@ -199,8 +219,8 @@
 
     @pl.when(lax.axis_index("tm") == 0)
     def _():
-        fold_first(v_ref, 32, 224)
-        dh_ref[32:224] += times_taps(v_ref[0, 32:224], taps_ref, 1) + times_taps(v_ref[6, 32:224], taps_ref, 0)
+        both = (v_ref[1, 32:224].astype(F32) + v_ref[0, 32:224].astype(F32)).astype(BF16)
+        dh_ref[32:224] += times_taps(v_ref[0, 32:224], taps_ref, 1) + times_taps(both, taps_ref, 0)
 
 
 def fold_first(v_ref, lo, hi):
@@ -234,11 +254,12 @@
 
     @pl.when(lax.axis_index("tm") == 0)
     def _():
-        fold_first(v_ref, 0, 32)
-        fold_first(v_ref, 224, 256)
-
-
-def grad_kernel(x_ref, norm_ref, gain_ref, bias_ref, taps_ref, part_ref, v_ref, da_ref, sums_ref, dh_ref):
+        fold_first(v_ref, 0, 256)
+
+
+def grad_kernel(x_ref, norm_ref, gain_ref, bias_ref, taps_ref, part_ref, *refs):
+    v_ref = Frames(refs[:8])
+    da_ref, sums_ref, dh_ref = refs[8:]
     def edges(lo, hi):
         return jnp.concatenate([v_ref[lo:hi, 0:32], v_ref[lo:hi, 224:256]], axis=1).reshape((hi - lo) * 64, 1152)
 
@@ -282,8 +303,8 @@
 def product_of(turned, v_ref, a, lo, hi):
     if a == 2:
         return jnp.dot(turned, v_ref[0:4, :, lo:hi].reshape(1024, hi - lo), preferred_element_type=F32)
-    source = jnp.where(lax.axis_index("tm") == 0, 7 - a, 2 - a)
-    first = jnp.dot(turned[:, :256], v_ref[source, :, lo:hi], preferred_element_type=F32)
+    source = jnp.where(lax.axis_index("tm") == 0, v_ref[7 - a, :, lo:hi], v_ref[2 - a, :, lo:hi])
+    first = jnp.dot(turned[:, :256], source, preferred_element_type=F32)
     rest = v_ref[3 - a : 6 - a, :, lo:hi].reshape(768, hi - lo)
     return first + jnp.dot(turned[:, 256:], rest, preferred_element_type=F32)
 
@@ -306,10 +327,22 @@
 
 
 def away_kernel(
-    counted, near_ref, far_ref, later_ref, x_ref, stat_ref, gain_ref, bias_ref, begun_ref, w_ref, turned_ref, norm_ref, v_ref
+    counted,
+    near_ref,
+    far_ref,
+    later_ref,
+    x_ref,
+    stat_ref,
+    handed_ref,
+    gain_ref,
+    bias_ref,
+    *refs,
 ):
+    w_ref, turned_ref, norm_ref = refs[4:7]
+    v_ref = Frames(refs[7:15])
     spread_edges(near_ref, far_ref, later_ref, v_ref)
-    total, square = sums_to_pair(column_sum(stat_ref[...]))
+    row = jnp.where(lax.axis_index("sect") == 0, handed_ref[...], stat_ref[...])
+    total, square = sums_to_pair(jnp.broadcast_to(row, (8, 128)))
     mean = total / counted
     norm_ref[0:8] = mean
     norm_ref[8:16] = lax.rsqrt(square / counted - mean * mean + 1e-06)
@@ -328,7 +361,9 @@
         half_product(0, turned_ref[...], v_ref, w_ref)
 
 
-def home_kernel(turned_ref, v_ref, w_ref):
+def home_kernel(turned_ref, *refs):
+    v_ref = Frames(refs[:8])
+    w_ref = refs[8]
     left = lax.axis_index("sect") == 0
 
     @pl.when(left)
@@ -438,7 +473,7 @@
         entry_kernel,
         [
             shape_of(upstream.shape, BF16),
-            shape_of(activations.shape, BF16),
+            pltpu.VMEM(activations.shape, BF16),
             shape_of((1, channels)),
             shape_of((1, channels)),
             shape_of(kernel.shape, BF16),
@@ -456,10 +491,13 @@
         [pltpu.SemaphoreType.DMA((5,))],
     )
     side = lax.ppermute(facing, "sect", swap)
-    spread, taps = call(
-        taps_kernel,
-        [pltpu.VMEM((8, 256, 1152), BF16), shape_of((3, channels, 9 * channels), BF16)],
-        [up, weights],
+    frame = pltpu.VMEM((256, 1152), BF16)
+
+    def kept(arrays):
+        return [held(array, pltpu.VMEM) for array in arrays]
+
+    taps, *spread = call(
+        taps_kernel, [pltpu.VMEM((3, channels, 9 * channels), BF16)] + [frame] * 4, [up, weights]
     )
     side, taps = lax.optimization_barrier((side, taps))
     nearer, farther, stat = call(
@@ -469,41 +507,43 @@
     )
     nearer = lax.ppermute(nearer, "rows", near)
     farther = lax.ppermute(farther, "rows", far)
-    spread, inner = call(
+    *spread, inner = call(
         own_kernel,
-        [pltpu.VMEM((8, 256, 1152), BF16), shape_of((cells, channels))],
-        [up, side, taps, held(spread, pltpu.VMEM)],
+        [frame] * 4 + [pltpu.VMEM((cells, channels), F32)],
+        [up, side] + kept([taps] + spread),
         flops=cells * TAPS * channels * channels,
-        aliases={3: 0},
+        aliases={3 + f: f for f in range(4)},
     )
     nearer, inner = lax.optimization_barrier((nearer, inner))
     groups = [[t * n_rows + r for t in range(n_time) for r in chosen] for chosen in ((1, 2, 4, 7), (0, 3, 5, 6))]
-    early, stat = call(
+    strip = pltpu.VMEM((144, channels), BF16)
+    early, stat, nearer, farther = call(
         early_kernel,
-        [shape_of((672, channels), BF16), shape_of((len(groups[0]), channels))],
+        [shape_of((672, channels), BF16), shape_of((len(groups[0]), channels)), strip, strip],
         [up, side, nearer, farther, stat],
-        [VMEM, VMEM, VMEM, VMEM, VMEM],
     )
     later = lax.ppermute(early, "tm", [(i + 1, i) for i in range(n_time - 1)])
-    stat = lax.all_to_all(stat[:, None], ("tm", "rows"), 0, 0, axis_index_groups=groups).reshape(-1, channels)
-    stat, later = lax.optimization_barrier((stat, later))
-    away, turned, norm, spread = call(
+
+    def over_groups(row):
+        rows = lax.all_to_all(row[:, None], ("tm", "rows"), 0, 0, axis_index_groups=groups)
+        return jnp.sum(rows, axis=0)
+
+    on_second = lax.axis_index("sect") == 1
+    stat = lax.cond(on_second, over_groups, lambda row: row[:1], stat)
+    handed = lax.ppermute(stat, "sect", [(1, 0)])
+    handed, later = lax.optimization_barrier((handed, later))
+    away, turned, norm, *spread = call(
         functools.partial(away_kernel, counted),
-        [
-            shape_of((16, HALF, 8, 128)),
-            shape_of((channels, cells), BF16),
-            shape_of((16, channels)),
-            pltpu.VMEM((8, 256, 1152), BF16),
-        ],
-        [nearer, farther, later, x, stat, gain, bias, held(spread, pltpu.VMEM)],
+        [shape_of((16, HALF, 8, 128)), shape_of((channels, cells), BF16), shape_of((16, channels))] + [frame] * 8,
+        kept([nearer, farther]) + [later] + kept([x]) + [stat, handed, gain, bias] + kept(spread),
         flops=cells * TAPS * channels * channels,
-        aliases={7: 3},
+        aliases={8 + f: 3 + f for f in range(4)},
     )
     arrived = lax.ppermute(away, "sect", swap)
     da, sums = call(
         grad_kernel,
         [shape_of((cells, channels)), shape_of((8, channels))],
-        [x, norm, gain, bias, taps, inner, held(spread, pltpu.VMEM)],
+        kept([x]) + [norm, gain, bias] + kept([taps, inner] + spread),
         scratch=[pltpu.VMEM((cells, channels), F32)],
         flops=cells * TAPS * channels * channels,
     )
@@ -511,7 +551,7 @@
     (home,) = call(
         home_kernel,
         [shape_of((16, HALF, 8, 128))],
-        [turned, held(spread, pltpu.VMEM)],
+        [turned] + kept(spread),
         flops=cells * TAPS * channels * channels,
     )
     (sent,) = call(
@@ -530,7 +570,7 @@
     input_gradient, gain_grad, bias_grad = call(
         functools.partial(finish_kernel, counted, scaling),
         [shape_of(activations.shape, BF16), shape_of((1, 128)), shape_of((1, 128))],
-        [x, da, norm, sums, gain],
+        kept([x]) + [da, norm, sums, gain],
     )
     (whole,) = call(join_kernel, [shape_of((TAPS * 8, 128))], [half, other])
     weight_grad = whole.reshape(3, 3, 3, 8, 128).transpose(0, 1, 2, 4, 3)

time: 73.8 us -> 77.7 us (1.053)
  local copies, waits for them, and re-layouts: 0.04 us -> 2.22 us
  Pallas kernels: 9.37 us -> 11.2 us
  starting transfers between devices: 16.1 us -> 14.8 us
  other arithmetic: 0.04 us -> 0.88 us
    ppermute x1, starting transfers between devices: 3.16 us -> 0.25 us  [local(): arrived = lax.ppermute(away, 'sect', swap)]
    unnamed x0 -> x8, local copies, waits for them, and re-layouts: none -> 2.18 us
    pallas_call x13, Pallas kernels: 9.37 us -> 11.2 us  [call(): pl.pallas_call(body, out_shape=outs, in_specs=specs or [VMEM] * len(args)...]
    ppermute x0 -> x1, starting transfers between devices: none -> 1.28 us  [local(): handed = lax.ppermute(stat, 'sect', [(1, 0)])]
    reduce_sum x0 -> x1, other arithmetic: none -> 0.84 us  [over_groups(): return jnp.sum(rows, axis=0)]
    ppermute x0 -> x1, waiting for transfers between devices: none -> 0.8 us  [local(): handed = lax.ppermute(stat, 'sect', [(1, 0)])]
  transfers between devices with their start and end apart: 7 -> 8, of which waited for: 2 -> 3; matrix products, arithmetic and copies ran while one was open for 0% -> 1% of each run, Pallas kernels for 7% -> 7%
where the time goes in v12:
time: 77.7 us; the launch traced here: 77.2 us
  blocking collectives  45.9 us (59%)
  starting transfers between devices  14.8 us (19%)
  Pallas kernels  11.2 us (14%)
  local copies, waits for them, and re-layouts  2.22 us (3%)
  waiting for transfers between devices  1.47 us (2%)
  other arithmetic  0.88 us (1%)
    all_to_all x1, blocking collectives, over_groups(): lax.all_to_all(row[:, None], ('tm', 'rows'), 0, 0, axis_index_groups=groups)  20.4 us
    all_to_all x1, blocking collectives, local(): gathered = lax.all_to_all(sent, 'tm', 0, 0)  13.3 us
    all_to_all x1, blocking collectives, local(): shares = lax.all_to_all(share, 'rows', 0, 0).astype(F32)  12.2 us
    pallas_call x13, Pallas kernels, call(): pl.pallas_call(body, out_shape=outs, in_specs=specs or [VMEM] * len(args)...  11.2 us
    ppermute x1, starting transfers between devices, local(): farther = lax.ppermute(farther, 'rows', far)  4.55 us
    ppermute x1, starting transfers between devices, local(): other = lax.ppermute(half, 'sect', swap)  3.62 us
    ppermute x1, starting transfers between devices, local(): side = lax.ppermute(facing, 'sect', swap)  3.33 us
    unnamed x8, local copies, waits for them, and re-layouts  2.18 us
  transfers between devices with their start and end apart: 8, of which 3 were waited for; matrix products, arithmetic and copies ran while one was open for 1% of the time, Pallas kernels for 7%

profile of v12, /device:TPU:1, one launch (start us, length us, event | category | flops | bytes accessed | tf_op | source)
XLA Modules:
  0.0 77.2 jit_solution(11174766848656514702)
XLA Ops:
  0.6 1.4 %shard_map.84 = (bf16[4,8,32,128]{3,2,1,0:T(8,128)(2,1)S(1)}, bf16[4,8,32,128]{3,2,1,0:T(8,128)(2,1)S(1)}, f32[1,128]{1,0:T(1,128)S(1)}, f32[1,128]{1,0:T(1,128)...) custom-call(bf16[4,8,32,128]{3,2,1,0:T(8,128)(2,1)} %up_hbm.1, ...), custom_call_target="tpu_custom_call" | custom-call | bytes 2836480 | tf_op jit(solution)/shard_map/pallas_call | solution.py:27
  2.0 3.3 %collective-permute-start = (bf16[48,128]{1,0:T(8,128)(2,1)S(1)}, bf16[48,128]{1,0:T(8,128)(2,1)S(1)}, u32[]{:S(2)}, u32[]{:S(2)}) collective-permute-start(bf16[48,128]{1,0:T(8,128)(2,1)S(1)} %get-tuple-element.59), channel_id=1, source_target_pairs={{0,1},{1,0},{2,3},{3,2},{4,5},{5,4},{6,7},{7,6},{8,9},{9,8},{10,11... | collective-permute-start | bytes 36872 | tf_op jit(solution)/shard_map/ppermute | solution.py:493
  5.4 0.2 shard_map.85
  5.6 0.6 collective-permute-done.side_ref
  6.2 0.1 collective-permute-start.1
  6.3 4.6 %collective-permute-start.2 = (bf16[144,128]{1,0:T(8,128)(2,1)S(1)}, bf16[144,128]{1,0:T(8,128)(2,1)S(1)}, u32[]{:S(2)}, u32[]{:S(2)}) collective-permute-start(bf16[144,128]{1,0:T(8,128)(2,1)S(1)} %get-tuple-element.72), channel_id=1, source_target_pairs={{0,14},{2,4},{4,2},{6,8},{8,6},{10,12},{12,10},{14,0},{1,15},{3,5}... | collective-permute-start | bytes 110600 | tf_op jit(solution)/shard_map/ppermute | solution.py:509
  10.9 1.7 %shard_map.87 = (bf16[256,1152]{1,0:T(8,128)(2,1)S(1)}, bf16[256,1152]{1,0:T(8,128)(2,1)S(1)}, bf16[256,1152]{1,0:T(8,128)(2,1)S(1)}, bf16[256,1152]{1,0:T(8,128)(2,1)S(1)}, f32[1024,128]{1,0:T(8,128)S(1)}) custom-call(bf16[4,8,32,128]{3,2,1,0:T(8,128)(2,1)S(1)} %get-tuple-element.58.up_ref, ...), custom_call_target="tpu_custom_call", output_to_operand_aliasing={{0}: (3, {}), {1}: (4, {}), {2}: (5, {}), {3}: (6, {})} | custom-call | flops 452984832 | bytes 6402048 | tf_op jit(solution)/shard_map/pallas_call | solution.py:27
  12.6 0.0 copy-start
  12.6 0.8 %copy-done = f32[1024,128]{1,0:T(8,128)} copy-done((f32[1024,128]{1,0:T(8,128)}, f32[1024,128]{1,0:T(8,128)S(1)}, u32[]{:S(2)}) %copy-start) | copy-done | bytes 524312
  13.4 0.0 collective-permute-done.1.near_ref
  13.4 0.0 collective-permute-done.2.far_ref
  13.4 0.7 shard_map.88
  14.1 0.0 copy-start.2
  14.1 0.6 copy-done.2
  14.8 1.3 %collective-permute-start.4 = (bf16[672,128]{1,0:T(8,128)(2,1)}, bf16[672,128]{1,0:T(8,128)(2,1)}, u32[]{:S(2)}, u32[]{:S(2)}) collective-permute-start(bf16[672,128]{1,0:T(8,128)(2,1)} %get-tuple-element.77), channel_id=1, source_target_pairs={{16,0},{32,16},{48,32},{64,48},{80,64},{96,80},{112,96},{128,112},... | collective-permute-start | bytes 516104 | tf_op jit(solution)/shard_map/ppermute | solution.py:525
  16.0 21.2 %conditional.1 = (f32[1,128]{1,0:T(1,128)S(1)}) conditional(s32[]{:T(128)} %convert_element_type.9, f32[64,128]{1,0:T(8,128)} %get-tuple-element.76, f32[64,128]{1,0:T(8,128)} %get-tuple-element.76), branch_computations={%region_0.0_spmd, %region_1.0_spmd} | conditional | flops 8064 | bytes 98828 | solution.py:532
  16.1 20.4 %all_to_all.14 = f32[64,1,128]{2,1,0:T(1,128)} all-to-all(f32[64,1,128]{2,1,0:T(1,128)} %bitcast.10), channel_id=1, replica_groups={{2,4,8,14,18,20,24,30,34,36,40,46,50,52,56,62,66,68,72,78,82,84,88,94,9..., dimensions={0} | all-to-all | bytes 65536 | tf_op jit(solution)/shard_map/cond/branch_1_fun/all_to_all | solution.py:528
  36.4 0.8 %reduce_sum.6 = f32[128]{0:T(128)S(1)} reduce(f32[64,1,128]{2,1,0:T(1,128)} %all_to_all.14, f32[]{:T(128)} %constant.3.clone), dimensions={0,1}, to_apply=%region_2.0 | reduce | flops 8064 | bytes 33284 | tf_op jit(solution)/shard_map/cond/branch_1_fun/reduce_sum | solution.py:529
  37.3 1.3 %collective-permute-start.3 = (f32[1,128]{1,0:T(1,128)S(1)}, f32[1,128]{1,0:T(1,128)S(1)}, u32[]{:S(2)}, u32[]{:S(2)}) collective-permute-start(f32[1,128]{1,0:T(1,128)S(1)} %get-tuple-element.105.stat_ref), channel_id=1, source_target_pairs={{1,0},{3,2},{5,4},{7,6},{9,8},{11,10},{13,12},{15,14},{17,16},{19,... | collective-permute-start | bytes 1544 | tf_op jit(solution)/shard_map/ppermute | solution.py:533
  38.6 0.8 %collective-permute-done.3.handed_ref = f32[1,128]{1,0:T(1,128)S(1)} collective-permute-done((f32[1,128]{1,0:T(1,128)S(1)}, f32[1,128]{1,0:T(1,128)S(1)}, u32[]{:S(2)}, u32[]{:S(2)}) %collective-permute-start.3) | collective-permute-done | bytes 544 | tf_op jit(solution)/shard_map/ppermute | solution.py:533
  39.4 0.0 collective-permute-done.4.later_ref
  39.4 0.0 copy-start.3
  39.4 0.8 copy-done.3
  40.1 0.0 copy-start.1
  40.1 2.7 %shard_map.89 = (f32[16,14,8,128]{3,2,1,0:T(8,128)S(1)}, bf16[128,1024]{1,0:T(8,128)(2,1)S(1)}, f32[16,128]{1,0:T(8,128)S(1)}, bf16[256,1152]{1,0:T(8,128)(2,1)S...) custom-call(bf16[144,128]{1,0:T(8,128)(2,1)S(1)} %get-tuple-element., ...), custom_call_target="tpu_custom_call", output_to_operand_aliasing={{3}: (8, {}), {4}: (9, {}), {5}: (10, {}), {6}: (11, {})} | custom-call | flops 452984832 | bytes 8775680 | tf_op jit(solution)/shard_map/pallas_call | solution.py:27
  42.9 0.3 collective-permute-start.5
  43.1 0.0 copy-done.1
  43.1 1.6 %shard_map.90 = (f32[1024,128]{1,0:T(8,128)S(1)}, f32[8,128]{1,0:T(8,128)S(1)}) custom-call(bf16[4,8,32,128]{3,2,1,0:T(8,128)(2,1)S(1)} %get-tuple-element.57.x_ref, f32[16,128]{1,0:T(8,128)S(1)} %get-tuple-element.86.norm_ref, f32[1,128]{1,0:T(1,128)S(1)} %get-tuple-element.80.gain_ref, f32[1,128]{1,0:T(1,128)S(1)} %get-tuple-element.81.bias_ref, ...), custom_call_target="tpu_custom_call" | custom-call | flops 452984832 | bytes 6927360 | tf_op jit(solution)/shard_map/pallas_call | solution.py:27
  44.8 0.4 collective-permute-start.6
  45.2 0.8 shard_map.91.own_ref
  46.0 0.1 collective-permute-done.6.other_sums_ref
  46.0 0.0 collective-permute-done.5.other_ref
  46.1 0.1 shard_map.92
  46.1 13.3 %all_to_all.15.in_ref = bf16[16,120,128]{2,1,0:T(8,128)(2,1)S(1)} all-to-all(bf16[16,120,128]{2,1,0:T(8,128)(2,1)S(1)} %shard_map.92), channel_id=1, replica_groups=mesh['tm'=16,'rows'=8,'sect'=2] {'tm'}, dimensions={0} | all-to-all | bytes 983040 | tf_op jit(solution)/shard_map/all_to_all | solution.py:560
  59.4 0.2 shard_map.93
  59.7 12.2 %all_to_all.16 = f16[8,120,128]{2,1,0:T(8,128)(2,1)S(1)} all-to-all(f16[8,120,128]{2,1,0:T(8,128)(2,1)S(1)} %broadcast_in_dim.5), channel_id=1, replica_groups=mesh['tm'=16,'rows'=8,'sect'=2] {'rows'}, dimensions={0} | all-to-all | bytes 491520 | tf_op jit(solution)/shard_map/all_to_all | solution.py:563
  72.0 3.6 %collective-permute-start.7 = (f32[112,128]{1,0:T(8,128)S(1)}, f32[112,128]{1,0:T(8,128)S(1)}, u32[]{:S(2)}, u32[]{:S(2)}) collective-permute-start(f32[112,128]{1,0:T(8,128)S(1)} %get-tuple-element.104.half_ref), channel_id=1, source_target_pairs={{0,1},{1,0},{2,3},{3,2},{4,5},{5,4},{6,7},{7,6},{8,9},{9,8},{10,11... | collective-permute-start | bytes 172040 | tf_op jit(solution)/shard_map/ppermute | solution.py:569
  75.6 1.0 %shard_map.95 = (bf16[4,8,32,128]{3,2,1,0:T(8,128)(2,1)}, f32[1,128]{1,0:T(1,128)}, f32[1,128]{1,0:T(1,128)}) custom-call(bf16[4,8,32,128]{3,2,1,0:T(8,128)(2,1)S(1)} %get-tuple-element.57.x_ref, f32[1024,128]{1,0:T(8,128)S(1)} %get-tuple-element.96.da_ref, f32[16,128]{1,0:T(8,128)S(1)} %get-tuple-element.86.norm_ref, ...), custom_call_target="tpu_custom_call" | custom-call | bytes 1062400 | tf_op jit(solution)/shard_map/pallas_call | solution.py:27
  76.6 0.0 collective-permute-done.7.other_ref
  76.6 0.7 shard_map.96
  (5 shorter events, 0.2 us)
Async XLA Ops:
  2.0 4.2 %collective-permute-start = (bf16[48,128]{1,0:T(8,128)(2,1)S(1)}, bf16[48,128]{1,0:T(8,128)(2,1)S(1)}, u32[]{:S(2)}, u32[]{:S(2)}) collective-permute-start(bf16[48,128]{1,0:T(8,128)(2,1)S(1)} %get-tuple-element.59), channel_id=1, source_target_pairs={{0,1},{1,0},{2,3},{3,2},{4,5},{5,4},{6,7},{7,6},{8,9},{9,8},{10,11... | collective-permute-start | bytes 36872 | tf_op jit(solution)/shard_map/ppermute | solution.py:493
  6.2 7.2 %collective-permute-start.1 = (bf16[144,128]{1,0:T(8,128)(2,1)S(1)}, bf16[144,128]{1,0:T(8,128)(2,1)S(1)}, u32[]{:S(2)}, u32[]{:S(2)}) collective-permute-start(bf16[144,128]{1,0:T(8,128)(2,1)S(1)} %get-tuple-element.64), channel_id=1, source_target_pairs={{0,2},{2,0},{4,6},{6,4},{8,10},{10,8},{12,14},{14,12},{1,3},{3,1},... | collective-permute-start | bytes 110600 | tf_op jit(solution)/shard_map/ppermute | solution.py:508
  6.3 7.1 %collective-permute-start.2 = (bf16[144,128]{1,0:T(8,128)(2,1)S(1)}, bf16[144,128]{1,0:T(8,128)(2,1)S(1)}, u32[]{:S(2)}, u32[]{:S(2)}) collective-permute-start(bf16[144,128]{1,0:T(8,128)(2,1)S(1)} %get-tuple-element.72), channel_id=1, source_target_pairs={{0,14},{2,4},{4,2},{6,8},{8,6},{10,12},{12,10},{14,0},{1,15},{3,5}... | collective-permute-start | bytes 110600 | tf_op jit(solution)/shard_map/ppermute | solution.py:509
  12.6 0.8 %copy-start = (f32[1024,128]{1,0:T(8,128)}, f32[1024,128]{1,0:T(8,128)S(1)}, u32[]{:S(2)}) copy-start(f32[1024,128]{1,0:T(8,128)S(1)} %get-tuple-element.87.part_ref) | copy-start | bytes 1572868
  14.1 0.6 copy-start.2
  14.8 24.6 %collective-permute-start.4 = (bf16[672,128]{1,0:T(8,128)(2,1)}, bf16[672,128]{1,0:T(8,128)(2,1)}, u32[]{:S(2)}, u32[]{:S(2)}) collective-permute-start(bf16[672,128]{1,0:T(8,128)(2,1)} %get-tuple-element.77), channel_id=1, source_target_pairs={{16,0},{32,16},{48,32},{64,48},{80,64},{96,80},{112,96},{128,112},... | collective-permute-start | bytes 516104 | tf_op jit(solution)/shard_map/ppermute | solution.py:525
  37.3 2.1 %collective-permute-start.3 = (f32[1,128]{1,0:T(1,128)S(1)}, f32[1,128]{1,0:T(1,128)S(1)}, u32[]{:S(2)}, u32[]{:S(2)}) collective-permute-start(f32[1,128]{1,0:T(1,128)S(1)} %get-tuple-element.105.stat_ref), channel_id=1, source_target_pairs={{1,0},{3,2},{5,4},{7,6},{9,8},{11,10},{13,12},{15,14},{17,16},{19,... | collective-permute-start | bytes 1544 | tf_op jit(solution)/shard_map/ppermute | solution.py:533
  39.4 0.8 copy-start.3
  40.1 3.0 %copy-start.1 = (f32[1024,128]{1,0:T(8,128)S(1)}, f32[1024,128]{1,0:T(8,128)}, u32[]{:S(2)}) copy-start(f32[1024,128]{1,0:T(8,128)} %copy-done) | copy-start | bytes 1572868
  42.9 3.2 %collective-permute-start.5 = (f32[16,14,8,128]{3,2,1,0:T(8,128)S(1)}, f32[16,14,8,128]{3,2,1,0:T(8,128)S(1)}, u32[]{:S(2)}, u32[]{:S(2)}) collective-permute-start(f32[16,14,8,128]{3,2,1,0:T(8,128)S(1)} %get-tuple-element.98), channel_id=1, source_target_pairs={{0,1},{1,0},{2,3},{3,2},{4,5},{5,4},{6,7},{7,6},{8,9},{9,8},{10,11... | collective-permute-start | bytes 2752520 | tf_op jit(solution)/shard_map/ppermute | solution.py:542
  44.8 1.3 %collective-permute-start.6 = (f32[8,128]{1,0:T(8,128)S(1)}, f32[8,128]{1,0:T(8,128)S(1)}, u32[]{:S(2)}, u32[]{:S(2)}) collective-permute-start(f32[8,128]{1,0:T(8,128)S(1)} %get-tuple-element.99.sums_ref), channel_id=1, source_target_pairs={{0,1},{1,0},{2,3},{3,2},{4,5},{5,4},{6,7},{7,6},{8,9},{9,8},{10,11... | collective-permute-start | bytes 12296 | tf_op jit(solution)/shard_map/ppermute | solution.py:550
  72.0 4.6 %collective-permute-start.7 = (f32[112,128]{1,0:T(8,128)S(1)}, f32[112,128]{1,0:T(8,128)S(1)}, u32[]{:S(2)}, u32[]{:S(2)}) collective-permute-start(f32[112,128]{1,0:T(8,128)S(1)} %get-tuple-element.104.half_ref), channel_id=1, source_target_pairs={{0,1},{1,0},{2,3},{3,2},{4,5},{5,4},{6,7},{7,6},{8,9},{9,8},{10,11... | collective-permute-start | bytes 172040 | tf_op jit(solution)/shard_map/ppermute | solution.py:569

commit v13 on v11

--- a/solution.py
+++ b/solution.py
@@ -316,7 +316,7 @@
     for block in range(8):
         _, pre = block_of(x_ref, norm_ref, gain_ref, bias_ref, block)
         hidden = pre * (1.0 / (1.0 + jnp.exp(-pre)))
-        turned_ref[:, block * 128 : (block + 1) * 128] = hidden.T.astype(BF16)
+        turned_ref[:, block * 128 : (block + 1) * 128] = hidden.astype(BF16).T
     left = lax.axis_index("sect") == 0
 
     @pl.when(left)

time: 73.8 us -> 73.8 us (level)
  no operation moved by 1% of the time
where the time goes in v13:
time: 73.8 us; the launch traced here: 73.6 us
  blocking collectives  46.3 us (63%)
  starting transfers between devices  16.1 us (22%)
  Pallas kernels  9.37 us (13%)
  waiting for transfers between devices  1.02 us (1%)
  between operations  0.74 us (1%)
    all_to_all x1, blocking collectives, local(): lax.all_to_all(stat[:, None], ('tm', 'rows'), 0, 0, axis_index_groups=gro...  20.2 us
    all_to_all x1, blocking collectives, local(): gathered = lax.all_to_all(sent, 'tm', 0, 0)  13.2 us
    all_to_all x1, blocking collectives, local(): shares = lax.all_to_all(share, 'rows', 0, 0).astype(F32)  12.8 us
    pallas_call x13, Pallas kernels, call(): pl.pallas_call(body, out_shape=outs, in_specs=specs or [VMEM] * len(args)...  9.37 us
    ppermute x1, starting transfers between devices, local(): farther = lax.ppermute(farther, 'rows', far)  4.55 us
    ppermute x1, starting transfers between devices, local(): other = lax.ppermute(half, 'sect', swap)  3.59 us
    ppermute x1, starting transfers between devices, local(): side = lax.ppermute(facing, 'sect', swap)  3.33 us
    ppermute x1, starting transfers between devices, local(): arrived = lax.ppermute(away, 'sect', swap)  3.16 us
  transfers between devices with their start and end apart: 7, of which 2 were waited for; matrix products, arithmetic and copies ran while one was open for 0% of the time, Pallas kernels for 7%

profile of v13, /device:TPU:1, one launch (start us, length us, event | category | flops | bytes accessed | tf_op | source)
XLA Modules:
  0.0 73.6 jit_solution(15725669648051605160)
XLA Ops:
  0.6 1.4 %shard_map.84 = (bf16[4,8,32,128]{3,2,1,0:T(8,128)(2,1)S(1)}, bf16[4,8,32,128]{3,2,1,0:T(8,128)(2,1)S(1)}, f32[1,128]{1,0:T(1,128)S(1)}, f32[1,128]{1,0:T(1,128)...) custom-call(bf16[4,8,32,128]{3,2,1,0:T(8,128)(2,1)} %up_hbm.1, ...), custom_call_target="tpu_custom_call" | custom-call | bytes 2836480 | tf_op jit(solution)/shard_map/pallas_call | solution.py:27
  2.0 3.3 %collective-permute-start = (bf16[48,128]{1,0:T(8,128)(2,1)S(1)}, bf16[48,128]{1,0:T(8,128)(2,1)S(1)}, u32[]{:S(2)}, u32[]{:S(2)}) collective-permute-start(bf16[48,128]{1,0:T(8,128)(2,1)S(1)} %get-tuple-element.39), channel_id=1, source_target_pairs={{0,1},{1,0},{2,3},{3,2},{4,5},{5,4},{6,7},{7,6},{8,9},{9,8},{10,11... | collective-permute-start | bytes 36872 | tf_op jit(solution)/shard_map/ppermute | solution.py:458
  5.4 0.2 shard_map.85
  5.6 0.6 collective-permute-done.side_ref
  6.2 0.1 collective-permute-start.1
  6.3 4.6 %collective-permute-start.2 = (bf16[144,128]{1,0:T(8,128)(2,1)S(1)}, bf16[144,128]{1,0:T(8,128)(2,1)S(1)}, u32[]{:S(2)}, u32[]{:S(2)}) collective-permute-start(bf16[144,128]{1,0:T(8,128)(2,1)S(1)} %get-tuple-element.49), channel_id=1, source_target_pairs={{0,14},{2,4},{4,2},{6,8},{8,6},{10,12},{12,10},{14,0},{1,15},{3,5}... | collective-permute-start | bytes 110600 | tf_op jit(solution)/shard_map/ppermute | solution.py:471
  10.9 1.7 %shard_map.87 = (bf16[8,256,1152]{2,1,0:T(8,128)(2,1)S(1)}, f32[1024,128]{1,0:T(8,128)S(1)}) custom-call(bf16[4,8,32,128]{3,2,1,0:T(8,128)(2,1)S(1)} %get-tuple-element.38.up_ref, bf16[48,128]{1,0:T(8,128)(2,1)S(1)} %collective-permute-done.side_ref, bf16[3,128,1152]{2,1,0:T(8,128)(2,1)S(1)} %get-tuple-element.45.taps_ref, ...), custom_call_target="tpu_custom_call", output_to_operand_aliasing={{0}: (3, {})} | custom-call | flops 452984832 | bytes 11120640 | tf_op jit(solution)/shard_map/pallas_call | solution.py:27
  12.6 0.0 collective-permute-done.1.near_ref
  12.6 0.0 collective-permute-done.2.far_ref
  12.7 1.3 %collective-permute-start.3 = (bf16[672,128]{1,0:T(8,128)(2,1)S(1)}, bf16[672,128]{1,0:T(8,128)(2,1)S(1)}, u32[]{:S(2)}, u32[]{:S(2)}) collective-permute-start(bf16[672,128]{1,0:T(8,128)(2,1)S(1)} %get-tuple-element.52), channel_id=1, source_target_pairs={{16,0},{32,16},{48,32},{64,48},{80,64},{96,80},{112,96},{128,112},... | collective-permute-start | bytes 516104 | tf_op jit(solution)/shard_map/ppermute | solution.py:487
  14.0 20.2 %all_to_all.15 = f32[64,1,128]{2,1,0:T(1,128)S(1)} all-to-all(f32[64,1,128]{2,1,0:T(1,128)S(1)} %bitcast.12), channel_id=1, replica_groups={{2,4,8,14,18,20,24,30,34,36,40,46,50,52,56,62,66,68,72,78,82,84,88,94,9..., dimensions={0} | all-to-all | bytes 65536 | tf_op jit(solution)/shard_map/all_to_all | solution.py:488
  34.2 0.0 collective-permute-done.3.later_ref
  34.2 1.5 %shard_map.89 = (f32[16,14,8,128]{3,2,1,0:T(8,128)S(1)}, bf16[128,1024]{1,0:T(8,128)(2,1)S(1)}, f32[16,128]{1,0:T(8,128)S(1)}, bf16[8,256,1152]{2,1,0:T(8,128)(2,1)S(1)}) custom-call(bf16[144,128]{1,0:T(8,128)(2,1)S(1)} %collective-permute-done.1.near_ref, bf16[144,128]{1,0:T(8,128)(2,1)S(1)} %collective-permute-done.2.far_ref, ...), custom_call_target="tpu_custom_call", output_to_operand_aliasing={{3}: (7, {})} | custom-call | flops 452984832 | bytes 11166720 | tf_op jit(solution)/shard_map/pallas_call | solution.py:27
  35.7 3.2 %collective-permute-start.4 = (f32[16,14,8,128]{3,2,1,0:T(8,128)S(1)}, f32[16,14,8,128]{3,2,1,0:T(8,128)S(1)}, u32[]{:S(2)}, u32[]{:S(2)}) collective-permute-start(f32[16,14,8,128]{3,2,1,0:T(8,128)S(1)} %get-tuple-element.63), channel_id=1, source_target_pairs={{0,1},{1,0},{2,3},{3,2},{4,5},{5,4},{6,7},{7,6},{8,9},{9,8},{10,11... | collective-permute-start | bytes 2752520 | tf_op jit(solution)/shard_map/ppermute | solution.py:502
  38.9 1.7 %shard_map.90 = (f32[1024,128]{1,0:T(8,128)S(1)}, f32[8,128]{1,0:T(8,128)S(1)}) custom-call(bf16[4,8,32,128]{3,2,1,0:T(8,128)(2,1)S(1)} %get-tuple-element.37.x_ref, f32[16,128]{1,0:T(8,128)S(1)} %get-tuple-element.58.norm_ref, f32[1,128]{1,0:T(1,128)S(1)} %get-tuple-element.55.gain_ref, f32[1,128]{1,0:T(1,128)S(1)} %get-tuple-element.56.bias_ref, ...), custom_call_target="tpu_custom_call" | custom-call | flops 452984832 | bytes 6927360 | tf_op jit(solution)/shard_map/pallas_call | solution.py:27
  40.5 0.1 collective-permute-start.5
  40.7 0.7 shard_map.91.own_ref
  41.4 0.4 collective-permute-done.5.other_sums_ref
  41.8 0.0 collective-permute-done.4.other_ref
  41.8 0.2 shard_map.92
  42.0 13.2 %all_to_all.16.in_ref = bf16[16,120,128]{2,1,0:T(8,128)(2,1)S(1)} all-to-all(bf16[16,120,128]{2,1,0:T(8,128)(2,1)S(1)} %shard_map.92), channel_id=1, replica_groups=mesh['tm'=16,'rows'=8,'sect'=2] {'tm'}, dimensions={0} | all-to-all | bytes 983040 | tf_op jit(solution)/shard_map/all_to_all | solution.py:520
  55.2 0.2 shard_map.93
  55.4 12.8 %all_to_all.17 = f16[8,120,128]{2,1,0:T(8,128)(2,1)S(1)} all-to-all(f16[8,120,128]{2,1,0:T(8,128)(2,1)S(1)} %broadcast_in_dim.10), channel_id=1, replica_groups=mesh['tm'=16,'rows'=8,'sect'=2] {'rows'}, dimensions={0} | all-to-all | bytes 491520 | tf_op jit(solution)/shard_map/all_to_all | solution.py:523
  68.3 3.6 %collective-permute-start.6 = (f32[112,128]{1,0:T(8,128)S(1)}, f32[112,128]{1,0:T(8,128)S(1)}, u32[]{:S(2)}, u32[]{:S(2)}) collective-permute-start(f32[112,128]{1,0:T(8,128)S(1)} %get-tuple-element.69.half_ref), channel_id=1, source_target_pairs={{0,1},{1,0},{2,3},{3,2},{4,5},{5,4},{6,7},{7,6},{8,9},{9,8},{10,11... | collective-permute-start | bytes 172040 | tf_op jit(solution)/shard_map/ppermute | solution.py:529
  71.9 1.0 %shard_map.95 = (bf16[4,8,32,128]{3,2,1,0:T(8,128)(2,1)}, f32[1,128]{1,0:T(1,128)}, f32[1,128]{1,0:T(1,128)}) custom-call(bf16[4,8,32,128]{3,2,1,0:T(8,128)(2,1)S(1)} %get-tuple-element.37.x_ref, f32[1024,128]{1,0:T(8,128)S(1)} %get-tuple-element.61.da_ref, f32[16,128]{1,0:T(8,128)S(1)} %get-tuple-element.58.norm_ref, ...), custom_call_target="tpu_custom_call" | custom-call | bytes 1062400 | tf_op jit(solution)/shard_map/pallas_call | solution.py:27
  72.9 0.0 collective-permute-done.6.other_ref
  72.9 0.7 shard_map.96
  (6 shorter events, 0.2 us)
Async XLA Ops:
  2.0 4.2 %collective-permute-start = (bf16[48,128]{1,0:T(8,128)(2,1)S(1)}, bf16[48,128]{1,0:T(8,128)(2,1)S(1)}, u32[]{:S(2)}, u32[]{:S(2)}) collective-permute-start(bf16[48,128]{1,0:T(8,128)(2,1)S(1)} %get-tuple-element.39), channel_id=1, source_target_pairs={{0,1},{1,0},{2,3},{3,2},{4,5},{5,4},{6,7},{7,6},{8,9},{9,8},{10,11... | collective-permute-start | bytes 36872 | tf_op jit(solution)/shard_map/ppermute | solution.py:458
  6.2 6.4 %collective-permute-start.1 = (bf16[144,128]{1,0:T(8,128)(2,1)S(1)}, bf16[144,128]{1,0:T(8,128)(2,1)S(1)}, u32[]{:S(2)}, u32[]{:S(2)}) collective-permute-start(bf16[144,128]{1,0:T(8,128)(2,1)S(1)} %get-tuple-element.44), channel_id=1, source_target_pairs={{0,2},{2,0},{4,6},{6,4},{8,10},{10,8},{12,14},{14,12},{1,3},{3,1},... | collective-permute-start | bytes 110600 | tf_op jit(solution)/shard_map/ppermute | solution.py:470
  6.3 6.3 %collective-permute-start.2 = (bf16[144,128]{1,0:T(8,128)(2,1)S(1)}, bf16[144,128]{1,0:T(8,128)(2,1)S(1)}, u32[]{:S(2)}, u32[]{:S(2)}) collective-permute-start(bf16[144,128]{1,0:T(8,128)(2,1)S(1)} %get-tuple-element.49), channel_id=1, source_target_pairs={{0,14},{2,4},{4,2},{6,8},{8,6},{10,12},{12,10},{14,0},{1,15},{3,5}... | collective-permute-start | bytes 110600 | tf_op jit(solution)/shard_map/ppermute | solution.py:471
  12.7 21.5 %collective-permute-start.3 = (bf16[672,128]{1,0:T(8,128)(2,1)S(1)}, bf16[672,128]{1,0:T(8,128)(2,1)S(1)}, u32[]{:S(2)}, u32[]{:S(2)}) collective-permute-start(bf16[672,128]{1,0:T(8,128)(2,1)S(1)} %get-tuple-element.52), channel_id=1, source_target_pairs={{16,0},{32,16},{48,32},{64,48},{80,64},{96,80},{112,96},{128,112},... | collective-permute-start | bytes 516104 | tf_op jit(solution)/shard_map/ppermute | solution.py:487
  35.7 6.1 %collective-permute-start.4 = (f32[16,14,8,128]{3,2,1,0:T(8,128)S(1)}, f32[16,14,8,128]{3,2,1,0:T(8,128)S(1)}, u32[]{:S(2)}, u32[]{:S(2)}) collective-permute-start(f32[16,14,8,128]{3,2,1,0:T(8,128)S(1)} %get-tuple-element.63), channel_id=1, source_target_pairs={{0,1},{1,0},{2,3},{3,2},{4,5},{5,4},{6,7},{7,6},{8,9},{9,8},{10,11... | collective-permute-start | bytes 2752520 | tf_op jit(solution)/shard_map/ppermute | solution.py:502
  40.5 1.3 %collective-permute-start.5 = (f32[8,128]{1,0:T(8,128)S(1)}, f32[8,128]{1,0:T(8,128)S(1)}, u32[]{:S(2)}, u32[]{:S(2)}) collective-permute-start(f32[8,128]{1,0:T(8,128)S(1)} %get-tuple-element.64.sums_ref), channel_id=1, source_target_pairs={{0,1},{1,0},{2,3},{3,2},{4,5},{5,4},{6,7},{7,6},{8,9},{9,8},{10,11... | collective-permute-start | bytes 12296 | tf_op jit(solution)/shard_map/ppermute | solution.py:510
  68.3 4.6 %collective-permute-start.6 = (f32[112,128]{1,0:T(8,128)S(1)}, f32[112,128]{1,0:T(8,128)S(1)}, u32[]{:S(2)}, u32[]{:S(2)}) collective-permute-start(f32[112,128]{1,0:T(8,128)S(1)} %get-tuple-element.69.half_ref), channel_id=1, source_target_pairs={{0,1},{1,0},{2,3},{3,2},{4,5},{5,4},{6,7},{7,6},{8,9},{9,8},{10,11... | collective-permute-start | bytes 172040 | tf_op jit(solution)/shard_map/ppermute | solution.py:529

commit v14 on v13

--- a/solution.py
+++ b/solution.py
@@ -406,8 +406,8 @@
     averages = group_total(gain * sums) / counted
     leading = averages[0:1]
     trailing = averages[1:2]
-    xhat = (x_ref[...].astype(F32).reshape(-1, 128) - mean) * rstd
-    grad = rstd * (da_ref[...] * gain - leading - xhat * trailing)
+    centred = x_ref[...].astype(F32).reshape(-1, 128) - mean
+    grad = da_ref[...] * (rstd * gain) - rstd * leading - centred * (rstd * rstd * trailing)
     out_ref[...] = grad.astype(BF16).reshape(out_ref.shape)
 
 

time: 73.8 us -> 73.8 us (level)
  no operation moved by 1% of the time
where the time goes in v14:
time: 73.8 us; the launch traced here: 73.5 us
  blocking collectives  46.3 us (63%)
  starting transfers between devices  16.1 us (22%)
  Pallas kernels  9.31 us (13%)
  waiting for transfers between devices  1.02 us (1%)
  between operations  0.74 us (1%)
    all_to_all x1, blocking collectives, local(): lax.all_to_all(stat[:, None], ('tm', 'rows'), 0, 0, axis_index_groups=gro...  20.2 us
    all_to_all x1, blocking collectives, local(): gathered = lax.all_to_all(sent, 'tm', 0, 0)  13.2 us
    all_to_all x1, blocking collectives, local(): shares = lax.all_to_all(share, 'rows', 0, 0).astype(F32)  12.8 us
    pallas_call x13, Pallas kernels, call(): pl.pallas_call(body, out_shape=outs, in_specs=specs or [VMEM] * len(args)...  9.31 us
    ppermute x1, starting transfers between devices, local(): farther = lax.ppermute(farther, 'rows', far)  4.55 us
    ppermute x1, starting transfers between devices, local(): other = lax.ppermute(half, 'sect', swap)  3.59 us
    ppermute x1, starting transfers between devices, local(): side = lax.ppermute(facing, 'sect', swap)  3.33 us
    ppermute x1, starting transfers between devices, local(): arrived = lax.ppermute(away, 'sect', swap)  3.16 us
  transfers between devices with their start and end apart: 7, of which 2 were waited for; matrix products, arithmetic and copies ran while one was open for 0% of the time, Pallas kernels for 7%

profile of v14, /device:TPU:1, one launch (start us, length us, event | category | flops | bytes accessed | tf_op | source)
XLA Modules:
  0.0 73.5 jit_solution(12064926119071202584)
XLA Ops:
  0.6 1.4 %shard_map.84 = (bf16[4,8,32,128]{3,2,1,0:T(8,128)(2,1)S(1)}, bf16[4,8,32,128]{3,2,1,0:T(8,128)(2,1)S(1)}, f32[1,128]{1,0:T(1,128)S(1)}, f32[1,128]{1,0:T(1,128)...) custom-call(bf16[4,8,32,128]{3,2,1,0:T(8,128)(2,1)} %up_hbm.1, ...), custom_call_target="tpu_custom_call" | custom-call | bytes 2836480 | tf_op jit(solution)/shard_map/pallas_call | solution.py:27
  2.0 3.3 %collective-permute-start = (bf16[48,128]{1,0:T(8,128)(2,1)S(1)}, bf16[48,128]{1,0:T(8,128)(2,1)S(1)}, u32[]{:S(2)}, u32[]{:S(2)}) collective-permute-start(bf16[48,128]{1,0:T(8,128)(2,1)S(1)} %get-tuple-element.39), channel_id=1, source_target_pairs={{0,1},{1,0},{2,3},{3,2},{4,5},{5,4},{6,7},{7,6},{8,9},{9,8},{10,11... | collective-permute-start | bytes 36872 | tf_op jit(solution)/shard_map/ppermute | solution.py:458
  5.4 0.2 shard_map.85
  5.6 0.6 collective-permute-done.side_ref
  6.2 0.1 collective-permute-start.1
  6.3 4.6 %collective-permute-start.2 = (bf16[144,128]{1,0:T(8,128)(2,1)S(1)}, bf16[144,128]{1,0:T(8,128)(2,1)S(1)}, u32[]{:S(2)}, u32[]{:S(2)}) collective-permute-start(bf16[144,128]{1,0:T(8,128)(2,1)S(1)} %get-tuple-element.49), channel_id=1, source_target_pairs={{0,14},{2,4},{4,2},{6,8},{8,6},{10,12},{12,10},{14,0},{1,15},{3,5}... | collective-permute-start | bytes 110600 | tf_op jit(solution)/shard_map/ppermute | solution.py:471
  10.9 1.7 %shard_map.87 = (bf16[8,256,1152]{2,1,0:T(8,128)(2,1)S(1)}, f32[1024,128]{1,0:T(8,128)S(1)}) custom-call(bf16[4,8,32,128]{3,2,1,0:T(8,128)(2,1)S(1)} %get-tuple-element.38.up_ref, bf16[48,128]{1,0:T(8,128)(2,1)S(1)} %collective-permute-done.side_ref, bf16[3,128,1152]{2,1,0:T(8,128)(2,1)S(1)} %get-tuple-element.45.taps_ref, ...), custom_call_target="tpu_custom_call", output_to_operand_aliasing={{0}: (3, {})} | custom-call | flops 452984832 | bytes 11120640 | tf_op jit(solution)/shard_map/pallas_call | solution.py:27
  12.6 0.0 collective-permute-done.1.near_ref
  12.6 0.0 collective-permute-done.2.far_ref
  12.7 1.3 %collective-permute-start.3 = (bf16[672,128]{1,0:T(8,128)(2,1)S(1)}, bf16[672,128]{1,0:T(8,128)(2,1)S(1)}, u32[]{:S(2)}, u32[]{:S(2)}) collective-permute-start(bf16[672,128]{1,0:T(8,128)(2,1)S(1)} %get-tuple-element.52), channel_id=1, source_target_pairs={{16,0},{32,16},{48,32},{64,48},{80,64},{96,80},{112,96},{128,112},... | collective-permute-start | bytes 516104 | tf_op jit(solution)/shard_map/ppermute | solution.py:487
  14.0 20.2 %all_to_all.15 = f32[64,1,128]{2,1,0:T(1,128)S(1)} all-to-all(f32[64,1,128]{2,1,0:T(1,128)S(1)} %bitcast.12), channel_id=1, replica_groups={{2,4,8,14,18,20,24,30,34,36,40,46,50,52,56,62,66,68,72,78,82,84,88,94,9..., dimensions={0} | all-to-all | bytes 65536 | tf_op jit(solution)/shard_map/all_to_all | solution.py:488
  34.2 0.0 collective-permute-done.3.later_ref
  34.2 1.5 %shard_map.89 = (f32[16,14,8,128]{3,2,1,0:T(8,128)S(1)}, bf16[128,1024]{1,0:T(8,128)(2,1)S(1)}, f32[16,128]{1,0:T(8,128)S(1)}, bf16[8,256,1152]{2,1,0:T(8,128)(2,1)S(1)}) custom-call(bf16[144,128]{1,0:T(8,128)(2,1)S(1)} %collective-permute-done.1.near_ref, bf16[144,128]{1,0:T(8,128)(2,1)S(1)} %collective-permute-done.2.far_ref, ...), custom_call_target="tpu_custom_call", output_to_operand_aliasing={{3}: (7, {})} | custom-call | flops 452984832 | bytes 11166720 | tf_op jit(solution)/shard_map/pallas_call | solution.py:27
  35.7 3.2 %collective-permute-start.4 = (f32[16,14,8,128]{3,2,1,0:T(8,128)S(1)}, f32[16,14,8,128]{3,2,1,0:T(8,128)S(1)}, u32[]{:S(2)}, u32[]{:S(2)}) collective-permute-start(f32[16,14,8,128]{3,2,1,0:T(8,128)S(1)} %get-tuple-element.63), channel_id=1, source_target_pairs={{0,1},{1,0},{2,3},{3,2},{4,5},{5,4},{6,7},{7,6},{8,9},{9,8},{10,11... | collective-permute-start | bytes 2752520 | tf_op jit(solution)/shard_map/ppermute | solution.py:502
  38.9 1.7 %shard_map.90 = (f32[1024,128]{1,0:T(8,128)S(1)}, f32[8,128]{1,0:T(8,128)S(1)}) custom-call(bf16[4,8,32,128]{3,2,1,0:T(8,128)(2,1)S(1)} %get-tuple-element.37.x_ref, f32[16,128]{1,0:T(8,128)S(1)} %get-tuple-element.58.norm_ref, f32[1,128]{1,0:T(1,128)S(1)} %get-tuple-element.55.gain_ref, f32[1,128]{1,0:T(1,128)S(1)} %get-tuple-element.56.bias_ref, ...), custom_call_target="tpu_custom_call" | custom-call | flops 452984832 | bytes 6927360 | tf_op jit(solution)/shard_map/pallas_call | solution.py:27
  40.5 0.1 collective-permute-start.5
  40.7 0.7 shard_map.91.own_ref
  41.4 0.4 collective-permute-done.5.other_sums_ref
  41.8 0.0 collective-permute-done.4.other_ref
  41.8 0.2 shard_map.92
  42.0 13.2 %all_to_all.16.in_ref = bf16[16,120,128]{2,1,0:T(8,128)(2,1)S(1)} all-to-all(bf16[16,120,128]{2,1,0:T(8,128)(2,1)S(1)} %shard_map.92), channel_id=1, replica_groups=mesh['tm'=16,'rows'=8,'sect'=2] {'tm'}, dimensions={0} | all-to-all | bytes 983040 | tf_op jit(solution)/shard_map/all_to_all | solution.py:520
  55.2 0.2 shard_map.93
  55.4 12.8 %all_to_all.17 = f16[8,120,128]{2,1,0:T(8,128)(2,1)S(1)} all-to-all(f16[8,120,128]{2,1,0:T(8,128)(2,1)S(1)} %broadcast_in_dim.10), channel_id=1, replica_groups=mesh['tm'=16,'rows'=8,'sect'=2] {'rows'}, dimensions={0} | all-to-all | bytes 491520 | tf_op jit(solution)/shard_map/all_to_all | solution.py:523
  68.3 3.6 %collective-permute-start.6 = (f32[112,128]{1,0:T(8,128)S(1)}, f32[112,128]{1,0:T(8,128)S(1)}, u32[]{:S(2)}, u32[]{:S(2)}) collective-permute-start(f32[112,128]{1,0:T(8,128)S(1)} %get-tuple-element.69.half_ref), channel_id=1, source_target_pairs={{0,1},{1,0},{2,3},{3,2},{4,5},{5,4},{6,7},{7,6},{8,9},{9,8},{10,11... | collective-permute-start | bytes 172040 | tf_op jit(solution)/shard_map/ppermute | solution.py:529
  71.9 0.9 %shard_map.95 = (bf16[4,8,32,128]{3,2,1,0:T(8,128)(2,1)}, f32[1,128]{1,0:T(1,128)}, f32[1,128]{1,0:T(1,128)}) custom-call(bf16[4,8,32,128]{3,2,1,0:T(8,128)(2,1)S(1)} %get-tuple-element.37.x_ref, f32[1024,128]{1,0:T(8,128)S(1)} %get-tuple-element.61.da_ref, f32[16,128]{1,0:T(8,128)S(1)} %get-tuple-element.58.norm_ref, ...), custom_call_target="tpu_custom_call" | custom-call | bytes 1062400 | tf_op jit(solution)/shard_map/pallas_call | solution.py:27
  72.9 0.0 collective-permute-done.6.other_ref
  72.9 0.7 shard_map.96
  (6 shorter events, 0.2 us)
Async XLA Ops:
  2.0 4.2 %collective-permute-start = (bf16[48,128]{1,0:T(8,128)(2,1)S(1)}, bf16[48,128]{1,0:T(8,128)(2,1)S(1)}, u32[]{:S(2)}, u32[]{:S(2)}) collective-permute-start(bf16[48,128]{1,0:T(8,128)(2,1)S(1)} %get-tuple-element.39), channel_id=1, source_target_pairs={{0,1},{1,0},{2,3},{3,2},{4,5},{5,4},{6,7},{7,6},{8,9},{9,8},{10,11... | collective-permute-start | bytes 36872 | tf_op jit(solution)/shard_map/ppermute | solution.py:458
  6.2 6.4 %collective-permute-start.1 = (bf16[144,128]{1,0:T(8,128)(2,1)S(1)}, bf16[144,128]{1,0:T(8,128)(2,1)S(1)}, u32[]{:S(2)}, u32[]{:S(2)}) collective-permute-start(bf16[144,128]{1,0:T(8,128)(2,1)S(1)} %get-tuple-element.44), channel_id=1, source_target_pairs={{0,2},{2,0},{4,6},{6,4},{8,10},{10,8},{12,14},{14,12},{1,3},{3,1},... | collective-permute-start | bytes 110600 | tf_op jit(solution)/shard_map/ppermute | solution.py:470
  6.3 6.3 %collective-permute-start.2 = (bf16[144,128]{1,0:T(8,128)(2,1)S(1)}, bf16[144,128]{1,0:T(8,128)(2,1)S(1)}, u32[]{:S(2)}, u32[]{:S(2)}) collective-permute-start(bf16[144,128]{1,0:T(8,128)(2,1)S(1)} %get-tuple-element.49), channel_id=1, source_target_pairs={{0,14},{2,4},{4,2},{6,8},{8,6},{10,12},{12,10},{14,0},{1,15},{3,5}... | collective-permute-start | bytes 110600 | tf_op jit(solution)/shard_map/ppermute | solution.py:471
  12.7 21.5 %collective-permute-start.3 = (bf16[672,128]{1,0:T(8,128)(2,1)S(1)}, bf16[672,128]{1,0:T(8,128)(2,1)S(1)}, u32[]{:S(2)}, u32[]{:S(2)}) collective-permute-start(bf16[672,128]{1,0:T(8,128)(2,1)S(1)} %get-tuple-element.52), channel_id=1, source_target_pairs={{16,0},{32,16},{48,32},{64,48},{80,64},{96,80},{112,96},{128,112},... | collective-permute-start | bytes 516104 | tf_op jit(solution)/shard_map/ppermute | solution.py:487
  35.7 6.1 %collective-permute-start.4 = (f32[16,14,8,128]{3,2,1,0:T(8,128)S(1)}, f32[16,14,8,128]{3,2,1,0:T(8,128)S(1)}, u32[]{:S(2)}, u32[]{:S(2)}) collective-permute-start(f32[16,14,8,128]{3,2,1,0:T(8,128)S(1)} %get-tuple-element.63), channel_id=1, source_target_pairs={{0,1},{1,0},{2,3},{3,2},{4,5},{5,4},{6,7},{7,6},{8,9},{9,8},{10,11... | collective-permute-start | bytes 2752520 | tf_op jit(solution)/shard_map/ppermute | solution.py:502
  40.5 1.3 %collective-permute-start.5 = (f32[8,128]{1,0:T(8,128)S(1)}, f32[8,128]{1,0:T(8,128)S(1)}, u32[]{:S(2)}, u32[]{:S(2)}) collective-permute-start(f32[8,128]{1,0:T(8,128)S(1)} %get-tuple-element.64.sums_ref), channel_id=1, source_target_pairs={{0,1},{1,0},{2,3},{3,2},{4,5},{5,4},{6,7},{7,6},{8,9},{9,8},{10,11... | collective-permute-start | bytes 12296 | tf_op jit(solution)/shard_map/ppermute | solution.py:510
  68.3 4.5 %collective-permute-start.6 = (f32[112,128]{1,0:T(8,128)S(1)}, f32[112,128]{1,0:T(8,128)S(1)}, u32[]{:S(2)}, u32[]{:S(2)}) collective-permute-start(f32[112,128]{1,0:T(8,128)S(1)} %get-tuple-element.69.half_ref), channel_id=1, source_target_pairs={{0,1},{1,0},{2,3},{3,2},{4,5},{5,4},{6,7},{7,6},{8,9},{9,8},{10,11... | collective-permute-start | bytes 172040 | tf_op jit(solution)/shard_map/ppermute | solution.py:529
